TPU v7x, 128 devices: a whole 4x4x4 slice. The times are simulated.
128 devices in a mesh: row: 16 (over x, y), col: 8 (over z, core).
Axes of the slice: x: 4, y: 4, z: 4, core: 2. Of those that a mesh axis runs over, the one named last changes fastest.
Arguments:
- parent_front: float32 [16384, 16384], P('row', 'col'), may hold values from -3 to 169.6, as said below
- children: float32 [20480, 10240], P('row', 'col'), may hold values from -1 to 1, as said below
- child_map: int32 [2, 80], replicated, may hold values from 0 to 127, as said below
- fill: int32 [2, 80, 80], replicated, may hold values from 0 to 1, as said below
Outputs:
- factored_front: float32 [16384, 16384], P('row', 'col')
Inputs may be any that keep to these rules, and one draw needn't show every extreme that they name: `parent_front`: Symmetric. Together with the children's terms, its leading block of order 2 * 512 is positive definite. `children`: each child's block of 10240 rows is symmetric. `child_map`: each row maps the 80 blocks of one child to distinct parent blocks. Child blocks a, b with a // 10 == b // 10 share one run of 16 parent blocks (parent block // 16) at most 2 times and one run of 8 parent blocks at most 1 times; both bounds are reached in every draw. Each child maps exactly 10 blocks into each run of 16 parent blocks. `fill`: symmetric in its last two dimensions, with ones on the diagonal.
All inputs are finite; a program needn't handle non-finite values.
Results may differ from a plain program's by a relative error of at most 0.00011.
Values sent between devices are 32-bit elements; how exact they have to be, the bound alone decides.
No kernel may reach another device: no remote copies, remote signals or barrier semaphores. Data moves between devices by JAX's collectives and lax.ppermute only.
A program may use at most 192 MiB of HBM per device.

v0:
```python
import jax
import jax.numpy as jnp
from jax import lax
from jax.sharding import PartitionSpec as P

BLOCK = 128
PANEL = 512
PANELS = 2


def broadcast(block, axis, holder):
    block = jnp.where(lax.axis_index(axis) == holder, block, jnp.zeros_like(block))
    return lax.psum(block, axis)


def earlier_count(keys):
    places = jnp.arange(keys.shape[0], dtype=jnp.int32)
    matches = keys[:, None] == keys[None, :]
    before = places[None, :] < places[:, None]
    return jnp.sum((matches & before).astype(jnp.int32), axis=1)


def invert_codes(codes, values, length, default):
    hits = codes[:, None] == jnp.arange(length, dtype=jnp.int32)[None, :]
    found = jnp.sum(jnp.where(hits, values[:, None], 0), axis=0)
    return jnp.where(jnp.any(hits, axis=0), found, default)


def describe(mapping, group_size, row_count, col_count, blocks_row, blocks_col):
    places = jnp.arange(mapping.shape[0], dtype=jnp.int32)
    groups_of = places // group_size
    dest_col = mapping // blocks_col
    slot_col = earlier_count(groups_of * col_count + dest_col)
    dest_row = mapping // blocks_row
    slot_row = earlier_count(groups_of * row_count + dest_row)
    return (groups_of, dest_col, slot_col, dest_row, slot_row)


def body(parent_front, children, child_map, fill):
    row_count = lax.axis_size("row")
    col_count = lax.axis_size("col")
    half_rows = row_count // 2
    tile_rows, tile_cols = parent_front.shape
    group_size = child_map.shape[1] // col_count
    cap_cols = -(-group_size // col_count)
    cap_rows = -(-cap_cols // 2)
    blocks_row = tile_rows // BLOCK
    blocks_col = tile_cols // BLOCK
    row_index = lax.axis_index("row")
    col_index = lax.axis_index("col")
    child_id = row_index // half_rows
    group_row = row_index % half_rows
    own_map = lax.dynamic_index_in_dim(child_map, child_id, 0, keepdims=False)
    own_fill = lax.dynamic_index_in_dim(fill, child_id, 0, keepdims=False)
    tile_fill = lax.dynamic_slice(
        own_fill, (group_row * group_size, col_index * group_size), (group_size, group_size)
    )
    weights = tile_fill.astype(jnp.float32)
    masked = children.reshape(group_size, BLOCK, group_size, BLOCK) * weights[:, None, :, None]
    groups_of, dest_col, slot_col, dest_row, slot_row = describe(
        own_map, group_size, row_count, col_count, blocks_row, blocks_col
    )
    places = jnp.arange(groups_of.shape[0], dtype=jnp.int32)
    in_cols = groups_of == col_index
    table_cols = invert_codes(
        jnp.where(in_cols, dest_col * cap_cols + slot_col, col_count * cap_cols),
        places - col_index * group_size,
        col_count * cap_cols,
        group_size,
    )
    in_rows = groups_of == group_row
    table_rows = invert_codes(
        jnp.where(in_rows, dest_row * cap_rows + slot_row, row_count * cap_rows),
        places - group_row * group_size,
        row_count * cap_rows,
        group_size,
    )
    padded = jnp.pad(masked, ((0, 0), (0, 0), (0, 1), (0, 0)))
    outgoing = jnp.take(padded, table_cols, axis=2).reshape(
        group_size * BLOCK, col_count * cap_cols * BLOCK
    )
    incoming = lax.all_to_all(outgoing, "col", split_axis=1, concat_axis=1, tiled=True)
    in_range = dest_col == col_index
    order = earlier_count(jnp.where(in_range, 0, 1))
    compact_table = invert_codes(
        jnp.where(in_range, order, group_size), groups_of * cap_cols + slot_col, group_size, 0
    )
    compact = jnp.take(
        incoming.reshape(group_size * BLOCK, col_count * cap_cols, BLOCK), compact_table, axis=1
    )
    compact = jnp.pad(
        compact.reshape(group_size, BLOCK, group_size * BLOCK), ((0, 1), (0, 0), (0, 0))
    )
    outgoing_rows = jnp.take(compact, table_rows, axis=0).reshape(
        row_count * cap_rows * BLOCK, group_size * BLOCK
    )
    incoming_rows = lax.all_to_all(outgoing_rows, "row", split_axis=0, concat_axis=0, tiled=True)
    arrived = incoming_rows.reshape(row_count * cap_rows, BLOCK, group_size, BLOCK)
    arrived = jnp.pad(arrived, ((0, 1), (0, 0), (0, 1), (0, 0)))
    current = parent_front
    for source_child in range(2):
        mapping = child_map[source_child]
        groups_src, dest_col_src, slot_col_src, dest_row_src, slot_row_src = describe(
            mapping, group_size, row_count, col_count, blocks_row, blocks_col
        )
        row_codes = jnp.where(
            dest_row_src == row_index, mapping - row_index * blocks_row, blocks_row
        )
        row_values = (source_child * half_rows + groups_src) * cap_rows + slot_row_src
        row_table = invert_codes(row_codes, row_values, blocks_row, row_count * cap_rows)
        in_range_src = dest_col_src == col_index
        col_values = earlier_count(jnp.where(in_range_src, 0, 1))
        col_codes = jnp.where(in_range_src, mapping - col_index * blocks_col, blocks_col)
        col_table = invert_codes(col_codes, col_values, blocks_col, group_size)
        placed = jnp.take(jnp.take(arrived, row_table, axis=0), col_table, axis=2)
        current = current + placed.reshape(tile_rows, tile_cols)
    global_rows = row_index * tile_rows + jnp.arange(tile_rows, dtype=jnp.int32)
    span = row_count // col_count
    for panel_step in range(PANELS):
        first_col = panel_step * PANEL
        local_cols = current[:, first_col : first_col + PANEL]
        panel_cols = broadcast(local_cols, "col", 0)
        low_row = max(first_col, 0)
        high_row = min(first_col + PANEL, tile_rows)
        pieces = broadcast(panel_cols[low_row:high_row], "row", 0)
        factor = jnp.linalg.cholesky(pieces)
        solved = lax.linalg.triangular_solve(
            factor, panel_cols, left_side=False, lower=True, transpose_a=True
        )
        panel_vals = jnp.where((global_rows >= first_col)[:, None], solved, 0.0)
        parts = []
        for offset in range(span):
            parts.append(broadcast(panel_vals, "row", col_index * span + offset))
        col_vals = jnp.concatenate(parts, axis=0)
        update = lax.dot_general(
            panel_vals,
            col_vals,
            (((1,), (1,)), ((), ())),
            precision=lax.Precision.HIGHEST,
            preferred_element_type=jnp.float32,
        )
        current = current - update
        kept = jnp.where(col_index == 0, panel_vals, current[:, first_col : first_col + PANEL])
        current = current.at[:, first_col : first_col + PANEL].set(kept)
    return current


def solution(mesh):
    in_specs = (P("row", "col"), P("row", "col"), P(), P())
    out_specs = P("row", "col")
    return jax.shard_map(body, mesh=mesh, in_specs=in_specs, out_specs=out_specs, check_vma=False)
```

profile of v0, /device:TPU:21, one launch (start us, length us, event | category | flops | bytes accessed | tf_op | source)
XLA Modules:
  0.0 1473.2 jit_solution(10244073185987762475)
XLA Ops:
  6.5 8.7 reshape.594
  17.0 7.2 copy_multiply_fusion
  24.2 3.6 pad.17
  27.9 8.1 gather_fusion
  36.0 14.5 copy.70
  50.4 12.4 gather.26
  63.1 4.4 broadcast_select_fusion.1
  67.5 7.0 copy.71
  74.5 6.0 all-to-all-start
  81.1 115.6 %all-to-all-done = f32[1280,8,256]{2,0,1:T(8,128)} async-done(((f32[1280,8,256]{2,0,1:T(8,128)}), f32[1280,8,256]{2,0,1:T(8,128)}, u32[]{:S(2)}, u32[]{:S(2)}) %all-to-all-start) | async-done | bytes 10485792 | tf_op jit(solution)/shard_map/all_to_all | solution.py:82
  196.7 11.2 copy.72
  207.9 11.3 copy.73
  219.2 7.7 gather_fusion.1
  226.9 13.0 copy.74
  240.0 9.1 gather.28
  249.1 3.4 broadcast_select_fusion.2
  252.5 3.6 pad.18
  256.1 8.2 gather_fusion.2
  264.4 9.1 broadcast_select_fusion
  273.4 6.7 all-to-all-start.1
  280.1 18.2 %copy.78 = f32[1024,2048]{0,1:T(8,128)} copy(f32[1024,2048]{1,0:T(8,128)} %param.15) | data formatting | bytes 16777216 | tf_op args[0]
  300.2 165.8 %all-to-all-done.1 = f32[16,128,1280]{2,1,0:T(8,128)} async-done(((f32[16,128,1280]{2,1,0:T(8,128)}), f32[16,128,1280]{2,1,0:T(8,128)}, u32[]{:S(2)}, u32[]{:S(2)}) %all-to-all-start.1) | async-done | bytes 10485792 | tf_op jit(solution)/shard_map/all_to_all | solution.py:97
  466.0 11.3 copy.75
  477.3 11.2 copy.76
  488.5 10.3 pad.19
  498.8 7.9 gather_fusion.3
  506.7 6.3 broadcast_select_fusion.4
  513.0 7.1 gather_fusion.4
  520.1 8.6 select_bitcast_fusion.1
  528.7 9.3 copy.77
  537.9 7.9 gather_fusion.5
  545.9 6.2 broadcast_select_fusion.3
  552.0 7.1 gather_fusion.6
  559.2 8.6 select_bitcast_fusion
  567.7 9.3 copy.79
  577.0 11.5 bitcast_add_fusion
  593.4 66.4 %all-reduce.13.cloned.1.call-done = f32[1024,512]{0,1:T(8,128)} async-done(((f32[1024,512]{0,1:T(8,128)}), f32[1024,512]{0,1:T(8,128)}) %all-reduce.13.cloned.1.call-update) | async-done | bytes 2097168 | tf_op jit(solution)/shard_map/psum | solution.py:13
  662.7 84.7 %all-reduce.15.cloned.1.call-done = f32[512,512]{0,1:T(8,128)} async-done(((f32[512,512]{0,1:T(8,128)}), f32[512,512]{0,1:T(8,128)}) %all-reduce.15.cloned.1.call-update) | async-done | bytes 1048592 | tf_op jit(solution)/shard_map/psum | solution.py:13
  749.3 11.7 cholesky.286
  761.2 9.8 custom-call.27
  771.7 11.7 cholesky.305
  784.7 9.9 custom-call.28
  796.2 11.7 cholesky.326
  808.6 9.8 custom-call.29
  819.9 11.7 cholesky.343
  836.2 11.8 while.6
  848.0 39.3 %custom-call.30 = f32[4,128,128]{1,2,0:T(8,128)S(1)} custom-call(f32[4,128,128]{2,1,0:T(8,128)S(1)} %get-tuple-element.47), custom_call_target="InvertDiagBlocksLowerTriangular" | custom-call | tf_op jit(solution)/shard_map/triangular_solve/custom-call.3 | solution.py:127
  898.5 104.7 %all-reduce.23.cloned.1.call-done = (f32[1024,512]{0,1:T(8,128)}, f32[1024,512]{0,1:T(8,128)}) async-done(((f32[1024,512]{0,1:T(8,128)}, f32[1024,512]{0,1:T(8,128)}), (f32[1024,512]{0,1:T(8,128)}, f32[1024,512]{0,1:T(8,128)})) %all-reduce.23.cloned.1.call-update) | async-done | bytes 4194320 | tf_op jit(solution)/shard_map/psum | solution.py:13
  1003.1 17.0 %fusion.11 = f32[1024,2048]{0,1:T(8,128)S(1)} fusion(f32[1024,2048]{0,1:T(8,128)} %copy-done.1, f32[1024,512]{0,1:T(8,128)} %get-tuple-element.67, f32[1024,512]{0,1:T(8,128)} %get-tuple-element.68, f32[1024,128]{0,1:T(8,128)S(1)} %fusion.68, f32[1024,128]{0,1:T(8,128)S(1)} %fusion.69, f32[1024,128]{0,1:T(8,128)S(1)} %fusion.70, ...), kind=kOutput, calls=%fused_computation.27 | convolution fusion | flops 12890144768 | bytes 23069696 | tf_op jit(solution)/shard_map/dot_general | solution.py:135
  1026.4 65.4 %all-reduce.17.cloned.1.call-done = f32[1024,512]{0,1:T(8,128)} async-done(((f32[1024,512]{0,1:T(8,128)}), f32[1024,512]{0,1:T(8,128)}) %all-reduce.17.cloned.1.call-update) | async-done | bytes 2097168 | tf_op jit(solution)/shard_map/psum | solution.py:13
  1094.4 84.8 %all-reduce.19.cloned.1.call-done = f32[512,512]{0,1:T(8,128)} async-done(((f32[512,512]{0,1:T(8,128)}), f32[512,512]{0,1:T(8,128)}) %all-reduce.19.cloned.1.call-update) | async-done | bytes 1048592 | tf_op jit(solution)/shard_map/psum | solution.py:13
  1181.1 11.7 cholesky.358
  1193.0 9.8 custom-call.31
  1203.5 11.7 cholesky.377
  1216.5 10.2 custom-call.32
  1228.3 11.7 cholesky.398
  1240.7 9.8 custom-call.33
  1251.9 11.7 cholesky.415
  1268.1 11.9 while.7
  1280.0 39.3 %custom-call.34 = f32[4,128,128]{1,2,0:T(8,128)S(1)} custom-call(f32[4,128,128]{2,1,0:T(8,128)S(1)} %get-tuple-element.48), custom_call_target="InvertDiagBlocksLowerTriangular" | custom-call | tf_op jit(solution)/shard_map/triangular_solve/custom-call.3 | solution.py:127
  1330.5 104.7 %all-reduce.21.cloned.1.call-done = (f32[1024,512]{0,1:T(8,128)}, f32[1024,512]{0,1:T(8,128)}) async-done(((f32[1024,512]{0,1:T(8,128)}, f32[1024,512]{0,1:T(8,128)}), (f32[1024,512]{0,1:T(8,128)}, f32[1024,512]{0,1:T(8,128)})) %all-reduce.21.cloned.1.call-update) | async-done | bytes 4194320 | tf_op jit(solution)/shard_map/psum | solution.py:13
  1435.1 17.9 %fusion.8 = f32[1024,2048]{0,1:T(8,128)} fusion(f32[1024,2048]{0,1:T(8,128)} %copy-done, f32[1024,512]{0,1:T(8,128)} %get-tuple-element.65, f32[1024,512]{0,1:T(8,128)} %get-tuple-element.66, f32[1024,128]{0,1:T(8,128)S(1)} %fusion.62, f32[1024,128]{0,1:T(8,128)S(1)} %fusion.63, f32[1024,128]{0,1:T(8,128)S(1)} %fusion.64, f32[1024,128]{0,1:T(8,128)S(1)} %bitcast.220, ...), kind=kOutput, calls=%fused_computation.26 | convolution fusion | flops 12890144768 | bytes 23069696 | tf_op jit(solution)/shard_map/dot_general | solution.py:135
  1453.0 4.0 fusion.15
  1457.1 9.1 copy.90
  (179 shorter events, 86.0 us)
Async XLA Ops:
  6.5 8.8 copy-start.8
  74.5 122.2 %all-to-all-start = ((f32[1280,8,256]{2,0,1:T(8,128)}), f32[1280,8,256]{2,0,1:T(8,128)}, u32[]{:S(2)}, u32[]{:S(2)}) async-start(f32[1280,8,256]{2,0,1:T(8,128)} %copy.71), calls=%async_computation | async-start | bytes 20971520 | tf_op jit(solution)/shard_map/all_to_all | solution.py:82
  273.4 192.6 %all-to-all-start.1 = ((f32[16,128,1280]{2,1,0:T(8,128)}), f32[16,128,1280]{2,1,0:T(8,128)}, u32[]{:S(2)}, u32[]{:S(2)}) async-start(f32[16,128,1280]{2,1,0:T(8,128)} %broadcast_select_fusion), calls=%async_computation.1 | async-start | bytes 20971520 | tf_op jit(solution)/shard_map/all_to_all | solution.py:97
  280.1 379.8 %all-reduce.13.cloned.1.call-start = ((), (), s32[]{:S(2)}) async-start(), calls=%async_computation.2 | async-start | bytes 4194304 | tf_op jit(solution)/shard_map/psum | solution.py:13
  588.5 3.4 copy-start.1
  593.4 154.0 %all-reduce.15.cloned.1.call-start = ((), (), s32[]{:S(2)}) async-start(), calls=%async_computation.3 | async-start | bytes 2097152 | tf_op jit(solution)/shard_map/psum | solution.py:13
  662.2 341.0 %all-reduce.23.cloned.1.call-start = ((), (), s32[]{:S(2)}) async-start(), calls=%async_computation.7 | async-start | bytes 8388608 | tf_op jit(solution)/shard_map/psum | solution.py:13
  747.4 1.7 copy-start.4
  749.3 34.1 %copy-start.6 = (f32[512,512]{1,0:T(8,128)}, f32[512,512]{1,0:T(8,128)S(1)}, u32[]{:S(2)}) copy-start(f32[512,512]{1,0:T(8,128)S(1)} %fusion.41) | copy-start | bytes 3145732
  783.4 103.9 %copy-start.2 = (f32[1024,512]{0,1:T(8,128)S(1)}, f32[1024,512]{0,1:T(8,128)}, u32[]{:S(2)}) copy-start(f32[1024,512]{0,1:T(8,128)} %all-reduce.13.cloned.1.call-done) | copy-start | bytes 6291460
  897.8 194.1 %all-reduce.17.cloned.1.call-start = ((), (), s32[]{:S(2)}) async-start(), calls=%async_computation.4 | async-start | bytes 4194304 | tf_op jit(solution)/shard_map/psum | solution.py:13
  1021.4 3.4 copy-start
  1026.4 152.8 %all-reduce.19.cloned.1.call-start = ((), (), s32[]{:S(2)}) async-start(), calls=%async_computation.5 | async-start | bytes 2097152 | tf_op jit(solution)/shard_map/psum | solution.py:13
  1094.2 341.0 %all-reduce.21.cloned.1.call-start = ((), (), s32[]{:S(2)}) async-start(), calls=%async_computation.6 | async-start | bytes 8388608 | tf_op jit(solution)/shard_map/psum | solution.py:13
  1179.2 1.7 copy-start.5
  1181.1 34.1 %copy-start.7 = (f32[512,512]{1,0:T(8,128)}, f32[512,512]{1,0:T(8,128)S(1)}, u32[]{:S(2)}) copy-start(f32[512,512]{1,0:T(8,128)S(1)} %fusion.40) | copy-start | bytes 3145732
  1215.2 104.1 %copy-start.3 = (f32[1024,512]{0,1:T(8,128)S(1)}, f32[1024,512]{0,1:T(8,128)}, u32[]{:S(2)}) copy-start(f32[1024,512]{0,1:T(8,128)} %all-reduce.17.cloned.1.call-done) | copy-start | bytes 6291460
Sparse Core Ops, SparseCore 0:
  593.5 66.3 all-reduce.12
  663.1 84.2 all-reduce.14
  897.9 105.2 all-reduce.22
  1026.5 65.2 all-reduce.16
  1094.9 84.2 all-reduce.18
  1329.9 105.2 all-reduce.20
where the time goes:
time: 1490 us; the launch traced here: 1470 us
  waiting for transfers between devices  792 us (53%)
  other arithmetic  329 us (22%)
  local copies, waits for them, and re-layouts  262 us (18%)
  matrix products  57.9 us (4%)
  between operations  19.3 us (1%)
    psum x6, waiting for transfers between devices, broadcast(): return lax.psum(block, axis)  511 us
    all_to_all x1, waiting for transfers between devices, body(): lax.all_to_all(outgoing_rows, 'row', split_axis=0, concat_axis=0, tiled=T...  166 us
    another operation x30, other arithmetic, body(): factor = jnp.linalg.cholesky(pieces)  159 us
    all_to_all x1, waiting for transfers between devices, body(): lax.all_to_all(outgoing, 'col', split_axis=1, concat_axis=1, tiled=True)  116 us
    another operation x5, other arithmetic, body(): lax.linalg.triangular_solve(factor, panel_cols, left_side=False, lower=Tr...  81.4 us
    dot_general x2, matrix products, body(): lax.dot_general(panel_vals, col_vals, (((1,), (1,)), ((), ())), precision...  34.9 us
    gather x3, local copies, waits for them, and re-layouts, body(): jnp.take(padded, table_cols, axis=2)  34.9 us
    gather x4, local copies, waits for them, and re-layouts, body(): placed = jnp.take(jnp.take(arrived, row_table, axis=0), col_table, axis=2)  30.1 us
  transfers between devices with their start and end apart: 8, of which 8 were waited for; matrix products, arithmetic and copies ran while one was open for 1% of the time, Pallas kernels for 0%

commit v1 on v0

v1 whole, which is shorter than its diff:
```python
import functools

import jax
import jax.numpy as jnp
from jax import lax
from jax.experimental import pallas as pl
from jax.experimental.pallas import tpu as pltpu
from jax.sharding import PartitionSpec as P

BLOCK = 128
LEAD = 1024
NLEAD = LEAD // BLOCK
GRP = 10
ROWS = 16
COLS = 8
VMEM = 56 * 1024 * 1024
F32 = jnp.float32
BF16 = jnp.bfloat16


def params(**kw):
    return pltpu.CompilerParams(vmem_limit_bytes=VMEM, **kw)


def cost(flops, bytes_accessed):
    return pl.CostEstimate(flops=flops, bytes_accessed=bytes_accessed, transcendentals=0)


def copy_kernel(table, src, dst):
    dst[...] = src[...].reshape(dst.shape)


def pack_columns(table, children):
    rows = children.shape[0]
    return pl.pallas_call(
        copy_kernel,
        grid_spec=pltpu.PrefetchScalarGridSpec(
            num_scalar_prefetch=1,
            grid=(2 * COLS,),
            in_specs=[pl.BlockSpec((rows, BLOCK), lambda s, t: (0, t[s]))],
            out_specs=pl.BlockSpec((1, rows, BLOCK), lambda s, t: (s, 0, 0)),
        ),
        out_shape=jax.ShapeDtypeStruct((2 * COLS, rows, BLOCK), F32),
        compiler_params=params(),
        cost_estimate=cost(0, 2 * 2 * COLS * rows * BLOCK * 4),
        name="pack_columns",
    )(table, children)


def pack_early(table, children):
    return pl.pallas_call(
        copy_kernel,
        grid_spec=pltpu.PrefetchScalarGridSpec(
            num_scalar_prefetch=1,
            grid=(2 * COLS,),
            in_specs=[pl.BlockSpec((BLOCK, BLOCK), lambda s, t: (t[2 * COLS], t[s]))],
            out_specs=pl.BlockSpec((1, BLOCK, BLOCK), lambda s, t: (s, 0, 0)),
        ),
        out_shape=jax.ShapeDtypeStruct((2 * COLS, BLOCK, BLOCK), F32),
        compiler_params=params(),
        cost_estimate=cost(0, 2 * 2 * COLS * BLOCK * BLOCK * 4),
        name="pack_early",
    )(table, children)


def pick_early(table, blocks):
    return pl.pallas_call(
        copy_kernel,
        grid_spec=pltpu.PrefetchScalarGridSpec(
            num_scalar_prefetch=1,
            grid=(ROWS,),
            in_specs=[pl.BlockSpec((1, BLOCK, BLOCK), lambda s, t: (t[s], 0, 0))],
            out_specs=pl.BlockSpec((1, BLOCK, BLOCK), lambda s, t: (s, 0, 0)),
        ),
        out_shape=jax.ShapeDtypeStruct((ROWS, BLOCK, BLOCK), F32),
        compiler_params=params(),
        cost_estimate=cost(0, 2 * ROWS * BLOCK * BLOCK * 4),
        name="pick_early",
    )(table, blocks)


def pack_rows_kernel(row_table, col_table, *refs):
    dst = refs[-1]
    for k in range(GRP):
        dst[0, k] = refs[k][0, 0]


def pack_rows(row_table, col_table, arrived):
    def spec(k):
        return pl.BlockSpec((1, 1, BLOCK, BLOCK), lambda d, rt, ct: (ct[k], rt[d], 0, 0))

    return pl.pallas_call(
        pack_rows_kernel,
        grid_spec=pltpu.PrefetchScalarGridSpec(
            num_scalar_prefetch=2,
            grid=(ROWS,),
            in_specs=[spec(k) for k in range(GRP)],
            out_specs=pl.BlockSpec((1, GRP, BLOCK, BLOCK), lambda d, rt, ct: (d, 0, 0, 0)),
        ),
        out_shape=jax.ShapeDtypeStruct((ROWS, GRP, BLOCK, BLOCK), F32),
        compiler_params=params(),
        cost_estimate=cost(0, 2 * ROWS * GRP * BLOCK * BLOCK * 4),
        name="pack_rows",
    )(row_table, col_table, *([arrived] * GRP))


def strip_kernel(place, keep, parent, blocks, out):
    out[...] = parent[...]
    for s in range(ROWS):

        @pl.when(keep[s] != 0)
        def _():
            at = pl.ds(pl.multiple_of(place[s] * BLOCK, BLOCK), BLOCK)
            out[:, at] = out[:, at] + blocks[s].T


def assemble_strip(place, keep, parent, blocks):
    return pl.pallas_call(
        strip_kernel,
        in_specs=[
            pl.BlockSpec(memory_space=pltpu.SMEM),
            pl.BlockSpec(memory_space=pltpu.SMEM),
            pl.BlockSpec(memory_space=pltpu.VMEM),
            pl.BlockSpec(memory_space=pltpu.VMEM),
        ],
        out_specs=pl.BlockSpec(memory_space=pltpu.VMEM),
        out_shape=jax.ShapeDtypeStruct((BLOCK, LEAD), F32),
        compiler_params=params(),
        cost_estimate=cost(0, 2 << 20),
        name="assemble_strip",
    )(place, keep, parent, blocks)


def split(x):
    hi = x.astype(BF16)
    return hi, (x - hi.astype(F32)).astype(BF16)


def dot3(a_hi, a_lo, b_hi, b_lo):
    dims = (((1,), (1,)), ((), ()))
    total = lax.dot_general(a_hi, b_lo, dims, preferred_element_type=F32)
    total += lax.dot_general(a_lo, b_hi, dims, preferred_element_type=F32)
    return total + lax.dot_general(a_hi, b_hi, dims, preferred_element_type=F32)


def dot_full(a, b, dims):
    return lax.dot_general(
        a, b, (dims, ((), ())), precision=lax.Precision.HIGHEST, preferred_element_type=F32
    )


def invert_diagonal(work):
    lanes = lax.broadcasted_iota(jnp.int32, (BLOCK, BLOCK), 1)
    rows = lax.broadcasted_iota(jnp.int32, (BLOCK, BLOCK), 0)
    lane8 = lax.broadcasted_iota(jnp.int32, (8, BLOCK), 1)
    row8 = lax.broadcasted_iota(jnp.int32, (8, BLOCK), 0)
    done = []
    for t in range(BLOCK // 8):
        base = 8 * t
        part = work[0:8]
        cols = [jnp.broadcast_to(part[:, base + i : base + i + 1], (8, BLOCK)) for i in range(8)]
        pivots = jnp.zeros((8, BLOCK), F32)
        for i in range(8):
            pivot = jnp.broadcast_to(cols[i][i : i + 1], (8, BLOCK))
            pivots = jnp.where(row8 == i, pivot, pivots)
            factor = jnp.where(row8 > i, cols[i] / pivot, 0.0)
            for other in range(i + 1, 8):
                cols[other] = cols[other] - factor * jnp.broadcast_to(cols[other][i : i + 1], (8, BLOCK))
            row = jnp.broadcast_to(part[i : i + 1], (8, BLOCK))
            row = jnp.where(lane8 == base + i, 1.0, row)
            part = jnp.where((lane8 == base + i) & (row8 > i), 0.0, part)
            part = jnp.where((lane8 == base + i) & (row8 == i), 1.0, part)
            part = part - factor * row
        part = part * lax.rsqrt(pivots)
        done.append(part)
        if t < BLOCK // 8 - 1:
            above = (lane8 > base + row8) & (lane8 < base + 8)
            update = dot_full(part[:, base + 8 :], jnp.where(above, 0.0, part), ((0,), (0,)))
            work = work[8:]
            inside = (lanes[: work.shape[0]] >= base) & (lanes[: work.shape[0]] < base + 8)
            work = jnp.where(inside, 0.0, work) - update
    whole = jnp.concatenate(done, axis=0)
    return jnp.where(rows >= lanes, whole, 0.0)


def factor_kernel(lead, inv_hi, inv_lo, work):
    work[...] = lead[...]
    count = LEAD // BLOCK

    def step(k, carry):
        here = pl.ds(pl.multiple_of(k * BLOCK, BLOCK), BLOCK)
        inverse = invert_diagonal(work[here, here])
        work[here, :] = dot_full(inverse, work[here, :], ((1,), (0,)))
        work[here, here] = inverse

        def below(i, carry):
            there = pl.ds(pl.multiple_of(i * BLOCK, BLOCK), BLOCK)
            lower = work[here, there]
            work[there, here] = jnp.zeros((BLOCK, BLOCK), F32)
            work[there, :] = work[there, :] - dot_full(lower, work[here, :], ((0,), (0,)))
            return carry

        return lax.fori_loop(k + 1, count, below, carry)

    lax.fori_loop(0, count, step, 0)

    def finish(k, carry):
        here = pl.ds(pl.multiple_of(k * BLOCK, BLOCK), BLOCK)
        rows = lax.broadcasted_iota(jnp.int32, (BLOCK, LEAD), 0) + k * BLOCK
        lanes = lax.broadcasted_iota(jnp.int32, (BLOCK, LEAD), 1)
        hi, lo = split(jnp.where(rows >= lanes, work[here, :], 0.0))
        inv_hi[here, :] = hi
        inv_lo[here, :] = lo
        return carry

    lax.fori_loop(0, count, finish, 0)


def factor_lead(lead):
    shape = jax.ShapeDtypeStruct((LEAD, LEAD), BF16)
    return pl.pallas_call(
        factor_kernel,
        in_specs=[pl.BlockSpec(memory_space=pltpu.VMEM)],
        out_specs=[pl.BlockSpec(memory_space=pltpu.VMEM)] * 2,
        out_shape=(shape, shape),
        scratch_shapes=[pltpu.VMEM((LEAD, LEAD), F32)],
        compiler_params=params(),
        cost_estimate=cost(100 * 10**9, 8 << 20),
        name="factor_lead",
    )(lead)


TILE = 256


def update_kernel(flags, row_strip, col_strip, inv_hi, inv_lo, parent, out, panel, hi, lo):
    step = pl.program_id(0)

    @pl.when(step == 0)
    def _():
        def chunk(n, carry):
            at = pl.ds(pl.multiple_of(n * TILE, TILE), TILE)
            values = dot3(*split(row_strip[at, :]), inv_hi[...], inv_lo[...])
            panel[at, :] = values
            hi[at, :], lo[at, :] = split(values)
            return carry

        lax.fori_loop(0, LEAD // TILE, chunk, 0)

    in_panel = (flags[1] == 0) & (step < LEAD // TILE)
    top = flags[0] == 0

    @pl.when(in_panel)
    def _():
        at = pl.ds(pl.multiple_of(step * TILE, TILE), TILE)
        rows = lax.broadcasted_iota(jnp.int32, (LEAD, TILE), 0)
        lanes = lax.broadcasted_iota(jnp.int32, (LEAD, TILE), 1) + step * TILE
        out[...] = jnp.where((rows >= lanes) | jnp.logical_not(top), panel[:, at], 0.0)

    @pl.when(jnp.logical_not(in_panel) & top)
    def _():
        out[...] = jnp.zeros_like(out)

    @pl.when(jnp.logical_not(in_panel) & jnp.logical_not(top))
    def _():
        right = split(dot3(*split(col_strip[...]), inv_hi[...], inv_lo[...]))

        def chunk(n, carry):
            at = pl.ds(pl.multiple_of(n * TILE, TILE), TILE)
            out[at, :] = parent[at, :] - dot3(hi[at, :], lo[at, :], *right)
            return carry

        lax.fori_loop(0, LEAD // TILE, chunk, 0)


def update_front(flags, row_strip, col_strip, inv_hi, inv_lo, parent):
    rows, columns = parent.shape
    whole = lambda t, f: (0, 0)
    return pl.pallas_call(
        update_kernel,
        grid_spec=pltpu.PrefetchScalarGridSpec(
            num_scalar_prefetch=1,
            grid=(columns // TILE,),
            in_specs=[
                pl.BlockSpec((LEAD, LEAD), whole),
                pl.BlockSpec((TILE, LEAD), lambda t, f: (t, 0)),
                pl.BlockSpec((LEAD, LEAD), whole),
                pl.BlockSpec((LEAD, LEAD), whole),
                pl.BlockSpec((rows, TILE), lambda t, f: (0, t)),
            ],
            out_specs=pl.BlockSpec((rows, TILE), lambda t, f: (0, t)),
            scratch_shapes=[
                pltpu.VMEM((LEAD, LEAD), F32),
                pltpu.VMEM((LEAD, LEAD), BF16),
                pltpu.VMEM((LEAD, LEAD), BF16),
            ],
        ),
        out_shape=jax.ShapeDtypeStruct((rows, columns), F32),
        compiler_params=params(),
        cost_estimate=cost(40 * 10**9, 32 << 20),
        name="update_front",
    )(flags, row_strip, col_strip, inv_hi, inv_lo, parent)


def place_kernel(source, rank, keep, front, first, second, out):
    i = pl.program_id(0)
    for j in range(16):
        at = pl.ds(j * BLOCK, BLOCK)
        value = front[:, at]
        for h, blocks in ((0, first), (1, second)):
            weight = keep[h, i * 16 + j]
            value = value + jnp.where(weight != 0, blocks[0, rank[h, j]], 0.0)
        out[:, at] = value


def place_children(source, rank, keep, front, arrived):
    rows, columns = front.shape

    def spec(h):
        return pl.BlockSpec((1, GRP, BLOCK, BLOCK), lambda i, s, r, k: (s[h, i], 0, 0, 0))

    return pl.pallas_call(
        place_kernel,
        grid_spec=pltpu.PrefetchScalarGridSpec(
            num_scalar_prefetch=3,
            grid=(rows // BLOCK,),
            in_specs=[pl.BlockSpec((BLOCK, columns), lambda i, s, r, k: (i, 0)), spec(0), spec(1)],
            out_specs=pl.BlockSpec((BLOCK, columns), lambda i, s, r, k: (i, 0)),
        ),
        out_shape=jax.ShapeDtypeStruct((rows, columns), F32),
        input_output_aliases={3: 0},
        compiler_params=params(),
        cost_estimate=cost(0, 24 << 20),
        name="place_children",
    )(source, rank, keep, front, arrived, arrived)


def earlier_count(keys):
    places = jnp.arange(keys.shape[-1], dtype=jnp.int32)
    matches = keys[..., :, None] == keys[..., None, :]
    before = places[None, :] < places[:, None]
    return jnp.sum((matches & before).astype(jnp.int32), axis=-1)


def lookup(codes, values, length):
    hits = codes[..., :, None] == jnp.arange(length, dtype=jnp.int32)
    found = jnp.sum(jnp.where(hits, values[..., :, None], 0), axis=-2)
    return found, jnp.any(hits, axis=-2)


def body(parent_front, children, child_map, fill):
    row_index = lax.axis_index("row")
    col_index = lax.axis_index("col")
    child_id = row_index // COLS
    group_row = row_index % COLS
    blocks = child_map.shape[1]
    places = jnp.arange(blocks, dtype=jnp.int32)
    groups = places // GRP
    within = places % GRP
    run16 = child_map // 16
    run8 = child_map // 8
    slot = earlier_count(groups * COLS + run16)
    pick = lambda x: lax.dynamic_index_in_dim(x, child_id, 0, keepdims=False)
    own_map, own_run16, own_run8, own_slot = pick(child_map), pick(run16), pick(run8), pick(slot)

    col_codes = jnp.where(groups == col_index, own_run16 * 2 + own_slot, -1)
    send_cols, _ = lookup(col_codes, within, 2 * COLS)
    row_codes = jnp.where(groups == group_row, own_run8, -1)
    send_rows, _ = lookup(row_codes, within, ROWS)
    rank_all = earlier_count(run16)
    rank_codes = jnp.where(own_run16 == col_index, pick(rank_all), -1)
    incoming = groups * 2 + own_slot
    pick_cols, _ = lookup(rank_codes, incoming, GRP)
    own_codes = jnp.where(own_run16 == col_index, own_map % 16, -1)
    pick_owner, _ = lookup(own_codes, incoming, 16)

    tile_rows = jnp.where(run8 == row_index, child_map % 8, -1)
    row_block, row_has = lookup(tile_rows, jnp.broadcast_to(places, (2, blocks)), 8)
    tile_cols = jnp.where(run16 == col_index, child_map % 16, -1)
    col_rank, col_has = lookup(tile_cols, rank_all, 16)
    row_hit = (tile_rows[:, None, :] == jnp.arange(8, dtype=jnp.int32)[None, :, None]).astype(F32)
    col_hit = (tile_cols[:, None, :] == jnp.arange(16, dtype=jnp.int32)[None, :, None]).astype(F32)
    present = fill.astype(F32)
    keep = jnp.einsum("hia,hab->hib", row_hit, present)
    keep = jnp.einsum("hib,hjb->hij", keep, col_hit)
    panel_col = (col_index == 0) & (jnp.arange(16) < NLEAD)
    keep = jnp.where(panel_col | (row_index == 0), 0.0, keep)
    keep = (keep > 0.5).astype(jnp.int32).reshape(2, 8 * 16)
    source = jnp.arange(2, dtype=jnp.int32)[:, None] * COLS + row_block // GRP

    owned = col_index * 16 + row_index
    lead_codes = jnp.where(run8 == 0, groups, -1)
    strip_place, strip_has = lookup(lead_codes, child_map, COLS)
    lead_hit = (lead_codes[:, None, :] == jnp.arange(COLS, dtype=jnp.int32)[None, :, None]).astype(F32)
    owned_hit = (child_map == owned).astype(F32)
    strip_keep = jnp.einsum("hga,hab->hgb", lead_hit, present)
    strip_keep = jnp.sum(strip_keep * owned_hit[:, None, :], axis=-1)
    strip_keep = (strip_keep > 0.5).astype(jnp.int32).reshape(ROWS)
    strip_place = jnp.where(strip_has, strip_place, 0).reshape(ROWS)

    axes = ("row", "col")
    number = lambda r, c: r * COLS + c

    parent_strip = None
    for i in range(NLEAD):
        pairs = [(number(r, 0), number((8 * r + i) % 16, r // 2)) for r in range(ROWS)]
        part = lax.ppermute(parent_front[i * BLOCK : (i + 1) * BLOCK, :LEAD], axes, pairs)
        parent_strip = part if parent_strip is None else parent_strip + part

    early = pack_early(jnp.concatenate([send_cols, send_rows[:1]]), children)
    early = lax.all_to_all(early, "col", split_axis=0, concat_axis=0, tiled=True)
    early = pick_early(pick_owner, early)
    early = lax.all_to_all(early, "row", split_axis=0, concat_axis=0, tiled=True)
    strip = assemble_strip(strip_place, strip_keep, parent_strip, early)

    half = BLOCK // 2
    lead = None
    for part in range(2):
        pairs = [(number(j, 0), number(2 * j + part, 0)) for j in range(NLEAD)]
        piece = lax.ppermute(strip[part * half : (part + 1) * half], axes, pairs)
        lead = piece if lead is None else lead + piece
    lead = lax.all_gather(lead, "col", axis=0, tiled=False)[0]
    lead = lax.all_gather(lead, "row", axis=0, tiled=True)

    col_strip = lax.all_gather(strip, "row", axis=0, tiled=True)
    pairs = [(number(j % 16, j // 16), number(j // 8, j % 8)) for j in range(128)]
    row_strip = lax.ppermute(strip, axes, pairs)
    row_strip = lax.all_gather(row_strip, "col", axis=0, tiled=True)

    outgoing = pack_columns(send_cols, children)
    arrived = lax.all_to_all(outgoing, "col", split_axis=0, concat_axis=0, tiled=True)
    arrived = arrived.reshape(2 * COLS, GRP, BLOCK, BLOCK)
    outgoing = pack_rows(send_rows, pick_cols, arrived)
    arrived = lax.all_to_all(outgoing, "row", split_axis=0, concat_axis=0, tiled=True)

    inv_hi, inv_lo = factor_lead(lead)
    flags = jnp.stack([row_index, col_index]).astype(jnp.int32)
    front = update_front(flags, row_strip, col_strip, inv_hi, inv_lo, parent_front)
    return place_children(source, col_rank, keep, front, arrived)


def solution(mesh):
    in_specs = (P("row", "col"), P("row", "col"), P(), P())
    out_specs = P("row", "col")
    return jax.shard_map(body, mesh=mesh, in_specs=in_specs, out_specs=out_specs, check_vma=False)
```

time: 1490 us -> 585 us (0.39)
  waiting for transfers between devices: 792 us -> 282 us
  other arithmetic: 329 us -> 10.5 us
  local copies, waits for them, and re-layouts: 262 us -> 11.4 us
  Pallas kernels: 0 us -> 199 us
  matrix products: 57.9 us -> 0.45 us
  starting transfers between devices: 13.5 us -> 63.8 us
    psum x6 -> x0, waiting for transfers between devices: 511 us -> none  [broadcast(): return lax.psum(block, axis)]
    another operation x37 -> x1, other arithmetic: 241 us -> 0.55 us  [body(): flags = jnp.stack([row_index, col_index]).astype(jnp.int32)]
    pallas_call x0 -> x8, Pallas kernels: none -> 199 us  [the longest x1 89.8 us: factor_lead(): pl.pallas_call(factor_kernel, in_specs=[pl.BlockSpec(memory_space=pltpu.V...]
    gather x11 -> x0, local copies, waits for them, and re-layouts: 103 us -> none  [the longest x3 34.9 us: body(): jnp.take(padded, table_cols, axis=2)]
    all_to_all x2 -> x4, waiting for transfers between devices: 281 us -> 183 us  [the longest x1 129 us: body(): lax.all_to_all(outgoing, 'col', split_axis=0, concat_axis=0, tiled=True)]
    select_n x20 -> x6, other arithmetic: 59.1 us -> 2.11 us  [the longest x1 0.7 us: body(): rank_codes = jnp.where(own_run16 == col_index, pick(rank_all), -1)]
    all_gather x0 -> x4, waiting for transfers between devices: none -> 54.2 us  [the longest x1 54.2 us: body(): lead = lax.all_gather(lead, 'col', axis=0, tiled=False)[0]]
    ppermute x0 -> x11, waiting for transfers between devices: none -> 44.4 us  [the longest x1 22.7 us: body(): row_strip = lax.ppermute(strip, axes, pairs)]
  transfers between devices with their start and end apart: 8 -> 19, of which waited for: 8 -> 6; matrix products, arithmetic and copies ran while one was open for 1% -> 2% of each run, Pallas kernels for 0% -> 30%
where the time goes in v1:
time: 585 us; the launch traced here: 580 us
  waiting for transfers between devices  282 us (48%)
  Pallas kernels  199 us (34%)
  starting transfers between devices  63.8 us (11%)
  between operations  13.3 us (2%)
  local copies, waits for them, and re-layouts  11.4 us (2%)
  other arithmetic  10.5 us (2%)
    all_to_all x1, waiting for transfers between devices, body(): lax.all_to_all(outgoing, 'col', split_axis=0, concat_axis=0, tiled=True)  129 us
    pallas_call x1, Pallas kernels, factor_lead(): pl.pallas_call(factor_kernel, in_specs=[pl.BlockSpec(memory_space=pltpu.V...  89.8 us
    all_gather x1, waiting for transfers between devices, body(): lead = lax.all_gather(lead, 'col', axis=0, tiled=False)[0]  54.2 us
    all_to_all x1, waiting for transfers between devices, body(): lax.all_to_all(outgoing, 'row', split_axis=0, concat_axis=0, tiled=True)  49.8 us
    pallas_call x1, Pallas kernels, update_front(): pl.pallas_call(update_kernel, grid_spec=pltpu.PrefetchScalarGridSpec(num_...  47.6 us
    ppermute x1, waiting for transfers between devices, body(): row_strip = lax.ppermute(strip, axes, pairs)  22.7 us
    all_to_all x1, starting transfers between devices, body(): lax.all_to_all(early, 'row', split_axis=0, concat_axis=0, tiled=True)  21.8 us
    ppermute x8, waiting for transfers between devices, body(): lax.ppermute(parent_front[i * BLOCK:(i + 1) * BLOCK, :LEAD], axes, pairs)  21.7 us
  transfers between devices with their start and end apart: 19, of which 6 were waited for; matrix products, arithmetic and copies ran while one was open for 2% of the time, Pallas kernels for 30%

profile of v1, /device:TPU:21, one launch (start us, length us, event | category | flops | bytes accessed | tf_op | source)
XLA Modules:
  0.0 580.1 jit_solution(8196792736765307658)
XLA Ops:
  6.6 0.7 compare_select_fusion.4
  7.3 0.7 compare_select_fusion.5
  8.0 0.2 convert_reduce_fusion
  8.2 0.7 bitcast_select_fusion
  8.9 0.1 select_reduce_fusion.3
  9.1 0.6 pad_add_fusion.1.table
  9.7 9.4 %pack_early.1 = f32[16,128,128]{2,1,0:T(8,128)} custom-call(s32[17]{0:T(128)} %pad_add_fusion.1.table, f32[1280,1280]{1,0:T(8,128)} %src.3), custom_call_target="tpu_custom_call" | custom-call | bytes 2097152 | tf_op jit(solution)/shard_map/pack_early/pallas_call | solution.py:51
  19.1 6.3 %all-to-all-start = ((f32[16,128,128]{2,1,0:T(8,128)}), f32[16,128,128]{2,1,0:T(8,128)S(1)}, u32[]{:S(2)}, u32[]{:S(2)}) async-start(f32[16,128,128]{2,1,0:T(8,128)} %pack_early.1), calls=%async_computation | async-start | bytes 2097152 | tf_op jit(solution)/shard_map/all_to_all | solution.py:411
  25.4 4.0 fusion.23
  29.3 0.7 collective-permute-start.1
  30.0 0.7 collective-permute-start.6
  30.7 1.5 collective-permute-start.5
  32.2 1.5 collective-permute-start.4
  33.7 1.5 collective-permute-start.3
  35.1 0.6 select_reduce_fusion.4.table
  35.8 0.2 fusion.8
  36.0 4.5 all-to-all-done.src
  40.5 1.0 copy-done
  41.4 8.7 %pick_early.1 = f32[16,128,128]{2,1,0:T(8,128)} custom-call(s32[16]{0:T(128)} %select_reduce_fusion.4.table, f32[16,128,128]{2,1,0:T(8,128)} %copy-done), custom_call_target="tpu_custom_call" | custom-call | bytes 2097152 | tf_op jit(solution)/shard_map/pick_early/pallas_call | solution.py:67
  50.1 21.8 %all-to-all-start.1 = ((f32[16,128,128]{2,1,0:T(8,128)}), f32[16,128,128]{2,1,0:T(8,128)S(1)}, u32[]{:S(2)}, u32[]{:S(2)}) async-start(f32[16,128,128]{2,1,0:T(8,128)} %pick_early.1), calls=%async_computation.1 | async-start | bytes 2097152 | tf_op jit(solution)/shard_map/all_to_all | solution.py:413
  72.0 0.0 all-gather.12.cloned.1.call-start
  72.0 1.3 collective-permute-start.2
  73.3 1.5 collective-permute-start
  74.8 1.4 collective-permute-start.7
  76.3 0.7 reshape.154.keep
  77.0 0.1 fusion.12
  77.1 0.2 select_reduce_fusion.5
  77.3 0.6 select_n.180.place
  77.9 21.7 %collective-permute-done.2 = f32[128,1024]{1,0:T(8,128)} collective-permute-done((f32[128,1024]{1,0:T(8,128)}, f32[128,1024]{1,0:T(8,128)}, u32[]{:S(2)}, u32[]{:S(2)}) %collective-permute-start.2) | collective-permute-done | bytes 524320 | tf_op jit(solution)/shard_map/ppermute | solution.py:407
  99.5 3.0 add_add_fusion.parent
  102.6 1.0 copy-done.1
  103.5 2.4 assemble_strip.1
  105.9 1.1 fusion.24
  107.0 0.7 collective-permute-start.10
  107.7 0.7 collective-permute-start.9
  108.4 0.7 add.138
  109.1 0.0 all-gather.12.cloned.1.call-update
  109.1 0.0 all-gather.14.cloned.1.call-start
  109.2 54.2 %all-gather.12.cloned.1.call-done = f32[512,1024]{1,0:T(8,128)} async-done(((f32[64,1024]{1,0:T(8,128)}), f32[512,1024]{1,0:T(8,128)}) %all-gather.12.cloned.1.call-update) | async-done | bytes 2097168 | tf_op jit(solution)/shard_map/all_gather | solution.py:422
  163.4 1.7 slice.51
  165.1 0.0 all-gather.14.cloned.1.call-update
  165.1 0.0 all-gather.8.cloned.1.call-start
  165.1 2.8 collective-permute-start.8
  167.9 22.7 %collective-permute-done.8 = f32[128,1024]{1,0:T(8,128)S(1)} collective-permute-done((f32[128,1024]{1,0:T(8,128)}, f32[128,1024]{1,0:T(8,128)S(1)}, u32[]{:S(2)}, u32[]{:S(2)}) %collective-permute-start.8) | collective-permute-done | bytes 524320 | tf_op jit(solution)/shard_map/ppermute | solution.py:427
  190.7 0.8 copy-done.2
  191.5 0.0 all-gather.8.cloned.1.call-update
  191.5 14.4 %pack_columns.1 = f32[16,1280,128]{2,1,0:T(8,128)} custom-call(s32[16]{0:T(128)} %copy-done.5, f32[1280,1280]{1,0:T(8,128)} %src.3), custom_call_target="tpu_custom_call" | custom-call | bytes 20971520 | tf_op jit(solution)/shard_map/pack_columns/pallas_call | solution.py:35
  205.9 11.3 %all-to-all-start.2 = ((f32[16,1280,128]{2,1,0:T(8,128)}), f32[16,1280,128]{2,1,0:T(8,128)}, u32[]{:S(2)}, u32[]{:S(2)}) async-start(f32[16,1280,128]{2,1,0:T(8,128)} %pack_columns.1), calls=%async_computation.2 | async-start | bytes 20971520 | tf_op jit(solution)/shard_map/all_to_all | solution.py:431
  217.3 0.6 all-gather.10.cloned.1.call-update
  217.8 0.2 fusion.5
  218.1 0.7 reshape.153.keep
  218.7 0.6 pad_add_fusion.flags
  219.3 0.1 select_reduce_fusion.6
  219.4 0.7 select_reduce_fusion.1.col_table
  220.1 0.7 select_reduce_fusion.rank
  220.8 0.7 fusion.17.source
  221.5 128.6 %all-to-all-done.2 = f32[16,1280,128]{2,1,0:T(8,128)} async-done(((f32[16,1280,128]{2,1,0:T(8,128)}), f32[16,1280,128]{2,1,0:T(8,128)}, u32[]{:S(2)}, u32[]{:S(2)}) %all-to-all-start.2) | async-done | bytes 10485792 | tf_op jit(solution)/shard_map/all_to_all | solution.py:431
  350.1 14.0 %pack_rows.1 = f32[16,10,128,128]{3,2,1,0:T(8,128)} custom-call(s32[16]{0:T(128)} %copy-done.6, s32[10]{0:T(128)} %select_reduce_fusion.1.col_table, f32[16,10,128,128]{3,2,1,0:T(8,128)} %bitcast.8.refs_0_.refs_1_.refs_2_.refs_3_.refs_4_.refs_5_.refs_6_.refs_7_.refs_8_.refs_9_, ...), custom_call_target="tpu_custom_call" | custom-call | bytes 20971520 | tf_op jit(solution)/shard_map/pack_rows/pallas_call | solution.py:92
  364.1 10.0 %all-to-all-start.3 = ((f32[16,10,128,128]{3,2,1,0:T(8,128)}), f32[16,10,128,128]{3,2,1,0:T(8,128)}, u32[]{:S(2)}, u32[]{:S(2)}) async-start(f32[16,10,128,128]{3,2,1,0:T(8,128)} %pack_rows.1), calls=%async_computation.3 | async-start | bytes 20971520 | tf_op jit(solution)/shard_map/all_to_all | solution.py:434
  374.1 0.0 all-gather.14.cloned.1.call-done.lead
  374.1 89.8 %factor_lead.1 = (bf16[1024,1024]{1,0:T(8,128)(2,1)}, bf16[1024,1024]{1,0:T(8,128)(2,1)}) custom-call(f32[1024,1024]{1,0:T(8,128)} %all-gather.14.cloned.1.call-done.lead), custom_call_target="tpu_custom_call" | custom-call | flops 99999997952 | bytes 8388608 | tf_op jit(solution)/shard_map/factor_lead/pallas_call | solution.py:221
  463.9 47.6 %update_front.1.front = f32[1024,2048]{1,0:T(8,128)} custom-call(s32[2]{0:T(128)} %pad_add_fusion.flags, f32[1024,1024]{1,0:T(8,128)} %all-gather.8.cloned.1.call-done.row_strip, f32[2048,1024]{1,0:T(8,128)} %all-gather.10.cloned.1.call-done.col_strip, bf16[1024,1024]{1,0:T(8,128)(2,1)} %get-tuple-element.7.inv_hi, ...), custom_call_target="tpu_custom_call" | custom-call | flops 40000000000 | bytes 33554432 | tf_op jit(solution)/shard_map/update_front/pallas_call | solution.py:279
  511.5 49.8 %all-to-all-done.3.first.second = f32[16,10,128,128]{3,2,1,0:T(8,128)} async-done(((f32[16,10,128,128]{3,2,1,0:T(8,128)}), f32[16,10,128,128]{3,2,1,0:T(8,128)}, u32[]{:S(2)}, u32[]{:S(2)}) %all-to-all-start.3) | async-done | bytes 10485792 | tf_op jit(solution)/shard_map/all_to_all | solution.py:434
  561.3 12.3 %place_children.1 = f32[1024,2048]{1,0:T(8,128)} custom-call(s32[2,8]{1,0:T(2,128)} %fusion.17.source, s32[2,16]{1,0:T(2,128)} %select_reduce_fusion.rank, s32[2,128]{1,0:T(2,128)} %reshape.153.keep, f32[1024,2048]{1,0:T(8,128)} %update_front.1.front, f32[16,10,128,128]{3,2,1,0:T(8,128)} %all-to-all-done.3.first.second, ...), custom_call_target="tpu_custom_call", output_to_operand_aliasing={{}: (3, {})} | custom-call | bytes 25165824 | tf_op jit(solution)/shard_map/place_children/pallas_call | solution.py:322
  (34 shorter events, 0.1 us)
Async XLA Ops:
  9.1 20.3 %copy-start.5 = (s32[16]{0:T(128)}, s32[16]{0:T(128)S(1)}, u32[]{:S(2)}) copy-start(s32[16]{0:T(128)S(1)} %get-tuple-element.11.table) | copy-start | bytes 196
  9.1 20.3 %copy-start.6 = (s32[16]{0:T(128)}, s32[16]{0:T(128)S(1)}, u32[]{:S(2)}) copy-start(s32[16]{0:T(128)S(1)} %get-tuple-element.12.row_table) | copy-start | bytes 196
  9.7 26.1 %copy-start.4 = (s32[2,80]{1,0:T(2,128)S(1)}, s32[2,80]{1,0:T(2,128)}, u32[]{:S(2)}) copy-start(s32[2,80]{1,0:T(2,128)} %param.6) | copy-start | bytes 1924
  9.7 26.1 %copy-start.3 = (s32[2,80,80]{2,1,0:T(8,128)S(1)}, s32[2,80,80]{2,1,0:T(8,128)}, u32[]{:S(2)}) copy-start(s32[2,80,80]{2,1,0:T(8,128)} %param.7) | copy-start | bytes 153604
  19.1 21.4 %all-to-all-start = ((f32[16,128,128]{2,1,0:T(8,128)}), f32[16,128,128]{2,1,0:T(8,128)S(1)}, u32[]{:S(2)}, u32[]{:S(2)}) async-start(f32[16,128,128]{2,1,0:T(8,128)} %pack_early.1), calls=%async_computation | async-start | bytes 2097152 | tf_op jit(solution)/shard_map/all_to_all | solution.py:411
  29.3 42.7 %collective-permute-start.1 = (f32[128,1024]{1,0:T(8,128)}, f32[128,1024]{1,0:T(8,128)S(1)}, u32[]{:S(2)}, u32[]{:S(2)}) collective-permute-start(f32[128,1024]{1,0:T(8,128)} %get-tuple-element.17), channel_id=1, source_target_pairs={{0,8},{8,72},{16,9},{24,73},{32,10},{40,74},{48,11},{56,75},{64,12... | collective-permute-start | bytes 1572872 | tf_op jit(solution)/shard_map/ppermute | solution.py:407
  30.0 43.3 %collective-permute-start.6 = (f32[128,1024]{1,0:T(8,128)}, f32[128,1024]{1,0:T(8,128)S(1)}, u32[]{:S(2)}, u32[]{:S(2)}) collective-permute-start(f32[128,1024]{1,0:T(8,128)} %get-tuple-element.18), channel_id=1, source_target_pairs={{0,48},{8,112},{16,49},{24,113},{32,50},{40,114},{48,51},{56,115},... | collective-permute-start | bytes 1572872 | tf_op jit(solution)/shard_map/ppermute | solution.py:407
  30.7 44.1 %collective-permute-start.5 = (f32[128,1024]{1,0:T(8,128)}, f32[128,1024]{1,0:T(8,128)}, u32[]{:S(2)}, u32[]{:S(2)}) collective-permute-start(f32[128,1024]{1,0:T(8,128)} %get-tuple-element.19), channel_id=1, source_target_pairs={{0,40},{8,104},{16,41},{24,105},{32,42},{40,106},{48,43},{56,107},... | collective-permute-start | bytes 1572872 | tf_op jit(solution)/shard_map/ppermute | solution.py:407
  32.2 45.6 %collective-permute-start.4 = (f32[128,1024]{1,0:T(8,128)}, f32[128,1024]{1,0:T(8,128)}, u32[]{:S(2)}, u32[]{:S(2)}) collective-permute-start(f32[128,1024]{1,0:T(8,128)} %get-tuple-element.20), channel_id=1, source_target_pairs={{0,32},{8,96},{16,33},{24,97},{32,34},{40,98},{48,35},{56,99},{64,... | collective-permute-start | bytes 1572872 | tf_op jit(solution)/shard_map/ppermute | solution.py:407
  33.7 44.2 %collective-permute-start.3 = (f32[128,1024]{1,0:T(8,128)}, f32[128,1024]{1,0:T(8,128)}, u32[]{:S(2)}, u32[]{:S(2)}) collective-permute-start(f32[128,1024]{1,0:T(8,128)} %get-tuple-element.21), channel_id=1, source_target_pairs={{0,24},{8,88},{16,25},{24,89},{32,26},{40,90},{48,27},{56,91},{64,... | collective-permute-start | bytes 1572872 | tf_op jit(solution)/shard_map/ppermute | solution.py:407
  40.5 1.0 copy-start
  50.1 52.4 %all-to-all-start.1 = ((f32[16,128,128]{2,1,0:T(8,128)}), f32[16,128,128]{2,1,0:T(8,128)S(1)}, u32[]{:S(2)}, u32[]{:S(2)}) async-start(f32[16,128,128]{2,1,0:T(8,128)} %pick_early.1), calls=%async_computation.1 | async-start | bytes 2097152 | tf_op jit(solution)/shard_map/all_to_all | solution.py:413
  72.0 91.4 %all-gather.12.cloned.1.call-start = ((), (), s32[]{:S(2)}) async-start(), calls=%async_computation.6 | async-start | bytes 2359296 | tf_op jit(solution)/shard_map/all_gather | solution.py:422
  72.0 27.5 %collective-permute-start.2 = (f32[128,1024]{1,0:T(8,128)}, f32[128,1024]{1,0:T(8,128)}, u32[]{:S(2)}, u32[]{:S(2)}) collective-permute-start(f32[128,1024]{1,0:T(8,128)} %get-tuple-element.22), channel_id=1, source_target_pairs={{0,16},{8,80},{16,17},{24,81},{32,18},{40,82},{48,19},{56,83},{64,... | collective-permute-start | bytes 1572872 | tf_op jit(solution)/shard_map/ppermute | solution.py:407
  73.3 26.2 %collective-permute-start = (f32[128,1024]{1,0:T(8,128)S(1)}, f32[128,1024]{1,0:T(8,128)}, u32[]{:S(2)}, u32[]{:S(2)}) collective-permute-start(f32[128,1024]{1,0:T(8,128)S(1)} %get-tuple-element.23), channel_id=1, source_target_pairs={{0,0},{8,64},{16,1},{24,65},{32,2},{40,66},{48,3},{56,67},{64,4},{... | collective-permute-start | bytes 1572872 | tf_op jit(solution)/shard_map/ppermute | solution.py:407
  74.8 24.7 %collective-permute-start.7 = (f32[128,1024]{1,0:T(8,128)S(1)}, f32[128,1024]{1,0:T(8,128)}, u32[]{:S(2)}, u32[]{:S(2)}) collective-permute-start(f32[128,1024]{1,0:T(8,128)S(1)} %get-tuple-element.24), channel_id=1, source_target_pairs={{0,56},{8,120},{16,57},{24,121},{32,58},{40,122},{48,59},{56,123},... | collective-permute-start | bytes 1572872 | tf_op jit(solution)/shard_map/ppermute | solution.py:407
  102.6 1.0 copy-start.1
  107.0 1.4 collective-permute-start.10
  107.7 0.7 collective-permute-start.9
  109.1 264.9 %all-gather.14.cloned.1.call-start = ((), (), s32[]{:S(2)}) async-start(), calls=%async_computation.7 | async-start | bytes 4456448 | tf_op jit(solution)/shard_map/all_gather | solution.py:423
  165.1 298.8 %all-gather.8.cloned.1.call-start = ((), (), s32[]{:S(2)}) async-start(), calls=%async_computation.4 | async-start | bytes 4718592 | tf_op jit(solution)/shard_map/all_gather | solution.py:428
  165.1 25.5 %collective-permute-start.8 = (f32[128,1024]{1,0:T(8,128)}, f32[128,1024]{1,0:T(8,128)S(1)}, u32[]{:S(2)}, u32[]{:S(2)}) collective-permute-start(f32[128,1024]{1,0:T(8,128)} %assemble_strip.1), channel_id=1, source_target_pairs={{0,0},{8,1},{16,2},{24,3},{32,4},{40,5},{48,6},{56,7},{64,8},{72,9... | collective-permute-start | bytes 1572872 | tf_op jit(solution)/shard_map/ppermute | solution.py:427
  190.7 0.8 copy-start.2
  205.9 144.2 %all-to-all-start.2 = ((f32[16,1280,128]{2,1,0:T(8,128)}), f32[16,1280,128]{2,1,0:T(8,128)}, u32[]{:S(2)}, u32[]{:S(2)}) async-start(f32[16,1280,128]{2,1,0:T(8,128)} %pack_columns.1), calls=%async_computation.2 | async-start | bytes 20971520 | tf_op jit(solution)/shard_map/all_to_all | solution.py:431
  217.3 246.6 %all-gather.10.cloned.1.call-start = ((), (), s32[]{:S(2)}) async-start(), calls=%async_computation.5 | async-start | bytes 8912896 | tf_op jit(solution)/shard_map/all_gather | solution.py:425
  364.1 197.2 %all-to-all-start.3 = ((f32[16,10,128,128]{3,2,1,0:T(8,128)}), f32[16,10,128,128]{3,2,1,0:T(8,128)}, u32[]{:S(2)}, u32[]{:S(2)}) async-start(f32[16,10,128,128]{3,2,1,0:T(8,128)} %pack_rows.1), calls=%async_computation.3 | async-start | bytes 20971520 | tf_op jit(solution)/shard_map/all_to_all | solution.py:434
Sparse Core Ops, SparseCore 0:
  109.3 54.0 all-gather.11
  165.5 61.5 all-gather.13
  228.8 53.3 all-gather.7
  284.2 69.1 all-gather.9

commit v2 on v1

--- a/solution.py
+++ b/solution.py
@@ -26,109 +26,195 @@
     return pl.CostEstimate(flops=flops, bytes_accessed=bytes_accessed, transcendentals=0)
 
 
-def copy_kernel(table, src, dst):
-    dst[...] = src[...].reshape(dst.shape)
-
-
-def pack_columns(table, children):
-    rows = children.shape[0]
+def gather_call(kernel, tables, arrays, shapes, scratch, sems, name, after=()):
+    moved = sum(4 * functools.reduce(lambda x, y: x * y, shape) for shape in shapes)
+    count = len(tables) + len(arrays)
+
+    def run(*refs):
+        kernel(*refs[:count], *refs[count + len(after) :])
+
     return pl.pallas_call(
-        copy_kernel,
-        grid_spec=pltpu.PrefetchScalarGridSpec(
-            num_scalar_prefetch=1,
-            grid=(2 * COLS,),
-            in_specs=[pl.BlockSpec((rows, BLOCK), lambda s, t: (0, t[s]))],
-            out_specs=pl.BlockSpec((1, rows, BLOCK), lambda s, t: (s, 0, 0)),
-        ),
-        out_shape=jax.ShapeDtypeStruct((2 * COLS, rows, BLOCK), F32),
+        run,
+        in_specs=[pl.BlockSpec(memory_space=pltpu.SMEM)] * len(tables)
+        + [pl.BlockSpec(memory_space=pl.ANY)] * (len(arrays) + len(after)),
+        out_specs=[pl.BlockSpec(memory_space=pl.ANY)] * len(shapes),
+        out_shape=[jax.ShapeDtypeStruct(shape, F32) for shape in shapes],
+        scratch_shapes=[pltpu.VMEM(shape, F32) for shape in scratch]
+        + [pltpu.SemaphoreType.DMA(sems), pltpu.SemaphoreType.DMA(sems)],
         compiler_params=params(),
-        cost_estimate=cost(0, 2 * 2 * COLS * rows * BLOCK * 4),
-        name="pack_columns",
-    )(table, children)
-
-
-def pack_early(table, children):
-    return pl.pallas_call(
-        copy_kernel,
-        grid_spec=pltpu.PrefetchScalarGridSpec(
-            num_scalar_prefetch=1,
-            grid=(2 * COLS,),
-            in_specs=[pl.BlockSpec((BLOCK, BLOCK), lambda s, t: (t[2 * COLS], t[s]))],
-            out_specs=pl.BlockSpec((1, BLOCK, BLOCK), lambda s, t: (s, 0, 0)),
-        ),
-        out_shape=jax.ShapeDtypeStruct((2 * COLS, BLOCK, BLOCK), F32),
-        compiler_params=params(),
-        cost_estimate=cost(0, 2 * 2 * COLS * BLOCK * BLOCK * 4),
-        name="pack_early",
-    )(table, children)
-
-
-def pick_early(table, blocks):
-    return pl.pallas_call(
-        copy_kernel,
-        grid_spec=pltpu.PrefetchScalarGridSpec(
-            num_scalar_prefetch=1,
-            grid=(ROWS,),
-            in_specs=[pl.BlockSpec((1, BLOCK, BLOCK), lambda s, t: (t[s], 0, 0))],
-            out_specs=pl.BlockSpec((1, BLOCK, BLOCK), lambda s, t: (s, 0, 0)),
-        ),
-        out_shape=jax.ShapeDtypeStruct((ROWS, BLOCK, BLOCK), F32),
-        compiler_params=params(),
-        cost_estimate=cost(0, 2 * ROWS * BLOCK * BLOCK * 4),
-        name="pick_early",
-    )(table, blocks)
-
-
-def pack_rows_kernel(row_table, col_table, *refs):
-    dst = refs[-1]
-    for k in range(GRP):
-        dst[0, k] = refs[k][0, 0]
-
-
-def pack_rows(row_table, col_table, arrived):
-    def spec(k):
-        return pl.BlockSpec((1, 1, BLOCK, BLOCK), lambda d, rt, ct: (ct[k], rt[d], 0, 0))
-
-    return pl.pallas_call(
+        cost_estimate=cost(0, 2 * moved),
+        name=name,
+    )(*tables, *arrays, *after)
+
+
+def lanes_of(block):
+    return pl.ds(pl.multiple_of(block * BLOCK, BLOCK), BLOCK)
+
+
+def relay(moves, sem_in, sem_out):
+    first = [pltpu.make_async_copy(s, v, sem_in.at[n]) for n, (s, v, t) in enumerate(moves)]
+    second = [pltpu.make_async_copy(v, t, sem_out.at[n]) for n, (s, v, t) in enumerate(moves)]
+    for copy in first:
+        copy.start()
+    for one, other in zip(first, second):
+        one.wait()
+        other.start()
+    for copy in second:
+        copy.wait()
+
+
+def pack_first_kernel(table, children, *refs):
+    outs, early = refs[:COLS], refs[COLS]
+    wide, small, sem_in, sem_out = refs[COLS + 1 :]
+    moves = []
+    for s in range(2 * COLS):
+        source = children.at[lanes_of(table[3 * COLS]), lanes_of(table[COLS + s])]
+        moves.append((source, small.at[s], early.at[s]))
+    for s in range(COLS):
+        moves.append((children.at[:, lanes_of(table[s])], wide.at[s], outs[s]))
+    relay(moves, sem_in, sem_out)
+
+
+def pack_first(table, children):
+    wide = (children.shape[0], BLOCK)
+    small = (2 * COLS, BLOCK, BLOCK)
+    return gather_call(
+        pack_first_kernel,
+        [table],
+        [children],
+        [wide] * COLS + [small],
+        [(COLS,) + wide, small],
+        (3 * COLS,),
+        "pack_first",
+    )
+
+
+def pack_second_kernel(table, children, *refs):
+    wide, sem_in, sem_out = refs[COLS:]
+    moves = [
+        (children.at[:, lanes_of(table[s])], wide.at[s], refs[s]) for s in range(COLS)
+    ]
+    relay(moves, sem_in, sem_out)
+
+
+def pack_second(table, children, after):
+    wide = (children.shape[0], BLOCK)
+    return gather_call(
+        pack_second_kernel,
+        [table],
+        [children],
+        [wide] * COLS,
+        [(COLS,) + wide],
+        (COLS,),
+        "pack_second",
+        after,
+    )
+
+
+def cut_kernel(parent, *refs):
+    held, sem_in, sem_out = refs[NLEAD:]
+    moves = []
+    for i in range(NLEAD):
+        source = parent.at[pl.ds(i * BLOCK, BLOCK), pl.ds(0, LEAD)]
+        moves.append((source, held.at[i], refs[i]))
+    relay(moves, sem_in, sem_out)
+
+
+def cut_strip(parent):
+    shape = (BLOCK, LEAD)
+    return gather_call(
+        cut_kernel, [], [parent], [shape] * NLEAD, [(NLEAD,) + shape], (NLEAD,), "cut_strip"
+    )
+
+
+def pick_early_kernel(table, blocks, out, held, sem_in, sem_out):
+    relay([(blocks.at[table[s]], held.at[s], out.at[s]) for s in range(ROWS)], sem_in, sem_out)
+
+
+def pick_early(table, blocks, after):
+    shape = (ROWS, BLOCK, BLOCK)
+    return gather_call(
+        pick_early_kernel, [table], [blocks], [shape], [shape], (ROWS,), "pick_early", after
+    )[0]
+
+
+HALF = GRP // 2
+
+
+def pack_rows_kernel(row_table, row_has, origin, *refs):
+    sources, (out, held, sem_in, sem_out) = refs[:-4], refs[-4:]
+
+    def each(act):
+        def one(r, carry):
+            @pl.when(row_has[r] != 0)
+            def _():
+                act(r)
+
+            return carry
+
+        lax.fori_loop(0, ROWS, one, 0)
+
+    def start(r):
+        for k in range(HALF):
+            for n, source in enumerate(sources):
+
+                @pl.when(origin[k] == n)
+                def _():
+                    pltpu.make_async_copy(
+                        source.at[row_table[r]], held.at[r, k], sem_in.at[r, k]
+                    ).start()
+
+    def leave(r):
+        return pltpu.make_async_copy(held.at[r], out.at[r], sem_out.at[r, 0])
+
+    def send(r):
+        for k in range(HALF):
+            pltpu.make_async_copy(sources[0].at[0], held.at[r, k], sem_in.at[r, k]).wait()
+        leave(r).start()
+
+    each(start)
+    each(send)
+    each(lambda r: leave(r).wait())
+
+
+def pack_rows(row_table, row_has, origin, arrays, after):
+    arrays = [x.reshape(GRP, BLOCK, BLOCK) for x in arrays]
+    shape = (ROWS, HALF, BLOCK, BLOCK)
+    return gather_call(
         pack_rows_kernel,
-        grid_spec=pltpu.PrefetchScalarGridSpec(
-            num_scalar_prefetch=2,
-            grid=(ROWS,),
-            in_specs=[spec(k) for k in range(GRP)],
-            out_specs=pl.BlockSpec((1, GRP, BLOCK, BLOCK), lambda d, rt, ct: (d, 0, 0, 0)),
-        ),
-        out_shape=jax.ShapeDtypeStruct((ROWS, GRP, BLOCK, BLOCK), F32),
-        compiler_params=params(),
-        cost_estimate=cost(0, 2 * ROWS * GRP * BLOCK * BLOCK * 4),
-        name="pack_rows",
-    )(row_table, col_table, *([arrived] * GRP))
-
-
-def strip_kernel(place, keep, parent, blocks, out):
+        [row_table, row_has, origin],
+        arrays,
+        [shape],
+        [shape],
+        (ROWS, HALF),
+        "pack_rows",
+        after,
+    )[0]
+
+
+def strip_kernel(place, keep, parent, blocks, *refs):
+    out = refs[-1]
     out[...] = parent[...]
     for s in range(ROWS):
 
         @pl.when(keep[s] != 0)
         def _():
-            at = pl.ds(pl.multiple_of(place[s] * BLOCK, BLOCK), BLOCK)
+            at = lanes_of(place[s])
             out[:, at] = out[:, at] + blocks[s].T
 
 
-def assemble_strip(place, keep, parent, blocks):
+def assemble_strip(place, keep, parent, blocks, after):
+    vmem = pl.BlockSpec(memory_space=pltpu.VMEM)
+    smem = pl.BlockSpec(memory_space=pltpu.SMEM)
     return pl.pallas_call(
         strip_kernel,
-        in_specs=[
-            pl.BlockSpec(memory_space=pltpu.SMEM),
-            pl.BlockSpec(memory_space=pltpu.SMEM),
-            pl.BlockSpec(memory_space=pltpu.VMEM),
-            pl.BlockSpec(memory_space=pltpu.VMEM),
-        ],
-        out_specs=pl.BlockSpec(memory_space=pltpu.VMEM),
+        in_specs=[smem, smem, vmem, vmem] + [pl.BlockSpec(memory_space=pl.ANY)] * len(after),
+        out_specs=vmem,
         out_shape=jax.ShapeDtypeStruct((BLOCK, LEAD), F32),
         compiler_params=params(),
         cost_estimate=cost(0, 2 << 20),
         name="assemble_strip",
-    )(place, keep, parent, blocks)
+    )(place, keep, parent, blocks, *after)
 
 
 def split(x):
@@ -183,29 +269,33 @@
     return jnp.where(rows >= lanes, whole, 0.0)
 
 
-def factor_kernel(lead, inv_hi, inv_lo, work):
-    work[...] = lead[...]
-    count = LEAD // BLOCK
+def factor_kernel(first, count, last, given, after, *refs):
+    work = refs[-1] if last else refs[0]
+    work[...] = given[...]
+    total = LEAD // BLOCK
 
     def step(k, carry):
-        here = pl.ds(pl.multiple_of(k * BLOCK, BLOCK), BLOCK)
+        here = lanes_of(k)
         inverse = invert_diagonal(work[here, here])
         work[here, :] = dot_full(inverse, work[here, :], ((1,), (0,)))
         work[here, here] = inverse
 
         def below(i, carry):
-            there = pl.ds(pl.multiple_of(i * BLOCK, BLOCK), BLOCK)
+            there = lanes_of(i)
             lower = work[here, there]
             work[there, here] = jnp.zeros((BLOCK, BLOCK), F32)
             work[there, :] = work[there, :] - dot_full(lower, work[here, :], ((0,), (0,)))
             return carry
 
-        return lax.fori_loop(k + 1, count, below, carry)
-
-    lax.fori_loop(0, count, step, 0)
+        return lax.fori_loop(k + 1, total, below, carry)
+
+    lax.fori_loop(first, first + count, step, 0)
+    if not last:
+        return
+    inv_hi, inv_lo = refs[0], refs[1]
 
     def finish(k, carry):
-        here = pl.ds(pl.multiple_of(k * BLOCK, BLOCK), BLOCK)
+        here = lanes_of(k)
         rows = lax.broadcasted_iota(jnp.int32, (BLOCK, LEAD), 0) + k * BLOCK
         lanes = lax.broadcasted_iota(jnp.int32, (BLOCK, LEAD), 1)
         hi, lo = split(jnp.where(rows >= lanes, work[here, :], 0.0))
@@ -213,24 +303,42 @@
         inv_lo[here, :] = lo
         return carry
 
-    lax.fori_loop(0, count, finish, 0)
-
-
-def factor_lead(lead):
-    shape = jax.ShapeDtypeStruct((LEAD, LEAD), BF16)
+    lax.fori_loop(0, total, finish, 0)
+
+
+PARTS = 4
+
+
+def factor_part(part, work, after):
+    count = LEAD // BLOCK // PARTS
+    whole = pl.BlockSpec(memory_space=pltpu.VMEM)
+    last = part == PARTS - 1
+    half = jax.ShapeDtypeStruct((LEAD, LEAD), BF16)
+    full = jax.ShapeDtypeStruct((LEAD, LEAD), F32)
     return pl.pallas_call(
-        factor_kernel,
-        in_specs=[pl.BlockSpec(memory_space=pltpu.VMEM)],
-        out_specs=[pl.BlockSpec(memory_space=pltpu.VMEM)] * 2,
-        out_shape=(shape, shape),
-        scratch_shapes=[pltpu.VMEM((LEAD, LEAD), F32)],
+        functools.partial(factor_kernel, part * count, count, last),
+        in_specs=[whole, pl.BlockSpec(memory_space=pl.ANY)],
+        out_specs=[whole] * 2 if last else whole,
+        out_shape=(half, half) if last else full,
+        scratch_shapes=[pltpu.VMEM((LEAD, LEAD), F32)] if last else [],
         compiler_params=params(),
-        cost_estimate=cost(100 * 10**9, 8 << 20),
+        cost_estimate=cost(25 * 10**9, 8 << 20),
         name="factor_lead",
-    )(lead)
+    )(work, after)
 
 
 TILE = 256
+
+
+def solve_rows(rows, inv_hi, inv_lo):
+    hi, lo = split(rows)
+    parts = []
+    for n in range(LEAD // TILE):
+        at, upto = pl.ds(n * TILE, TILE), (n + 1) * TILE
+        parts.append(
+            dot3(hi[:, :upto], lo[:, :upto], inv_hi[at, pl.ds(0, upto)], inv_lo[at, pl.ds(0, upto)])
+        )
+    return jnp.concatenate(parts, axis=1)
 
 
 def update_kernel(flags, row_strip, col_strip, inv_hi, inv_lo, parent, out, panel, hi, lo):
@@ -240,7 +348,7 @@
     def _():
         def chunk(n, carry):
             at = pl.ds(pl.multiple_of(n * TILE, TILE), TILE)
-            values = dot3(*split(row_strip[at, :]), inv_hi[...], inv_lo[...])
+            values = solve_rows(row_strip[at, :], inv_hi, inv_lo)
             panel[at, :] = values
             hi[at, :], lo[at, :] = split(values)
             return carry
@@ -263,7 +371,7 @@
 
     @pl.when(jnp.logical_not(in_panel) & jnp.logical_not(top))
     def _():
-        right = split(dot3(*split(col_strip[...]), inv_hi[...], inv_lo[...]))
+        right = split(solve_rows(col_strip[...], inv_hi, inv_lo))
 
         def chunk(n, carry):
             at = pl.ds(pl.multiple_of(n * TILE, TILE), TILE)
@@ -302,29 +410,35 @@
     )(flags, row_strip, col_strip, inv_hi, inv_lo, parent)
 
 
-def place_kernel(source, rank, keep, front, first, second, out):
+def place_kernel(source, rank, keep, front, *refs):
+    out = refs[-1]
     i = pl.program_id(0)
     for j in range(16):
         at = pl.ds(j * BLOCK, BLOCK)
         value = front[:, at]
-        for h, blocks in ((0, first), (1, second)):
-            weight = keep[h, i * 16 + j]
-            value = value + jnp.where(weight != 0, blocks[0, rank[h, j]], 0.0)
+        for h in range(2):
+            k = rank[h, j]
+            near, far = refs[2 * h], refs[2 * h + 1]
+            block = jnp.where(
+                k < HALF, near[0, jnp.minimum(k, HALF - 1)], far[0, jnp.maximum(k - HALF, 0)]
+            )
+            value = value + jnp.where(keep[h, i * 16 + j] != 0, block, 0.0)
         out[:, at] = value
 
 
-def place_children(source, rank, keep, front, arrived):
+def place_children(source, rank, keep, front, near, far):
     rows, columns = front.shape
 
     def spec(h):
-        return pl.BlockSpec((1, GRP, BLOCK, BLOCK), lambda i, s, r, k: (s[h, i], 0, 0, 0))
+        return pl.BlockSpec((1, HALF, BLOCK, BLOCK), lambda i, s, r, k: (s[h, i], 0, 0, 0))
 
     return pl.pallas_call(
         place_kernel,
         grid_spec=pltpu.PrefetchScalarGridSpec(
             num_scalar_prefetch=3,
             grid=(rows // BLOCK,),
-            in_specs=[pl.BlockSpec((BLOCK, columns), lambda i, s, r, k: (i, 0)), spec(0), spec(1)],
+            in_specs=[pl.BlockSpec((BLOCK, columns), lambda i, s, r, k: (i, 0))]
+            + [spec(0), spec(0), spec(1), spec(1)],
             out_specs=pl.BlockSpec((BLOCK, columns), lambda i, s, r, k: (i, 0)),
         ),
         out_shape=jax.ShapeDtypeStruct((rows, columns), F32),
@@ -332,7 +446,7 @@
         compiler_params=params(),
         cost_estimate=cost(0, 24 << 20),
         name="place_children",
-    )(source, rank, keep, front, arrived, arrived)
+    )(source, rank, keep, front, near, far, near, far)
 
 
 def earlier_count(keys):
@@ -366,11 +480,13 @@
     col_codes = jnp.where(groups == col_index, own_run16 * 2 + own_slot, -1)
     send_cols, _ = lookup(col_codes, within, 2 * COLS)
     row_codes = jnp.where(groups == group_row, own_run8, -1)
-    send_rows, _ = lookup(row_codes, within, ROWS)
-    rank_all = earlier_count(run16)
+    send_rows, sends = lookup(row_codes, within, ROWS)
+    ahead = slot[:, None, :] * blocks + places < (slot * blocks + places)[:, :, None]
+    rank_all = jnp.sum((ahead & (run16[:, None, :] == run16[:, :, None])).astype(jnp.int32), axis=-1)
     rank_codes = jnp.where(own_run16 == col_index, pick(rank_all), -1)
     incoming = groups * 2 + own_slot
-    pick_cols, _ = lookup(rank_codes, incoming, GRP)
+    origin = own_slot * COLS + (col_index - groups) % COLS
+    pick_cols, _ = lookup(rank_codes, origin, GRP)
     own_codes = jnp.where(own_run16 == col_index, own_map % 16, -1)
     pick_owner, _ = lookup(own_codes, incoming, 16)
 
@@ -401,42 +517,65 @@
     axes = ("row", "col")
     number = lambda r, c: r * COLS + c
 
-    parent_strip = None
-    for i in range(NLEAD):
-        pairs = [(number(r, 0), number((8 * r + i) % 16, r // 2)) for r in range(ROWS)]
-        part = lax.ppermute(parent_front[i * BLOCK : (i + 1) * BLOCK, :LEAD], axes, pairs)
-        parent_strip = part if parent_strip is None else parent_strip + part
-
-    early = pack_early(jnp.concatenate([send_cols, send_rows[:1]]), children)
+    total = lambda values: functools.reduce(lambda x, y: x + y, values)
+
+    total = lambda values: functools.reduce(lambda x, y: x + y, values)
+
+    pieces = cut_strip(parent_front)
+    own = total([jnp.where(col_index == 0, pieces[0], 0.0)] + [
+        lax.ppermute(pieces[i], axes, [(number(r, 0), number(r, i)) for r in range(ROWS)])
+        for i in range(1, NLEAD)
+    ])
+    pairs = [(number(j % 16, j // 16), number(j // 8, j % 8)) for j in range(128)]
+    strip_parent = lax.ppermute(own, axes, [(b, a) for a, b in pairs])
+
+    shifts = (col_index + jnp.arange(COLS, dtype=jnp.int32)) % COLS
+    table = jnp.concatenate([jnp.take(send_cols, shifts * 2), send_cols, send_rows[:1]])
+    *parts, early = pack_first(table, children)
+    shift = lambda parts: [parts[0]] + [
+        lax.ppermute(parts[d], "col", [(c, (c + d) % COLS) for c in range(COLS)])
+        for d in range(1, COLS)
+    ]
+    first = shift(parts)
     early = lax.all_to_all(early, "col", split_axis=0, concat_axis=0, tiled=True)
-    early = pick_early(pick_owner, early)
+    early = pick_early(pick_owner, early, [strip_parent])
     early = lax.all_to_all(early, "row", split_axis=0, concat_axis=0, tiled=True)
-    strip = assemble_strip(strip_place, strip_keep, parent_strip, early)
+    strip = assemble_strip(strip_place, strip_keep, strip_parent, early, first[1:])
 
     half = BLOCK // 2
-    lead = None
-    for part in range(2):
-        pairs = [(number(j, 0), number(2 * j + part, 0)) for j in range(NLEAD)]
-        piece = lax.ppermute(strip[part * half : (part + 1) * half], axes, pairs)
-        lead = piece if lead is None else lead + piece
-    lead = lax.all_gather(lead, "col", axis=0, tiled=False)[0]
-    lead = lax.all_gather(lead, "row", axis=0, tiled=True)
-
+    piece = total([
+        lax.ppermute(
+            strip[part * half : (part + 1) * half],
+            axes,
+            [(number(j, 0), number(2 * j + part, 0)) for j in range(NLEAD)],
+        )
+        for part in range(2)
+    ])
+    piece = total([piece] + [
+        lax.ppermute(piece, axes, [(number(r, 0), number(r, d)) for r in range(ROWS)])
+        for d in range(1, COLS)
+    ])
+    lead = lax.all_gather(piece, "row", axis=0, tiled=True)
+
+    row_piece = lax.ppermute(strip, axes, pairs)
     col_strip = lax.all_gather(strip, "row", axis=0, tiled=True)
-    pairs = [(number(j % 16, j // 16), number(j // 8, j % 8)) for j in range(128)]
-    row_strip = lax.ppermute(strip, axes, pairs)
-    row_strip = lax.all_gather(row_strip, "col", axis=0, tiled=True)
-
-    outgoing = pack_columns(send_cols, children)
-    arrived = lax.all_to_all(outgoing, "col", split_axis=0, concat_axis=0, tiled=True)
-    arrived = arrived.reshape(2 * COLS, GRP, BLOCK, BLOCK)
-    outgoing = pack_rows(send_rows, pick_cols, arrived)
-    arrived = lax.all_to_all(outgoing, "row", split_axis=0, concat_axis=0, tiled=True)
-
-    inv_hi, inv_lo = factor_lead(lead)
+    row_strip = lax.all_gather(row_piece, "col", axis=0, tiled=True)
+
+    sends = sends.astype(jnp.int32)
+    near_out = pack_rows(send_rows, sends, pick_cols[:HALF], first, [piece, row_piece])
+    near = lax.all_to_all(near_out, "row", split_axis=0, concat_axis=0, tiled=True)
+    parts = pack_second(jnp.take(send_cols, shifts * 2 + 1), children, [near_out])
+    second = shift(parts)
+    work = factor_part(0, lead, near_out)
+    far_out = pack_rows(send_rows, sends, pick_cols[HALF:], first + second, [near, work])
+    far = lax.all_to_all(far_out, "row", split_axis=0, concat_axis=0, tiled=True)
+
+    work = factor_part(1, work, far_out)
+    work = factor_part(2, work, far_out)
+    inv_hi, inv_lo = factor_part(3, work, far_out)
     flags = jnp.stack([row_index, col_index]).astype(jnp.int32)
     front = update_front(flags, row_strip, col_strip, inv_hi, inv_lo, parent_front)
-    return place_children(source, col_rank, keep, front, arrived)
+    return place_children(source, col_rank, keep, front, near, far)
 
 
 def solution(mesh):

time: 585 us -> 522 us (0.89)
  waiting for transfers between devices: 282 us -> 150 us
  starting transfers between devices: 63.8 us -> 141 us
  Pallas kernels: 199 us -> 190 us
    all_to_all x2, waiting for transfers between devices: 178 us -> 0.01 us  [the longest x1 0.01 us: body(): lax.all_to_all(near_out, 'row', split_axis=0, concat_axis=0, tiled=True)]
    ppermute x11 -> x32, starting transfers between devices: 14.2 us -> 78 us  [the longest x14 44 us: body(): lax.ppermute(parts[d], 'col', [(c, (c + d) % COLS) for c in range(COLS)])]
    ppermute x11 -> x32, waiting for transfers between devices: 44.4 us -> 98.7 us  [the longest x14 61.3 us: body(): lax.ppermute(parts[d], 'col', [(c, (c + d) % COLS) for c in range(COLS)])]
    all_gather x3 -> x2, waiting for transfers between devices: 54.2 us -> 0.01 us  [the longest x1 0.01 us: body(): row_strip = lax.all_gather(row_piece, 'col', axis=0, tiled=True)]
    all_gather x1, waiting for transfers between devices: 0.01 us -> 50.6 us  [body(): col_strip = lax.all_gather(strip, 'row', axis=0, tiled=True)]
    all_to_all x2, starting transfers between devices: 21.3 us -> 33.7 us  [the longest x1 17.9 us: body(): lax.all_to_all(near_out, 'row', split_axis=0, concat_axis=0, tiled=True)]
    pallas_call x1, Pallas kernels: 47.6 us -> 40.8 us  [update_front(): pl.pallas_call(update_kernel, grid_spec=pltpu.PrefetchScalarGridSpec(num_...]
    pallas_call x6 -> x11, Pallas kernels: 139 us -> 137 us  [the longest x4 104 us: factor_part(): pl.pallas_call(functools.partial(factor_kernel, part * count, count, last...]
  transfers between devices with their start and end apart: 19 -> 39, of which waited for: 6 -> 7; matrix products, arithmetic and copies ran while one was open for 2% -> 2% of each run, Pallas kernels for 30% -> 33%
where the time goes in v2:
time: 522 us; the launch traced here: 512 us
  Pallas kernels  190 us (36%)
  waiting for transfers between devices  150 us (29%)
  starting transfers between devices  141 us (27%)
  between operations  13.7 us (3%)
  other arithmetic  9.05 us (2%)
  local copies, waits for them, and re-layouts  8.56 us (2%)
    pallas_call x4, Pallas kernels, factor_part(): pl.pallas_call(functools.partial(factor_kernel, part * count, count, last...  104 us
    ppermute x14, waiting for transfers between devices, body(): lax.ppermute(parts[d], 'col', [(c, (c + d) % COLS) for c in range(COLS)])  61.3 us
    all_gather x1, waiting for transfers between devices, body(): col_strip = lax.all_gather(strip, 'row', axis=0, tiled=True)  50.6 us
    ppermute x14, starting transfers between devices, body(): lax.ppermute(parts[d], 'col', [(c, (c + d) % COLS) for c in range(COLS)])  44 us
    pallas_call x1, Pallas kernels, update_front(): pl.pallas_call(update_kernel, grid_spec=pltpu.PrefetchScalarGridSpec(num_...  40.8 us
    pallas_call x6, Pallas kernels, gather_call(): pl.pallas_call(run, in_specs=[pl.BlockSpec(memory_space=pltpu.SMEM)] * le...  30.7 us
    ppermute x1, waiting for transfers between devices, body(): row_piece = lax.ppermute(strip, axes, pairs)  21 us
    all_to_all x1, starting transfers between devices, body(): lax.all_to_all(near_out, 'row', split_axis=0, concat_axis=0, tiled=True)  17.9 us
  transfers between devices with their start and end apart: 39, of which 7 were waited for; matrix products, arithmetic and copies ran while one was open for 2% of the time, Pallas kernels for 33%

profile of v2, /device:TPU:21, one launch (start us, length us, event | category | flops | bytes accessed | tf_op | source)
XLA Modules:
  0.0 512.4 jit_solution(1352007811697781142)
XLA Ops:
  6.5 3.6 cut_strip.1
  10.2 1.4 collective-permute-start
  11.6 0.7 collective-permute-start.1
  12.3 0.7 collective-permute-start.2
  13.0 0.7 collective-permute-start.3
  13.7 0.7 collective-permute-start.4
  15.1 1.5 collective-permute-start.5
  16.5 1.4 collective-permute-start.6
  18.1 0.6 gather_fusion
  18.8 0.7 pad_add_fusion.1.refs_0_
  19.4 6.5 %pack_first.1 = (f32[1280,128]{1,0:T(8,128)}, f32[1280,128]{1,0:T(8,128)}, f32[1280,128]{1,0:T(8,128)}, f32[1280,128]{1,0:T(8,128)}, f32[1280,128]{1,0:T(8,128)}...) custom-call(s32[25]{0:T(128)} %pad_add_fusion.1.refs_0_, ...), custom_call_target="tpu_custom_call" | custom-call | bytes 12582912 | tf_op jit(solution)/shard_map/pack_first/pallas_call | solution.py:36
  25.9 11.2 %all-to-all-start = ((f32[16,128,128]{2,1,0:T(8,128)}), f32[16,128,128]{2,1,0:T(8,128)}, u32[]{:S(2)}, u32[]{:S(2)}) async-start(f32[16,128,128]{2,1,0:T(8,128)} %get-tuple-element.41), calls=%async_computation | async-start | bytes 2097152 | tf_op jit(solution)/shard_map/all_to_all | solution.py:540
  37.2 2.5 add_add_fusion
  39.6 8.3 %collective-permute-start.7 = (f32[128,1024]{1,0:T(8,128)}, f32[128,1024]{1,0:T(8,128)S(1)}, u32[]{:S(2)}, u32[]{:S(2)}) collective-permute-start(f32[128,1024]{1,0:T(8,128)} %add_add_fusion), channel_id=1, source_target_pairs={{0,0},{1,8},{2,16},{3,24},{4,32},{5,40},{6,48},{7,56},{8,64},{9,72... | collective-permute-start | bytes 1572872 | tf_op jit(solution)/shard_map/ppermute | solution.py:530
  48.5 2.4 collective-permute-start.11
  51.2 0.9 collective-permute-start.13
  52.1 0.7 select_reduce_fusion.4.refs_0_
  52.8 15.4 %collective-permute-done.7.refs_2_.parent = f32[128,1024]{1,0:T(8,128)S(1)} collective-permute-done((f32[128,1024]{1,0:T(8,128)}, f32[128,1024]{1,0:T(8,128)S(1)}, u32[]{:S(2)}, u32[]{:S(2)}) %collective-permute-start.7) | collective-permute-done | bytes 524320 | tf_op jit(solution)/shard_map/ppermute | solution.py:530
  68.2 0.8 copy-done.6
  69.0 3.2 collective-permute-start.14
  72.2 3.2 pick_early.1
  75.4 17.4 %all-to-all-start.1 = ((f32[16,128,128]{2,1,0:T(8,128)}), f32[16,128,128]{2,1,0:T(8,128)}, u32[]{:S(2)}, u32[]{:S(2)}) async-start(f32[16,128,128]{2,1,0:T(8,128)} %pick_early.1), calls=%async_computation.1 | async-start | bytes 2097152 | tf_op jit(solution)/shard_map/all_to_all | solution.py:542
  93.1 11.6 %collective-permute-start.8 = (f32[1280,128]{1,0:T(8,128)}, f32[1280,128]{1,0:T(8,128)}, u32[]{:S(2)}, u32[]{:S(2)}) collective-permute-start(f32[1280,128]{1,0:T(8,128)} %get-tuple-element.42), channel_id=1, source_target_pairs={{0,1},{1,2},{2,3},{3,4},{4,5},{5,6},{6,7},{7,0},{8,9},{9,10},{10,1... | collective-permute-start | bytes 1966088 | tf_op jit(solution)/shard_map/ppermute | solution.py:536
  104.7 4.7 collective-permute-start.9
  110.9 18.1 %collective-permute-done.13.refs_5_ = f32[1280,128]{1,0:T(8,128)S(1)} collective-permute-done((f32[1280,128]{1,0:T(8,128)}, f32[1280,128]{1,0:T(8,128)S(1)}, u32[]{:S(2)}, u32[]{:S(2)}) %collective-permute-start.13) | collective-permute-done | bytes 655392 | tf_op jit(solution)/shard_map/ppermute | solution.py:536
  130.4 2.4 assemble_strip.1
  132.7 1.1 fusion.28
  133.8 0.7 collective-permute-start.16
  134.5 0.7 collective-permute-start.17
  135.2 1.3 collective-permute-start.18
  136.5 0.7 collective-permute-start.19
  137.2 0.7 collective-permute-start.20
  137.9 0.7 collective-permute-start.21
  138.6 0.7 collective-permute-start.22
  139.3 0.9 collective-permute-done.18
  140.2 0.7 collective-permute-start.23
  140.8 0.7 collective-permute-start.24
  141.6 0.9 add_add_fusion.1.refs_11_
  142.5 11.9 %collective-permute-start.15 = (f32[128,1024]{1,0:T(8,128)}, f32[128,1024]{1,0:T(8,128)S(1)}, u32[]{:S(2)}, u32[]{:S(2)}) collective-permute-start(f32[128,1024]{1,0:T(8,128)} %assemble_strip.1), channel_id=1, source_target_pairs={{0,0},{8,1},{16,2},{24,3},{32,4},{40,5},{48,6},{56,7},{64,8},{72,9... | collective-permute-start | bytes 1572872 | tf_op jit(solution)/shard_map/ppermute | solution.py:560
  154.4 21.0 %collective-permute-done.15.refs_12_ = f32[128,1024]{1,0:T(8,128)S(1)} collective-permute-done((f32[128,1024]{1,0:T(8,128)}, f32[128,1024]{1,0:T(8,128)S(1)}, u32[]{:S(2)}, u32[]{:S(2)}) %collective-permute-start.15) | collective-permute-done | bytes 524320 | tf_op jit(solution)/shard_map/ppermute | solution.py:560
  175.4 0.8 copy-done.5
  176.3 0.7 all-gather.6.cloned.1.call-update
  177.8 0.7 fusion.29
  178.5 5.3 %pack_rows.2.after.refs_2_ = f32[16,5,128,128]{3,2,1,0:T(8,128)} custom-call(s32[16]{0:T(128)} %copy-done.15, s32[16]{0:T(128)} %convert_element_type.32.refs_1_, s32[5]{0:T(128)} %get-tuple-element.75.refs_2_, f32[10,128,128]{2,1,0:T(8,128)} %bitcast.56, f32[10,128,128]{2,1,0:T(8,128)} %bitcast.9.refs_4_, f32[10,128,128]{2,1,0:T(8,128)} %bitcast.10.refs_5_, ...), custom_call_target="tpu_custom_call" | custom-call | bytes 10485760 | tf_op jit(solution)/shard_map/pack_rows/pallas_call | solution.py:36
  183.7 17.9 %all-to-all-start.2 = ((f32[16,5,128,128]{3,2,1,0:T(8,128)}), f32[16,5,128,128]{3,2,1,0:T(8,128)}, u32[]{:S(2)}, u32[]{:S(2)}) async-start(f32[16,5,128,128]{3,2,1,0:T(8,128)} %pack_rows.2.after.refs_2_), calls=%async_computation.2 | async-start | bytes 10485760 | tf_op jit(solution)/shard_map/all_to_all | solution.py:566
  202.6 0.7 reshape.267.keep
  203.8 5.7 %pack_second.1 = (f32[1280,128]{1,0:T(8,128)}, f32[1280,128]{1,0:T(8,128)}, f32[1280,128]{1,0:T(8,128)}, f32[1280,128]{1,0:T(8,128)}, f32[1280,128]{1,0:T(8,128)...) custom-call(s32[8]{0:T(128)} %and_select_fusion.refs_0_, f32[1280,1280]{1,0:T(8,128)} %refs_1_.3, ...), custom_call_target="tpu_custom_call" | custom-call | bytes 10485760 | tf_op jit(solution)/shard_map/pack_second/pallas_call | solution.py:36
  209.5 2.5 collective-permute-start.25
  212.0 2.5 collective-permute-start.26
  215.3 0.7 select_reduce_fusion.rank
  216.7 4.2 collective-permute-start.28
  220.8 2.6 collective-permute-start.29
  223.5 8.4 %collective-permute-start.30 = (f32[1280,128]{1,0:T(8,128)}, f32[1280,128]{1,0:T(8,128)}, u32[]{:S(2)}, u32[]{:S(2)}) collective-permute-start(f32[1280,128]{1,0:T(8,128)} %get-tuple-element.56), channel_id=1, source_target_pairs={{0,6},{1,7},{2,0},{3,1},{4,2},{5,3},{6,4},{7,5},{8,14},{9,15},{10,... | collective-permute-start | bytes 1966088 | tf_op jit(solution)/shard_map/ppermute | solution.py:536
  231.9 42.7 %collective-permute-done.26 = f32[1280,128]{1,0:T(8,128)S(1)} collective-permute-done((f32[1280,128]{1,0:T(8,128)}, f32[1280,128]{1,0:T(8,128)S(1)}, u32[]{:S(2)}, u32[]{:S(2)}) %collective-permute-start.26) | collective-permute-done | bytes 655392 | tf_op jit(solution)/shard_map/ppermute | solution.py:536
  274.6 29.6 %factor_lead.4.refs_20_.given = f32[1024,1024]{1,0:T(8,128)} custom-call(f32[1024,1024]{1,0:T(8,128)} %all-gather.8.cloned.1.call-done.given, f32[16,5,128,128]{3,2,1,0:T(8,128)} %pack_rows.2.after.refs_2_), custom_call_target="tpu_custom_call" | custom-call | flops 24999999488 | bytes 8388608 | tf_op jit(solution)/shard_map/factor_lead/pallas_call | solution.py:318
  304.3 0.8 copy-done.9
  305.5 6.5 %pack_rows.3.after = f32[16,5,128,128]{3,2,1,0:T(8,128)} custom-call(s32[16]{0:T(128)} %copy-done.15, s32[16]{0:T(128)} %convert_element_type.32.refs_1_, s32[5]{0:T(128)} %get-tuple-element.74.refs_2_, f32[10,128,128]{2,1,0:T(8,128)} %bitcast.57, f32[10,128,128]{2,1,0:T(8,128)} %bitcast.9.refs_4_, f32[10,128,128]{2,1,0:T(8,128)} %bitcast.10.refs_5_, ...), custom_call_target="tpu_custom_call" | custom-call | bytes 10485760 | tf_op jit(solution)/shard_map/pack_rows/pallas_call | solution.py:36
  312.0 15.8 %all-to-all-start.3 = ((f32[16,5,128,128]{3,2,1,0:T(8,128)}), f32[16,5,128,128]{3,2,1,0:T(8,128)}, u32[]{:S(2)}, u32[]{:S(2)}) async-start(f32[16,5,128,128]{3,2,1,0:T(8,128)} %pack_rows.3.after), calls=%async_computation.3 | async-start | bytes 10485760 | tf_op jit(solution)/shard_map/all_to_all | solution.py:571
  327.8 26.9 %factor_lead.5.given = f32[1024,1024]{1,0:T(8,128)} custom-call(f32[1024,1024]{1,0:T(8,128)} %factor_lead.4.refs_20_.given, f32[16,5,128,128]{3,2,1,0:T(8,128)} %pack_rows.3.after), custom_call_target="tpu_custom_call" | custom-call | flops 24999999488 | bytes 8388608 | tf_op jit(solution)/shard_map/factor_lead/pallas_call | solution.py:318
  354.7 24.3 %factor_lead.6.given = f32[1024,1024]{1,0:T(8,128)} custom-call(f32[1024,1024]{1,0:T(8,128)} %factor_lead.5.given, f32[16,5,128,128]{3,2,1,0:T(8,128)} %pack_rows.3.after), custom_call_target="tpu_custom_call" | custom-call | flops 24999999488 | bytes 8388608 | tf_op jit(solution)/shard_map/factor_lead/pallas_call | solution.py:318
  379.1 22.7 %factor_lead.7 = (bf16[1024,1024]{1,0:T(8,128)(2,1)}, bf16[1024,1024]{1,0:T(8,128)(2,1)}) custom-call(f32[1024,1024]{1,0:T(8,128)} %factor_lead.6.given, f32[16,5,128,128]{3,2,1,0:T(8,128)} %pack_rows.3.after), custom_call_target="tpu_custom_call" | custom-call | flops 24999999488 | bytes 8388608 | tf_op jit(solution)/shard_map/factor_lead/pallas_call | solution.py:318
  401.8 50.6 %all-gather.6.cloned.1.call-done.col_strip = f32[2048,1024]{1,0:T(8,128)} async-done(((f32[128,1024]{1,0:T(8,128)}), f32[2048,1024]{1,0:T(8,128)}) %all-gather.6.cloned.1.call-update) | async-done | bytes 8388624 | tf_op jit(solution)/shard_map/all_gather | solution.py:561
  452.3 40.8 %update_front.1.front = f32[1024,2048]{1,0:T(8,128)} custom-call(s32[2]{0:T(128)} %pad_add_fusion.flags, f32[1024,1024]{1,0:T(8,128)} %all-gather.4.cloned.1.call-done.row_strip, f32[2048,1024]{1,0:T(8,128)} %all-gather.6.cloned.1.call-done.col_strip, bf16[1024,1024]{1,0:T(8,128)(2,1)} %get-tuple-element.58.inv_hi, ...), custom_call_target="tpu_custom_call" | custom-call | flops 40000000000 | bytes 33554432 | tf_op jit(solution)/shard_map/update_front/pallas_call | solution.py:387
  493.2 12.7 %place_children.1 = f32[1024,2048]{1,0:T(8,128)} custom-call(s32[2,8]{1,0:T(2,128)} %fusion.18.source, s32[2,16]{1,0:T(2,128)} %select_reduce_fusion.rank, s32[2,128]{1,0:T(2,128)} %reshape.267.keep, f32[1024,2048]{1,0:T(8,128)} %update_front.1.front, f32[16,5,128,128]{3,2,1,0:T(8,128)} %all-to-all-done.2.refs_19_.refs_0_.refs_2_, ...), custom_call_target="tpu_custom_call", output_to_operand_aliasing={{}: (3, {})} | custom-call | bytes 25165824 | tf_op jit(solution)/shard_map/place_children/pallas_call | solution.py:435
  (107 shorter events, 9.0 us)
Async XLA Ops:
  6.5 8.0 %copy-start.14 = (s32[2,80]{1,0:T(2,128)S(1)}, s32[2,80]{1,0:T(2,128)}, u32[]{:S(2)}) copy-start(s32[2,80]{1,0:T(2,128)} %param.8) | copy-start | bytes 1924
  10.2 27.0 %copy-start.12 = (f32[128,1024]{1,0:T(8,128)S(1)}, f32[128,1024]{1,0:T(8,128)}, u32[]{:S(2)}) copy-start(f32[128,1024]{1,0:T(8,128)} %get-tuple-element.33) | copy-start | bytes 1572868
  10.2 4.9 collective-permute-start
  11.6 4.9 collective-permute-start.1
  12.3 24.8 %collective-permute-start.2 = (f32[128,1024]{1,0:T(8,128)}, f32[128,1024]{1,0:T(8,128)S(1)}, u32[]{:S(2)}, u32[]{:S(2)}) collective-permute-start(f32[128,1024]{1,0:T(8,128)} %get-tuple-element.36), channel_id=1, source_target_pairs={{0,3},{8,11},{16,19},{24,27},{32,35},{40,43},{48,51},{56,59},{64,6... | collective-permute-start | bytes 1572872 | tf_op jit(solution)/shard_map/ppermute | solution.py:526
  13.0 24.1 %collective-permute-start.3 = (f32[128,1024]{1,0:T(8,128)}, f32[128,1024]{1,0:T(8,128)S(1)}, u32[]{:S(2)}, u32[]{:S(2)}) collective-permute-start(f32[128,1024]{1,0:T(8,128)} %get-tuple-element.37), channel_id=1, source_target_pairs={{0,4},{8,12},{16,20},{24,28},{32,36},{40,44},{48,52},{56,60},{64,6... | collective-permute-start | bytes 1572872 | tf_op jit(solution)/shard_map/ppermute | solution.py:526
  13.7 23.4 %collective-permute-start.4 = (f32[128,1024]{1,0:T(8,128)}, f32[128,1024]{1,0:T(8,128)S(1)}, u32[]{:S(2)}, u32[]{:S(2)}) collective-permute-start(f32[128,1024]{1,0:T(8,128)} %get-tuple-element.38), channel_id=1, source_target_pairs={{0,5},{8,13},{16,21},{24,29},{32,37},{40,45},{48,53},{56,61},{64,6... | collective-permute-start | bytes 1572872 | tf_op jit(solution)/shard_map/ppermute | solution.py:526
  15.1 22.1 %collective-permute-start.5 = (f32[128,1024]{1,0:T(8,128)}, f32[128,1024]{1,0:T(8,128)}, u32[]{:S(2)}, u32[]{:S(2)}) collective-permute-start(f32[128,1024]{1,0:T(8,128)} %get-tuple-element.39), channel_id=1, source_target_pairs={{0,6},{8,14},{16,22},{24,30},{32,38},{40,46},{48,54},{56,62},{64,7... | collective-permute-start | bytes 1572872 | tf_op jit(solution)/shard_map/ppermute | solution.py:526
  16.5 20.6 %collective-permute-start.6 = (f32[128,1024]{1,0:T(8,128)}, f32[128,1024]{1,0:T(8,128)}, u32[]{:S(2)}, u32[]{:S(2)}) collective-permute-start(f32[128,1024]{1,0:T(8,128)} %get-tuple-element.40), channel_id=1, source_target_pairs={{0,7},{8,15},{16,23},{24,31},{32,39},{40,47},{48,55},{56,63},{64,7... | collective-permute-start | bytes 1572872 | tf_op jit(solution)/shard_map/ppermute | solution.py:526
  18.1 21.5 %copy-start.15 = (s32[16]{0:T(128)}, s32[16]{0:T(128)S(1)}, u32[]{:S(2)}) copy-start(s32[16]{0:T(128)S(1)} %get-tuple-element.61.refs_0_) | copy-start | bytes 196
  25.9 46.3 %all-to-all-start = ((f32[16,128,128]{2,1,0:T(8,128)}), f32[16,128,128]{2,1,0:T(8,128)}, u32[]{:S(2)}, u32[]{:S(2)}) async-start(f32[16,128,128]{2,1,0:T(8,128)} %get-tuple-element.41), calls=%async_computation | async-start | bytes 2097152 | tf_op jit(solution)/shard_map/all_to_all | solution.py:540
  37.1 55.7 %copy-start.13 = (s32[2,80,80]{2,1,0:T(8,128)S(1)}, s32[2,80,80]{2,1,0:T(8,128)}, u32[]{:S(2)}) copy-start(s32[2,80,80]{2,1,0:T(8,128)} %param.9) | copy-start | bytes 153604
  39.6 28.6 %collective-permute-start.7 = (f32[128,1024]{1,0:T(8,128)}, f32[128,1024]{1,0:T(8,128)S(1)}, u32[]{:S(2)}, u32[]{:S(2)}) collective-permute-start(f32[128,1024]{1,0:T(8,128)} %add_add_fusion), channel_id=1, source_target_pairs={{0,0},{1,8},{2,16},{3,24},{4,32},{5,40},{6,48},{7,56},{8,64},{9,72... | collective-permute-start | bytes 1572872 | tf_op jit(solution)/shard_map/ppermute | solution.py:530
  47.9 45.1 %collective-permute-start.10 = (f32[1280,128]{1,0:T(8,128)}, f32[1280,128]{1,0:T(8,128)S(1)}, u32[]{:S(2)}, u32[]{:S(2)}) collective-permute-start(f32[1280,128]{1,0:T(8,128)} %get-tuple-element.44), channel_id=1, source_target_pairs={{0,3},{1,4},{2,5},{3,6},{4,7},{5,0},{6,1},{7,2},{8,11},{9,12},{10,... | collective-permute-start | bytes 1966088 | tf_op jit(solution)/shard_map/ppermute | solution.py:536
  48.5 56.2 %collective-permute-start.11 = (f32[1280,128]{1,0:T(8,128)}, f32[1280,128]{1,0:T(8,128)S(1)}, u32[]{:S(2)}, u32[]{:S(2)}) collective-permute-start(f32[1280,128]{1,0:T(8,128)} %get-tuple-element.45), channel_id=1, source_target_pairs={{0,4},{1,5},{2,6},{3,7},{4,0},{5,1},{6,2},{7,3},{8,12},{9,13},{10,... | collective-permute-start | bytes 1966088 | tf_op jit(solution)/shard_map/ppermute | solution.py:536
  50.9 60.1 %collective-permute-start.12 = (f32[1280,128]{1,0:T(8,128)}, f32[1280,128]{1,0:T(8,128)S(1)}, u32[]{:S(2)}, u32[]{:S(2)}) collective-permute-start(f32[1280,128]{1,0:T(8,128)} %get-tuple-element.46), channel_id=1, source_target_pairs={{0,5},{1,6},{2,7},{3,0},{4,1},{5,2},{6,3},{7,4},{8,13},{9,14},{10,... | collective-permute-start | bytes 1966088 | tf_op jit(solution)/shard_map/ppermute | solution.py:536
  51.2 77.9 %collective-permute-start.13 = (f32[1280,128]{1,0:T(8,128)}, f32[1280,128]{1,0:T(8,128)S(1)}, u32[]{:S(2)}, u32[]{:S(2)}) collective-permute-start(f32[1280,128]{1,0:T(8,128)} %get-tuple-element.47), channel_id=1, source_target_pairs={{0,6},{1,7},{2,0},{3,1},{4,2},{5,3},{6,4},{7,5},{8,14},{9,15},{10,... | collective-permute-start | bytes 1966088 | tf_op jit(solution)/shard_map/ppermute | solution.py:536
  68.2 0.8 copy-start.6
  69.0 60.5 %collective-permute-start.14 = (f32[1280,128]{1,0:T(8,128)}, f32[1280,128]{1,0:T(8,128)S(1)}, u32[]{:S(2)}, u32[]{:S(2)}) collective-permute-start(f32[1280,128]{1,0:T(8,128)} %get-tuple-element.48), channel_id=1, source_target_pairs={{0,7},{1,0},{2,1},{3,2},{4,3},{5,4},{6,5},{7,6},{8,15},{9,8},{10,9... | collective-permute-start | bytes 1966088 | tf_op jit(solution)/shard_map/ppermute | solution.py:536
  75.4 54.2 %all-to-all-start.1 = ((f32[16,128,128]{2,1,0:T(8,128)}), f32[16,128,128]{2,1,0:T(8,128)}, u32[]{:S(2)}, u32[]{:S(2)}) async-start(f32[16,128,128]{2,1,0:T(8,128)} %pick_early.1), calls=%async_computation.1 | async-start | bytes 2097152 | tf_op jit(solution)/shard_map/all_to_all | solution.py:542
  92.8 181.8 %all-gather.8.cloned.1.call-start = ((), (), s32[]{:S(2)}) async-start(), calls=%async_computation.6 | async-start | bytes 4456448 | tf_op jit(solution)/shard_map/all_gather | solution.py:558
  93.1 36.5 %copy-start = (f32[1280,128]{1,0:T(8,128)}, f32[1280,128]{1,0:T(8,128)S(1)}, u32[]{:S(2)}) copy-start(f32[1280,128]{1,0:T(8,128)S(1)} %collective-permute-done.10.refs_2_) | copy-start | bytes 1966084
  93.1 36.5 %collective-permute-start.8 = (f32[1280,128]{1,0:T(8,128)}, f32[1280,128]{1,0:T(8,128)}, u32[]{:S(2)}, u32[]{:S(2)}) collective-permute-start(f32[1280,128]{1,0:T(8,128)} %get-tuple-element.42), channel_id=1, source_target_pairs={{0,1},{1,2},{2,3},{3,4},{4,5},{5,6},{6,7},{7,0},{8,9},{9,10},{10,1... | collective-permute-start | bytes 1966088 | tf_op jit(solution)/shard_map/ppermute | solution.py:536
  104.7 24.9 %copy-start.1 = (f32[1280,128]{1,0:T(8,128)}, f32[1280,128]{1,0:T(8,128)S(1)}, u32[]{:S(2)}) copy-start(f32[1280,128]{1,0:T(8,128)S(1)} %collective-permute-done.11.refs_3_) | copy-start | bytes 1966084
  104.7 24.9 %collective-permute-start.9 = (f32[1280,128]{1,0:T(8,128)}, f32[1280,128]{1,0:T(8,128)}, u32[]{:S(2)}, u32[]{:S(2)}) collective-permute-start(f32[1280,128]{1,0:T(8,128)} %get-tuple-element.43), channel_id=1, source_target_pairs={{0,2},{1,3},{2,4},{3,5},{4,6},{5,7},{6,0},{7,1},{8,10},{9,11},{10,... | collective-permute-start | bytes 1966088 | tf_op jit(solution)/shard_map/ppermute | solution.py:536
  110.9 18.6 %copy-start.2 = (f32[1280,128]{1,0:T(8,128)}, f32[1280,128]{1,0:T(8,128)S(1)}, u32[]{:S(2)}) copy-start(f32[1280,128]{1,0:T(8,128)S(1)} %collective-permute-done.12.refs_4_) | copy-start | bytes 1966084
  129.1 0.9 copy-start.3
  129.5 0.8 copy-start.4
  133.8 1.4 collective-permute-start.16
  134.5 0.7 collective-permute-start.17
  135.2 4.9 collective-permute-start.18
  136.5 4.3 collective-permute-start.19
  137.2 4.3 collective-permute-start.20
  137.9 3.6 collective-permute-start.21
  138.6 3.0 collective-permute-start.22
  140.2 1.4 collective-permute-start.23
  140.8 0.7 collective-permute-start.24
  142.5 259.3 %all-gather.4.cloned.1.call-start = ((), (), s32[]{:S(2)}) async-start(), calls=%async_computation.4 | async-start | bytes 4718592 | tf_op jit(solution)/shard_map/all_gather | solution.py:562
  142.5 32.9 %collective-permute-start.15 = (f32[128,1024]{1,0:T(8,128)}, f32[128,1024]{1,0:T(8,128)S(1)}, u32[]{:S(2)}, u32[]{:S(2)}) collective-permute-start(f32[128,1024]{1,0:T(8,128)} %assemble_strip.1), channel_id=1, source_target_pairs={{0,0},{8,1},{16,2},{24,3},{32,4},{40,5},{48,6},{56,7},{64,8},{72,9... | collective-permute-start | bytes 1572872 | tf_op jit(solution)/shard_map/ppermute | solution.py:560
  175.4 0.8 copy-start.5
  176.2 276.1 %all-gather.6.cloned.1.call-start = ((), (), s32[]{:S(2)}) async-start(), calls=%async_computation.5 | async-start | bytes 8912896 | tf_op jit(solution)/shard_map/all_gather | solution.py:561
  183.7 120.6 %all-to-all-start.2 = ((f32[16,5,128,128]{3,2,1,0:T(8,128)}), f32[16,5,128,128]{3,2,1,0:T(8,128)}, u32[]{:S(2)}, u32[]{:S(2)}) async-start(f32[16,5,128,128]{3,2,1,0:T(8,128)} %pack_rows.2.after.refs_2_), calls=%async_computation.2 | async-start | bytes 10485760 | tf_op jit(solution)/shard_map/all_to_all | solution.py:566
  209.5 14.0 %collective-permute-start.25 = (f32[1280,128]{1,0:T(8,128)}, f32[1280,128]{1,0:T(8,128)S(1)}, u32[]{:S(2)}, u32[]{:S(2)}) collective-permute-start(f32[1280,128]{1,0:T(8,128)} %get-tuple-element.51), channel_id=1, source_target_pairs={{0,1},{1,2},{2,3},{3,4},{4,5},{5,6},{6,7},{7,0},{8,9},{9,10},{10,1... | collective-permute-start | bytes 1966088 | tf_op jit(solution)/shard_map/ppermute | solution.py:536
  212.0 62.6 %collective-permute-start.26 = (f32[1280,128]{1,0:T(8,128)}, f32[1280,128]{1,0:T(8,128)S(1)}, u32[]{:S(2)}, u32[]{:S(2)}) collective-permute-start(f32[1280,128]{1,0:T(8,128)} %get-tuple-element.52), channel_id=1, source_target_pairs={{0,2},{1,3},{2,4},{3,5},{4,6},{5,7},{6,0},{7,1},{8,10},{9,11},{10,... | collective-permute-start | bytes 1966088 | tf_op jit(solution)/shard_map/ppermute | solution.py:536
  216.5 87.7 %collective-permute-start.27 = (f32[1280,128]{1,0:T(8,128)}, f32[1280,128]{1,0:T(8,128)S(1)}, u32[]{:S(2)}, u32[]{:S(2)}) collective-permute-start(f32[1280,128]{1,0:T(8,128)} %get-tuple-element.53), channel_id=1, source_target_pairs={{0,3},{1,4},{2,5},{3,6},{4,7},{5,0},{6,1},{7,2},{8,11},{9,12},{10,... | collective-permute-start | bytes 1966088 | tf_op jit(solution)/shard_map/ppermute | solution.py:536
  216.7 87.6 %collective-permute-start.28 = (f32[1280,128]{1,0:T(8,128)}, f32[1280,128]{1,0:T(8,128)S(1)}, u32[]{:S(2)}, u32[]{:S(2)}) collective-permute-start(f32[1280,128]{1,0:T(8,128)} %get-tuple-element.54), channel_id=1, source_target_pairs={{0,4},{1,5},{2,6},{3,7},{4,0},{5,1},{6,2},{7,3},{8,12},{9,13},{10,... | collective-permute-start | bytes 1966088 | tf_op jit(solution)/shard_map/ppermute | solution.py:536
  220.8 83.4 %collective-permute-start.29 = (f32[1280,128]{1,0:T(8,128)}, f32[1280,128]{1,0:T(8,128)S(1)}, u32[]{:S(2)}, u32[]{:S(2)}) collective-permute-start(f32[1280,128]{1,0:T(8,128)} %get-tuple-element.55), channel_id=1, source_target_pairs={{0,5},{1,6},{2,7},{3,0},{4,1},{5,2},{6,3},{7,4},{8,13},{9,14},{10,... | collective-permute-start | bytes 1966088 | tf_op jit(solution)/shard_map/ppermute | solution.py:536
  223.5 80.7 %copy-start.7 = (f32[1280,128]{1,0:T(8,128)}, f32[1280,128]{1,0:T(8,128)S(1)}, u32[]{:S(2)}) copy-start(f32[1280,128]{1,0:T(8,128)S(1)} %collective-permute-done.25) | copy-start | bytes 1966084
  223.5 80.8 %collective-permute-start.30 = (f32[1280,128]{1,0:T(8,128)}, f32[1280,128]{1,0:T(8,128)}, u32[]{:S(2)}, u32[]{:S(2)}) collective-permute-start(f32[1280,128]{1,0:T(8,128)} %get-tuple-element.56), channel_id=1, source_target_pairs={{0,6},{1,7},{2,0},{3,1},{4,2},{5,3},{6,4},{7,5},{8,14},{9,15},{10,... | collective-permute-start | bytes 1966088 | tf_op jit(solution)/shard_map/ppermute | solution.py:536
  274.6 29.6 %copy-start.8 = (f32[1280,128]{1,0:T(8,128)}, f32[1280,128]{1,0:T(8,128)S(1)}, u32[]{:S(2)}) copy-start(f32[1280,128]{1,0:T(8,128)S(1)} %collective-permute-done.26) | copy-start | bytes 1966084
  274.6 29.7 %collective-permute-start.31 = (f32[1280,128]{1,0:T(8,128)}, f32[1280,128]{1,0:T(8,128)}, u32[]{:S(2)}, u32[]{:S(2)}) collective-permute-start(f32[1280,128]{1,0:T(8,128)} %get-tuple-element.57), channel_id=1, source_target_pairs={{0,7},{1,0},{2,1},{3,2},{4,3},{5,4},{6,5},{7,6},{8,15},{9,8},{10,9... | collective-permute-start | bytes 1966088 | tf_op jit(solution)/shard_map/ppermute | solution.py:536
  304.2 0.9 copy-start.9
  304.3 1.1 copy-start.10
  304.3 1.3 copy-start.11
  312.0 181.1 %all-to-all-start.3 = ((f32[16,5,128,128]{3,2,1,0:T(8,128)}), f32[16,5,128,128]{3,2,1,0:T(8,128)}, u32[]{:S(2)}, u32[]{:S(2)}) async-start(f32[16,5,128,128]{3,2,1,0:T(8,128)} %pack_rows.3.after), calls=%async_computation.3 | async-start | bytes 10485760 | tf_op jit(solution)/shard_map/all_to_all | solution.py:571
Sparse Core Ops, SparseCore 0:
  142.6 122.1 all-gather.7
  266.5 56.0 all-gather.3
  324.8 127.5 all-gather.5

commit v3 on v2

--- a/solution.py
+++ b/solution.py
@@ -63,30 +63,33 @@
         copy.wait()
 
 
-def pack_first_kernel(table, children, *refs):
-    outs, early = refs[:COLS], refs[COLS]
-    wide, small, sem_in, sem_out = refs[COLS + 1 :]
+def pack_early_kernel(table, children, out, held, sem_in, sem_out):
     moves = []
     for s in range(2 * COLS):
-        source = children.at[lanes_of(table[3 * COLS]), lanes_of(table[COLS + s])]
-        moves.append((source, small.at[s], early.at[s]))
-    for s in range(COLS):
-        moves.append((children.at[:, lanes_of(table[s])], wide.at[s], outs[s]))
+        source = children.at[lanes_of(table[2 * COLS]), lanes_of(table[s])]
+        moves.append((source, held.at[s], out.at[s]))
     relay(moves, sem_in, sem_out)
 
 
-def pack_first(table, children):
-    wide = (children.shape[0], BLOCK)
-    small = (2 * COLS, BLOCK, BLOCK)
+def pack_early(table, children):
+    shape = (2 * COLS, BLOCK, BLOCK)
     return gather_call(
-        pack_first_kernel,
-        [table],
-        [children],
-        [wide] * COLS + [small],
-        [(COLS,) + wide, small],
-        (3 * COLS,),
-        "pack_first",
-    )
+        pack_early_kernel, [table], [children], [shape], [shape], (2 * COLS,), "pack_early"
+    )[0]
+
+
+def pack_first_kernel(table, children, out, held, sem_in, sem_out):
+    moves = [
+        (children.at[:, lanes_of(table[s])], held.at[s], out.at[s]) for s in range(COLS)
+    ]
+    relay(moves, sem_in, sem_out)
+
+
+def pack_first(table, children, after):
+    shape = (COLS, children.shape[0], BLOCK)
+    return gather_call(
+        pack_first_kernel, [table], [children], [shape], [shape], (COLS,), "pack_first", after
+    )[0]
 
 
 def pack_second_kernel(table, children, *refs):
@@ -141,8 +144,8 @@
 HALF = GRP // 2
 
 
-def pack_rows_kernel(row_table, row_has, origin, *refs):
-    sources, (out, held, sem_in, sem_out) = refs[:-4], refs[-4:]
+def pack_rows_kernel(row_table, row_has, origin, first, *refs):
+    second, (out, held, sem_in, sem_out) = refs[:-4], refs[-4:]
 
     def each(act):
         def one(r, carry):
@@ -156,20 +159,24 @@
 
     def start(r):
         for k in range(HALF):
-            for n, source in enumerate(sources):
-
-                @pl.when(origin[k] == n)
+            target = (held.at[r, k], sem_in.at[r, k])
+
+            @pl.when(origin[k] < COLS)
+            def _():
+                pltpu.make_async_copy(first.at[origin[k], row_table[r]], *target).start()
+
+            for n, source in enumerate(second):
+
+                @pl.when(origin[k] == COLS + n)
                 def _():
-                    pltpu.make_async_copy(
-                        source.at[row_table[r]], held.at[r, k], sem_in.at[r, k]
-                    ).start()
+                    pltpu.make_async_copy(source.at[row_table[r]], *target).start()
 
     def leave(r):
         return pltpu.make_async_copy(held.at[r], out.at[r], sem_out.at[r, 0])
 
     def send(r):
         for k in range(HALF):
-            pltpu.make_async_copy(sources[0].at[0], held.at[r, k], sem_in.at[r, k]).wait()
+            pltpu.make_async_copy(first.at[0, 0], held.at[r, k], sem_in.at[r, k]).wait()
         leave(r).start()
 
     each(start)
@@ -177,13 +184,14 @@
     each(lambda r: leave(r).wait())
 
 
-def pack_rows(row_table, row_has, origin, arrays, after):
-    arrays = [x.reshape(GRP, BLOCK, BLOCK) for x in arrays]
+def pack_rows(row_table, row_has, origin, first, second, after):
+    first = first.reshape(COLS, GRP, BLOCK, BLOCK)
+    second = [x.reshape(GRP, BLOCK, BLOCK) for x in second]
     shape = (ROWS, HALF, BLOCK, BLOCK)
     return gather_call(
         pack_rows_kernel,
         [row_table, row_has, origin],
-        arrays,
+        [first] + second,
         [shape],
         [shape],
         (ROWS, HALF),
@@ -269,9 +277,25 @@
     return jnp.where(rows >= lanes, whole, 0.0)
 
 
-def factor_kernel(first, count, last, given, after, *refs):
-    work = refs[-1] if last else refs[0]
-    work[...] = given[...]
+def factor_kernel(first, count, last, *refs):
+    if first == 0:
+        parity, mine, other, _, work = refs
+        rows = LEAD // 2 // ROWS
+
+        def join(r, carry):
+            source = pl.ds(pl.multiple_of(r * rows, rows), rows)
+            low = pl.ds(pl.multiple_of(2 * r * rows, rows), rows)
+            high = pl.ds(pl.multiple_of((2 * r + 1) * rows, rows), rows)
+            even = parity[0] == 0
+            work[low, :] = jnp.where(even, mine[source, :], other[source, :])
+            work[high, :] = jnp.where(even, other[source, :], mine[source, :])
+            return carry
+
+        lax.fori_loop(0, ROWS, join, 0)
+    else:
+        given, _, *refs = refs
+        work = refs[-1] if last else refs[0]
+        work[...] = given[...]
     total = LEAD // BLOCK
 
     def step(k, carry):
@@ -309,7 +333,7 @@
 PARTS = 4
 
 
-def factor_part(part, work, after):
+def factor_part(part, given, after):
     count = LEAD // BLOCK // PARTS
     whole = pl.BlockSpec(memory_space=pltpu.VMEM)
     last = part == PARTS - 1
@@ -317,14 +341,15 @@
     full = jax.ShapeDtypeStruct((LEAD, LEAD), F32)
     return pl.pallas_call(
         functools.partial(factor_kernel, part * count, count, last),
-        in_specs=[whole, pl.BlockSpec(memory_space=pl.ANY)],
+        in_specs=([pl.BlockSpec(memory_space=pltpu.SMEM), whole] if part == 0 else [])
+        + [whole, pl.BlockSpec(memory_space=pl.ANY)],
         out_specs=[whole] * 2 if last else whole,
         out_shape=(half, half) if last else full,
         scratch_shapes=[pltpu.VMEM((LEAD, LEAD), F32)] if last else [],
         compiler_params=params(),
         cost_estimate=cost(25 * 10**9, 8 << 20),
         name="factor_lead",
-    )(work, after)
+    )(*given, after)
 
 
 TILE = 256
@@ -484,11 +509,10 @@
     ahead = slot[:, None, :] * blocks + places < (slot * blocks + places)[:, :, None]
     rank_all = jnp.sum((ahead & (run16[:, None, :] == run16[:, :, None])).astype(jnp.int32), axis=-1)
     rank_codes = jnp.where(own_run16 == col_index, pick(rank_all), -1)
-    incoming = groups * 2 + own_slot
-    origin = own_slot * COLS + (col_index - groups) % COLS
+    origin = jnp.where(own_slot == 0, groups, COLS + (col_index - groups) % COLS)
     pick_cols, _ = lookup(rank_codes, origin, GRP)
     own_codes = jnp.where(own_run16 == col_index, own_map % 16, -1)
-    pick_owner, _ = lookup(own_codes, incoming, 16)
+    pick_owner, _ = lookup(own_codes, groups * 2 + own_slot, 16)
 
     tile_rows = jnp.where(run8 == row_index, child_map % 8, -1)
     row_block, row_has = lookup(tile_rows, jnp.broadcast_to(places, (2, blocks)), 8)
@@ -529,18 +553,14 @@
     pairs = [(number(j % 16, j // 16), number(j // 8, j % 8)) for j in range(128)]
     strip_parent = lax.ppermute(own, axes, [(b, a) for a, b in pairs])
 
-    shifts = (col_index + jnp.arange(COLS, dtype=jnp.int32)) % COLS
-    table = jnp.concatenate([jnp.take(send_cols, shifts * 2), send_cols, send_rows[:1]])
-    *parts, early = pack_first(table, children)
-    shift = lambda parts: [parts[0]] + [
-        lax.ppermute(parts[d], "col", [(c, (c + d) % COLS) for c in range(COLS)])
-        for d in range(1, COLS)
-    ]
-    first = shift(parts)
+    early = pack_early(jnp.concatenate([send_cols, send_rows[:1]]), children)
     early = lax.all_to_all(early, "col", split_axis=0, concat_axis=0, tiled=True)
-    early = pick_early(pick_owner, early, [strip_parent])
+    early = pick_early(pick_owner, early, [])
     early = lax.all_to_all(early, "row", split_axis=0, concat_axis=0, tiled=True)
-    strip = assemble_strip(strip_place, strip_keep, strip_parent, early, first[1:])
+    strip = assemble_strip(strip_place, strip_keep, strip_parent, early, [])
+
+    first = pack_first(send_cols[0::2], children, [])
+    first = lax.all_to_all(first, "col", split_axis=0, concat_axis=0, tiled=True)
 
     half = BLOCK // 2
     piece = total([
@@ -551,28 +571,34 @@
         )
         for part in range(2)
     ])
-    piece = total([piece] + [
-        lax.ppermute(piece, axes, [(number(r, 0), number(r, d)) for r in range(ROWS)])
+    halves = [piece[: half // 2], piece[half // 2 :]]
+    piece = total([jnp.where(col_index == 0, halves[0], 0.0)] + [
+        lax.ppermute(halves[d % 2], axes, [(number(r, 0), number(r, d)) for r in range(ROWS)])
         for d in range(1, COLS)
     ])
     lead = lax.all_gather(piece, "row", axis=0, tiled=True)
+    other = lax.ppermute(lead, "col", [(c, c ^ 1) for c in range(COLS)])
+    parity = (col_index % 2).astype(jnp.int32).reshape(1)
 
     row_piece = lax.ppermute(strip, axes, pairs)
     col_strip = lax.all_gather(strip, "row", axis=0, tiled=True)
     row_strip = lax.all_gather(row_piece, "col", axis=0, tiled=True)
 
     sends = sends.astype(jnp.int32)
-    near_out = pack_rows(send_rows, sends, pick_cols[:HALF], first, [piece, row_piece])
+    near_out = pack_rows(send_rows, sends, pick_cols[:HALF], first, [], [])
     near = lax.all_to_all(near_out, "row", split_axis=0, concat_axis=0, tiled=True)
+    shifts = (col_index + jnp.arange(COLS, dtype=jnp.int32)) % COLS
     parts = pack_second(jnp.take(send_cols, shifts * 2 + 1), children, [near_out])
-    second = shift(parts)
-    work = factor_part(0, lead, near_out)
-    far_out = pack_rows(send_rows, sends, pick_cols[HALF:], first + second, [near, work])
+    second = [parts[0]] + [
+        lax.ppermute(parts[d], "col", [(c, (c + d) % COLS) for c in range(COLS)])
+        for d in range(1, COLS)
+    ]
+    work = factor_part(0, [parity, lead, other], near_out)
+    far_out = pack_rows(send_rows, sends, pick_cols[HALF:], first, second, [near, work])
     far = lax.all_to_all(far_out, "row", split_axis=0, concat_axis=0, tiled=True)
-
-    work = factor_part(1, work, far_out)
-    work = factor_part(2, work, far_out)
-    inv_hi, inv_lo = factor_part(3, work, far_out)
+    work = factor_part(1, [work], far_out)
+    work = factor_part(2, [work], far_out)
+    inv_hi, inv_lo = factor_part(3, [work], far_out)
     flags = jnp.stack([row_index, col_index]).astype(jnp.int32)
     front = update_front(flags, row_strip, col_strip, inv_hi, inv_lo, parent_front)
     return place_children(source, col_rank, keep, front, near, far)

time: 522 us -> 500 us (0.958); the launches traced: 512 us -> 497 us
  starting transfers between devices: 141 us -> 93.6 us
  waiting for transfers between devices: 150 us -> 181 us
    all_to_all x0 -> x1, waiting for transfers between devices: none -> 75 us  [body(): lax.all_to_all(first, 'col', split_axis=0, concat_axis=0, tiled=True)]
    all_gather x1, waiting for transfers between devices: 50.6 us -> 0.01 us  [body(): col_strip = lax.all_gather(strip, 'row', axis=0, tiled=True)]
    ppermute x14 -> x7, starting transfers between devices: 44 us -> 6.94 us  [body(): lax.ppermute(parts[d], 'col', [(c, (c + d) % COLS) for c in range(COLS)])]
    ppermute x14 -> x7, waiting for transfers between devices: 61.3 us -> 24.6 us  [body(): lax.ppermute(parts[d], 'col', [(c, (c + d) % COLS) for c in range(COLS)])]
    all_to_all x1, waiting for transfers between devices: 0.01 us -> 19.8 us  [body(): lax.all_to_all(near_out, 'row', split_axis=0, concat_axis=0, tiled=True)]
    all_to_all x0 -> x1, starting transfers between devices: none -> 17.1 us  [body(): lax.all_to_all(first, 'col', split_axis=0, concat_axis=0, tiled=True)]
    ppermute x7 -> x8, waiting for transfers between devices: 0.91 us -> 14.4 us  [the longest x7 14.4 us: body(): lax.ppermute(halves[d % 2], axes, [(number(r, 0), number(r, d)) for r in...]
    all_to_all x1, starting transfers between devices: 17.4 us -> 6.68 us  [body(): lax.all_to_all(early, 'row', split_axis=0, concat_axis=0, tiled=True)]
  transfers between devices with their start and end apart: 39 -> 34, of which waited for: 7 -> 10; matrix products, arithmetic and copies ran while one was open for 2% -> 3% of each run, Pallas kernels for 33% -> 35%
where the time goes in v3:
time: 500 us; the launch traced here: 497 us
  Pallas kernels  191 us (38%)
  waiting for transfers between devices  181 us (36%)
  starting transfers between devices  93.6 us (19%)
  between operations  13.7 us (3%)
  other arithmetic  9.18 us (2%)
  local copies, waits for them, and re-layouts  8.18 us (2%)
    pallas_call x4, Pallas kernels, factor_part(): pl.pallas_call(functools.partial(factor_kernel, part * count, count, last...  104 us
    all_to_all x1, waiting for transfers between devices, body(): lax.all_to_all(first, 'col', split_axis=0, concat_axis=0, tiled=True)  75 us
    pallas_call x1, Pallas kernels, update_front(): pl.pallas_call(update_kernel, grid_spec=pltpu.PrefetchScalarGridSpec(num_...  40.8 us
    pallas_call x7, Pallas kernels, gather_call(): pl.pallas_call(run, in_specs=[pl.BlockSpec(memory_space=pltpu.SMEM)] * le...  31.7 us
    ppermute x7, waiting for transfers between devices, body(): lax.ppermute(parts[d], 'col', [(c, (c + d) % COLS) for c in range(COLS)])  24.6 us
    ppermute x1, waiting for transfers between devices, body(): strip_parent = lax.ppermute(own, axes, [(b, a) for a, b in pairs])  23.1 us
    all_to_all x1, waiting for transfers between devices, body(): lax.all_to_all(near_out, 'row', split_axis=0, concat_axis=0, tiled=True)  19.8 us
    all_to_all x1, starting transfers between devices, body(): lax.all_to_all(first, 'col', split_axis=0, concat_axis=0, tiled=True)  17.1 us
  transfers between devices with their start and end apart: 34, of which 10 were waited for; matrix products, arithmetic and copies ran while one was open for 3% of the time, Pallas kernels for 35%

profile of v3, /device:TPU:21, one launch (start us, length us, event | category | flops | bytes accessed | tf_op | source)
XLA Modules:
  0.0 497.2 jit_solution(2595268946836762801)
XLA Ops:
  6.5 3.6 cut_strip.1
  10.1 1.4 collective-permute-start
  11.6 0.7 collective-permute-start.1
  13.0 0.7 pad_add_fusion.1.refs_0_
  13.7 3.3 pack_early.1
  17.0 6.7 %all-to-all-start = ((f32[16,128,128]{2,1,0:T(8,128)}), f32[16,128,128]{2,1,0:T(8,128)S(1)}, u32[]{:S(2)}, u32[]{:S(2)}) async-start(f32[16,128,128]{2,1,0:T(8,128)} %pack_early.1), calls=%async_computation | async-start | bytes 2097152 | tf_op jit(solution)/shard_map/all_to_all | solution.py:557
  23.8 0.7 collective-permute-start.2
  24.5 1.5 collective-permute-start.3
  25.9 1.5 collective-permute-start.4
  27.4 1.5 collective-permute-start.5
  28.9 1.5 collective-permute-start.6
  30.3 0.7 select_reduce_fusion.4.refs_0_
  31.2 7.7 %all-to-all-done.refs_1_ = f32[16,128,128]{2,1,0:T(8,128)S(1)} async-done(((f32[16,128,128]{2,1,0:T(8,128)}), f32[16,128,128]{2,1,0:T(8,128)S(1)}, u32[]{:S(2)}, u32[]{:S(2)}) %all-to-all-start) | async-done | bytes 1048608 | tf_op jit(solution)/shard_map/all_to_all | solution.py:557
  38.9 1.0 copy-done
  39.9 3.1 pick_early.1
  43.0 6.7 %all-to-all-start.1 = ((f32[16,128,128]{2,1,0:T(8,128)}), f32[16,128,128]{2,1,0:T(8,128)S(1)}, u32[]{:S(2)}, u32[]{:S(2)}) async-start(f32[16,128,128]{2,1,0:T(8,128)} %pick_early.1), calls=%async_computation.1 | async-start | bytes 2097152 | tf_op jit(solution)/shard_map/all_to_all | solution.py:559
  49.8 2.8 add_add_fusion
  52.6 7.9 %collective-permute-start.7 = (f32[128,1024]{1,0:T(8,128)}, f32[128,1024]{1,0:T(8,128)S(1)}, u32[]{:S(2)}, u32[]{:S(2)}) collective-permute-start(f32[128,1024]{1,0:T(8,128)} %add_add_fusion), channel_id=1, source_target_pairs={{0,0},{1,8},{2,16},{3,24},{4,32},{5,40},{6,48},{7,56},{8,64},{9,72... | collective-permute-start | bytes 1572872 | tf_op jit(solution)/shard_map/ppermute | solution.py:554
  61.4 0.6 select_n.259.place
  62.0 23.1 %collective-permute-done.7.parent = f32[128,1024]{1,0:T(8,128)S(1)} collective-permute-done((f32[128,1024]{1,0:T(8,128)}, f32[128,1024]{1,0:T(8,128)S(1)}, u32[]{:S(2)}, u32[]{:S(2)}) %collective-permute-start.7) | collective-permute-done | bytes 524320 | tf_op jit(solution)/shard_map/ppermute | solution.py:554
  85.1 0.8 copy-done.9
  85.9 1.0 copy-done.1
  86.8 2.3 assemble_strip.1
  89.2 1.1 fusion.31
  90.3 0.7 collective-permute-start.10
  90.9 0.7 collective-permute-start.9
  91.7 1.3 collective-permute-start.11
  93.0 0.7 collective-permute-start.12
  93.7 0.7 collective-permute-start.13
  94.4 0.7 collective-permute-start.14
  95.0 0.7 collective-permute-start.15
  95.7 14.4 %collective-permute-done.11 = f32[32,1024]{1,0:T(8,128)S(1)} collective-permute-done((f32[32,1024]{1,0:T(8,128)S(1)}, f32[32,1024]{1,0:T(8,128)S(1)}, u32[]{:S(2)}, u32[]{:S(2)}) %collective-permute-start.11) | collective-permute-done | bytes 131104 | tf_op jit(solution)/shard_map/ppermute | solution.py:576
  110.1 0.7 collective-permute-start.16
  110.8 0.7 collective-permute-start.17
  111.5 0.7 add_add_fusion.1
  112.3 10.7 %collective-permute-start.8 = (f32[128,1024]{1,0:T(8,128)}, f32[128,1024]{1,0:T(8,128)S(1)}, u32[]{:S(2)}, u32[]{:S(2)}) collective-permute-start(f32[128,1024]{1,0:T(8,128)} %assemble_strip.1), channel_id=1, source_target_pairs={{0,0},{8,1},{16,2},{24,3},{32,4},{40,5},{48,6},{56,7},{64,8},{72,9... | collective-permute-start | bytes 1572872 | tf_op jit(solution)/shard_map/ppermute | solution.py:583
  123.0 15.5 %collective-permute-done.8 = f32[128,1024]{1,0:T(8,128)S(1)} collective-permute-done((f32[128,1024]{1,0:T(8,128)}, f32[128,1024]{1,0:T(8,128)S(1)}, u32[]{:S(2)}, u32[]{:S(2)}) %collective-permute-start.8) | collective-permute-done | bytes 524320 | tf_op jit(solution)/shard_map/ppermute | solution.py:583
  138.5 0.8 copy-done.8
  139.9 5.6 %pack_first.1 = f32[8,1280,128]{2,1,0:T(8,128)} custom-call(s32[8]{0:T(128)} %slice.30.refs_0_, f32[1280,1280]{1,0:T(8,128)} %refs_1_.5), custom_call_target="tpu_custom_call" | custom-call | bytes 10485760 | tf_op jit(solution)/shard_map/pack_first/pallas_call | solution.py:36
  145.4 17.1 %all-to-all-start.2 = ((f32[8,1280,128]{2,1,0:T(8,128)}), f32[8,1280,128]{2,1,0:T(8,128)}, u32[]{:S(2)}, u32[]{:S(2)}) async-start(f32[8,1280,128]{2,1,0:T(8,128)} %pack_first.1), calls=%async_computation.2 | async-start | bytes 10485760 | tf_op jit(solution)/shard_map/all_to_all | solution.py:563
  162.5 0.7 all-gather.6.cloned.1.call-update
  164.6 75.0 %all-to-all-done.2 = f32[8,1280,128]{2,1,0:T(8,128)} async-done(((f32[8,1280,128]{2,1,0:T(8,128)}), f32[8,1280,128]{2,1,0:T(8,128)}, u32[]{:S(2)}, u32[]{:S(2)}) %all-to-all-start.2) | async-done | bytes 5242912 | tf_op jit(solution)/shard_map/all_to_all | solution.py:563
  239.5 5.1 %pack_rows.2.refs_3_.refs_2_ = f32[16,5,128,128]{3,2,1,0:T(8,128)} custom-call(s32[16]{0:T(128)} %copy-done.12, s32[16]{0:T(128)} %convert_element_type.32.refs_1_, s32[5]{0:T(128)} %get-tuple-element.58.refs_2_, f32[8,10,128,128]{3,2,1,0:T(8,128)} %bitcast.9.refs_3_), custom_call_target="tpu_custom_call" | custom-call | bytes 10485760 | tf_op jit(solution)/shard_map/pack_rows/pallas_call | solution.py:36
  244.6 10.5 %all-to-all-start.3 = ((f32[16,5,128,128]{3,2,1,0:T(8,128)}), f32[16,5,128,128]{3,2,1,0:T(8,128)}, u32[]{:S(2)}, u32[]{:S(2)}) async-start(f32[16,5,128,128]{3,2,1,0:T(8,128)} %pack_rows.2.refs_3_.refs_2_), calls=%async_computation.3 | async-start | bytes 10485760 | tf_op jit(solution)/shard_map/all_to_all | solution.py:589
  255.1 1.5 collective-permute-start.18
  256.7 0.6 gather_fusion
  258.7 5.7 %pack_second.1 = (f32[1280,128]{1,0:T(8,128)}, f32[1280,128]{1,0:T(8,128)}, f32[1280,128]{1,0:T(8,128)}, f32[1280,128]{1,0:T(8,128)}, f32[1280,128]{1,0:T(8,128)...) custom-call(s32[8]{0:T(128)} %and_select_fusion.1.refs_0_, f32[1280,1280]{1,0:T(8,128)} %refs_1_.5, ...), custom_call_target="tpu_custom_call" | custom-call | bytes 10485760 | tf_op jit(solution)/shard_map/pack_second/pallas_call | solution.py:36
  265.5 0.6 select_reduce_fusion.rank
  266.1 0.7 fusion.18.source
  266.8 2.3 collective-permute-start.21
  269.1 1.2 collective-permute-start.22
  270.3 8.1 %collective-permute-done.19 = f32[1280,128]{1,0:T(8,128)S(1)} collective-permute-done((f32[1280,128]{1,0:T(8,128)}, f32[1280,128]{1,0:T(8,128)S(1)}, u32[]{:S(2)}, u32[]{:S(2)}) %collective-permute-start.19) | collective-permute-done | bytes 655392 | tf_op jit(solution)/shard_map/ppermute | solution.py:593
  278.4 3.0 collective-permute-start.23
  281.4 14.8 %collective-permute-done.20 = f32[1280,128]{1,0:T(8,128)S(1)} collective-permute-done((f32[1280,128]{1,0:T(8,128)}, f32[1280,128]{1,0:T(8,128)S(1)}, u32[]{:S(2)}, u32[]{:S(2)}) %collective-permute-start.20) | collective-permute-done | bytes 655392 | tf_op jit(solution)/shard_map/ppermute | solution.py:593
  296.2 29.8 %factor_lead.4.refs_13_.refs_0_ = f32[1024,1024]{1,0:T(8,128)} custom-call(s32[1]{0:T(128)} %bitcast.7.refs_0_, f32[512,1024]{1,0:T(8,128)} %all-gather.8.cloned.1.call-done.refs_1_, f32[512,1024]{1,0:T(8,128)} %collective-permute-done.18.refs_2_, f32[16,5,128,128]{3,2,1,0:T(8,128)} %pack_rows.2.refs_3_.refs_2_), custom_call_target="tpu_custom_call" | custom-call | flops 24999999488 | bytes 8388608 | tf_op jit(solution)/shard_map/factor_lead/pallas_call | solution.py:342
  326.0 1.4 collective-permute-done.24
  327.8 19.8 %all-to-all-done.3.refs_12_.refs_0_.refs_2_ = f32[16,5,128,128]{3,2,1,0:T(8,128)} async-done(((f32[16,5,128,128]{3,2,1,0:T(8,128)}), f32[16,5,128,128]{3,2,1,0:T(8,128)}, u32[]{:S(2)}, u32[]{:S(2)}) %all-to-all-start.3) | async-done | bytes 5242912 | tf_op jit(solution)/shard_map/all_to_all | solution.py:589
  347.6 5.4 %pack_rows.3.refs_1_ = f32[16,5,128,128]{3,2,1,0:T(8,128)} custom-call(s32[16]{0:T(128)} %copy-done.12, s32[16]{0:T(128)} %convert_element_type.32.refs_1_, s32[5]{0:T(128)} %get-tuple-element.57.refs_2_, f32[8,10,128,128]{3,2,1,0:T(8,128)} %bitcast.9.refs_3_, f32[10,128,128]{2,1,0:T(8,128)} %bitcast.42, f32[10,128,128]{2,1,0:T(8,128)} %bitcast.43, ...), custom_call_target="tpu_custom_call" | custom-call | bytes 10485760 | tf_op jit(solution)/shard_map/pack_rows/pallas_call | solution.py:36
  353.0 10.1 %all-to-all-start.4 = ((f32[16,5,128,128]{3,2,1,0:T(8,128)}), f32[16,5,128,128]{3,2,1,0:T(8,128)}, u32[]{:S(2)}, u32[]{:S(2)}) async-start(f32[16,5,128,128]{3,2,1,0:T(8,128)} %pack_rows.3.refs_1_), calls=%async_computation.4 | async-start | bytes 10485760 | tf_op jit(solution)/shard_map/all_to_all | solution.py:598
  363.2 26.9 %factor_lead.5.refs_0_ = f32[1024,1024]{1,0:T(8,128)} custom-call(f32[1024,1024]{1,0:T(8,128)} %factor_lead.4.refs_13_.refs_0_, f32[16,5,128,128]{3,2,1,0:T(8,128)} %pack_rows.3.refs_1_), custom_call_target="tpu_custom_call" | custom-call | flops 24999999488 | bytes 8388608 | tf_op jit(solution)/shard_map/factor_lead/pallas_call | solution.py:342
  390.1 24.3 %factor_lead.6.refs_0_ = f32[1024,1024]{1,0:T(8,128)} custom-call(f32[1024,1024]{1,0:T(8,128)} %factor_lead.5.refs_0_, f32[16,5,128,128]{3,2,1,0:T(8,128)} %pack_rows.3.refs_1_), custom_call_target="tpu_custom_call" | custom-call | flops 24999999488 | bytes 8388608 | tf_op jit(solution)/shard_map/factor_lead/pallas_call | solution.py:342
  414.4 22.7 %factor_lead.7 = (bf16[1024,1024]{1,0:T(8,128)(2,1)}, bf16[1024,1024]{1,0:T(8,128)(2,1)}) custom-call(f32[1024,1024]{1,0:T(8,128)} %factor_lead.6.refs_0_, f32[16,5,128,128]{3,2,1,0:T(8,128)} %pack_rows.3.refs_1_), custom_call_target="tpu_custom_call" | custom-call | flops 24999999488 | bytes 8388608 | tf_op jit(solution)/shard_map/factor_lead/pallas_call | solution.py:342
  437.1 40.8 %update_front.1.front = f32[1024,2048]{1,0:T(8,128)} custom-call(s32[2]{0:T(128)} %pad_add_fusion.flags, f32[1024,1024]{1,0:T(8,128)} %all-gather.4.cloned.1.call-done.row_strip, f32[2048,1024]{1,0:T(8,128)} %all-gather.6.cloned.1.call-done.col_strip, bf16[1024,1024]{1,0:T(8,128)(2,1)} %get-tuple-element.39.inv_hi, ...), custom_call_target="tpu_custom_call" | custom-call | flops 40000000000 | bytes 33554432 | tf_op jit(solution)/shard_map/update_front/pallas_call | solution.py:412
  478.0 12.7 %place_children.1 = f32[1024,2048]{1,0:T(8,128)} custom-call(s32[2,8]{1,0:T(2,128)} %fusion.18.source, s32[2,16]{1,0:T(2,128)} %select_reduce_fusion.rank, s32[2,128]{1,0:T(2,128)} %reshape.292.keep, f32[1024,2048]{1,0:T(8,128)} %update_front.1.front, f32[16,5,128,128]{3,2,1,0:T(8,128)} %all-to-all-done.3.refs_12_.refs_0_.refs_2_, ...), custom_call_target="tpu_custom_call", output_to_operand_aliasing={{}: (3, {})} | custom-call | bytes 25165824 | tf_op jit(solution)/shard_map/place_children/pallas_call | solution.py:460
  (91 shorter events, 6.8 us)
Async XLA Ops:
  6.5 5.8 %copy-start.11 = (s32[2,80]{1,0:T(2,128)S(1)}, s32[2,80]{1,0:T(2,128)}, u32[]{:S(2)}) copy-start(s32[2,80]{1,0:T(2,128)} %param.6) | copy-start | bytes 1924
  10.1 20.9 %copy-start.10 = (s32[2,80,80]{2,1,0:T(8,128)S(1)}, s32[2,80,80]{2,1,0:T(8,128)}, u32[]{:S(2)}) copy-start(s32[2,80,80]{2,1,0:T(8,128)} %param.7) | copy-start | bytes 153604
  10.1 17.3 %collective-permute-start = (f32[128,1024]{1,0:T(8,128)}, f32[128,1024]{1,0:T(8,128)S(1)}, u32[]{:S(2)}, u32[]{:S(2)}) collective-permute-start(f32[128,1024]{1,0:T(8,128)} %get-tuple-element.24), channel_id=1, source_target_pairs={{0,1},{8,9},{16,17},{24,25},{32,33},{40,41},{48,49},{56,57},{64,65... | collective-permute-start | bytes 1572872 | tf_op jit(solution)/shard_map/ppermute | solution.py:550
  11.6 17.3 %collective-permute-start.1 = (f32[128,1024]{1,0:T(8,128)}, f32[128,1024]{1,0:T(8,128)S(1)}, u32[]{:S(2)}, u32[]{:S(2)}) collective-permute-start(f32[128,1024]{1,0:T(8,128)} %get-tuple-element.25), channel_id=1, source_target_pairs={{0,2},{8,10},{16,18},{24,26},{32,34},{40,42},{48,50},{56,58},{64,6... | collective-permute-start | bytes 1572872 | tf_op jit(solution)/shard_map/ppermute | solution.py:550
  13.0 30.0 %copy-start.12 = (s32[16]{0:T(128)}, s32[16]{0:T(128)S(1)}, u32[]{:S(2)}) copy-start(s32[16]{0:T(128)S(1)} %get-tuple-element.42.refs_0_) | copy-start | bytes 196
  13.7 36.1 %copy-start.7 = (f32[128,1024]{1,0:T(8,128)S(1)}, f32[128,1024]{1,0:T(8,128)}, u32[]{:S(2)}) copy-start(f32[128,1024]{1,0:T(8,128)} %get-tuple-element.23) | copy-start | bytes 1572868
  17.0 21.9 %all-to-all-start = ((f32[16,128,128]{2,1,0:T(8,128)}), f32[16,128,128]{2,1,0:T(8,128)S(1)}, u32[]{:S(2)}, u32[]{:S(2)}) async-start(f32[16,128,128]{2,1,0:T(8,128)} %pack_early.1), calls=%async_computation | async-start | bytes 2097152 | tf_op jit(solution)/shard_map/all_to_all | solution.py:557
  23.8 26.0 %collective-permute-start.2 = (f32[128,1024]{1,0:T(8,128)}, f32[128,1024]{1,0:T(8,128)S(1)}, u32[]{:S(2)}, u32[]{:S(2)}) collective-permute-start(f32[128,1024]{1,0:T(8,128)} %get-tuple-element.26), channel_id=1, source_target_pairs={{0,3},{8,11},{16,19},{24,27},{32,35},{40,43},{48,51},{56,59},{64,6... | collective-permute-start | bytes 1572872 | tf_op jit(solution)/shard_map/ppermute | solution.py:550
  24.5 25.3 %collective-permute-start.3 = (f32[128,1024]{1,0:T(8,128)}, f32[128,1024]{1,0:T(8,128)}, u32[]{:S(2)}, u32[]{:S(2)}) collective-permute-start(f32[128,1024]{1,0:T(8,128)} %get-tuple-element.27), channel_id=1, source_target_pairs={{0,4},{8,12},{16,20},{24,28},{32,36},{40,44},{48,52},{56,60},{64,6... | collective-permute-start | bytes 1572872 | tf_op jit(solution)/shard_map/ppermute | solution.py:550
  25.9 23.8 %collective-permute-start.4 = (f32[128,1024]{1,0:T(8,128)}, f32[128,1024]{1,0:T(8,128)}, u32[]{:S(2)}, u32[]{:S(2)}) collective-permute-start(f32[128,1024]{1,0:T(8,128)} %get-tuple-element.28), channel_id=1, source_target_pairs={{0,5},{8,13},{16,21},{24,29},{32,37},{40,45},{48,53},{56,61},{64,6... | collective-permute-start | bytes 1572872 | tf_op jit(solution)/shard_map/ppermute | solution.py:550
  27.4 22.4 %collective-permute-start.5 = (f32[128,1024]{1,0:T(8,128)}, f32[128,1024]{1,0:T(8,128)}, u32[]{:S(2)}, u32[]{:S(2)}) collective-permute-start(f32[128,1024]{1,0:T(8,128)} %get-tuple-element.29), channel_id=1, source_target_pairs={{0,6},{8,14},{16,22},{24,30},{32,38},{40,46},{48,54},{56,62},{64,7... | collective-permute-start | bytes 1572872 | tf_op jit(solution)/shard_map/ppermute | solution.py:550
  28.9 20.9 %collective-permute-start.6 = (f32[128,1024]{1,0:T(8,128)}, f32[128,1024]{1,0:T(8,128)}, u32[]{:S(2)}, u32[]{:S(2)}) collective-permute-start(f32[128,1024]{1,0:T(8,128)} %get-tuple-element.30), channel_id=1, source_target_pairs={{0,7},{8,15},{16,23},{24,31},{32,39},{40,47},{48,55},{56,63},{64,7... | collective-permute-start | bytes 1572872 | tf_op jit(solution)/shard_map/ppermute | solution.py:550
  38.9 1.0 copy-start
  43.0 42.1 %all-to-all-start.1 = ((f32[16,128,128]{2,1,0:T(8,128)}), f32[16,128,128]{2,1,0:T(8,128)S(1)}, u32[]{:S(2)}, u32[]{:S(2)}) async-start(f32[16,128,128]{2,1,0:T(8,128)} %pick_early.1), calls=%async_computation.1 | async-start | bytes 2097152 | tf_op jit(solution)/shard_map/all_to_all | solution.py:559
  49.7 205.4 %all-gather.8.cloned.1.call-start = ((), (), s32[]{:S(2)}) async-start(), calls=%async_computation.7 | async-start | bytes 2228224 | tf_op jit(solution)/shard_map/all_gather | solution.py:579
  52.6 32.5 %collective-permute-start.7 = (f32[128,1024]{1,0:T(8,128)}, f32[128,1024]{1,0:T(8,128)S(1)}, u32[]{:S(2)}, u32[]{:S(2)}) collective-permute-start(f32[128,1024]{1,0:T(8,128)} %add_add_fusion), channel_id=1, source_target_pairs={{0,0},{1,8},{2,16},{3,24},{4,32},{5,40},{6,48},{7,56},{8,64},{9,72... | collective-permute-start | bytes 1572872 | tf_op jit(solution)/shard_map/ppermute | solution.py:554
  85.1 0.8 copy-start.9
  85.9 1.0 copy-start.1
  90.3 1.4 collective-permute-start.10
  90.9 0.7 collective-permute-start.9
  91.7 18.4 %collective-permute-start.11 = (f32[32,1024]{1,0:T(8,128)S(1)}, f32[32,1024]{1,0:T(8,128)S(1)}, u32[]{:S(2)}, u32[]{:S(2)}) collective-permute-start(f32[32,1024]{1,0:T(8,128)S(1)} %get-tuple-element.50), channel_id=1, source_target_pairs={{0,1},{8,9},{16,17},{24,25},{32,33},{40,41},{48,49},{56,57},{64,65... | collective-permute-start | bytes 393224 | tf_op jit(solution)/shard_map/ppermute | solution.py:576
  93.0 17.8 %collective-permute-start.12 = (f32[32,1024]{1,0:T(8,128)S(1)}, f32[32,1024]{1,0:T(8,128)S(1)}, u32[]{:S(2)}, u32[]{:S(2)}) collective-permute-start(f32[32,1024]{1,0:T(8,128)S(1)} %get-tuple-element.49), channel_id=1, source_target_pairs={{0,2},{8,10},{16,18},{24,26},{32,34},{40,42},{48,50},{56,58},{64,6... | collective-permute-start | bytes 393224 | tf_op jit(solution)/shard_map/ppermute | solution.py:576
  93.7 17.8 %collective-permute-start.13 = (f32[32,1024]{1,0:T(8,128)S(1)}, f32[32,1024]{1,0:T(8,128)S(1)}, u32[]{:S(2)}, u32[]{:S(2)}) collective-permute-start(f32[32,1024]{1,0:T(8,128)S(1)} %get-tuple-element.50), channel_id=1, source_target_pairs={{0,3},{8,11},{16,19},{24,27},{32,35},{40,43},{48,51},{56,59},{64,6... | collective-permute-start | bytes 393224 | tf_op jit(solution)/shard_map/ppermute | solution.py:576
  94.4 17.1 %collective-permute-start.14 = (f32[32,1024]{1,0:T(8,128)S(1)}, f32[32,1024]{1,0:T(8,128)S(1)}, u32[]{:S(2)}, u32[]{:S(2)}) collective-permute-start(f32[32,1024]{1,0:T(8,128)S(1)} %get-tuple-element.49), channel_id=1, source_target_pairs={{0,4},{8,12},{16,20},{24,28},{32,36},{40,44},{48,52},{56,60},{64,6... | collective-permute-start | bytes 393224 | tf_op jit(solution)/shard_map/ppermute | solution.py:576
  95.0 16.4 %collective-permute-start.15 = (f32[32,1024]{1,0:T(8,128)S(1)}, f32[32,1024]{1,0:T(8,128)S(1)}, u32[]{:S(2)}, u32[]{:S(2)}) collective-permute-start(f32[32,1024]{1,0:T(8,128)S(1)} %get-tuple-element.50), channel_id=1, source_target_pairs={{0,5},{8,13},{16,21},{24,29},{32,37},{40,45},{48,53},{56,61},{64,6... | collective-permute-start | bytes 393224 | tf_op jit(solution)/shard_map/ppermute | solution.py:576
  110.1 1.4 collective-permute-start.16
  110.8 0.7 collective-permute-start.17
  112.2 324.9 %all-gather.4.cloned.1.call-start = ((), (), s32[]{:S(2)}) async-start(), calls=%async_computation.5 | async-start | bytes 4718592 | tf_op jit(solution)/shard_map/all_gather | solution.py:585
  112.3 26.2 %collective-permute-start.8 = (f32[128,1024]{1,0:T(8,128)}, f32[128,1024]{1,0:T(8,128)S(1)}, u32[]{:S(2)}, u32[]{:S(2)}) collective-permute-start(f32[128,1024]{1,0:T(8,128)} %assemble_strip.1), channel_id=1, source_target_pairs={{0,0},{8,1},{16,2},{24,3},{32,4},{40,5},{48,6},{56,7},{64,8},{72,9... | collective-permute-start | bytes 1572872 | tf_op jit(solution)/shard_map/ppermute | solution.py:583
  138.5 0.8 copy-start.8
  145.4 94.1 %all-to-all-start.2 = ((f32[8,1280,128]{2,1,0:T(8,128)}), f32[8,1280,128]{2,1,0:T(8,128)}, u32[]{:S(2)}, u32[]{:S(2)}) async-start(f32[8,1280,128]{2,1,0:T(8,128)} %pack_first.1), calls=%async_computation.2 | async-start | bytes 10485760 | tf_op jit(solution)/shard_map/all_to_all | solution.py:563
  162.5 274.6 %all-gather.6.cloned.1.call-start = ((), (), s32[]{:S(2)}) async-start(), calls=%async_computation.6 | async-start | bytes 8912896 | tf_op jit(solution)/shard_map/all_gather | solution.py:584
  244.6 103.0 %all-to-all-start.3 = ((f32[16,5,128,128]{3,2,1,0:T(8,128)}), f32[16,5,128,128]{3,2,1,0:T(8,128)}, u32[]{:S(2)}, u32[]{:S(2)}) async-start(f32[16,5,128,128]{3,2,1,0:T(8,128)} %pack_rows.2.refs_3_.refs_2_), calls=%async_computation.3 | async-start | bytes 10485760 | tf_op jit(solution)/shard_map/all_to_all | solution.py:589
  255.1 41.0 %collective-permute-start.18 = (f32[512,1024]{1,0:T(8,128)}, f32[512,1024]{1,0:T(8,128)}, u32[]{:S(2)}, u32[]{:S(2)}) collective-permute-start(f32[512,1024]{1,0:T(8,128)} %all-gather.8.cloned.1.call-done.refs_1_), channel_id=1, source_target_pairs={{0,1},{1,0},{2,3},{3,2},{4,5},{5,4},{6,7},{7,6},{8,9},{9,8},{10,11... | collective-permute-start | bytes 6291464 | tf_op jit(solution)/shard_map/ppermute | solution.py:580
  264.4 14.0 %collective-permute-start.19 = (f32[1280,128]{1,0:T(8,128)}, f32[1280,128]{1,0:T(8,128)S(1)}, u32[]{:S(2)}, u32[]{:S(2)}) collective-permute-start(f32[1280,128]{1,0:T(8,128)} %get-tuple-element.32), channel_id=1, source_target_pairs={{0,1},{1,2},{2,3},{3,4},{4,5},{5,6},{6,7},{7,0},{8,9},{9,10},{10,1... | collective-permute-start | bytes 1966088 | tf_op jit(solution)/shard_map/ppermute | solution.py:593
  264.6 31.6 %collective-permute-start.20 = (f32[1280,128]{1,0:T(8,128)}, f32[1280,128]{1,0:T(8,128)S(1)}, u32[]{:S(2)}, u32[]{:S(2)}) collective-permute-start(f32[1280,128]{1,0:T(8,128)} %get-tuple-element.33), channel_id=1, source_target_pairs={{0,2},{1,3},{2,4},{3,5},{4,6},{5,7},{6,0},{7,1},{8,10},{9,11},{10,... | collective-permute-start | bytes 1966088 | tf_op jit(solution)/shard_map/ppermute | solution.py:593
  266.8 59.2 %collective-permute-start.21 = (f32[1280,128]{1,0:T(8,128)}, f32[1280,128]{1,0:T(8,128)S(1)}, u32[]{:S(2)}, u32[]{:S(2)}) collective-permute-start(f32[1280,128]{1,0:T(8,128)} %get-tuple-element.34), channel_id=1, source_target_pairs={{0,3},{1,4},{2,5},{3,6},{4,7},{5,0},{6,1},{7,2},{8,11},{9,12},{10,... | collective-permute-start | bytes 1966088 | tf_op jit(solution)/shard_map/ppermute | solution.py:593
  269.1 56.8 %collective-permute-start.22 = (f32[1280,128]{1,0:T(8,128)}, f32[1280,128]{1,0:T(8,128)S(1)}, u32[]{:S(2)}, u32[]{:S(2)}) collective-permute-start(f32[1280,128]{1,0:T(8,128)} %get-tuple-element.35), channel_id=1, source_target_pairs={{0,4},{1,5},{2,6},{3,7},{4,0},{5,1},{6,2},{7,3},{8,12},{9,13},{10,... | collective-permute-start | bytes 1966088 | tf_op jit(solution)/shard_map/ppermute | solution.py:593
  278.4 47.5 %copy-start.2 = (f32[1280,128]{1,0:T(8,128)}, f32[1280,128]{1,0:T(8,128)S(1)}, u32[]{:S(2)}) copy-start(f32[1280,128]{1,0:T(8,128)S(1)} %collective-permute-done.19) | copy-start | bytes 1966084
  278.4 47.6 %collective-permute-start.23 = (f32[1280,128]{1,0:T(8,128)}, f32[1280,128]{1,0:T(8,128)S(1)}, u32[]{:S(2)}, u32[]{:S(2)}) collective-permute-start(f32[1280,128]{1,0:T(8,128)} %get-tuple-element.36), channel_id=1, source_target_pairs={{0,5},{1,6},{2,7},{3,0},{4,1},{5,2},{6,3},{7,4},{8,13},{9,14},{10,... | collective-permute-start | bytes 1966088 | tf_op jit(solution)/shard_map/ppermute | solution.py:593
  296.1 29.8 %copy-start.3 = (f32[1280,128]{1,0:T(8,128)}, f32[1280,128]{1,0:T(8,128)S(1)}, u32[]{:S(2)}) copy-start(f32[1280,128]{1,0:T(8,128)S(1)} %collective-permute-done.20) | copy-start | bytes 1966084
  296.1 31.3 %collective-permute-start.24 = (f32[1280,128]{1,0:T(8,128)}, f32[1280,128]{1,0:T(8,128)}, u32[]{:S(2)}, u32[]{:S(2)}) collective-permute-start(f32[1280,128]{1,0:T(8,128)} %get-tuple-element.37), channel_id=1, source_target_pairs={{0,6},{1,7},{2,0},{3,1},{4,2},{5,3},{6,4},{7,5},{8,14},{9,15},{10,... | collective-permute-start | bytes 1966088 | tf_op jit(solution)/shard_map/ppermute | solution.py:593
  296.1 31.7 %collective-permute-start.25 = (f32[1280,128]{1,0:T(8,128)}, f32[1280,128]{1,0:T(8,128)}, u32[]{:S(2)}, u32[]{:S(2)}) collective-permute-start(f32[1280,128]{1,0:T(8,128)} %get-tuple-element.38), channel_id=1, source_target_pairs={{0,7},{1,0},{2,1},{3,2},{4,3},{5,4},{6,5},{7,6},{8,15},{9,8},{10,9... | collective-permute-start | bytes 1966088 | tf_op jit(solution)/shard_map/ppermute | solution.py:593
  325.9 21.6 %copy-start.4 = (f32[1280,128]{1,0:T(8,128)}, f32[1280,128]{1,0:T(8,128)S(1)}, u32[]{:S(2)}) copy-start(f32[1280,128]{1,0:T(8,128)S(1)} %collective-permute-done.21) | copy-start | bytes 1966084
  326.0 21.6 %copy-start.5 = (f32[1280,128]{1,0:T(8,128)}, f32[1280,128]{1,0:T(8,128)S(1)}, u32[]{:S(2)}) copy-start(f32[1280,128]{1,0:T(8,128)S(1)} %collective-permute-done.22) | copy-start | bytes 1966084
  326.0 21.6 %copy-start.6 = (f32[1280,128]{1,0:T(8,128)}, f32[1280,128]{1,0:T(8,128)S(1)}, u32[]{:S(2)}) copy-start(f32[1280,128]{1,0:T(8,128)S(1)} %collective-permute-done.23) | copy-start | bytes 1966084
  353.0 124.9 %all-to-all-start.4 = ((f32[16,5,128,128]{3,2,1,0:T(8,128)}), f32[16,5,128,128]{3,2,1,0:T(8,128)}, u32[]{:S(2)}, u32[]{:S(2)}) async-start(f32[16,5,128,128]{3,2,1,0:T(8,128)} %pack_rows.3.refs_1_), calls=%async_computation.4 | async-start | bytes 10485760 | tf_op jit(solution)/shard_map/all_to_all | solution.py:598
Sparse Core Ops, SparseCore 0:
  112.4 68.4 all-gather.7
  182.6 51.4 all-gather.3
  236.2 173.2 all-gather.5

commit v4 on v3

--- a/solution.py
+++ b/solution.py
@@ -223,6 +223,23 @@
         cost_estimate=cost(0, 2 << 20),
         name="assemble_strip",
     )(place, keep, parent, blocks, *after)
+
+
+def hand_on_kernel(given, *refs):
+    refs[-1][...] = given[...]
+
+
+def hand_on(given, after):
+    vmem = pl.BlockSpec(memory_space=pltpu.VMEM)
+    return pl.pallas_call(
+        hand_on_kernel,
+        in_specs=[vmem] + [pl.BlockSpec(memory_space=pl.ANY)] * len(after),
+        out_specs=vmem,
+        out_shape=jax.ShapeDtypeStruct(given.shape, F32),
+        compiler_params=params(),
+        cost_estimate=cost(0, 1 << 20),
+        name="hand_on",
+    )(given, *after)
 
 
 def split(x):
@@ -580,11 +597,10 @@
     other = lax.ppermute(lead, "col", [(c, c ^ 1) for c in range(COLS)])
     parity = (col_index % 2).astype(jnp.int32).reshape(1)
 
-    row_piece = lax.ppermute(strip, axes, pairs)
     col_strip = lax.all_gather(strip, "row", axis=0, tiled=True)
-    row_strip = lax.all_gather(row_piece, "col", axis=0, tiled=True)
 
     sends = sends.astype(jnp.int32)
+    work = factor_part(0, [parity, lead, other], strip)
     near_out = pack_rows(send_rows, sends, pick_cols[:HALF], first, [], [])
     near = lax.all_to_all(near_out, "row", split_axis=0, concat_axis=0, tiled=True)
     shifts = (col_index + jnp.arange(COLS, dtype=jnp.int32)) % COLS
@@ -593,12 +609,13 @@
         lax.ppermute(parts[d], "col", [(c, (c + d) % COLS) for c in range(COLS)])
         for d in range(1, COLS)
     ]
-    work = factor_part(0, [parity, lead, other], near_out)
+    work = factor_part(1, [work], near_out)
     far_out = pack_rows(send_rows, sends, pick_cols[HALF:], first, second, [near, work])
     far = lax.all_to_all(far_out, "row", split_axis=0, concat_axis=0, tiled=True)
-    work = factor_part(1, [work], far_out)
     work = factor_part(2, [work], far_out)
     inv_hi, inv_lo = factor_part(3, [work], far_out)
+    row_piece = hand_on(lax.ppermute(strip, axes, pairs), [near_out])
+    row_strip = lax.all_gather(row_piece, "col", axis=0, tiled=True)
     flags = jnp.stack([row_index, col_index]).astype(jnp.int32)
     front = update_front(flags, row_strip, col_strip, inv_hi, inv_lo, parent_front)
     return place_children(source, col_rank, keep, front, near, far)

time: 500 us -> 503 us (level)
  the two profiles are of different devices: /device:TPU:21 before, /device:TPU:51 now
where the time goes in v4:
time: 503 us; the launch traced here: 502 us
  Pallas kernels  194 us (39%)
  waiting for transfers between devices  187 us (37%)
  starting transfers between devices  88.7 us (18%)
  between operations  13.7 us (3%)
  other arithmetic  8.98 us (2%)
  local copies, waits for them, and re-layouts  8.46 us (2%)
    pallas_call x4, Pallas kernels, factor_part(): pl.pallas_call(functools.partial(factor_kernel, part * count, count, last...  104 us
    ppermute x7, waiting for transfers between devices, body(): lax.ppermute(halves[d % 2], axes, [(number(r, 0), number(r, d)) for r in...  54.8 us
    all_gather x1, waiting for transfers between devices, body(): col_strip = lax.all_gather(strip, 'row', axis=0, tiled=True)  52.6 us
    pallas_call x1, Pallas kernels, update_front(): pl.pallas_call(update_kernel, grid_spec=pltpu.PrefetchScalarGridSpec(num_...  40.4 us
    all_gather x1, waiting for transfers between devices, body(): lead = lax.all_gather(piece, 'row', axis=0, tiled=True)  36.9 us
    pallas_call x7, Pallas kernels, gather_call(): pl.pallas_call(run, in_specs=[pl.BlockSpec(memory_space=pltpu.SMEM)] * le...  31.8 us
    all_to_all x1, starting transfers between devices, body(): lax.all_to_all(first, 'col', split_axis=0, concat_axis=0, tiled=True)  24.2 us
    ppermute x1, waiting for transfers between devices, body(): strip_parent = lax.ppermute(own, axes, [(b, a) for a, b in pairs])  16.5 us
  transfers between devices with their start and end apart: 34, of which 8 were waited for; matrix products, arithmetic and copies ran while one was open for 3% of the time, Pallas kernels for 35%

profile of v4, /device:TPU:51, one launch (start us, length us, event | category | flops | bytes accessed | tf_op | source)
XLA Modules:
  0.0 501.5 jit_solution(15368169233147511123)
XLA Ops:
  6.5 3.6 cut_strip.1
  10.2 0.8 collective-permute-start
  11.0 0.7 collective-permute-start.1
  13.1 3.2 pack_early.1
  16.3 7.1 %all-to-all-start = ((f32[16,128,128]{2,1,0:T(8,128)}), f32[16,128,128]{2,1,0:T(8,128)S(1)}, u32[]{:S(2)}, u32[]{:S(2)}) async-start(f32[16,128,128]{2,1,0:T(8,128)} %pack_early.1), calls=%async_computation | async-start | bytes 2097152 | tf_op jit(solution)/shard_map/all_to_all | solution.py:574
  23.4 1.3 collective-permute-start.2
  24.7 1.5 collective-permute-start.3
  26.2 1.5 collective-permute-start.4
  27.7 1.5 collective-permute-start.5
  29.2 1.5 collective-permute-start.6
  31.5 6.0 %all-to-all-done.refs_1_ = f32[16,128,128]{2,1,0:T(8,128)S(1)} async-done(((f32[16,128,128]{2,1,0:T(8,128)}), f32[16,128,128]{2,1,0:T(8,128)S(1)}, u32[]{:S(2)}, u32[]{:S(2)}) %all-to-all-start) | async-done | bytes 1048608 | tf_op jit(solution)/shard_map/all_to_all | solution.py:574
  37.5 1.0 copy-done.1
  38.4 3.2 pick_early.1
  41.6 6.6 %all-to-all-start.1 = ((f32[16,128,128]{2,1,0:T(8,128)}), f32[16,128,128]{2,1,0:T(8,128)S(1)}, u32[]{:S(2)}, u32[]{:S(2)}) async-start(f32[16,128,128]{2,1,0:T(8,128)} %pick_early.1), calls=%async_computation.1 | async-start | bytes 2097152 | tf_op jit(solution)/shard_map/all_to_all | solution.py:576
  48.3 2.7 add_add_fusion
  51.1 2.8 collective-permute-start.7
  53.9 0.6 reshape.293.keep
  54.8 0.7 select_n.259.place
  55.5 16.5 %collective-permute-done.7.parent = f32[128,1024]{1,0:T(8,128)S(1)} collective-permute-done((f32[128,1024]{1,0:T(8,128)}, f32[128,1024]{1,0:T(8,128)S(1)}, u32[]{:S(2)}, u32[]{:S(2)}) %collective-permute-start.7) | collective-permute-done | bytes 524320 | tf_op jit(solution)/shard_map/ppermute | solution.py:571
  72.0 0.8 copy-done.10
  72.8 1.0 copy-done.2
  73.8 3.8 assemble_strip.1.refs_3_
  77.5 1.1 fusion.31
  78.6 0.7 collective-permute-start.10
  79.3 0.7 collective-permute-start.9
  80.0 0.7 slice.26.refs_0_
  80.7 5.6 %pack_first.1 = f32[8,1280,128]{2,1,0:T(8,128)} custom-call(s32[8]{0:T(128)} %slice.26.refs_0_, f32[1280,1280]{1,0:T(8,128)} %refs_1_.5), custom_call_target="tpu_custom_call" | custom-call | bytes 10485760 | tf_op jit(solution)/shard_map/pack_first/pallas_call | solution.py:36
  86.2 24.2 %all-to-all-start.2 = ((f32[8,1280,128]{2,1,0:T(8,128)}), f32[8,1280,128]{2,1,0:T(8,128)}, u32[]{:S(2)}, u32[]{:S(2)}) async-start(f32[8,1280,128]{2,1,0:T(8,128)} %pack_first.1), calls=%async_computation.2 | async-start | bytes 10485760 | tf_op jit(solution)/shard_map/all_to_all | solution.py:580
  110.5 0.7 collective-permute-start.11
  111.2 0.7 collective-permute-start.12
  111.9 1.3 collective-permute-start.13
  113.2 0.7 collective-permute-start.14
  113.9 0.7 collective-permute-start.15
  114.5 0.7 collective-permute-start.16
  115.2 0.7 collective-permute-start.17
  115.9 54.8 %collective-permute-done.13 = f32[32,1024]{1,0:T(8,128)S(1)} collective-permute-done((f32[32,1024]{1,0:T(8,128)S(1)}, f32[32,1024]{1,0:T(8,128)S(1)}, u32[]{:S(2)}, u32[]{:S(2)}) %collective-permute-start.13) | collective-permute-done | bytes 131104 | tf_op jit(solution)/shard_map/ppermute | solution.py:593
  170.7 0.7 add_add_fusion.1
  171.5 2.8 collective-permute-start.8
  175.7 5.1 %pack_rows.2.refs_0_.refs_1_.refs_2_ = f32[16,5,128,128]{3,2,1,0:T(8,128)} custom-call(s32[16]{0:T(128)} %copy-done.13, s32[16]{0:T(128)} %convert_element_type.32.refs_1_, s32[5]{0:T(128)} %get-tuple-element.58.refs_2_, f32[8,10,128,128]{3,2,1,0:T(8,128)} %bitcast.8.refs_3_), custom_call_target="tpu_custom_call" | custom-call | bytes 10485760 | tf_op jit(solution)/shard_map/pack_rows/pallas_call | solution.py:36
  180.7 11.5 %collective-permute-done.8.given = f32[128,1024]{1,0:T(8,128)S(1)} collective-permute-done((f32[128,1024]{1,0:T(8,128)S(1)}, f32[128,1024]{1,0:T(8,128)S(1)}, u32[]{:S(2)}, u32[]{:S(2)}) %collective-permute-start.8) | collective-permute-done | bytes 524320 | tf_op jit(solution)/shard_map/ppermute | solution.py:617
  192.3 0.8 copy-done.9
  193.0 1.9 hand_on.1
  195.0 0.7 all-gather.6.cloned.1.call-update
  195.7 36.9 %all-gather.8.cloned.1.call-done.refs_1_ = f32[512,1024]{1,0:T(8,128)} async-done(((f32[32,1024]{1,0:T(8,128)}), f32[512,1024]{1,0:T(8,128)}) %all-gather.8.cloned.1.call-update) | async-done | bytes 2097168 | tf_op jit(solution)/shard_map/all_gather | solution.py:596
  232.5 1.5 collective-permute-start.18
  234.9 0.7 select_reduce_fusion.rank
  236.3 6.7 %all-to-all-start.3 = ((f32[16,5,128,128]{3,2,1,0:T(8,128)}), f32[16,5,128,128]{3,2,1,0:T(8,128)}, u32[]{:S(2)}, u32[]{:S(2)}) async-start(f32[16,5,128,128]{3,2,1,0:T(8,128)} %pack_rows.2.refs_0_.refs_1_.refs_2_), calls=%async_computation.3 | async-start | bytes 10485760 | tf_op jit(solution)/shard_map/all_to_all | solution.py:605
  244.7 5.7 %pack_second.1 = (f32[1280,128]{1,0:T(8,128)}, f32[1280,128]{1,0:T(8,128)}, f32[1280,128]{1,0:T(8,128)}, f32[1280,128]{1,0:T(8,128)}, f32[1280,128]{1,0:T(8,128)...) custom-call(s32[8]{0:T(128)} %and_select_fusion.1.refs_0_, f32[1280,1280]{1,0:T(8,128)} %refs_1_.5, ...), custom_call_target="tpu_custom_call" | custom-call | bytes 10485760 | tf_op jit(solution)/shard_map/pack_second/pallas_call | solution.py:36
  250.4 1.7 collective-permute-start.19
  252.1 1.0 collective-permute-start.20
  253.2 2.3 collective-permute-start.22
  255.5 1.3 collective-permute-start.23
  256.8 29.6 %factor_lead.4.refs_0_ = f32[1024,1024]{1,0:T(8,128)} custom-call(s32[1]{0:T(128)} %bitcast.9.refs_0_, f32[512,1024]{1,0:T(8,128)} %all-gather.8.cloned.1.call-done.refs_1_, f32[512,1024]{1,0:T(8,128)} %collective-permute-done.18.refs_2_, f32[128,1024]{1,0:T(8,128)} %assemble_strip.1.refs_3_), custom_call_target="tpu_custom_call" | custom-call | flops 24999999488 | bytes 8388608 | tf_op jit(solution)/shard_map/factor_lead/pallas_call | solution.py:359
  286.4 1.1 collective-permute-start.24
  287.5 5.3 %collective-permute-done.20 = f32[1280,128]{1,0:T(8,128)S(1)} collective-permute-done((f32[1280,128]{1,0:T(8,128)}, f32[1280,128]{1,0:T(8,128)S(1)}, u32[]{:S(2)}, u32[]{:S(2)}) %collective-permute-start.20) | collective-permute-done | bytes 655392 | tf_op jit(solution)/shard_map/ppermute | solution.py:609
  292.8 27.0 %factor_lead.5.refs_13_.refs_0_ = f32[1024,1024]{1,0:T(8,128)} custom-call(f32[1024,1024]{1,0:T(8,128)} %factor_lead.4.refs_0_, f32[16,5,128,128]{3,2,1,0:T(8,128)} %pack_rows.2.refs_0_.refs_1_.refs_2_), custom_call_target="tpu_custom_call" | custom-call | flops 24999999488 | bytes 8388608 | tf_op jit(solution)/shard_map/factor_lead/pallas_call | solution.py:359
  319.9 2.6 collective-permute-done.25
  322.5 5.4 %pack_rows.3.refs_1_ = f32[16,5,128,128]{3,2,1,0:T(8,128)} custom-call(s32[16]{0:T(128)} %copy-done.13, s32[16]{0:T(128)} %convert_element_type.32.refs_1_, s32[5]{0:T(128)} %get-tuple-element.57.refs_2_, f32[8,10,128,128]{3,2,1,0:T(8,128)} %bitcast.8.refs_3_, f32[10,128,128]{2,1,0:T(8,128)} %bitcast.42, f32[10,128,128]{2,1,0:T(8,128)} %bitcast.43, ...), custom_call_target="tpu_custom_call" | custom-call | bytes 10485760 | tf_op jit(solution)/shard_map/pack_rows/pallas_call | solution.py:36
  328.0 14.1 %all-to-all-start.4 = ((f32[16,5,128,128]{3,2,1,0:T(8,128)}), f32[16,5,128,128]{3,2,1,0:T(8,128)}, u32[]{:S(2)}, u32[]{:S(2)}) async-start(f32[16,5,128,128]{3,2,1,0:T(8,128)} %pack_rows.3.refs_1_), calls=%async_computation.4 | async-start | bytes 10485760 | tf_op jit(solution)/shard_map/all_to_all | solution.py:614
  342.1 24.7 %factor_lead.6.refs_0_ = f32[1024,1024]{1,0:T(8,128)} custom-call(f32[1024,1024]{1,0:T(8,128)} %factor_lead.5.refs_13_.refs_0_, f32[16,5,128,128]{3,2,1,0:T(8,128)} %pack_rows.3.refs_1_), custom_call_target="tpu_custom_call" | custom-call | flops 24999999488 | bytes 8388608 | tf_op jit(solution)/shard_map/factor_lead/pallas_call | solution.py:359
  366.8 22.7 %factor_lead.7 = (bf16[1024,1024]{1,0:T(8,128)(2,1)}, bf16[1024,1024]{1,0:T(8,128)(2,1)}) custom-call(f32[1024,1024]{1,0:T(8,128)} %factor_lead.6.refs_0_, f32[16,5,128,128]{3,2,1,0:T(8,128)} %pack_rows.3.refs_1_), custom_call_target="tpu_custom_call" | custom-call | flops 24999999488 | bytes 8388608 | tf_op jit(solution)/shard_map/factor_lead/pallas_call | solution.py:359
  389.5 52.6 %all-gather.6.cloned.1.call-done.col_strip = f32[2048,1024]{1,0:T(8,128)} async-done(((f32[128,1024]{1,0:T(8,128)}), f32[2048,1024]{1,0:T(8,128)}) %all-gather.6.cloned.1.call-update) | async-done | bytes 8388624 | tf_op jit(solution)/shard_map/all_gather | solution.py:600
  442.1 40.4 %update_front.1.front = f32[1024,2048]{1,0:T(8,128)} custom-call(s32[2]{0:T(128)} %pad_add_fusion.flags, f32[1024,1024]{1,0:T(8,128)} %all-gather.4.cloned.1.call-done.row_strip, f32[2048,1024]{1,0:T(8,128)} %all-gather.6.cloned.1.call-done.col_strip, bf16[1024,1024]{1,0:T(8,128)(2,1)} %get-tuple-element.39.inv_hi, ...), custom_call_target="tpu_custom_call" | custom-call | flops 40000000000 | bytes 33554432 | tf_op jit(solution)/shard_map/update_front/pallas_call | solution.py:429
  482.6 12.4 %place_children.1 = f32[1024,2048]{1,0:T(8,128)} custom-call(s32[2,8]{1,0:T(2,128)} %fusion.18.source, s32[2,16]{1,0:T(2,128)} %select_reduce_fusion.rank, s32[2,128]{1,0:T(2,128)} %reshape.292.keep, f32[1024,2048]{1,0:T(8,128)} %update_front.1.front, f32[16,5,128,128]{3,2,1,0:T(8,128)} %all-to-all-done.3.refs_12_.refs_0_.refs_2_, ...), custom_call_target="tpu_custom_call", output_to_operand_aliasing={{}: (3, {})} | custom-call | bytes 25165824 | tf_op jit(solution)/shard_map/place_children/pallas_call | solution.py:477
  (98 shorter events, 7.4 us)
Async XLA Ops:
  6.5 5.3 %copy-start.12 = (s32[2,80]{1,0:T(2,128)S(1)}, s32[2,80]{1,0:T(2,128)}, u32[]{:S(2)}) copy-start(s32[2,80]{1,0:T(2,128)} %param.6) | copy-start | bytes 1924
  10.2 21.1 %copy-start.11 = (s32[2,80,80]{2,1,0:T(8,128)S(1)}, s32[2,80,80]{2,1,0:T(8,128)}, u32[]{:S(2)}) copy-start(s32[2,80,80]{2,1,0:T(8,128)} %param.7) | copy-start | bytes 153604
  10.2 17.5 %collective-permute-start = (f32[128,1024]{1,0:T(8,128)}, f32[128,1024]{1,0:T(8,128)S(1)}, u32[]{:S(2)}, u32[]{:S(2)}) collective-permute-start(f32[128,1024]{1,0:T(8,128)} %get-tuple-element.24), channel_id=1, source_target_pairs={{0,1},{8,9},{16,17},{24,25},{32,33},{40,41},{48,49},{56,57},{64,65... | collective-permute-start | bytes 1572872 | tf_op jit(solution)/shard_map/ppermute | solution.py:567
  11.0 18.2 %collective-permute-start.1 = (f32[128,1024]{1,0:T(8,128)}, f32[128,1024]{1,0:T(8,128)S(1)}, u32[]{:S(2)}, u32[]{:S(2)}) collective-permute-start(f32[128,1024]{1,0:T(8,128)} %get-tuple-element.25), channel_id=1, source_target_pairs={{0,2},{8,10},{16,18},{24,26},{32,34},{40,42},{48,50},{56,58},{64,6... | collective-permute-start | bytes 1572872 | tf_op jit(solution)/shard_map/ppermute | solution.py:567
  12.4 29.2 %copy-start.13 = (s32[16]{0:T(128)}, s32[16]{0:T(128)S(1)}, u32[]{:S(2)}) copy-start(s32[16]{0:T(128)S(1)} %get-tuple-element.42.refs_0_) | copy-start | bytes 196
  13.1 35.2 %copy-start.8 = (f32[128,1024]{1,0:T(8,128)S(1)}, f32[128,1024]{1,0:T(8,128)}, u32[]{:S(2)}) copy-start(f32[128,1024]{1,0:T(8,128)} %get-tuple-element.23) | copy-start | bytes 1572868
  16.3 21.1 %all-to-all-start = ((f32[16,128,128]{2,1,0:T(8,128)}), f32[16,128,128]{2,1,0:T(8,128)S(1)}, u32[]{:S(2)}, u32[]{:S(2)}) async-start(f32[16,128,128]{2,1,0:T(8,128)} %pack_early.1), calls=%async_computation | async-start | bytes 2097152 | tf_op jit(solution)/shard_map/all_to_all | solution.py:574
  23.4 24.8 %collective-permute-start.2 = (f32[128,1024]{1,0:T(8,128)}, f32[128,1024]{1,0:T(8,128)S(1)}, u32[]{:S(2)}, u32[]{:S(2)}) collective-permute-start(f32[128,1024]{1,0:T(8,128)} %get-tuple-element.26), channel_id=1, source_target_pairs={{0,3},{8,11},{16,19},{24,27},{32,35},{40,43},{48,51},{56,59},{64,6... | collective-permute-start | bytes 1572872 | tf_op jit(solution)/shard_map/ppermute | solution.py:567
  24.7 23.5 %collective-permute-start.3 = (f32[128,1024]{1,0:T(8,128)}, f32[128,1024]{1,0:T(8,128)}, u32[]{:S(2)}, u32[]{:S(2)}) collective-permute-start(f32[128,1024]{1,0:T(8,128)} %get-tuple-element.27), channel_id=1, source_target_pairs={{0,4},{8,12},{16,20},{24,28},{32,36},{40,44},{48,52},{56,60},{64,6... | collective-permute-start | bytes 1572872 | tf_op jit(solution)/shard_map/ppermute | solution.py:567
  26.2 22.1 %collective-permute-start.4 = (f32[128,1024]{1,0:T(8,128)}, f32[128,1024]{1,0:T(8,128)}, u32[]{:S(2)}, u32[]{:S(2)}) collective-permute-start(f32[128,1024]{1,0:T(8,128)} %get-tuple-element.28), channel_id=1, source_target_pairs={{0,5},{8,13},{16,21},{24,29},{32,37},{40,45},{48,53},{56,61},{64,6... | collective-permute-start | bytes 1572872 | tf_op jit(solution)/shard_map/ppermute | solution.py:567
  27.7 20.6 %collective-permute-start.5 = (f32[128,1024]{1,0:T(8,128)}, f32[128,1024]{1,0:T(8,128)}, u32[]{:S(2)}, u32[]{:S(2)}) collective-permute-start(f32[128,1024]{1,0:T(8,128)} %get-tuple-element.29), channel_id=1, source_target_pairs={{0,6},{8,14},{16,22},{24,30},{32,38},{40,46},{48,54},{56,62},{64,7... | collective-permute-start | bytes 1572872 | tf_op jit(solution)/shard_map/ppermute | solution.py:567
  29.2 19.2 %collective-permute-start.6 = (f32[128,1024]{1,0:T(8,128)}, f32[128,1024]{1,0:T(8,128)}, u32[]{:S(2)}, u32[]{:S(2)}) collective-permute-start(f32[128,1024]{1,0:T(8,128)} %get-tuple-element.30), channel_id=1, source_target_pairs={{0,7},{8,15},{16,23},{24,31},{32,39},{40,47},{48,55},{56,63},{64,7... | collective-permute-start | bytes 1572872 | tf_op jit(solution)/shard_map/ppermute | solution.py:567
  37.5 1.0 copy-start.1
  41.6 30.4 %all-to-all-start.1 = ((f32[16,128,128]{2,1,0:T(8,128)}), f32[16,128,128]{2,1,0:T(8,128)S(1)}, u32[]{:S(2)}, u32[]{:S(2)}) async-start(f32[16,128,128]{2,1,0:T(8,128)} %pick_early.1), calls=%async_computation.1 | async-start | bytes 2097152 | tf_op jit(solution)/shard_map/all_to_all | solution.py:576
  51.1 21.0 %collective-permute-start.7 = (f32[128,1024]{1,0:T(8,128)}, f32[128,1024]{1,0:T(8,128)S(1)}, u32[]{:S(2)}, u32[]{:S(2)}) collective-permute-start(f32[128,1024]{1,0:T(8,128)} %add_add_fusion), channel_id=1, source_target_pairs={{0,0},{1,8},{2,16},{3,24},{4,32},{5,40},{6,48},{7,56},{8,64},{9,72... | collective-permute-start | bytes 1572872 | tf_op jit(solution)/shard_map/ppermute | solution.py:571
  72.0 0.8 copy-start.10
  72.8 1.0 copy-start.2
  78.6 31.8 %collective-permute-start.10 = (f32[64,1024]{1,0:T(8,128)S(1)}, f32[64,1024]{1,0:T(8,128)S(1)}, u32[]{:S(2)}, u32[]{:S(2)}) collective-permute-start(f32[64,1024]{1,0:T(8,128)S(1)} %get-tuple-element.47), channel_id=1, source_target_pairs={{0,8},{8,24},{16,40},{24,56},{32,72},{40,88},{48,104},{56,120}} | collective-permute-start | bytes 786440 | tf_op jit(solution)/shard_map/ppermute | solution.py:584
  79.3 31.2 %collective-permute-start.9 = (f32[64,1024]{1,0:T(8,128)S(1)}, f32[64,1024]{1,0:T(8,128)S(1)}, u32[]{:S(2)}, u32[]{:S(2)}) collective-permute-start(f32[64,1024]{1,0:T(8,128)S(1)} %get-tuple-element.48), channel_id=1, source_target_pairs={{0,0},{8,16},{16,32},{24,48},{32,64},{40,80},{48,96},{56,112}} | collective-permute-start | bytes 786440 | tf_op jit(solution)/shard_map/ppermute | solution.py:584
  86.2 85.2 %copy-start = (f32[128,1024]{1,0:T(8,128)S(1)}, f32[128,1024]{1,0:T(8,128)}, u32[]{:S(2)}) copy-start(f32[128,1024]{1,0:T(8,128)} %assemble_strip.1.refs_3_) | copy-start | bytes 1572868
  86.2 89.4 %all-to-all-start.2 = ((f32[8,1280,128]{2,1,0:T(8,128)}), f32[8,1280,128]{2,1,0:T(8,128)}, u32[]{:S(2)}, u32[]{:S(2)}) async-start(f32[8,1280,128]{2,1,0:T(8,128)} %pack_first.1), calls=%async_computation.2 | async-start | bytes 10485760 | tf_op jit(solution)/shard_map/all_to_all | solution.py:580
  110.4 122.1 %all-gather.8.cloned.1.call-start = ((), (), s32[]{:S(2)}) async-start(), calls=%async_computation.7 | async-start | bytes 2228224 | tf_op jit(solution)/shard_map/all_gather | solution.py:596
  110.5 4.0 collective-permute-start.11
  111.2 4.0 collective-permute-start.12
  111.9 58.8 %collective-permute-start.13 = (f32[32,1024]{1,0:T(8,128)S(1)}, f32[32,1024]{1,0:T(8,128)S(1)}, u32[]{:S(2)}, u32[]{:S(2)}) collective-permute-start(f32[32,1024]{1,0:T(8,128)S(1)} %get-tuple-element.50), channel_id=1, source_target_pairs={{0,3},{8,11},{16,19},{24,27},{32,35},{40,43},{48,51},{56,59},{64,6... | collective-permute-start | bytes 393224 | tf_op jit(solution)/shard_map/ppermute | solution.py:593
  113.2 57.5 %collective-permute-start.14 = (f32[32,1024]{1,0:T(8,128)S(1)}, f32[32,1024]{1,0:T(8,128)S(1)}, u32[]{:S(2)}, u32[]{:S(2)}) collective-permute-start(f32[32,1024]{1,0:T(8,128)S(1)} %get-tuple-element.49), channel_id=1, source_target_pairs={{0,4},{8,12},{16,20},{24,28},{32,36},{40,44},{48,52},{56,60},{64,6... | collective-permute-start | bytes 393224 | tf_op jit(solution)/shard_map/ppermute | solution.py:593
  113.9 56.8 %collective-permute-start.15 = (f32[32,1024]{1,0:T(8,128)S(1)}, f32[32,1024]{1,0:T(8,128)S(1)}, u32[]{:S(2)}, u32[]{:S(2)}) collective-permute-start(f32[32,1024]{1,0:T(8,128)S(1)} %get-tuple-element.50), channel_id=1, source_target_pairs={{0,5},{8,13},{16,21},{24,29},{32,37},{40,45},{48,53},{56,61},{64,6... | collective-permute-start | bytes 393224 | tf_op jit(solution)/shard_map/ppermute | solution.py:593
  114.5 56.1 %collective-permute-start.16 = (f32[32,1024]{1,0:T(8,128)S(1)}, f32[32,1024]{1,0:T(8,128)S(1)}, u32[]{:S(2)}, u32[]{:S(2)}) collective-permute-start(f32[32,1024]{1,0:T(8,128)S(1)} %get-tuple-element.49), channel_id=1, source_target_pairs={{0,6},{8,14},{16,22},{24,30},{32,38},{40,46},{48,54},{56,62},{64,7... | collective-permute-start | bytes 393224 | tf_op jit(solution)/shard_map/ppermute | solution.py:593
  115.2 55.4 %collective-permute-start.17 = (f32[32,1024]{1,0:T(8,128)S(1)}, f32[32,1024]{1,0:T(8,128)S(1)}, u32[]{:S(2)}, u32[]{:S(2)}) collective-permute-start(f32[32,1024]{1,0:T(8,128)S(1)} %get-tuple-element.50), channel_id=1, source_target_pairs={{0,7},{8,15},{16,23},{24,31},{32,39},{40,47},{48,55},{56,63},{64,7... | collective-permute-start | bytes 393224 | tf_op jit(solution)/shard_map/ppermute | solution.py:593
  171.4 218.1 %all-gather.4.cloned.1.call-start = ((), (), s32[]{:S(2)}) async-start(), calls=%async_computation.5 | async-start | bytes 4718592 | tf_op jit(solution)/shard_map/all_gather | solution.py:618
  171.5 20.8 %collective-permute-start.8 = (f32[128,1024]{1,0:T(8,128)S(1)}, f32[128,1024]{1,0:T(8,128)S(1)}, u32[]{:S(2)}, u32[]{:S(2)}) collective-permute-start(f32[128,1024]{1,0:T(8,128)S(1)} %copy-done), channel_id=1, source_target_pairs={{0,0},{8,1},{16,2},{24,3},{32,4},{40,5},{48,6},{56,7},{64,8},{72,9... | collective-permute-start | bytes 1572872 | tf_op jit(solution)/shard_map/ppermute | solution.py:617
  192.2 0.8 copy-start.9
  194.9 247.2 %all-gather.6.cloned.1.call-start = ((), (), s32[]{:S(2)}) async-start(), calls=%async_computation.6 | async-start | bytes 8912896 | tf_op jit(solution)/shard_map/all_gather | solution.py:600
  232.5 22.9 %collective-permute-start.18 = (f32[512,1024]{1,0:T(8,128)}, f32[512,1024]{1,0:T(8,128)}, u32[]{:S(2)}, u32[]{:S(2)}) collective-permute-start(f32[512,1024]{1,0:T(8,128)} %all-gather.8.cloned.1.call-done.refs_1_), channel_id=1, source_target_pairs={{0,1},{1,0},{2,3},{3,2},{4,5},{5,4},{6,7},{7,6},{8,9},{9,8},{10,11... | collective-permute-start | bytes 6291464 | tf_op jit(solution)/shard_map/ppermute | solution.py:597
  236.3 86.2 %all-to-all-start.3 = ((f32[16,5,128,128]{3,2,1,0:T(8,128)}), f32[16,5,128,128]{3,2,1,0:T(8,128)}, u32[]{:S(2)}, u32[]{:S(2)}) async-start(f32[16,5,128,128]{3,2,1,0:T(8,128)} %pack_rows.2.refs_0_.refs_1_.refs_2_), calls=%async_computation.3 | async-start | bytes 10485760 | tf_op jit(solution)/shard_map/all_to_all | solution.py:605
  250.4 36.0 %collective-permute-start.19 = (f32[1280,128]{1,0:T(8,128)}, f32[1280,128]{1,0:T(8,128)S(1)}, u32[]{:S(2)}, u32[]{:S(2)}) collective-permute-start(f32[1280,128]{1,0:T(8,128)} %get-tuple-element.32), channel_id=1, source_target_pairs={{0,1},{1,2},{2,3},{3,4},{4,5},{5,6},{6,7},{7,0},{8,9},{9,10},{10,1... | collective-permute-start | bytes 1966088 | tf_op jit(solution)/shard_map/ppermute | solution.py:609
  252.1 40.6 %collective-permute-start.20 = (f32[1280,128]{1,0:T(8,128)}, f32[1280,128]{1,0:T(8,128)S(1)}, u32[]{:S(2)}, u32[]{:S(2)}) collective-permute-start(f32[1280,128]{1,0:T(8,128)} %get-tuple-element.33), channel_id=1, source_target_pairs={{0,2},{1,3},{2,4},{3,5},{4,6},{5,7},{6,0},{7,1},{8,10},{9,11},{10,... | collective-permute-start | bytes 1966088 | tf_op jit(solution)/shard_map/ppermute | solution.py:609
  253.1 66.7 %collective-permute-start.21 = (f32[1280,128]{1,0:T(8,128)}, f32[1280,128]{1,0:T(8,128)S(1)}, u32[]{:S(2)}, u32[]{:S(2)}) collective-permute-start(f32[1280,128]{1,0:T(8,128)} %get-tuple-element.34), channel_id=1, source_target_pairs={{0,3},{1,4},{2,5},{3,6},{4,7},{5,0},{6,1},{7,2},{8,11},{9,12},{10,... | collective-permute-start | bytes 1966088 | tf_op jit(solution)/shard_map/ppermute | solution.py:609
  253.2 66.6 %collective-permute-start.22 = (f32[1280,128]{1,0:T(8,128)}, f32[1280,128]{1,0:T(8,128)S(1)}, u32[]{:S(2)}, u32[]{:S(2)}) collective-permute-start(f32[1280,128]{1,0:T(8,128)} %get-tuple-element.35), channel_id=1, source_target_pairs={{0,4},{1,5},{2,6},{3,7},{4,0},{5,1},{6,2},{7,3},{8,12},{9,13},{10,... | collective-permute-start | bytes 1966088 | tf_op jit(solution)/shard_map/ppermute | solution.py:609
  255.5 64.4 %collective-permute-start.23 = (f32[1280,128]{1,0:T(8,128)}, f32[1280,128]{1,0:T(8,128)S(1)}, u32[]{:S(2)}, u32[]{:S(2)}) collective-permute-start(f32[1280,128]{1,0:T(8,128)} %get-tuple-element.36), channel_id=1, source_target_pairs={{0,5},{1,6},{2,7},{3,0},{4,1},{5,2},{6,3},{7,4},{8,13},{9,14},{10,... | collective-permute-start | bytes 1966088 | tf_op jit(solution)/shard_map/ppermute | solution.py:609
  256.7 29.7 %copy-start.15 = (f32[1280,128]{1,0:T(8,128)S(1)}, f32[1280,128]{1,0:T(8,128)}, u32[]{:S(2)}) copy-start(f32[1280,128]{1,0:T(8,128)} %get-tuple-element.37) | copy-start | bytes 1966084
  256.7 36.0 %copy-start.14 = (f32[1280,128]{1,0:T(8,128)S(1)}, f32[1280,128]{1,0:T(8,128)}, u32[]{:S(2)}) copy-start(f32[1280,128]{1,0:T(8,128)} %get-tuple-element.38) | copy-start | bytes 1966084
  286.4 33.4 %copy-start.3 = (f32[1280,128]{1,0:T(8,128)}, f32[1280,128]{1,0:T(8,128)S(1)}, u32[]{:S(2)}) copy-start(f32[1280,128]{1,0:T(8,128)S(1)} %collective-permute-done.19) | copy-start | bytes 1966084
  286.4 33.5 %collective-permute-start.24 = (f32[1280,128]{1,0:T(8,128)S(1)}, f32[1280,128]{1,0:T(8,128)}, u32[]{:S(2)}, u32[]{:S(2)}) collective-permute-start(f32[1280,128]{1,0:T(8,128)S(1)} %copy-done.15), channel_id=1, source_target_pairs={{0,6},{1,7},{2,0},{3,1},{4,2},{5,3},{6,4},{7,5},{8,14},{9,15},{10,... | collective-permute-start | bytes 1966088 | tf_op jit(solution)/shard_map/ppermute | solution.py:609
  292.8 27.1 %copy-start.4 = (f32[1280,128]{1,0:T(8,128)}, f32[1280,128]{1,0:T(8,128)S(1)}, u32[]{:S(2)}) copy-start(f32[1280,128]{1,0:T(8,128)S(1)} %collective-permute-done.20) | copy-start | bytes 1966084
  292.8 29.7 %collective-permute-start.25 = (f32[1280,128]{1,0:T(8,128)S(1)}, f32[1280,128]{1,0:T(8,128)}, u32[]{:S(2)}, u32[]{:S(2)}) collective-permute-start(f32[1280,128]{1,0:T(8,128)S(1)} %copy-done.14), channel_id=1, source_target_pairs={{0,7},{1,0},{2,1},{3,2},{4,3},{5,4},{6,5},{7,6},{8,15},{9,8},{10,9... | collective-permute-start | bytes 1966088 | tf_op jit(solution)/shard_map/ppermute | solution.py:609
  319.8 2.7 copy-start.5
  319.9 2.6 copy-start.6
  319.9 2.6 copy-start.7
  328.0 154.6 %all-to-all-start.4 = ((f32[16,5,128,128]{3,2,1,0:T(8,128)}), f32[16,5,128,128]{3,2,1,0:T(8,128)}, u32[]{:S(2)}, u32[]{:S(2)}) async-start(f32[16,5,128,128]{3,2,1,0:T(8,128)} %pack_rows.3.refs_1_), calls=%async_computation.4 | async-start | bytes 10485760 | tf_op jit(solution)/shard_map/all_to_all | solution.py:614
Sparse Core Ops, SparseCore 0:
  171.5 60.9 all-gather.7
  234.2 67.5 all-gather.3
  304.0 138.0 all-gather.5

commit v5 on v4

--- a/solution.py
+++ b/solution.py
@@ -263,56 +263,44 @@
 def invert_diagonal(work):
     lanes = lax.broadcasted_iota(jnp.int32, (BLOCK, BLOCK), 1)
     rows = lax.broadcasted_iota(jnp.int32, (BLOCK, BLOCK), 0)
-    lane8 = lax.broadcasted_iota(jnp.int32, (8, BLOCK), 1)
-    row8 = lax.broadcasted_iota(jnp.int32, (8, BLOCK), 0)
+    here, below, rest = work[0:8], work[8:16], work[16:]
     done = []
     for t in range(BLOCK // 8):
         base = 8 * t
-        part = work[0:8]
-        cols = [jnp.broadcast_to(part[:, base + i : base + i + 1], (8, BLOCK)) for i in range(8)]
-        pivots = jnp.zeros((8, BLOCK), F32)
+        last = t == BLOCK // 8 - 1
+        part = here if last else jnp.concatenate([here, below], axis=0)
+        shape = part.shape
+        lane = lanes[: shape[0]]
+        row_id = rows[: shape[0]]
+        cols = [jnp.broadcast_to(part[:, base + i : base + i + 1], shape) for i in range(8)]
+        scale = jnp.zeros((8, BLOCK), F32)
         for i in range(8):
-            pivot = jnp.broadcast_to(cols[i][i : i + 1], (8, BLOCK))
-            pivots = jnp.where(row8 == i, pivot, pivots)
-            factor = jnp.where(row8 > i, cols[i] / pivot, 0.0)
+            root = lax.rsqrt(cols[i][i : i + 1])
+            scale = jnp.where(row_id[:8] == i, root, scale)
+            factor = jnp.where(row_id > i, cols[i] * (root * root), 0.0)
             for other in range(i + 1, 8):
-                cols[other] = cols[other] - factor * jnp.broadcast_to(cols[other][i : i + 1], (8, BLOCK))
-            row = jnp.broadcast_to(part[i : i + 1], (8, BLOCK))
-            row = jnp.where(lane8 == base + i, 1.0, row)
-            part = jnp.where((lane8 == base + i) & (row8 > i), 0.0, part)
-            part = jnp.where((lane8 == base + i) & (row8 == i), 1.0, part)
+                cols[other] = cols[other] - factor * cols[other][i : i + 1]
+            row = jnp.where(lane[:1] == base + i, 1.0, part[i : i + 1])
+            part = jnp.where(lane == base + i, jnp.where(row_id == i, 1.0, jnp.where(row_id > i, 0.0, part)), part)
             part = part - factor * row
-        part = part * lax.rsqrt(pivots)
-        done.append(part)
-        if t < BLOCK // 8 - 1:
-            above = (lane8 > base + row8) & (lane8 < base + 8)
-            update = dot_full(part[:, base + 8 :], jnp.where(above, 0.0, part), ((0,), (0,)))
-            work = work[8:]
-            inside = (lanes[: work.shape[0]] >= base) & (lanes[: work.shape[0]] < base + 8)
-            work = jnp.where(inside, 0.0, work) - update
+        here = part[:8] * scale
+        done.append(here)
+        if t < BLOCK // 8 - 2:
+            above = (lane[:8] > base + row_id[:8]) & (lane[:8] < base + 8)
+            update = dot_full(here[:, base + 16 :], jnp.where(above, 0.0, here), ((0,), (0,)))
+            inside = (lanes[: rest.shape[0]] >= base) & (lanes[: rest.shape[0]] < base + 8)
+            rest = jnp.where(inside, 0.0, rest) - update
+        if not last:
+            here = part[8:]
+            below, rest = rest[:8], rest[8:]
     whole = jnp.concatenate(done, axis=0)
     return jnp.where(rows >= lanes, whole, 0.0)
 
 
 def factor_kernel(first, count, last, *refs):
-    if first == 0:
-        parity, mine, other, _, work = refs
-        rows = LEAD // 2 // ROWS
-
-        def join(r, carry):
-            source = pl.ds(pl.multiple_of(r * rows, rows), rows)
-            low = pl.ds(pl.multiple_of(2 * r * rows, rows), rows)
-            high = pl.ds(pl.multiple_of((2 * r + 1) * rows, rows), rows)
-            even = parity[0] == 0
-            work[low, :] = jnp.where(even, mine[source, :], other[source, :])
-            work[high, :] = jnp.where(even, other[source, :], mine[source, :])
-            return carry
-
-        lax.fori_loop(0, ROWS, join, 0)
-    else:
-        given, _, *refs = refs
-        work = refs[-1] if last else refs[0]
-        work[...] = given[...]
+    given, _, *refs = refs
+    work = refs[-1] if last else refs[0]
+    work[...] = given[...]
     total = LEAD // BLOCK
 
     def step(k, carry):
@@ -358,25 +346,25 @@
     full = jax.ShapeDtypeStruct((LEAD, LEAD), F32)
     return pl.pallas_call(
         functools.partial(factor_kernel, part * count, count, last),
-        in_specs=([pl.BlockSpec(memory_space=pltpu.SMEM), whole] if part == 0 else [])
-        + [whole, pl.BlockSpec(memory_space=pl.ANY)],
+        in_specs=[whole, pl.BlockSpec(memory_space=pl.ANY)],
         out_specs=[whole] * 2 if last else whole,
         out_shape=(half, half) if last else full,
         scratch_shapes=[pltpu.VMEM((LEAD, LEAD), F32)] if last else [],
         compiler_params=params(),
         cost_estimate=cost(25 * 10**9, 8 << 20),
         name="factor_lead",
-    )(*given, after)
-
-
-TILE = 256
+    )(given, after)
+
+
+TILE = 512
+CHUNK = 1024
 
 
 def solve_rows(rows, inv_hi, inv_lo):
     hi, lo = split(rows)
     parts = []
-    for n in range(LEAD // TILE):
-        at, upto = pl.ds(n * TILE, TILE), (n + 1) * TILE
+    for n in range(LEAD // 256):
+        at, upto = pl.ds(n * 256, 256), (n + 1) * 256
         parts.append(
             dot3(hi[:, :upto], lo[:, :upto], inv_hi[at, pl.ds(0, upto)], inv_lo[at, pl.ds(0, upto)])
         )
@@ -389,13 +377,13 @@
     @pl.when(step == 0)
     def _():
         def chunk(n, carry):
-            at = pl.ds(pl.multiple_of(n * TILE, TILE), TILE)
+            at = pl.ds(pl.multiple_of(n * CHUNK, CHUNK), CHUNK)
             values = solve_rows(row_strip[at, :], inv_hi, inv_lo)
             panel[at, :] = values
             hi[at, :], lo[at, :] = split(values)
             return carry
 
-        lax.fori_loop(0, LEAD // TILE, chunk, 0)
+        lax.fori_loop(0, LEAD // CHUNK, chunk, 0)
 
     in_panel = (flags[1] == 0) & (step < LEAD // TILE)
     top = flags[0] == 0
@@ -416,11 +404,11 @@
         right = split(solve_rows(col_strip[...], inv_hi, inv_lo))
 
         def chunk(n, carry):
-            at = pl.ds(pl.multiple_of(n * TILE, TILE), TILE)
+            at = pl.ds(pl.multiple_of(n * CHUNK, CHUNK), CHUNK)
             out[at, :] = parent[at, :] - dot3(hi[at, :], lo[at, :], *right)
             return carry
 
-        lax.fori_loop(0, LEAD // TILE, chunk, 0)
+        lax.fori_loop(0, LEAD // CHUNK, chunk, 0)
 
 
 def update_front(flags, row_strip, col_strip, inv_hi, inv_lo, parent):
@@ -579,6 +567,8 @@
     first = pack_first(send_cols[0::2], children, [])
     first = lax.all_to_all(first, "col", split_axis=0, concat_axis=0, tiled=True)
 
+    col_strip = lax.all_gather(strip, "row", axis=0, tiled=True)
+
     half = BLOCK // 2
     piece = total([
         lax.ppermute(
@@ -588,20 +578,16 @@
         )
         for part in range(2)
     ])
-    halves = [piece[: half // 2], piece[half // 2 :]]
-    piece = total([jnp.where(col_index == 0, halves[0], 0.0)] + [
-        lax.ppermute(halves[d % 2], axes, [(number(r, 0), number(r, d)) for r in range(ROWS)])
+    piece = total([piece] + [
+        lax.ppermute(piece, axes, [(number(r, 0), number(r, d)) for r in range(ROWS)])
         for d in range(1, COLS)
     ])
-    lead = lax.all_gather(piece, "row", axis=0, tiled=True)
-    other = lax.ppermute(lead, "col", [(c, c ^ 1) for c in range(COLS)])
-    parity = (col_index % 2).astype(jnp.int32).reshape(1)
-
-    col_strip = lax.all_gather(strip, "row", axis=0, tiled=True)
+    lead = lax.all_gather(hand_on(piece, [first]), "row", axis=0, tiled=True)
+
 
     sends = sends.astype(jnp.int32)
-    work = factor_part(0, [parity, lead, other], strip)
-    near_out = pack_rows(send_rows, sends, pick_cols[:HALF], first, [], [])
+    work = factor_part(0, lead, strip)
+    near_out = pack_rows(send_rows, sends, pick_cols[:HALF], first, [], [col_strip])
     near = lax.all_to_all(near_out, "row", split_axis=0, concat_axis=0, tiled=True)
     shifts = (col_index + jnp.arange(COLS, dtype=jnp.int32)) % COLS
     parts = pack_second(jnp.take(send_cols, shifts * 2 + 1), children, [near_out])
@@ -609,11 +595,11 @@
         lax.ppermute(parts[d], "col", [(c, (c + d) % COLS) for c in range(COLS)])
         for d in range(1, COLS)
     ]
-    work = factor_part(1, [work], near_out)
     far_out = pack_rows(send_rows, sends, pick_cols[HALF:], first, second, [near, work])
     far = lax.all_to_all(far_out, "row", split_axis=0, concat_axis=0, tiled=True)
-    work = factor_part(2, [work], far_out)
-    inv_hi, inv_lo = factor_part(3, [work], far_out)
+    work = factor_part(1, work, far_out)
+    work = factor_part(2, work, far_out)
+    inv_hi, inv_lo = factor_part(3, work, far_out)
     row_piece = hand_on(lax.ppermute(strip, axes, pairs), [near_out])
     row_strip = lax.all_gather(row_piece, "col", axis=0, tiled=True)
     flags = jnp.stack([row_index, col_index]).astype(jnp.int32)

time: 503 us -> 466 us (0.926)
  the two profiles are of different devices: /device:TPU:51 before, /device:TPU:21 now
where the time goes in v5:
time: 466 us; the launch traced here: 463 us
  waiting for transfers between devices  168 us (36%)
  Pallas kernels  162 us (35%)
  starting transfers between devices  101 us (22%)
  between operations  13.7 us (3%)
  other arithmetic  9.36 us (2%)
  local copies, waits for them, and re-layouts  8.43 us (2%)
    pallas_call x4, Pallas kernels, factor_part(): pl.pallas_call(functools.partial(factor_kernel, part * count, count, last...  78.6 us
    ppermute x1, waiting for transfers between devices, body(): row_piece = hand_on(lax.ppermute(strip, axes, pairs), [near_out])  64.9 us
    ppermute x7, waiting for transfers between devices, body(): lax.ppermute(piece, axes, [(number(r, 0), number(r, d)) for r in range(RO...  58.3 us
    pallas_call x1, Pallas kernels, update_front(): pl.pallas_call(update_kernel, grid_spec=pltpu.PrefetchScalarGridSpec(num_...  33.4 us
    pallas_call x7, Pallas kernels, gather_call(): pl.pallas_call(run, in_specs=[pl.BlockSpec(memory_space=pltpu.SMEM)] * le...  31.8 us
    all_to_all x1, starting transfers between devices, body(): lax.all_to_all(far_out, 'row', split_axis=0, concat_axis=0, tiled=True)  25.1 us
    ppermute x1, waiting for transfers between devices, body(): strip_parent = lax.ppermute(own, axes, [(b, a) for a, b in pairs])  22.7 us
    ppermute x7, starting transfers between devices, body(): lax.ppermute(parts[d], 'col', [(c, (c + d) % COLS) for c in range(COLS)])  16.4 us
  transfers between devices with their start and end apart: 33, of which 5 were waited for; matrix products, arithmetic and copies ran while one was open for 3% of the time, Pallas kernels for 31%

profile of v5, /device:TPU:21, one launch (start us, length us, event | category | flops | bytes accessed | tf_op | source)
XLA Modules:
  0.0 463.4 jit_solution(8603523870624489870)
XLA Ops:
  6.5 3.6 cut_strip.1
  10.1 1.4 collective-permute-start
  11.6 0.7 collective-permute-start.1
  13.6 3.3 pack_early.1
  16.9 6.7 %all-to-all-start = ((f32[16,128,128]{2,1,0:T(8,128)}), f32[16,128,128]{2,1,0:T(8,128)S(1)}, u32[]{:S(2)}, u32[]{:S(2)}) async-start(f32[16,128,128]{2,1,0:T(8,128)} %pack_early.1), calls=%async_computation | async-start | bytes 2097152 | tf_op jit(solution)/shard_map/all_to_all | solution.py:562
  23.7 0.7 collective-permute-start.2
  24.4 1.5 collective-permute-start.3
  25.8 1.5 collective-permute-start.4
  27.3 1.5 collective-permute-start.5
  28.8 1.5 collective-permute-start.6
  30.3 0.7 select_reduce_fusion.4.refs_0_
  31.2 7.6 %all-to-all-done.refs_1_ = f32[16,128,128]{2,1,0:T(8,128)S(1)} async-done(((f32[16,128,128]{2,1,0:T(8,128)}), f32[16,128,128]{2,1,0:T(8,128)S(1)}, u32[]{:S(2)}, u32[]{:S(2)}) %all-to-all-start) | async-done | bytes 1048608 | tf_op jit(solution)/shard_map/all_to_all | solution.py:562
  38.8 1.0 copy-done.1
  39.8 3.2 pick_early.1
  42.9 6.7 %all-to-all-start.1 = ((f32[16,128,128]{2,1,0:T(8,128)}), f32[16,128,128]{2,1,0:T(8,128)S(1)}, u32[]{:S(2)}, u32[]{:S(2)}) async-start(f32[16,128,128]{2,1,0:T(8,128)} %pick_early.1), calls=%async_computation.1 | async-start | bytes 2097152 | tf_op jit(solution)/shard_map/all_to_all | solution.py:564
  49.7 2.7 add_add_fusion
  52.5 8.2 %collective-permute-start.7 = (f32[128,1024]{1,0:T(8,128)}, f32[128,1024]{1,0:T(8,128)S(1)}, u32[]{:S(2)}, u32[]{:S(2)}) collective-permute-start(f32[128,1024]{1,0:T(8,128)} %add_add_fusion), channel_id=1, source_target_pairs={{0,0},{1,8},{2,16},{3,24},{4,32},{5,40},{6,48},{7,56},{8,64},{9,72... | collective-permute-start | bytes 1572872 | tf_op jit(solution)/shard_map/ppermute | solution.py:559
  60.7 0.7 reshape.289.keep
  62.2 22.7 %collective-permute-done.7.parent = f32[128,1024]{1,0:T(8,128)S(1)} collective-permute-done((f32[128,1024]{1,0:T(8,128)}, f32[128,1024]{1,0:T(8,128)S(1)}, u32[]{:S(2)}, u32[]{:S(2)}) %collective-permute-start.7) | collective-permute-done | bytes 524320 | tf_op jit(solution)/shard_map/ppermute | solution.py:559
  84.9 0.8 copy-done.9
  85.7 1.0 copy-done.2
  86.7 2.4 assemble_strip.1.refs_1_
  89.1 0.6 slice.20.refs_0_
  89.7 5.6 %pack_first.1 = f32[8,1280,128]{2,1,0:T(8,128)} custom-call(s32[8]{0:T(128)} %slice.20.refs_0_, f32[1280,1280]{1,0:T(8,128)} %refs_1_.5), custom_call_target="tpu_custom_call" | custom-call | bytes 10485760 | tf_op jit(solution)/shard_map/pack_first/pallas_call | solution.py:36
  95.2 6.3 %all-to-all-start.2 = ((f32[8,1280,128]{2,1,0:T(8,128)}), f32[8,1280,128]{2,1,0:T(8,128)}, u32[]{:S(2)}, u32[]{:S(2)}) async-start(f32[8,1280,128]{2,1,0:T(8,128)} %pack_first.1), calls=%async_computation.2 | async-start | bytes 10485760 | tf_op jit(solution)/shard_map/all_to_all | solution.py:568
  101.6 0.7 collective-permute-start.10
  102.3 0.7 collective-permute-start.9
  103.1 0.7 collective-permute-start.17
  103.7 0.7 collective-permute-start.16
  104.4 0.7 collective-permute-start.15
  105.1 0.7 collective-permute-start.14
  105.8 0.7 collective-permute-start.13
  106.5 0.7 collective-permute-start.12
  107.2 1.3 collective-permute-start.11
  108.5 58.2 %collective-permute-done.11 = f32[64,1024]{1,0:T(8,128)S(1)} collective-permute-done((f32[64,1024]{1,0:T(8,128)S(1)}, f32[64,1024]{1,0:T(8,128)S(1)}, u32[]{:S(2)}, u32[]{:S(2)}) %collective-permute-start.11) | collective-permute-done | bytes 262176 | tf_op jit(solution)/shard_map/ppermute | solution.py:582
  166.8 0.9 add_add_fusion.1.given
  167.6 1.7 hand_on.3
  170.7 5.1 %pack_rows.2.refs_0_.refs_2_ = f32[16,5,128,128]{3,2,1,0:T(8,128)} custom-call(s32[16]{0:T(128)} %copy-done.12, s32[16]{0:T(128)} %convert_element_type.32.refs_1_, s32[5]{0:T(128)} %get-tuple-element.56.refs_2_, f32[8,10,128,128]{3,2,1,0:T(8,128)} %bitcast.8.refs_3_, f32[2048,1024]{1,0:T(8,128)} %all-gather.4.cloned.1.call-done.refs_4_.col_strip), custom_call_target="tpu_custom_call" | custom-call | bytes 10485760 | tf_op jit(solution)/shard_map/pack_rows/pallas_call | solution.py:36
  175.7 14.1 %all-to-all-start.3 = ((f32[16,5,128,128]{3,2,1,0:T(8,128)}), f32[16,5,128,128]{3,2,1,0:T(8,128)}, u32[]{:S(2)}, u32[]{:S(2)}) async-start(f32[16,5,128,128]{3,2,1,0:T(8,128)} %pack_rows.2.refs_0_.refs_2_), calls=%async_computation.3 | async-start | bytes 10485760 | tf_op jit(solution)/shard_map/all_to_all | solution.py:591
  190.2 0.7 reshape.288.keep
  190.9 0.6 gather_fusion
  191.5 0.6 and_select_fusion.1.refs_0_
  192.1 5.7 %pack_second.1 = (f32[1280,128]{1,0:T(8,128)}, f32[1280,128]{1,0:T(8,128)}, f32[1280,128]{1,0:T(8,128)}, f32[1280,128]{1,0:T(8,128)}, f32[1280,128]{1,0:T(8,128)...) custom-call(s32[8]{0:T(128)} %and_select_fusion.1.refs_0_, f32[1280,1280]{1,0:T(8,128)} %refs_1_.5, ...), custom_call_target="tpu_custom_call" | custom-call | bytes 10485760 | tf_op jit(solution)/shard_map/pack_second/pallas_call | solution.py:36
  197.8 6.0 %collective-permute-start.18 = (f32[1280,128]{1,0:T(8,128)}, f32[1280,128]{1,0:T(8,128)S(1)}, u32[]{:S(2)}, u32[]{:S(2)}) collective-permute-start(f32[1280,128]{1,0:T(8,128)} %get-tuple-element.32), channel_id=1, source_target_pairs={{0,1},{1,2},{2,3},{3,4},{4,5},{5,6},{6,7},{7,0},{8,9},{9,10},{10,1... | collective-permute-start | bytes 1966088 | tf_op jit(solution)/shard_map/ppermute | solution.py:595
  203.8 2.3 collective-permute-start.8
  206.1 0.7 pad_add_fusion.flags
  206.9 0.7 select_reduce_fusion.rank
  207.5 0.6 fusion.18.source
  208.2 1.7 collective-permute-start.20
  209.9 1.2 collective-permute-start.21
  211.1 64.9 %collective-permute-done.8.given = f32[128,1024]{1,0:T(8,128)S(1)} collective-permute-done((f32[128,1024]{1,0:T(8,128)S(1)}, f32[128,1024]{1,0:T(8,128)S(1)}, u32[]{:S(2)}, u32[]{:S(2)}) %collective-permute-start.8) | collective-permute-done | bytes 524320 | tf_op jit(solution)/shard_map/ppermute | solution.py:603
  276.1 0.8 copy-done.8
  276.9 1.9 hand_on.2
  279.2 7.2 %collective-permute-start.24 = (f32[1280,128]{1,0:T(8,128)}, f32[1280,128]{1,0:T(8,128)}, u32[]{:S(2)}, u32[]{:S(2)}) collective-permute-start(f32[1280,128]{1,0:T(8,128)} %get-tuple-element.38), channel_id=1, source_target_pairs={{0,7},{1,0},{2,1},{3,2},{4,3},{5,4},{6,5},{7,6},{8,15},{9,8},{10,9... | collective-permute-start | bytes 1966088 | tf_op jit(solution)/shard_map/ppermute | solution.py:595
  286.3 14.4 %all-gather.8.cloned.1.call-done.refs_0_ = f32[1024,1024]{1,0:T(8,128)} async-done(((f32[64,1024]{1,0:T(8,128)}), f32[1024,1024]{1,0:T(8,128)}) %all-gather.8.cloned.1.call-update) | async-done | bytes 4194320 | tf_op jit(solution)/shard_map/all_gather | solution.py:585
  300.8 23.2 %factor_lead.4.refs_13_.refs_0_ = f32[1024,1024]{1,0:T(8,128)} custom-call(f32[1024,1024]{1,0:T(8,128)} %all-gather.8.cloned.1.call-done.refs_0_, f32[128,1024]{1,0:T(8,128)} %assemble_strip.1.refs_1_), custom_call_target="tpu_custom_call" | custom-call | flops 24999999488 | bytes 8388608 | tf_op jit(solution)/shard_map/factor_lead/pallas_call | solution.py:347
  324.1 0.8 copy-done.5
  325.1 5.4 %pack_rows.3.refs_1_ = f32[16,5,128,128]{3,2,1,0:T(8,128)} custom-call(s32[16]{0:T(128)} %copy-done.12, s32[16]{0:T(128)} %convert_element_type.32.refs_1_, s32[5]{0:T(128)} %get-tuple-element.55.refs_2_, f32[8,10,128,128]{3,2,1,0:T(8,128)} %bitcast.8.refs_3_, f32[10,128,128]{2,1,0:T(8,128)} %bitcast.41, f32[10,128,128]{2,1,0:T(8,128)} %bitcast.42, ...), custom_call_target="tpu_custom_call" | custom-call | bytes 10485760 | tf_op jit(solution)/shard_map/pack_rows/pallas_call | solution.py:36
  330.5 25.1 %all-to-all-start.4 = ((f32[16,5,128,128]{3,2,1,0:T(8,128)}), f32[16,5,128,128]{3,2,1,0:T(8,128)}, u32[]{:S(2)}, u32[]{:S(2)}) async-start(f32[16,5,128,128]{3,2,1,0:T(8,128)} %pack_rows.3.refs_1_), calls=%async_computation.4 | async-start | bytes 10485760 | tf_op jit(solution)/shard_map/all_to_all | solution.py:599
  355.7 20.7 %factor_lead.5.refs_0_ = f32[1024,1024]{1,0:T(8,128)} custom-call(f32[1024,1024]{1,0:T(8,128)} %factor_lead.4.refs_13_.refs_0_, f32[16,5,128,128]{3,2,1,0:T(8,128)} %pack_rows.3.refs_1_), custom_call_target="tpu_custom_call" | custom-call | flops 24999999488 | bytes 8388608 | tf_op jit(solution)/shard_map/factor_lead/pallas_call | solution.py:347
  376.4 18.2 %factor_lead.6.refs_0_ = f32[1024,1024]{1,0:T(8,128)} custom-call(f32[1024,1024]{1,0:T(8,128)} %factor_lead.5.refs_0_, f32[16,5,128,128]{3,2,1,0:T(8,128)} %pack_rows.3.refs_1_), custom_call_target="tpu_custom_call" | custom-call | flops 24999999488 | bytes 8388608 | tf_op jit(solution)/shard_map/factor_lead/pallas_call | solution.py:347
  394.6 16.5 %factor_lead.7 = (bf16[1024,1024]{1,0:T(8,128)(2,1)}, bf16[1024,1024]{1,0:T(8,128)(2,1)}) custom-call(f32[1024,1024]{1,0:T(8,128)} %factor_lead.6.refs_0_, f32[16,5,128,128]{3,2,1,0:T(8,128)} %pack_rows.3.refs_1_), custom_call_target="tpu_custom_call" | custom-call | flops 24999999488 | bytes 8388608 | tf_op jit(solution)/shard_map/factor_lead/pallas_call | solution.py:347
  411.1 33.4 %update_front.1.front = f32[1024,2048]{1,0:T(8,128)} custom-call(s32[2]{0:T(128)} %pad_add_fusion.flags, f32[1024,1024]{1,0:T(8,128)} %all-gather.6.cloned.1.call-done.row_strip, f32[2048,1024]{1,0:T(8,128)} %all-gather.4.cloned.1.call-done.refs_4_.col_strip, bf16[1024,1024]{1,0:T(8,128)(2,1)} %get-tuple-element.39.inv_hi, ...), custom_call_target="tpu_custom_call" | custom-call | flops 40000000000 | bytes 33554432 | tf_op jit(solution)/shard_map/update_front/pallas_call | solution.py:417
  444.5 12.4 %place_children.1 = f32[1024,2048]{1,0:T(8,128)} custom-call(s32[2,8]{1,0:T(2,128)} %fusion.18.source, s32[2,16]{1,0:T(2,128)} %select_reduce_fusion.rank, s32[2,128]{1,0:T(2,128)} %reshape.288.keep, f32[1024,2048]{1,0:T(8,128)} %update_front.1.front, f32[16,5,128,128]{3,2,1,0:T(8,128)} %all-to-all-done.3.refs_12_.refs_0_.refs_2_, ...), custom_call_target="tpu_custom_call", output_to_operand_aliasing={{}: (3, {})} | custom-call | bytes 25165824 | tf_op jit(solution)/shard_map/place_children/pallas_call | solution.py:465
  (90 shorter events, 4.9 us)
Async XLA Ops:
  6.5 5.8 %copy-start.11 = (s32[2,80]{1,0:T(2,128)S(1)}, s32[2,80]{1,0:T(2,128)}, u32[]{:S(2)}) copy-start(s32[2,80]{1,0:T(2,128)} %param.6) | copy-start | bytes 1924
  10.1 20.8 %copy-start.10 = (s32[2,80,80]{2,1,0:T(8,128)S(1)}, s32[2,80,80]{2,1,0:T(8,128)}, u32[]{:S(2)}) copy-start(s32[2,80,80]{2,1,0:T(8,128)} %param.7) | copy-start | bytes 153604
  10.1 17.2 %collective-permute-start = (f32[128,1024]{1,0:T(8,128)}, f32[128,1024]{1,0:T(8,128)S(1)}, u32[]{:S(2)}, u32[]{:S(2)}) collective-permute-start(f32[128,1024]{1,0:T(8,128)} %get-tuple-element.24), channel_id=1, source_target_pairs={{0,1},{8,9},{16,17},{24,25},{32,33},{40,41},{48,49},{56,57},{64,65... | collective-permute-start | bytes 1572872 | tf_op jit(solution)/shard_map/ppermute | solution.py:555
  11.6 17.2 %collective-permute-start.1 = (f32[128,1024]{1,0:T(8,128)}, f32[128,1024]{1,0:T(8,128)S(1)}, u32[]{:S(2)}, u32[]{:S(2)}) collective-permute-start(f32[128,1024]{1,0:T(8,128)} %get-tuple-element.25), channel_id=1, source_target_pairs={{0,2},{8,10},{16,18},{24,26},{32,34},{40,42},{48,50},{56,58},{64,6... | collective-permute-start | bytes 1572872 | tf_op jit(solution)/shard_map/ppermute | solution.py:555
  13.0 29.9 %copy-start.12 = (s32[16]{0:T(128)}, s32[16]{0:T(128)S(1)}, u32[]{:S(2)}) copy-start(s32[16]{0:T(128)S(1)} %get-tuple-element.42.refs_0_) | copy-start | bytes 196
  13.6 36.1 %copy-start.7 = (f32[128,1024]{1,0:T(8,128)S(1)}, f32[128,1024]{1,0:T(8,128)}, u32[]{:S(2)}) copy-start(f32[128,1024]{1,0:T(8,128)} %get-tuple-element.23) | copy-start | bytes 1572868
  16.9 21.9 %all-to-all-start = ((f32[16,128,128]{2,1,0:T(8,128)}), f32[16,128,128]{2,1,0:T(8,128)S(1)}, u32[]{:S(2)}, u32[]{:S(2)}) async-start(f32[16,128,128]{2,1,0:T(8,128)} %pack_early.1), calls=%async_computation | async-start | bytes 2097152 | tf_op jit(solution)/shard_map/all_to_all | solution.py:562
  23.7 26.0 %collective-permute-start.2 = (f32[128,1024]{1,0:T(8,128)}, f32[128,1024]{1,0:T(8,128)S(1)}, u32[]{:S(2)}, u32[]{:S(2)}) collective-permute-start(f32[128,1024]{1,0:T(8,128)} %get-tuple-element.26), channel_id=1, source_target_pairs={{0,3},{8,11},{16,19},{24,27},{32,35},{40,43},{48,51},{56,59},{64,6... | collective-permute-start | bytes 1572872 | tf_op jit(solution)/shard_map/ppermute | solution.py:555
  24.4 25.3 %collective-permute-start.3 = (f32[128,1024]{1,0:T(8,128)}, f32[128,1024]{1,0:T(8,128)}, u32[]{:S(2)}, u32[]{:S(2)}) collective-permute-start(f32[128,1024]{1,0:T(8,128)} %get-tuple-element.27), channel_id=1, source_target_pairs={{0,4},{8,12},{16,20},{24,28},{32,36},{40,44},{48,52},{56,60},{64,6... | collective-permute-start | bytes 1572872 | tf_op jit(solution)/shard_map/ppermute | solution.py:555
  25.8 23.8 %collective-permute-start.4 = (f32[128,1024]{1,0:T(8,128)}, f32[128,1024]{1,0:T(8,128)}, u32[]{:S(2)}, u32[]{:S(2)}) collective-permute-start(f32[128,1024]{1,0:T(8,128)} %get-tuple-element.28), channel_id=1, source_target_pairs={{0,5},{8,13},{16,21},{24,29},{32,37},{40,45},{48,53},{56,61},{64,6... | collective-permute-start | bytes 1572872 | tf_op jit(solution)/shard_map/ppermute | solution.py:555
  27.3 22.4 %collective-permute-start.5 = (f32[128,1024]{1,0:T(8,128)}, f32[128,1024]{1,0:T(8,128)}, u32[]{:S(2)}, u32[]{:S(2)}) collective-permute-start(f32[128,1024]{1,0:T(8,128)} %get-tuple-element.29), channel_id=1, source_target_pairs={{0,6},{8,14},{16,22},{24,30},{32,38},{40,46},{48,54},{56,62},{64,7... | collective-permute-start | bytes 1572872 | tf_op jit(solution)/shard_map/ppermute | solution.py:555
  28.8 20.9 %collective-permute-start.6 = (f32[128,1024]{1,0:T(8,128)}, f32[128,1024]{1,0:T(8,128)}, u32[]{:S(2)}, u32[]{:S(2)}) collective-permute-start(f32[128,1024]{1,0:T(8,128)} %get-tuple-element.30), channel_id=1, source_target_pairs={{0,7},{8,15},{16,23},{24,31},{32,39},{40,47},{48,55},{56,63},{64,7... | collective-permute-start | bytes 1572872 | tf_op jit(solution)/shard_map/ppermute | solution.py:555
  38.8 1.0 copy-start.1
  42.9 42.0 %all-to-all-start.1 = ((f32[16,128,128]{2,1,0:T(8,128)}), f32[16,128,128]{2,1,0:T(8,128)S(1)}, u32[]{:S(2)}, u32[]{:S(2)}) async-start(f32[16,128,128]{2,1,0:T(8,128)} %pick_early.1), calls=%async_computation.1 | async-start | bytes 2097152 | tf_op jit(solution)/shard_map/all_to_all | solution.py:564
  49.6 121.1 %all-gather.4.cloned.1.call-start = ((), (), s32[]{:S(2)}) async-start(), calls=%async_computation.5 | async-start | bytes 8912896 | tf_op jit(solution)/shard_map/all_gather | solution.py:570
  52.5 32.5 %collective-permute-start.7 = (f32[128,1024]{1,0:T(8,128)}, f32[128,1024]{1,0:T(8,128)S(1)}, u32[]{:S(2)}, u32[]{:S(2)}) collective-permute-start(f32[128,1024]{1,0:T(8,128)} %add_add_fusion), channel_id=1, source_target_pairs={{0,0},{1,8},{2,16},{3,24},{4,32},{5,40},{6,48},{7,56},{8,64},{9,72... | collective-permute-start | bytes 1572872 | tf_op jit(solution)/shard_map/ppermute | solution.py:559
  84.9 0.8 copy-start.9
  85.7 1.0 copy-start.2
  95.2 6.3 %copy-start = (f32[128,1024]{1,0:T(8,128)S(1)}, f32[128,1024]{1,0:T(8,128)}, u32[]{:S(2)}) copy-start(f32[128,1024]{1,0:T(8,128)} %assemble_strip.1.refs_1_) | copy-start | bytes 1572868
  95.2 72.4 %all-to-all-start.2 = ((f32[8,1280,128]{2,1,0:T(8,128)}), f32[8,1280,128]{2,1,0:T(8,128)}, u32[]{:S(2)}, u32[]{:S(2)}) async-start(f32[8,1280,128]{2,1,0:T(8,128)} %pack_first.1), calls=%async_computation.2 | async-start | bytes 10485760 | tf_op jit(solution)/shard_map/all_to_all | solution.py:568
  101.6 199.2 %all-gather.8.cloned.1.call-start = ((), (), s32[]{:S(2)}) async-start(), calls=%async_computation.7 | async-start | bytes 4456448 | tf_op jit(solution)/shard_map/all_gather | solution.py:585
  101.6 1.4 collective-permute-start.10
  102.3 0.7 collective-permute-start.9
  103.1 3.4 collective-permute-start.17
  103.7 3.4 collective-permute-start.16
  104.4 4.1 collective-permute-start.15
  105.1 3.4 collective-permute-start.14
  105.8 2.7 collective-permute-start.13
  106.5 2.0 collective-permute-start.12
  107.2 59.6 %collective-permute-start.11 = (f32[64,1024]{1,0:T(8,128)S(1)}, f32[64,1024]{1,0:T(8,128)S(1)}, u32[]{:S(2)}, u32[]{:S(2)}) collective-permute-start(f32[64,1024]{1,0:T(8,128)S(1)} %add.273), channel_id=1, source_target_pairs={{0,1},{8,9},{16,17},{24,25},{32,33},{40,41},{48,49},{56,57},{64,65... | collective-permute-start | bytes 786440 | tf_op jit(solution)/shard_map/ppermute | solution.py:582
  175.7 148.3 %all-to-all-start.3 = ((f32[16,5,128,128]{3,2,1,0:T(8,128)}), f32[16,5,128,128]{3,2,1,0:T(8,128)}, u32[]{:S(2)}, u32[]{:S(2)}) async-start(f32[16,5,128,128]{3,2,1,0:T(8,128)} %pack_rows.2.refs_0_.refs_2_), calls=%async_computation.3 | async-start | bytes 10485760 | tf_op jit(solution)/shard_map/all_to_all | solution.py:591
  189.9 221.2 %all-gather.6.cloned.1.call-start = ((), (), s32[]{:S(2)}) async-start(), calls=%async_computation.6 | async-start | bytes 4718592 | tf_op jit(solution)/shard_map/all_gather | solution.py:604
  197.8 81.1 %collective-permute-start.18 = (f32[1280,128]{1,0:T(8,128)}, f32[1280,128]{1,0:T(8,128)S(1)}, u32[]{:S(2)}, u32[]{:S(2)}) collective-permute-start(f32[1280,128]{1,0:T(8,128)} %get-tuple-element.32), channel_id=1, source_target_pairs={{0,1},{1,2},{2,3},{3,4},{4,5},{5,6},{6,7},{7,0},{8,9},{9,10},{10,1... | collective-permute-start | bytes 1966088 | tf_op jit(solution)/shard_map/ppermute | solution.py:595
  203.8 75.3 %collective-permute-start.19 = (f32[1280,128]{1,0:T(8,128)}, f32[1280,128]{1,0:T(8,128)S(1)}, u32[]{:S(2)}, u32[]{:S(2)}) collective-permute-start(f32[1280,128]{1,0:T(8,128)} %get-tuple-element.33), channel_id=1, source_target_pairs={{0,2},{1,3},{2,4},{3,5},{4,6},{5,7},{6,0},{7,1},{8,10},{9,11},{10,... | collective-permute-start | bytes 1966088 | tf_op jit(solution)/shard_map/ppermute | solution.py:595
  203.8 72.3 %collective-permute-start.8 = (f32[128,1024]{1,0:T(8,128)S(1)}, f32[128,1024]{1,0:T(8,128)S(1)}, u32[]{:S(2)}, u32[]{:S(2)}) collective-permute-start(f32[128,1024]{1,0:T(8,128)S(1)} %copy-done), channel_id=1, source_target_pairs={{0,0},{8,1},{16,2},{24,3},{32,4},{40,5},{48,6},{56,7},{64,8},{72,9... | collective-permute-start | bytes 1572872 | tf_op jit(solution)/shard_map/ppermute | solution.py:603
  208.2 115.8 %collective-permute-start.20 = (f32[1280,128]{1,0:T(8,128)}, f32[1280,128]{1,0:T(8,128)S(1)}, u32[]{:S(2)}, u32[]{:S(2)}) collective-permute-start(f32[1280,128]{1,0:T(8,128)} %get-tuple-element.34), channel_id=1, source_target_pairs={{0,3},{1,4},{2,5},{3,6},{4,7},{5,0},{6,1},{7,2},{8,11},{9,12},{10,... | collective-permute-start | bytes 1966088 | tf_op jit(solution)/shard_map/ppermute | solution.py:595
  209.9 114.1 %collective-permute-start.21 = (f32[1280,128]{1,0:T(8,128)}, f32[1280,128]{1,0:T(8,128)S(1)}, u32[]{:S(2)}, u32[]{:S(2)}) collective-permute-start(f32[1280,128]{1,0:T(8,128)} %get-tuple-element.35), channel_id=1, source_target_pairs={{0,4},{1,5},{2,6},{3,7},{4,0},{5,1},{6,2},{7,3},{8,12},{9,13},{10,... | collective-permute-start | bytes 1966088 | tf_op jit(solution)/shard_map/ppermute | solution.py:595
  276.1 0.8 copy-start.8
  276.1 47.9 %collective-permute-start.22 = (f32[1280,128]{1,0:T(8,128)}, f32[1280,128]{1,0:T(8,128)}, u32[]{:S(2)}, u32[]{:S(2)}) collective-permute-start(f32[1280,128]{1,0:T(8,128)} %get-tuple-element.36), channel_id=1, source_target_pairs={{0,5},{1,6},{2,7},{3,0},{4,1},{5,2},{6,3},{7,4},{8,13},{9,14},{10,... | collective-permute-start | bytes 1966088 | tf_op jit(solution)/shard_map/ppermute | solution.py:595
  278.9 45.1 %copy-start.3 = (f32[1280,128]{1,0:T(8,128)}, f32[1280,128]{1,0:T(8,128)S(1)}, u32[]{:S(2)}) copy-start(f32[1280,128]{1,0:T(8,128)S(1)} %collective-permute-done.18) | copy-start | bytes 1966084
  278.9 45.2 %collective-permute-start.23 = (f32[1280,128]{1,0:T(8,128)}, f32[1280,128]{1,0:T(8,128)}, u32[]{:S(2)}, u32[]{:S(2)}) collective-permute-start(f32[1280,128]{1,0:T(8,128)} %get-tuple-element.37), channel_id=1, source_target_pairs={{0,6},{1,7},{2,0},{3,1},{4,2},{5,3},{6,4},{7,5},{8,14},{9,15},{10,... | collective-permute-start | bytes 1966088 | tf_op jit(solution)/shard_map/ppermute | solution.py:595
  279.1 44.8 %copy-start.4 = (f32[1280,128]{1,0:T(8,128)}, f32[1280,128]{1,0:T(8,128)S(1)}, u32[]{:S(2)}) copy-start(f32[1280,128]{1,0:T(8,128)S(1)} %collective-permute-done.19) | copy-start | bytes 1966084
  279.2 44.9 %collective-permute-start.24 = (f32[1280,128]{1,0:T(8,128)}, f32[1280,128]{1,0:T(8,128)}, u32[]{:S(2)}, u32[]{:S(2)}) collective-permute-start(f32[1280,128]{1,0:T(8,128)} %get-tuple-element.38), channel_id=1, source_target_pairs={{0,7},{1,0},{2,1},{3,2},{4,3},{5,4},{6,5},{7,6},{8,15},{9,8},{10,9... | collective-permute-start | bytes 1966088 | tf_op jit(solution)/shard_map/ppermute | solution.py:595
  324.0 0.9 copy-start.5
  324.0 1.1 copy-start.6
  330.5 113.9 %all-to-all-start.4 = ((f32[16,5,128,128]{3,2,1,0:T(8,128)}), f32[16,5,128,128]{3,2,1,0:T(8,128)}, u32[]{:S(2)}, u32[]{:S(2)}) async-start(f32[16,5,128,128]{3,2,1,0:T(8,128)} %pack_rows.3.refs_1_), calls=%async_computation.4 | async-start | bytes 10485760 | tf_op jit(solution)/shard_map/all_to_all | solution.py:599
Sparse Core Ops, SparseCore 0:
  89.2 78.3 all-gather.3
  169.8 130.9 all-gather.7
  302.5 34.7 all-gather.5

commit v6 on v5

--- a/solution.py
+++ b/solution.py
@@ -567,8 +567,6 @@
     first = pack_first(send_cols[0::2], children, [])
     first = lax.all_to_all(first, "col", split_axis=0, concat_axis=0, tiled=True)
 
-    col_strip = lax.all_gather(strip, "row", axis=0, tiled=True)
-
     half = BLOCK // 2
     piece = total([
         lax.ppermute(
@@ -582,12 +580,15 @@
         lax.ppermute(piece, axes, [(number(r, 0), number(r, d)) for r in range(ROWS)])
         for d in range(1, COLS)
     ])
-    lead = lax.all_gather(hand_on(piece, [first]), "row", axis=0, tiled=True)
-
+    lead = lax.all_gather(piece, "row", axis=0, tiled=True)
+
+    col_strip = lax.all_gather(strip, "row", axis=0, tiled=True)
+
+    row_raw = lax.ppermute(strip, axes, pairs)
 
     sends = sends.astype(jnp.int32)
     work = factor_part(0, lead, strip)
-    near_out = pack_rows(send_rows, sends, pick_cols[:HALF], first, [], [col_strip])
+    near_out = pack_rows(send_rows, sends, pick_cols[:HALF], first, [], [row_raw])
     near = lax.all_to_all(near_out, "row", split_axis=0, concat_axis=0, tiled=True)
     shifts = (col_index + jnp.arange(COLS, dtype=jnp.int32)) % COLS
     parts = pack_second(jnp.take(send_cols, shifts * 2 + 1), children, [near_out])
@@ -599,8 +600,8 @@
     far = lax.all_to_all(far_out, "row", split_axis=0, concat_axis=0, tiled=True)
     work = factor_part(1, work, far_out)
     work = factor_part(2, work, far_out)
-    inv_hi, inv_lo = factor_part(3, work, far_out)
-    row_piece = hand_on(lax.ppermute(strip, axes, pairs), [near_out])
+    inv_hi, inv_lo = factor_part(3, work, col_strip)
+    row_piece = hand_on(row_raw, [near_out])
     row_strip = lax.all_gather(row_piece, "col", axis=0, tiled=True)
     flags = jnp.stack([row_index, col_index]).astype(jnp.int32)
     front = update_front(flags, row_strip, col_strip, inv_hi, inv_lo, parent_front)

time: 466 us -> 455 us (0.976)
  starting transfers between devices: 101 us -> 86.4 us
    all_to_all x1, waiting for transfers between devices: 0.01 us -> 59.1 us  [body(): lax.all_to_all(first, 'col', split_axis=0, concat_axis=0, tiled=True)]
    ppermute x1, waiting for transfers between devices: 64.9 us -> 13.2 us  [body(): row_raw = lax.ppermute(strip, axes, pairs)]
    ppermute x7, waiting for transfers between devices: 58.3 us -> 12.5 us  [body(): lax.ppermute(piece, axes, [(number(r, 0), number(r, d)) for r in range(RO...]
    ppermute x7, waiting for transfers between devices: 0.02 us -> 29.5 us  [body(): lax.ppermute(parts[d], 'col', [(c, (c + d) % COLS) for c in range(COLS)])]
    all_to_all x1, waiting for transfers between devices: 0.01 us -> 25.4 us  [body(): lax.all_to_all(near_out, 'row', split_axis=0, concat_axis=0, tiled=True)]
    all_to_all x1, starting transfers between devices: 25.1 us -> 6.68 us  [body(): lax.all_to_all(far_out, 'row', split_axis=0, concat_axis=0, tiled=True)]
    all_gather x1, waiting for transfers between devices: 14.4 us -> 0.01 us  [body(): lead = lax.all_gather(piece, 'row', axis=0, tiled=True)]
    all_to_all x1, starting transfers between devices: 6.32 us -> 16 us  [body(): lax.all_to_all(first, 'col', split_axis=0, concat_axis=0, tiled=True)]
  transfers between devices with their start and end apart: 33 -> 33, of which waited for: 5 -> 12; matrix products, arithmetic and copies ran while one was open for 3% -> 3% of each run, Pallas kernels for 31% -> 32%
where the time goes in v6:
time: 455 us; the launch traced here: 449 us
  waiting for transfers between devices  171 us (38%)
  Pallas kernels  161 us (35%)
  starting transfers between devices  86.4 us (19%)
  between operations  13.6 us (3%)
  other arithmetic  9.12 us (2%)
  local copies, waits for them, and re-layouts  7.54 us (2%)
    pallas_call x4, Pallas kernels, factor_part(): pl.pallas_call(functools.partial(factor_kernel, part * count, count, last...  79.2 us
    all_to_all x1, waiting for transfers between devices, body(): lax.all_to_all(first, 'col', split_axis=0, concat_axis=0, tiled=True)  59.1 us
    pallas_call x1, Pallas kernels, update_front(): pl.pallas_call(update_kernel, grid_spec=pltpu.PrefetchScalarGridSpec(num_...  33.4 us
    pallas_call x7, Pallas kernels, gather_call(): pl.pallas_call(run, in_specs=[pl.BlockSpec(memory_space=pltpu.SMEM)] * le...  31.5 us
    ppermute x7, waiting for transfers between devices, body(): lax.ppermute(parts[d], 'col', [(c, (c + d) % COLS) for c in range(COLS)])  29.5 us
    all_to_all x1, waiting for transfers between devices, body(): lax.all_to_all(near_out, 'row', split_axis=0, concat_axis=0, tiled=True)  25.4 us
    ppermute x1, waiting for transfers between devices, body(): strip_parent = lax.ppermute(own, axes, [(b, a) for a, b in pairs])  22.5 us
    all_to_all x1, starting transfers between devices, body(): lax.all_to_all(first, 'col', split_axis=0, concat_axis=0, tiled=True)  16 us
  transfers between devices with their start and end apart: 33, of which 12 were waited for; matrix products, arithmetic and copies ran while one was open for 3% of the time, Pallas kernels for 32%

profile of v6, /device:TPU:21, one launch (start us, length us, event | category | flops | bytes accessed | tf_op | source)
XLA Modules:
  0.0 449.3 jit_solution(6039453294575421155)
XLA Ops:
  6.5 3.6 cut_strip.1
  10.1 1.4 collective-permute-start
  11.6 0.7 collective-permute-start.1
  13.0 0.7 pad_add_fusion.1.refs_0_
  13.7 3.0 pack_early.1
  16.7 6.7 %all-to-all-start = ((f32[16,128,128]{2,1,0:T(8,128)}), f32[16,128,128]{2,1,0:T(8,128)S(1)}, u32[]{:S(2)}, u32[]{:S(2)}) async-start(f32[16,128,128]{2,1,0:T(8,128)} %pack_early.1), calls=%async_computation | async-start | bytes 2097152 | tf_op jit(solution)/shard_map/all_to_all | solution.py:562
  23.4 0.7 collective-permute-start.2
  24.1 1.5 collective-permute-start.3
  25.6 1.5 collective-permute-start.4
  27.1 1.5 collective-permute-start.5
  28.6 1.5 collective-permute-start.6
  30.0 0.6 select_reduce_fusion.4.refs_0_
  30.9 7.7 %all-to-all-done.refs_1_ = f32[16,128,128]{2,1,0:T(8,128)S(1)} async-done(((f32[16,128,128]{2,1,0:T(8,128)}), f32[16,128,128]{2,1,0:T(8,128)S(1)}, u32[]{:S(2)}, u32[]{:S(2)}) %all-to-all-start) | async-done | bytes 1048608 | tf_op jit(solution)/shard_map/all_to_all | solution.py:562
  38.6 1.0 copy-done.1
  39.5 3.1 pick_early.1
  42.7 6.7 %all-to-all-start.1 = ((f32[16,128,128]{2,1,0:T(8,128)}), f32[16,128,128]{2,1,0:T(8,128)S(1)}, u32[]{:S(2)}, u32[]{:S(2)}) async-start(f32[16,128,128]{2,1,0:T(8,128)} %pick_early.1), calls=%async_computation.1 | async-start | bytes 2097152 | tf_op jit(solution)/shard_map/all_to_all | solution.py:564
  49.5 2.7 add_add_fusion
  52.2 8.4 %collective-permute-start.7 = (f32[128,1024]{1,0:T(8,128)}, f32[128,1024]{1,0:T(8,128)S(1)}, u32[]{:S(2)}, u32[]{:S(2)}) collective-permute-start(f32[128,1024]{1,0:T(8,128)} %add_add_fusion), channel_id=1, source_target_pairs={{0,0},{1,8},{2,16},{3,24},{4,32},{5,40},{6,48},{7,56},{8,64},{9,72... | collective-permute-start | bytes 1572872 | tf_op jit(solution)/shard_map/ppermute | solution.py:559
  62.2 22.5 %collective-permute-done.7.parent = f32[128,1024]{1,0:T(8,128)S(1)} collective-permute-done((f32[128,1024]{1,0:T(8,128)}, f32[128,1024]{1,0:T(8,128)S(1)}, u32[]{:S(2)}, u32[]{:S(2)}) %collective-permute-start.7) | collective-permute-done | bytes 524320 | tf_op jit(solution)/shard_map/ppermute | solution.py:559
  84.8 0.8 copy-done.10
  85.6 1.0 copy-done.2
  86.5 3.1 assemble_strip.1.refs_1_
  89.6 1.1 fusion.31
  90.7 0.7 collective-permute-start.10
  91.4 0.7 collective-permute-start.9
  92.1 1.3 collective-permute-start.11
  93.4 0.7 collective-permute-start.12
  94.1 0.7 collective-permute-start.13
  94.8 0.7 collective-permute-start.14
  95.5 0.7 collective-permute-start.15
  96.2 12.5 %collective-permute-done.11 = f32[64,1024]{1,0:T(8,128)S(1)} collective-permute-done((f32[64,1024]{1,0:T(8,128)S(1)}, f32[64,1024]{1,0:T(8,128)S(1)}, u32[]{:S(2)}, u32[]{:S(2)}) %collective-permute-start.11) | collective-permute-done | bytes 262176 | tf_op jit(solution)/shard_map/ppermute | solution.py:580
  108.7 0.7 collective-permute-start.16
  109.3 0.7 collective-permute-start.17
  110.1 0.9 add_add_fusion.1
  111.0 0.7 all-gather.6.cloned.1.call-update
  112.3 5.6 %pack_first.1 = f32[8,1280,128]{2,1,0:T(8,128)} custom-call(s32[8]{0:T(128)} %slice.20.refs_0_, f32[1280,1280]{1,0:T(8,128)} %refs_1_.5), custom_call_target="tpu_custom_call" | custom-call | bytes 10485760 | tf_op jit(solution)/shard_map/pack_first/pallas_call | solution.py:36
  117.9 16.0 %all-to-all-start.2 = ((f32[8,1280,128]{2,1,0:T(8,128)}), f32[8,1280,128]{2,1,0:T(8,128)}, u32[]{:S(2)}, u32[]{:S(2)}) async-start(f32[8,1280,128]{2,1,0:T(8,128)} %pack_first.1), calls=%async_computation.2 | async-start | bytes 10485760 | tf_op jit(solution)/shard_map/all_to_all | solution.py:568
  133.9 9.0 %collective-permute-start.8 = (f32[128,1024]{1,0:T(8,128)S(1)}, f32[128,1024]{1,0:T(8,128)S(1)}, u32[]{:S(2)}, u32[]{:S(2)}) collective-permute-start(f32[128,1024]{1,0:T(8,128)S(1)} %copy-done), channel_id=1, source_target_pairs={{0,0},{8,1},{16,2},{24,3},{32,4},{40,5},{48,6},{56,7},{64,8},{72,9... | collective-permute-start | bytes 1572872 | tf_op jit(solution)/shard_map/ppermute | solution.py:587
  144.3 13.2 %collective-permute-done.8.refs_4_.given = f32[128,1024]{1,0:T(8,128)S(1)} collective-permute-done((f32[128,1024]{1,0:T(8,128)S(1)}, f32[128,1024]{1,0:T(8,128)S(1)}, u32[]{:S(2)}, u32[]{:S(2)}) %collective-permute-start.8) | collective-permute-done | bytes 524320 | tf_op jit(solution)/shard_map/ppermute | solution.py:587
  157.5 59.1 %all-to-all-done.2 = f32[8,1280,128]{2,1,0:T(8,128)} async-done(((f32[8,1280,128]{2,1,0:T(8,128)}), f32[8,1280,128]{2,1,0:T(8,128)}, u32[]{:S(2)}, u32[]{:S(2)}) %all-to-all-start.2) | async-done | bytes 5242912 | tf_op jit(solution)/shard_map/all_to_all | solution.py:568
  216.5 5.2 %pack_rows.2.refs_0_.refs_2_ = f32[16,5,128,128]{3,2,1,0:T(8,128)} custom-call(s32[16]{0:T(128)} %copy-done.13, s32[16]{0:T(128)} %convert_element_type.32.refs_1_, s32[5]{0:T(128)} %get-tuple-element.56.refs_2_, f32[8,10,128,128]{3,2,1,0:T(8,128)} %bitcast.8.refs_3_, f32[128,1024]{1,0:T(8,128)} %copy-done.3), custom_call_target="tpu_custom_call" | custom-call | bytes 10485760 | tf_op jit(solution)/shard_map/pack_rows/pallas_call | solution.py:36
  221.8 7.5 %all-to-all-start.3 = ((f32[16,5,128,128]{3,2,1,0:T(8,128)}), f32[16,5,128,128]{3,2,1,0:T(8,128)}, u32[]{:S(2)}, u32[]{:S(2)}) async-start(f32[16,5,128,128]{3,2,1,0:T(8,128)} %pack_rows.2.refs_0_.refs_2_), calls=%async_computation.3 | async-start | bytes 10485760 | tf_op jit(solution)/shard_map/all_to_all | solution.py:592
  229.3 0.6 gather_fusion
  230.2 0.7 reshape.288.keep
  231.4 5.6 %pack_second.1 = (f32[1280,128]{1,0:T(8,128)}, f32[1280,128]{1,0:T(8,128)}, f32[1280,128]{1,0:T(8,128)}, f32[1280,128]{1,0:T(8,128)}, f32[1280,128]{1,0:T(8,128)...) custom-call(s32[8]{0:T(128)} %and_select_fusion.1.refs_0_, f32[1280,1280]{1,0:T(8,128)} %refs_1_.5, ...), custom_call_target="tpu_custom_call" | custom-call | bytes 10485760 | tf_op jit(solution)/shard_map/pack_second/pallas_call | solution.py:36
  237.0 4.3 collective-permute-start.18
  242.0 0.7 select_reduce_fusion.rank
  243.3 3.3 collective-permute-start.20
  246.6 2.2 collective-permute-start.22
  248.8 1.9 hand_on.1
  250.7 4.8 %collective-permute-done.18 = f32[1280,128]{1,0:T(8,128)S(1)} collective-permute-done((f32[1280,128]{1,0:T(8,128)}, f32[1280,128]{1,0:T(8,128)S(1)}, u32[]{:S(2)}, u32[]{:S(2)}) %collective-permute-start.18) | collective-permute-done | bytes 655392 | tf_op jit(solution)/shard_map/ppermute | solution.py:596
  255.5 14.0 %collective-permute-done.19 = f32[1280,128]{1,0:T(8,128)S(1)} collective-permute-done((f32[1280,128]{1,0:T(8,128)}, f32[1280,128]{1,0:T(8,128)S(1)}, u32[]{:S(2)}, u32[]{:S(2)}) %collective-permute-start.19) | collective-permute-done | bytes 655392 | tf_op jit(solution)/shard_map/ppermute | solution.py:596
  269.6 23.4 %factor_lead.4.refs_13_.refs_0_ = f32[1024,1024]{1,0:T(8,128)} custom-call(f32[1024,1024]{1,0:T(8,128)} %all-gather.8.cloned.1.call-done.refs_0_, f32[128,1024]{1,0:T(8,128)} %assemble_strip.1.refs_1_), custom_call_target="tpu_custom_call" | custom-call | flops 24999999488 | bytes 8388608 | tf_op jit(solution)/shard_map/factor_lead/pallas_call | solution.py:347
  293.0 7.9 %collective-permute-done.21 = f32[1280,128]{1,0:T(8,128)S(1)} collective-permute-done((f32[1280,128]{1,0:T(8,128)}, f32[1280,128]{1,0:T(8,128)S(1)}, u32[]{:S(2)}, u32[]{:S(2)}) %collective-permute-start.21) | collective-permute-done | bytes 655392 | tf_op jit(solution)/shard_map/ppermute | solution.py:596
  301.6 1.0 collective-permute-done.23
  302.5 1.2 collective-permute-done.24
  303.7 25.4 %all-to-all-done.3.refs_12_.refs_0_.refs_2_ = f32[16,5,128,128]{3,2,1,0:T(8,128)} async-done(((f32[16,5,128,128]{3,2,1,0:T(8,128)}), f32[16,5,128,128]{3,2,1,0:T(8,128)}, u32[]{:S(2)}, u32[]{:S(2)}) %all-to-all-start.3) | async-done | bytes 5242912 | tf_op jit(solution)/shard_map/all_to_all | solution.py:592
  329.1 5.4 %pack_rows.3.refs_1_ = f32[16,5,128,128]{3,2,1,0:T(8,128)} custom-call(s32[16]{0:T(128)} %copy-done.13, s32[16]{0:T(128)} %convert_element_type.32.refs_1_, s32[5]{0:T(128)} %get-tuple-element.55.refs_2_, f32[8,10,128,128]{3,2,1,0:T(8,128)} %bitcast.8.refs_3_, f32[10,128,128]{2,1,0:T(8,128)} %bitcast.41, f32[10,128,128]{2,1,0:T(8,128)} %bitcast.42, ...), custom_call_target="tpu_custom_call" | custom-call | bytes 10485760 | tf_op jit(solution)/shard_map/pack_rows/pallas_call | solution.py:36
  334.5 6.7 %all-to-all-start.4 = ((f32[16,5,128,128]{3,2,1,0:T(8,128)}), f32[16,5,128,128]{3,2,1,0:T(8,128)}, u32[]{:S(2)}, u32[]{:S(2)}) async-start(f32[16,5,128,128]{3,2,1,0:T(8,128)} %pack_rows.3.refs_1_), calls=%async_computation.4 | async-start | bytes 10485760 | tf_op jit(solution)/shard_map/all_to_all | solution.py:600
  341.2 21.1 %factor_lead.5.refs_0_ = f32[1024,1024]{1,0:T(8,128)} custom-call(f32[1024,1024]{1,0:T(8,128)} %factor_lead.4.refs_13_.refs_0_, f32[16,5,128,128]{3,2,1,0:T(8,128)} %pack_rows.3.refs_1_), custom_call_target="tpu_custom_call" | custom-call | flops 24999999488 | bytes 8388608 | tf_op jit(solution)/shard_map/factor_lead/pallas_call | solution.py:347
  362.3 18.2 %factor_lead.6.refs_0_ = f32[1024,1024]{1,0:T(8,128)} custom-call(f32[1024,1024]{1,0:T(8,128)} %factor_lead.5.refs_0_, f32[16,5,128,128]{3,2,1,0:T(8,128)} %pack_rows.3.refs_1_), custom_call_target="tpu_custom_call" | custom-call | flops 24999999488 | bytes 8388608 | tf_op jit(solution)/shard_map/factor_lead/pallas_call | solution.py:347
  380.4 16.5 %factor_lead.7 = (bf16[1024,1024]{1,0:T(8,128)(2,1)}, bf16[1024,1024]{1,0:T(8,128)(2,1)}) custom-call(f32[1024,1024]{1,0:T(8,128)} %factor_lead.6.refs_0_, f32[2048,1024]{1,0:T(8,128)} %all-gather.6.cloned.1.call-done.refs_1_.col_strip), custom_call_target="tpu_custom_call" | custom-call | flops 24999999488 | bytes 8388608 | tf_op jit(solution)/shard_map/factor_lead/pallas_call | solution.py:347
  396.9 33.4 %update_front.1.front = f32[1024,2048]{1,0:T(8,128)} custom-call(s32[2]{0:T(128)} %pad_add_fusion.flags, f32[1024,1024]{1,0:T(8,128)} %all-gather.4.cloned.1.call-done.row_strip, f32[2048,1024]{1,0:T(8,128)} %all-gather.6.cloned.1.call-done.refs_1_.col_strip, bf16[1024,1024]{1,0:T(8,128)(2,1)} %get-tuple-element.39.inv_hi, ...), custom_call_target="tpu_custom_call" | custom-call | flops 40000000000 | bytes 33554432 | tf_op jit(solution)/shard_map/update_front/pallas_call | solution.py:417
  430.3 12.4 %place_children.1 = f32[1024,2048]{1,0:T(8,128)} custom-call(s32[2,8]{1,0:T(2,128)} %fusion.18.source, s32[2,16]{1,0:T(2,128)} %select_reduce_fusion.rank, s32[2,128]{1,0:T(2,128)} %reshape.288.keep, f32[1024,2048]{1,0:T(8,128)} %update_front.1.front, f32[16,5,128,128]{3,2,1,0:T(8,128)} %all-to-all-done.3.refs_12_.refs_0_.refs_2_, ...), custom_call_target="tpu_custom_call", output_to_operand_aliasing={{}: (3, {})} | custom-call | bytes 25165824 | tf_op jit(solution)/shard_map/place_children/pallas_call | solution.py:465
  (91 shorter events, 7.2 us)
Async XLA Ops:
  6.5 5.8 %copy-start.12 = (s32[2,80]{1,0:T(2,128)S(1)}, s32[2,80]{1,0:T(2,128)}, u32[]{:S(2)}) copy-start(s32[2,80]{1,0:T(2,128)} %param.6) | copy-start | bytes 1924
  10.1 20.5 %copy-start.11 = (s32[2,80,80]{2,1,0:T(8,128)S(1)}, s32[2,80,80]{2,1,0:T(8,128)}, u32[]{:S(2)}) copy-start(s32[2,80,80]{2,1,0:T(8,128)} %param.7) | copy-start | bytes 153604
  10.1 16.9 %collective-permute-start = (f32[128,1024]{1,0:T(8,128)}, f32[128,1024]{1,0:T(8,128)S(1)}, u32[]{:S(2)}, u32[]{:S(2)}) collective-permute-start(f32[128,1024]{1,0:T(8,128)} %get-tuple-element.24), channel_id=1, source_target_pairs={{0,1},{8,9},{16,17},{24,25},{32,33},{40,41},{48,49},{56,57},{64,65... | collective-permute-start | bytes 1572872 | tf_op jit(solution)/shard_map/ppermute | solution.py:555
  11.6 17.0 %collective-permute-start.1 = (f32[128,1024]{1,0:T(8,128)}, f32[128,1024]{1,0:T(8,128)S(1)}, u32[]{:S(2)}, u32[]{:S(2)}) collective-permute-start(f32[128,1024]{1,0:T(8,128)} %get-tuple-element.25), channel_id=1, source_target_pairs={{0,2},{8,10},{16,18},{24,26},{32,34},{40,42},{48,50},{56,58},{64,6... | collective-permute-start | bytes 1572872 | tf_op jit(solution)/shard_map/ppermute | solution.py:555
  13.0 29.7 %copy-start.13 = (s32[16]{0:T(128)}, s32[16]{0:T(128)S(1)}, u32[]{:S(2)}) copy-start(s32[16]{0:T(128)S(1)} %get-tuple-element.42.refs_0_) | copy-start | bytes 196
  13.7 35.8 %copy-start.9 = (f32[128,1024]{1,0:T(8,128)S(1)}, f32[128,1024]{1,0:T(8,128)}, u32[]{:S(2)}) copy-start(f32[128,1024]{1,0:T(8,128)} %get-tuple-element.23) | copy-start | bytes 1572868
  16.7 21.8 %all-to-all-start = ((f32[16,128,128]{2,1,0:T(8,128)}), f32[16,128,128]{2,1,0:T(8,128)S(1)}, u32[]{:S(2)}, u32[]{:S(2)}) async-start(f32[16,128,128]{2,1,0:T(8,128)} %pack_early.1), calls=%async_computation | async-start | bytes 2097152 | tf_op jit(solution)/shard_map/all_to_all | solution.py:562
  23.4 26.0 %collective-permute-start.2 = (f32[128,1024]{1,0:T(8,128)}, f32[128,1024]{1,0:T(8,128)S(1)}, u32[]{:S(2)}, u32[]{:S(2)}) collective-permute-start(f32[128,1024]{1,0:T(8,128)} %get-tuple-element.26), channel_id=1, source_target_pairs={{0,3},{8,11},{16,19},{24,27},{32,35},{40,43},{48,51},{56,59},{64,6... | collective-permute-start | bytes 1572872 | tf_op jit(solution)/shard_map/ppermute | solution.py:555
  24.1 25.3 %collective-permute-start.3 = (f32[128,1024]{1,0:T(8,128)}, f32[128,1024]{1,0:T(8,128)}, u32[]{:S(2)}, u32[]{:S(2)}) collective-permute-start(f32[128,1024]{1,0:T(8,128)} %get-tuple-element.27), channel_id=1, source_target_pairs={{0,4},{8,12},{16,20},{24,28},{32,36},{40,44},{48,52},{56,60},{64,6... | collective-permute-start | bytes 1572872 | tf_op jit(solution)/shard_map/ppermute | solution.py:555
  25.6 23.8 %collective-permute-start.4 = (f32[128,1024]{1,0:T(8,128)}, f32[128,1024]{1,0:T(8,128)}, u32[]{:S(2)}, u32[]{:S(2)}) collective-permute-start(f32[128,1024]{1,0:T(8,128)} %get-tuple-element.28), channel_id=1, source_target_pairs={{0,5},{8,13},{16,21},{24,29},{32,37},{40,45},{48,53},{56,61},{64,6... | collective-permute-start | bytes 1572872 | tf_op jit(solution)/shard_map/ppermute | solution.py:555
  27.1 22.4 %collective-permute-start.5 = (f32[128,1024]{1,0:T(8,128)}, f32[128,1024]{1,0:T(8,128)}, u32[]{:S(2)}, u32[]{:S(2)}) collective-permute-start(f32[128,1024]{1,0:T(8,128)} %get-tuple-element.29), channel_id=1, source_target_pairs={{0,6},{8,14},{16,22},{24,30},{32,38},{40,46},{48,54},{56,62},{64,7... | collective-permute-start | bytes 1572872 | tf_op jit(solution)/shard_map/ppermute | solution.py:555
  28.6 20.9 %collective-permute-start.6 = (f32[128,1024]{1,0:T(8,128)}, f32[128,1024]{1,0:T(8,128)}, u32[]{:S(2)}, u32[]{:S(2)}) collective-permute-start(f32[128,1024]{1,0:T(8,128)} %get-tuple-element.30), channel_id=1, source_target_pairs={{0,7},{8,15},{16,23},{24,31},{32,39},{40,47},{48,55},{56,63},{64,7... | collective-permute-start | bytes 1572872 | tf_op jit(solution)/shard_map/ppermute | solution.py:555
  38.6 1.0 copy-start.1
  42.7 42.1 %all-to-all-start.1 = ((f32[16,128,128]{2,1,0:T(8,128)}), f32[16,128,128]{2,1,0:T(8,128)S(1)}, u32[]{:S(2)}, u32[]{:S(2)}) async-start(f32[16,128,128]{2,1,0:T(8,128)} %pick_early.1), calls=%async_computation.1 | async-start | bytes 2097152 | tf_op jit(solution)/shard_map/all_to_all | solution.py:564
  49.4 220.2 %all-gather.8.cloned.1.call-start = ((), (), s32[]{:S(2)}) async-start(), calls=%async_computation.7 | async-start | bytes 4456448 | tf_op jit(solution)/shard_map/all_gather | solution.py:583
  52.2 32.5 %collective-permute-start.7 = (f32[128,1024]{1,0:T(8,128)}, f32[128,1024]{1,0:T(8,128)S(1)}, u32[]{:S(2)}, u32[]{:S(2)}) collective-permute-start(f32[128,1024]{1,0:T(8,128)} %add_add_fusion), channel_id=1, source_target_pairs={{0,0},{1,8},{2,16},{3,24},{4,32},{5,40},{6,48},{7,56},{8,64},{9,72... | collective-permute-start | bytes 1572872 | tf_op jit(solution)/shard_map/ppermute | solution.py:559
  84.7 0.8 copy-start.10
  85.6 1.0 copy-start.2
  90.7 1.4 collective-permute-start.10
  91.4 0.7 collective-permute-start.9
  92.1 16.5 %collective-permute-start.11 = (f32[64,1024]{1,0:T(8,128)S(1)}, f32[64,1024]{1,0:T(8,128)S(1)}, u32[]{:S(2)}, u32[]{:S(2)}) collective-permute-start(f32[64,1024]{1,0:T(8,128)S(1)} %add.273), channel_id=1, source_target_pairs={{0,1},{8,9},{16,17},{24,25},{32,33},{40,41},{48,49},{56,57},{64,65... | collective-permute-start | bytes 786440 | tf_op jit(solution)/shard_map/ppermute | solution.py:580
  93.4 15.9 %collective-permute-start.12 = (f32[64,1024]{1,0:T(8,128)S(1)}, f32[64,1024]{1,0:T(8,128)S(1)}, u32[]{:S(2)}, u32[]{:S(2)}) collective-permute-start(f32[64,1024]{1,0:T(8,128)S(1)} %add.273), channel_id=1, source_target_pairs={{0,2},{8,10},{16,18},{24,26},{32,34},{40,42},{48,50},{56,58},{64,6... | collective-permute-start | bytes 786440 | tf_op jit(solution)/shard_map/ppermute | solution.py:580
  94.1 15.9 %collective-permute-start.13 = (f32[64,1024]{1,0:T(8,128)S(1)}, f32[64,1024]{1,0:T(8,128)S(1)}, u32[]{:S(2)}, u32[]{:S(2)}) collective-permute-start(f32[64,1024]{1,0:T(8,128)S(1)} %add.273), channel_id=1, source_target_pairs={{0,3},{8,11},{16,19},{24,27},{32,35},{40,43},{48,51},{56,59},{64,6... | collective-permute-start | bytes 786440 | tf_op jit(solution)/shard_map/ppermute | solution.py:580
  94.8 15.2 %collective-permute-start.14 = (f32[64,1024]{1,0:T(8,128)S(1)}, f32[64,1024]{1,0:T(8,128)S(1)}, u32[]{:S(2)}, u32[]{:S(2)}) collective-permute-start(f32[64,1024]{1,0:T(8,128)S(1)} %add.273), channel_id=1, source_target_pairs={{0,4},{8,12},{16,20},{24,28},{32,36},{40,44},{48,52},{56,60},{64,6... | collective-permute-start | bytes 786440 | tf_op jit(solution)/shard_map/ppermute | solution.py:580
  95.5 14.6 %collective-permute-start.15 = (f32[64,1024]{1,0:T(8,128)S(1)}, f32[64,1024]{1,0:T(8,128)S(1)}, u32[]{:S(2)}, u32[]{:S(2)}) collective-permute-start(f32[64,1024]{1,0:T(8,128)S(1)} %add.273), channel_id=1, source_target_pairs={{0,5},{8,13},{16,21},{24,29},{32,37},{40,45},{48,53},{56,61},{64,6... | collective-permute-start | bytes 786440 | tf_op jit(solution)/shard_map/ppermute | solution.py:580
  108.7 1.4 collective-permute-start.16
  109.3 0.7 collective-permute-start.17
  111.0 269.5 %all-gather.6.cloned.1.call-start = ((), (), s32[]{:S(2)}) async-start(), calls=%async_computation.6 | async-start | bytes 8912896 | tf_op jit(solution)/shard_map/all_gather | solution.py:585
  117.9 16.0 %copy-start = (f32[128,1024]{1,0:T(8,128)S(1)}, f32[128,1024]{1,0:T(8,128)}, u32[]{:S(2)}) copy-start(f32[128,1024]{1,0:T(8,128)} %assemble_strip.1.refs_1_) | copy-start | bytes 1572868
  117.9 98.6 %all-to-all-start.2 = ((f32[8,1280,128]{2,1,0:T(8,128)}), f32[8,1280,128]{2,1,0:T(8,128)}, u32[]{:S(2)}, u32[]{:S(2)}) async-start(f32[8,1280,128]{2,1,0:T(8,128)} %pack_first.1), calls=%async_computation.2 | async-start | bytes 10485760 | tf_op jit(solution)/shard_map/all_to_all | solution.py:568
  133.9 23.5 %collective-permute-start.8 = (f32[128,1024]{1,0:T(8,128)S(1)}, f32[128,1024]{1,0:T(8,128)S(1)}, u32[]{:S(2)}, u32[]{:S(2)}) collective-permute-start(f32[128,1024]{1,0:T(8,128)S(1)} %copy-done), channel_id=1, source_target_pairs={{0,0},{8,1},{16,2},{24,3},{32,4},{40,5},{48,6},{56,7},{64,8},{72,9... | collective-permute-start | bytes 1572872 | tf_op jit(solution)/shard_map/ppermute | solution.py:587
  157.5 59.1 %copy-start.3 = (f32[128,1024]{1,0:T(8,128)}, f32[128,1024]{1,0:T(8,128)S(1)}, u32[]{:S(2)}) copy-start(f32[128,1024]{1,0:T(8,128)S(1)} %collective-permute-done.8.refs_4_.given) | copy-start | bytes 1572868
  221.8 107.3 %all-to-all-start.3 = ((f32[16,5,128,128]{3,2,1,0:T(8,128)}), f32[16,5,128,128]{3,2,1,0:T(8,128)}, u32[]{:S(2)}, u32[]{:S(2)}) async-start(f32[16,5,128,128]{3,2,1,0:T(8,128)} %pack_rows.2.refs_0_.refs_2_), calls=%async_computation.3 | async-start | bytes 10485760 | tf_op jit(solution)/shard_map/all_to_all | solution.py:592
  229.3 167.7 %all-gather.4.cloned.1.call-start = ((), (), s32[]{:S(2)}) async-start(), calls=%async_computation.5 | async-start | bytes 4718592 | tf_op jit(solution)/shard_map/all_gather | solution.py:605
  237.0 18.6 %collective-permute-start.18 = (f32[1280,128]{1,0:T(8,128)}, f32[1280,128]{1,0:T(8,128)S(1)}, u32[]{:S(2)}, u32[]{:S(2)}) collective-permute-start(f32[1280,128]{1,0:T(8,128)} %get-tuple-element.32), channel_id=1, source_target_pairs={{0,1},{1,2},{2,3},{3,4},{4,5},{5,6},{6,7},{7,0},{8,9},{9,10},{10,1... | collective-permute-start | bytes 1966088 | tf_op jit(solution)/shard_map/ppermute | solution.py:596
  241.3 28.3 %collective-permute-start.19 = (f32[1280,128]{1,0:T(8,128)}, f32[1280,128]{1,0:T(8,128)S(1)}, u32[]{:S(2)}, u32[]{:S(2)}) collective-permute-start(f32[1280,128]{1,0:T(8,128)} %get-tuple-element.33), channel_id=1, source_target_pairs={{0,2},{1,3},{2,4},{3,5},{4,6},{5,7},{6,0},{7,1},{8,10},{9,11},{10,... | collective-permute-start | bytes 1966088 | tf_op jit(solution)/shard_map/ppermute | solution.py:596
  243.3 49.7 %collective-permute-start.20 = (f32[1280,128]{1,0:T(8,128)}, f32[1280,128]{1,0:T(8,128)S(1)}, u32[]{:S(2)}, u32[]{:S(2)}) collective-permute-start(f32[1280,128]{1,0:T(8,128)} %get-tuple-element.34), channel_id=1, source_target_pairs={{0,3},{1,4},{2,5},{3,6},{4,7},{5,0},{6,1},{7,2},{8,11},{9,12},{10,... | collective-permute-start | bytes 1966088 | tf_op jit(solution)/shard_map/ppermute | solution.py:596
  246.6 54.4 %collective-permute-start.21 = (f32[1280,128]{1,0:T(8,128)}, f32[1280,128]{1,0:T(8,128)S(1)}, u32[]{:S(2)}, u32[]{:S(2)}) collective-permute-start(f32[1280,128]{1,0:T(8,128)} %get-tuple-element.35), channel_id=1, source_target_pairs={{0,4},{1,5},{2,6},{3,7},{4,0},{5,1},{6,2},{7,3},{8,12},{9,13},{10,... | collective-permute-start | bytes 1966088 | tf_op jit(solution)/shard_map/ppermute | solution.py:596
  246.6 55.0 %collective-permute-start.22 = (f32[1280,128]{1,0:T(8,128)}, f32[1280,128]{1,0:T(8,128)S(1)}, u32[]{:S(2)}, u32[]{:S(2)}) collective-permute-start(f32[1280,128]{1,0:T(8,128)} %get-tuple-element.36), channel_id=1, source_target_pairs={{0,5},{1,6},{2,7},{3,0},{4,1},{5,2},{6,3},{7,4},{8,13},{9,14},{10,... | collective-permute-start | bytes 1966088 | tf_op jit(solution)/shard_map/ppermute | solution.py:596
  255.5 37.5 %copy-start.4 = (f32[1280,128]{1,0:T(8,128)}, f32[1280,128]{1,0:T(8,128)S(1)}, u32[]{:S(2)}) copy-start(f32[1280,128]{1,0:T(8,128)S(1)} %collective-permute-done.18) | copy-start | bytes 1966084
  255.5 47.0 %collective-permute-start.23 = (f32[1280,128]{1,0:T(8,128)}, f32[1280,128]{1,0:T(8,128)}, u32[]{:S(2)}, u32[]{:S(2)}) collective-permute-start(f32[1280,128]{1,0:T(8,128)} %get-tuple-element.37), channel_id=1, source_target_pairs={{0,6},{1,7},{2,0},{3,1},{4,2},{5,3},{6,4},{7,5},{8,14},{9,15},{10,... | collective-permute-start | bytes 1966088 | tf_op jit(solution)/shard_map/ppermute | solution.py:596
  269.6 23.4 %copy-start.5 = (f32[1280,128]{1,0:T(8,128)}, f32[1280,128]{1,0:T(8,128)S(1)}, u32[]{:S(2)}) copy-start(f32[1280,128]{1,0:T(8,128)S(1)} %collective-permute-done.19) | copy-start | bytes 1966084
  269.6 34.1 %collective-permute-start.24 = (f32[1280,128]{1,0:T(8,128)}, f32[1280,128]{1,0:T(8,128)}, u32[]{:S(2)}, u32[]{:S(2)}) collective-permute-start(f32[1280,128]{1,0:T(8,128)} %get-tuple-element.38), channel_id=1, source_target_pairs={{0,7},{1,0},{2,1},{3,2},{4,3},{5,4},{6,5},{7,6},{8,15},{9,8},{10,9... | collective-permute-start | bytes 1966088 | tf_op jit(solution)/shard_map/ppermute | solution.py:596
  293.0 36.1 %copy-start.6 = (f32[1280,128]{1,0:T(8,128)}, f32[1280,128]{1,0:T(8,128)S(1)}, u32[]{:S(2)}) copy-start(f32[1280,128]{1,0:T(8,128)S(1)} %collective-permute-done.20) | copy-start | bytes 1966084
  300.9 28.2 %copy-start.7 = (f32[1280,128]{1,0:T(8,128)}, f32[1280,128]{1,0:T(8,128)S(1)}, u32[]{:S(2)}) copy-start(f32[1280,128]{1,0:T(8,128)S(1)} %collective-permute-done.21) | copy-start | bytes 1966084
  301.6 27.6 %copy-start.8 = (f32[1280,128]{1,0:T(8,128)}, f32[1280,128]{1,0:T(8,128)S(1)}, u32[]{:S(2)}) copy-start(f32[1280,128]{1,0:T(8,128)S(1)} %collective-permute-done.22) | copy-start | bytes 1966084
  334.5 95.8 %all-to-all-start.4 = ((f32[16,5,128,128]{3,2,1,0:T(8,128)}), f32[16,5,128,128]{3,2,1,0:T(8,128)}, u32[]{:S(2)}, u32[]{:S(2)}) async-start(f32[16,5,128,128]{3,2,1,0:T(8,128)} %pack_rows.3.refs_1_), calls=%async_computation.4 | async-start | bytes 10485760 | tf_op jit(solution)/shard_map/all_to_all | solution.py:600
Sparse Core Ops, SparseCore 0:
  111.1 88.5 all-gather.7
  201.8 120.7 all-gather.5
  324.2 39.4 all-gather.3

commit v7 on v5

--- a/solution.py
+++ b/solution.py
@@ -564,10 +564,12 @@
     early = lax.all_to_all(early, "row", split_axis=0, concat_axis=0, tiled=True)
     strip = assemble_strip(strip_place, strip_keep, strip_parent, early, [])
 
-    first = pack_first(send_cols[0::2], children, [])
+    first = pack_first(send_cols[0::2], children, [strip])
     first = lax.all_to_all(first, "col", split_axis=0, concat_axis=0, tiled=True)
 
     col_strip = lax.all_gather(strip, "row", axis=0, tiled=True)
+
+    row_raw = lax.ppermute(strip, axes, pairs)
 
     half = BLOCK // 2
     piece = total([
@@ -582,12 +584,12 @@
         lax.ppermute(piece, axes, [(number(r, 0), number(r, d)) for r in range(ROWS)])
         for d in range(1, COLS)
     ])
-    lead = lax.all_gather(hand_on(piece, [first]), "row", axis=0, tiled=True)
+    lead = lax.all_gather(hand_on(piece, [first, row_raw, col_strip]), "row", axis=0, tiled=True)
 
 
     sends = sends.astype(jnp.int32)
     work = factor_part(0, lead, strip)
-    near_out = pack_rows(send_rows, sends, pick_cols[:HALF], first, [], [col_strip])
+    near_out = pack_rows(send_rows, sends, pick_cols[:HALF], first, [], [lead])
     near = lax.all_to_all(near_out, "row", split_axis=0, concat_axis=0, tiled=True)
     shifts = (col_index + jnp.arange(COLS, dtype=jnp.int32)) % COLS
     parts = pack_second(jnp.take(send_cols, shifts * 2 + 1), children, [near_out])
@@ -595,12 +597,12 @@
         lax.ppermute(parts[d], "col", [(c, (c + d) % COLS) for c in range(COLS)])
         for d in range(1, COLS)
     ]
+    work = factor_part(1, work, near_out)
     far_out = pack_rows(send_rows, sends, pick_cols[HALF:], first, second, [near, work])
     far = lax.all_to_all(far_out, "row", split_axis=0, concat_axis=0, tiled=True)
-    work = factor_part(1, work, far_out)
     work = factor_part(2, work, far_out)
     inv_hi, inv_lo = factor_part(3, work, far_out)
-    row_piece = hand_on(lax.ppermute(strip, axes, pairs), [near_out])
+    row_piece = hand_on(row_raw, [near_out])
     row_strip = lax.all_gather(row_piece, "col", axis=0, tiled=True)
     flags = jnp.stack([row_index, col_index]).astype(jnp.int32)
     front = update_front(flags, row_strip, col_strip, inv_hi, inv_lo, parent_front)

time: 466 us -> 476 us (1.021)
  waiting for transfers between devices: 168 us -> 201 us
  starting transfers between devices: 101 us -> 79.5 us
    all_gather x1, waiting for transfers between devices: 14.4 us -> 61 us  [body(): lax.all_gather(hand_on(piece, [first, row_raw, col_strip]), 'row', axis=0...]
    ppermute x1, waiting for transfers between devices: 64.9 us -> 22.2 us  [body(): row_raw = lax.ppermute(strip, axes, pairs)]
    ppermute x7, waiting for transfers between devices: 0.02 us -> 26 us  [body(): lax.ppermute(parts[d], 'col', [(c, (c + d) % COLS) for c in range(COLS)])]
    all_to_all x1, starting transfers between devices: 25.1 us -> 6.68 us  [body(): lax.all_to_all(far_out, 'row', split_axis=0, concat_axis=0, tiled=True)]
    all_to_all x1, waiting for transfers between devices: 0.01 us -> 15.8 us  [body(): lax.all_to_all(far_out, 'row', split_axis=0, concat_axis=0, tiled=True)]
    ppermute x7, waiting for transfers between devices: 58.3 us -> 45 us  [body(): lax.ppermute(piece, axes, [(number(r, 0), number(r, d)) for r in range(RO...]
    ppermute x1, starting transfers between devices: 2.3 us -> 13.2 us  [body(): row_raw = lax.ppermute(strip, axes, pairs)]
    all_to_all x1, starting transfers between devices: 14.1 us -> 6.68 us  [body(): lax.all_to_all(near_out, 'row', split_axis=0, concat_axis=0, tiled=True)]
  transfers between devices with their start and end apart: 33 -> 33, of which waited for: 5 -> 10; matrix products, arithmetic and copies ran while one was open for 3% -> 3% of each run, Pallas kernels for 31% -> 29%
where the time goes in v7:
time: 476 us; the launch traced here: 475 us
  waiting for transfers between devices  201 us (42%)
  Pallas kernels  163 us (34%)
  starting transfers between devices  79.5 us (17%)
  between operations  13.6 us (3%)
  other arithmetic  9.32 us (2%)
  local copies, waits for them, and re-layouts  8.19 us (2%)
    pallas_call x4, Pallas kernels, factor_part(): pl.pallas_call(functools.partial(factor_kernel, part * count, count, last...  79 us
    all_gather x1, waiting for transfers between devices, body(): lax.all_gather(hand_on(piece, [first, row_raw, col_strip]), 'row', axis=0...  61 us
    ppermute x7, waiting for transfers between devices, body(): lax.ppermute(piece, axes, [(number(r, 0), number(r, d)) for r in range(RO...  45 us
    pallas_call x1, Pallas kernels, update_front(): pl.pallas_call(update_kernel, grid_spec=pltpu.PrefetchScalarGridSpec(num_...  33.4 us
    pallas_call x7, Pallas kernels, gather_call(): pl.pallas_call(run, in_specs=[pl.BlockSpec(memory_space=pltpu.SMEM)] * le...  31.6 us
    ppermute x7, waiting for transfers between devices, body(): lax.ppermute(parts[d], 'col', [(c, (c + d) % COLS) for c in range(COLS)])  26 us
    ppermute x1, waiting for transfers between devices, body(): strip_parent = lax.ppermute(own, axes, [(b, a) for a, b in pairs])  22.7 us
    ppermute x1, waiting for transfers between devices, body(): row_raw = lax.ppermute(strip, axes, pairs)  22.2 us
  transfers between devices with their start and end apart: 33, of which 10 were waited for; matrix products, arithmetic and copies ran while one was open for 3% of the time, Pallas kernels for 29%

profile of v7, /device:TPU:21, one launch (start us, length us, event | category | flops | bytes accessed | tf_op | source)
XLA Modules:
  0.0 474.6 jit_solution(13562137525082458767)
XLA Ops:
  6.5 3.6 cut_strip.1
  10.1 1.4 collective-permute-start
  11.6 0.7 collective-permute-start.1
  13.0 0.7 pad_add_fusion.1.refs_0_
  13.7 3.3 pack_early.1
  17.0 6.7 %all-to-all-start = ((f32[16,128,128]{2,1,0:T(8,128)}), f32[16,128,128]{2,1,0:T(8,128)S(1)}, u32[]{:S(2)}, u32[]{:S(2)}) async-start(f32[16,128,128]{2,1,0:T(8,128)} %pack_early.1), calls=%async_computation | async-start | bytes 2097152 | tf_op jit(solution)/shard_map/all_to_all | solution.py:562
  23.7 0.7 collective-permute-start.2
  24.4 1.5 collective-permute-start.3
  25.9 1.5 collective-permute-start.4
  27.4 1.4 collective-permute-start.5
  28.9 1.5 collective-permute-start.6
  31.1 7.7 %all-to-all-done.refs_1_ = f32[16,128,128]{2,1,0:T(8,128)S(1)} async-done(((f32[16,128,128]{2,1,0:T(8,128)}), f32[16,128,128]{2,1,0:T(8,128)S(1)}, u32[]{:S(2)}, u32[]{:S(2)}) %all-to-all-start) | async-done | bytes 1048608 | tf_op jit(solution)/shard_map/all_to_all | solution.py:562
  38.9 1.0 copy-done.1
  39.8 3.1 pick_early.1
  43.0 6.7 %all-to-all-start.1 = ((f32[16,128,128]{2,1,0:T(8,128)}), f32[16,128,128]{2,1,0:T(8,128)S(1)}, u32[]{:S(2)}, u32[]{:S(2)}) async-start(f32[16,128,128]{2,1,0:T(8,128)} %pick_early.1), calls=%async_computation.1 | async-start | bytes 2097152 | tf_op jit(solution)/shard_map/all_to_all | solution.py:564
  49.8 2.7 add_add_fusion
  52.5 8.2 %collective-permute-start.7 = (f32[128,1024]{1,0:T(8,128)}, f32[128,1024]{1,0:T(8,128)S(1)}, u32[]{:S(2)}, u32[]{:S(2)}) collective-permute-start(f32[128,1024]{1,0:T(8,128)} %add_add_fusion), channel_id=1, source_target_pairs={{0,0},{1,8},{2,16},{3,24},{4,32},{5,40},{6,48},{7,56},{8,64},{9,72... | collective-permute-start | bytes 1572872 | tf_op jit(solution)/shard_map/ppermute | solution.py:559
  60.7 0.7 reshape.289.keep
  62.3 22.7 %collective-permute-done.7.parent = f32[128,1024]{1,0:T(8,128)S(1)} collective-permute-done((f32[128,1024]{1,0:T(8,128)}, f32[128,1024]{1,0:T(8,128)S(1)}, u32[]{:S(2)}, u32[]{:S(2)}) %collective-permute-start.7) | collective-permute-done | bytes 524320 | tf_op jit(solution)/shard_map/ppermute | solution.py:559
  85.0 0.8 copy-done.10
  85.8 1.0 copy-done.2
  86.7 3.1 assemble_strip.1.refs_2_.refs_1_
  90.5 5.6 %pack_first.1 = f32[8,1280,128]{2,1,0:T(8,128)} custom-call(s32[8]{0:T(128)} %slice.20.refs_0_, f32[1280,1280]{1,0:T(8,128)} %refs_1_.5, f32[128,1024]{1,0:T(8,128)} %assemble_strip.1.refs_2_.refs_1_), custom_call_target="tpu_custom_call" | custom-call | bytes 10485760 | tf_op jit(solution)/shard_map/pack_first/pallas_call | solution.py:36
  96.0 6.7 %all-to-all-start.2 = ((f32[8,1280,128]{2,1,0:T(8,128)}), f32[8,1280,128]{2,1,0:T(8,128)}, u32[]{:S(2)}, u32[]{:S(2)}) async-start(f32[8,1280,128]{2,1,0:T(8,128)} %pack_first.1), calls=%async_computation.2 | async-start | bytes 10485760 | tf_op jit(solution)/shard_map/all_to_all | solution.py:568
  102.8 0.7 collective-permute-start.10
  103.4 0.7 collective-permute-start.9
  104.2 0.7 collective-permute-start.17
  104.9 0.7 collective-permute-start.16
  105.6 0.7 collective-permute-start.15
  106.2 0.7 collective-permute-start.14
  106.9 0.7 collective-permute-start.13
  107.6 0.7 collective-permute-start.12
  108.3 1.3 collective-permute-start.11
  109.6 13.2 %collective-permute-start.8 = (f32[128,1024]{1,0:T(8,128)S(1)}, f32[128,1024]{1,0:T(8,128)S(1)}, u32[]{:S(2)}, u32[]{:S(2)}) collective-permute-start(f32[128,1024]{1,0:T(8,128)S(1)} %copy-done), channel_id=1, source_target_pairs={{0,0},{8,1},{16,2},{24,3},{32,4},{40,5},{48,6},{56,7},{64,8},{72,9... | collective-permute-start | bytes 1572872 | tf_op jit(solution)/shard_map/ppermute | solution.py:572
  122.9 45.0 %collective-permute-done.11 = f32[64,1024]{1,0:T(8,128)S(1)} collective-permute-done((f32[64,1024]{1,0:T(8,128)S(1)}, f32[64,1024]{1,0:T(8,128)S(1)}, u32[]{:S(2)}, u32[]{:S(2)}) %collective-permute-start.11) | collective-permute-done | bytes 262176 | tf_op jit(solution)/shard_map/ppermute | solution.py:584
  167.9 0.9 add_add_fusion.1.given
  168.8 22.2 %collective-permute-done.8.refs_1_.given = f32[128,1024]{1,0:T(8,128)S(1)} collective-permute-done((f32[128,1024]{1,0:T(8,128)S(1)}, f32[128,1024]{1,0:T(8,128)S(1)}, u32[]{:S(2)}, u32[]{:S(2)}) %collective-permute-start.8) | collective-permute-done | bytes 524320 | tf_op jit(solution)/shard_map/ppermute | solution.py:572
  191.0 0.8 copy-done.3
  191.8 1.7 hand_on.2
  195.2 0.7 select_reduce_fusion.rank
  196.4 0.7 fusion.32
  197.3 61.0 %all-gather.6.cloned.1.call-done.refs_4_.refs_0_ = f32[1024,1024]{1,0:T(8,128)} async-done(((f32[64,1024]{1,0:T(8,128)}), f32[1024,1024]{1,0:T(8,128)}) %all-gather.6.cloned.1.call-update) | async-done | bytes 4194320 | tf_op jit(solution)/shard_map/all_gather | solution.py:587
  258.3 5.1 %pack_rows.2.refs_0_.refs_1_.refs_2_ = f32[16,5,128,128]{3,2,1,0:T(8,128)} custom-call(s32[16]{0:T(128)} %copy-done.13, s32[16]{0:T(128)} %convert_element_type.32.refs_1_, s32[5]{0:T(128)} %get-tuple-element.56.refs_2_, f32[8,10,128,128]{3,2,1,0:T(8,128)} %bitcast.8.refs_3_, f32[1024,1024]{1,0:T(8,128)} %all-gather.6.cloned.1.call-done.refs_4_.refs_0_), custom_call_target="tpu_custom_call" | custom-call | bytes 10485760 | tf_op jit(solution)/shard_map/pack_rows/pallas_call | solution.py:36
  263.4 6.7 %all-to-all-start.3 = ((f32[16,5,128,128]{3,2,1,0:T(8,128)}), f32[16,5,128,128]{3,2,1,0:T(8,128)}, u32[]{:S(2)}, u32[]{:S(2)}) async-start(f32[16,5,128,128]{3,2,1,0:T(8,128)} %pack_rows.2.refs_0_.refs_1_.refs_2_), calls=%async_computation.3 | async-start | bytes 10485760 | tf_op jit(solution)/shard_map/all_to_all | solution.py:593
  270.1 0.7 pad_add_fusion.flags
  270.8 0.7 reshape.288.keep
  272.0 1.9 hand_on.3
  273.9 5.6 %pack_second.1 = (f32[1280,128]{1,0:T(8,128)}, f32[1280,128]{1,0:T(8,128)}, f32[1280,128]{1,0:T(8,128)}, f32[1280,128]{1,0:T(8,128)}, f32[1280,128]{1,0:T(8,128)...) custom-call(s32[8]{0:T(128)} %and_select_fusion.1.refs_0_, f32[1280,1280]{1,0:T(8,128)} %refs_1_.5, ...), custom_call_target="tpu_custom_call" | custom-call | bytes 10485760 | tf_op jit(solution)/shard_map/pack_second/pallas_call | solution.py:36
  279.5 2.4 collective-permute-start.18
  281.9 1.3 collective-permute-start.19
  283.2 1.7 collective-permute-start.20
  285.2 1.9 collective-permute-start.22
  287.2 23.1 %factor_lead.4.refs_0_ = f32[1024,1024]{1,0:T(8,128)} custom-call(f32[1024,1024]{1,0:T(8,128)} %all-gather.6.cloned.1.call-done.refs_4_.refs_0_, f32[128,1024]{1,0:T(8,128)} %assemble_strip.1.refs_2_.refs_1_), custom_call_target="tpu_custom_call" | custom-call | flops 24999999488 | bytes 8388608 | tf_op jit(solution)/shard_map/factor_lead/pallas_call | solution.py:347
  310.3 1.5 collective-permute-start.23
  311.8 15.2 %collective-permute-done.19 = f32[1280,128]{1,0:T(8,128)S(1)} collective-permute-done((f32[1280,128]{1,0:T(8,128)}, f32[1280,128]{1,0:T(8,128)S(1)}, u32[]{:S(2)}, u32[]{:S(2)}) %collective-permute-start.19) | collective-permute-done | bytes 655392 | tf_op jit(solution)/shard_map/ppermute | solution.py:597
  327.1 21.0 %factor_lead.5.refs_13_.refs_0_ = f32[1024,1024]{1,0:T(8,128)} custom-call(f32[1024,1024]{1,0:T(8,128)} %factor_lead.4.refs_0_, f32[16,5,128,128]{3,2,1,0:T(8,128)} %pack_rows.2.refs_0_.refs_1_.refs_2_), custom_call_target="tpu_custom_call" | custom-call | flops 24999999488 | bytes 8388608 | tf_op jit(solution)/shard_map/factor_lead/pallas_call | solution.py:347
  348.1 10.1 %collective-permute-done.21 = f32[1280,128]{1,0:T(8,128)S(1)} collective-permute-done((f32[1280,128]{1,0:T(8,128)}, f32[1280,128]{1,0:T(8,128)S(1)}, u32[]{:S(2)}, u32[]{:S(2)}) %collective-permute-start.21) | collective-permute-done | bytes 655392 | tf_op jit(solution)/shard_map/ppermute | solution.py:597
  359.6 5.4 %pack_rows.3.refs_1_ = f32[16,5,128,128]{3,2,1,0:T(8,128)} custom-call(s32[16]{0:T(128)} %copy-done.13, s32[16]{0:T(128)} %convert_element_type.32.refs_1_, s32[5]{0:T(128)} %get-tuple-element.55.refs_2_, f32[8,10,128,128]{3,2,1,0:T(8,128)} %bitcast.8.refs_3_, f32[10,128,128]{2,1,0:T(8,128)} %bitcast.41, f32[10,128,128]{2,1,0:T(8,128)} %bitcast.42, ...), custom_call_target="tpu_custom_call" | custom-call | bytes 10485760 | tf_op jit(solution)/shard_map/pack_rows/pallas_call | solution.py:36
  365.0 6.7 %all-to-all-start.4 = ((f32[16,5,128,128]{3,2,1,0:T(8,128)}), f32[16,5,128,128]{3,2,1,0:T(8,128)}, u32[]{:S(2)}, u32[]{:S(2)}) async-start(f32[16,5,128,128]{3,2,1,0:T(8,128)} %pack_rows.3.refs_1_), calls=%async_computation.4 | async-start | bytes 10485760 | tf_op jit(solution)/shard_map/all_to_all | solution.py:602
  371.7 18.2 %factor_lead.6.refs_0_ = f32[1024,1024]{1,0:T(8,128)} custom-call(f32[1024,1024]{1,0:T(8,128)} %factor_lead.5.refs_13_.refs_0_, f32[16,5,128,128]{3,2,1,0:T(8,128)} %pack_rows.3.refs_1_), custom_call_target="tpu_custom_call" | custom-call | flops 24999999488 | bytes 8388608 | tf_op jit(solution)/shard_map/factor_lead/pallas_call | solution.py:347
  389.9 16.6 %factor_lead.7 = (bf16[1024,1024]{1,0:T(8,128)(2,1)}, bf16[1024,1024]{1,0:T(8,128)(2,1)}) custom-call(f32[1024,1024]{1,0:T(8,128)} %factor_lead.6.refs_0_, f32[16,5,128,128]{3,2,1,0:T(8,128)} %pack_rows.3.refs_1_), custom_call_target="tpu_custom_call" | custom-call | flops 24999999488 | bytes 8388608 | tf_op jit(solution)/shard_map/factor_lead/pallas_call | solution.py:347
  406.5 33.4 %update_front.1.front = f32[1024,2048]{1,0:T(8,128)} custom-call(s32[2]{0:T(128)} %pad_add_fusion.flags, f32[1024,1024]{1,0:T(8,128)} %all-gather.8.cloned.1.call-done.row_strip, f32[2048,1024]{1,0:T(8,128)} %all-gather.4.cloned.1.call-done.refs_2_.col_strip, bf16[1024,1024]{1,0:T(8,128)(2,1)} %get-tuple-element.39.inv_hi, ...), custom_call_target="tpu_custom_call" | custom-call | flops 40000000000 | bytes 33554432 | tf_op jit(solution)/shard_map/update_front/pallas_call | solution.py:417
  439.9 15.8 %all-to-all-done.4.refs_1_.refs_3_ = f32[16,5,128,128]{3,2,1,0:T(8,128)} async-done(((f32[16,5,128,128]{3,2,1,0:T(8,128)}), f32[16,5,128,128]{3,2,1,0:T(8,128)}, u32[]{:S(2)}, u32[]{:S(2)}) %all-to-all-start.4) | async-done | bytes 5242912 | tf_op jit(solution)/shard_map/all_to_all | solution.py:602
  455.7 12.4 %place_children.1 = f32[1024,2048]{1,0:T(8,128)} custom-call(s32[2,8]{1,0:T(2,128)} %fusion.18.source, s32[2,16]{1,0:T(2,128)} %select_reduce_fusion.rank, s32[2,128]{1,0:T(2,128)} %reshape.288.keep, f32[1024,2048]{1,0:T(8,128)} %update_front.1.front, f32[16,5,128,128]{3,2,1,0:T(8,128)} %all-to-all-done.3.refs_12_.refs_0_.refs_2_, ...), custom_call_target="tpu_custom_call", output_to_operand_aliasing={{}: (3, {})} | custom-call | bytes 25165824 | tf_op jit(solution)/shard_map/place_children/pallas_call | solution.py:465
  (96 shorter events, 8.1 us)
Async XLA Ops:
  6.5 5.8 %copy-start.12 = (s32[2,80]{1,0:T(2,128)S(1)}, s32[2,80]{1,0:T(2,128)}, u32[]{:S(2)}) copy-start(s32[2,80]{1,0:T(2,128)} %param.6) | copy-start | bytes 1924
  10.1 20.8 %copy-start.11 = (s32[2,80,80]{2,1,0:T(8,128)S(1)}, s32[2,80,80]{2,1,0:T(8,128)}, u32[]{:S(2)}) copy-start(s32[2,80,80]{2,1,0:T(8,128)} %param.7) | copy-start | bytes 153604
  10.1 17.3 %collective-permute-start = (f32[128,1024]{1,0:T(8,128)}, f32[128,1024]{1,0:T(8,128)S(1)}, u32[]{:S(2)}, u32[]{:S(2)}) collective-permute-start(f32[128,1024]{1,0:T(8,128)} %get-tuple-element.24), channel_id=1, source_target_pairs={{0,1},{8,9},{16,17},{24,25},{32,33},{40,41},{48,49},{56,57},{64,65... | collective-permute-start | bytes 1572872 | tf_op jit(solution)/shard_map/ppermute | solution.py:555
  11.6 17.3 %collective-permute-start.1 = (f32[128,1024]{1,0:T(8,128)}, f32[128,1024]{1,0:T(8,128)S(1)}, u32[]{:S(2)}, u32[]{:S(2)}) collective-permute-start(f32[128,1024]{1,0:T(8,128)} %get-tuple-element.25), channel_id=1, source_target_pairs={{0,2},{8,10},{16,18},{24,26},{32,34},{40,42},{48,50},{56,58},{64,6... | collective-permute-start | bytes 1572872 | tf_op jit(solution)/shard_map/ppermute | solution.py:555
  13.0 30.0 %copy-start.13 = (s32[16]{0:T(128)}, s32[16]{0:T(128)S(1)}, u32[]{:S(2)}) copy-start(s32[16]{0:T(128)S(1)} %get-tuple-element.42.refs_0_) | copy-start | bytes 196
  13.7 36.1 %copy-start.9 = (f32[128,1024]{1,0:T(8,128)S(1)}, f32[128,1024]{1,0:T(8,128)}, u32[]{:S(2)}) copy-start(f32[128,1024]{1,0:T(8,128)} %get-tuple-element.23) | copy-start | bytes 1572868
  17.0 21.9 %all-to-all-start = ((f32[16,128,128]{2,1,0:T(8,128)}), f32[16,128,128]{2,1,0:T(8,128)S(1)}, u32[]{:S(2)}, u32[]{:S(2)}) async-start(f32[16,128,128]{2,1,0:T(8,128)} %pack_early.1), calls=%async_computation | async-start | bytes 2097152 | tf_op jit(solution)/shard_map/all_to_all | solution.py:562
  23.7 26.0 %collective-permute-start.2 = (f32[128,1024]{1,0:T(8,128)}, f32[128,1024]{1,0:T(8,128)S(1)}, u32[]{:S(2)}, u32[]{:S(2)}) collective-permute-start(f32[128,1024]{1,0:T(8,128)} %get-tuple-element.26), channel_id=1, source_target_pairs={{0,3},{8,11},{16,19},{24,27},{32,35},{40,43},{48,51},{56,59},{64,6... | collective-permute-start | bytes 1572872 | tf_op jit(solution)/shard_map/ppermute | solution.py:555
  24.4 25.3 %collective-permute-start.3 = (f32[128,1024]{1,0:T(8,128)}, f32[128,1024]{1,0:T(8,128)}, u32[]{:S(2)}, u32[]{:S(2)}) collective-permute-start(f32[128,1024]{1,0:T(8,128)} %get-tuple-element.27), channel_id=1, source_target_pairs={{0,4},{8,12},{16,20},{24,28},{32,36},{40,44},{48,52},{56,60},{64,6... | collective-permute-start | bytes 1572872 | tf_op jit(solution)/shard_map/ppermute | solution.py:555
  25.9 23.8 %collective-permute-start.4 = (f32[128,1024]{1,0:T(8,128)}, f32[128,1024]{1,0:T(8,128)}, u32[]{:S(2)}, u32[]{:S(2)}) collective-permute-start(f32[128,1024]{1,0:T(8,128)} %get-tuple-element.28), channel_id=1, source_target_pairs={{0,5},{8,13},{16,21},{24,29},{32,37},{40,45},{48,53},{56,61},{64,6... | collective-permute-start | bytes 1572872 | tf_op jit(solution)/shard_map/ppermute | solution.py:555
  27.4 22.3 %collective-permute-start.5 = (f32[128,1024]{1,0:T(8,128)}, f32[128,1024]{1,0:T(8,128)}, u32[]{:S(2)}, u32[]{:S(2)}) collective-permute-start(f32[128,1024]{1,0:T(8,128)} %get-tuple-element.29), channel_id=1, source_target_pairs={{0,6},{8,14},{16,22},{24,30},{32,38},{40,46},{48,54},{56,62},{64,7... | collective-permute-start | bytes 1572872 | tf_op jit(solution)/shard_map/ppermute | solution.py:555
  28.9 20.9 %collective-permute-start.6 = (f32[128,1024]{1,0:T(8,128)}, f32[128,1024]{1,0:T(8,128)}, u32[]{:S(2)}, u32[]{:S(2)}) collective-permute-start(f32[128,1024]{1,0:T(8,128)} %get-tuple-element.30), channel_id=1, source_target_pairs={{0,7},{8,15},{16,23},{24,31},{32,39},{40,47},{48,55},{56,63},{64,7... | collective-permute-start | bytes 1572872 | tf_op jit(solution)/shard_map/ppermute | solution.py:555
  38.9 1.0 copy-start.1
  43.0 42.0 %all-to-all-start.1 = ((f32[16,128,128]{2,1,0:T(8,128)}), f32[16,128,128]{2,1,0:T(8,128)S(1)}, u32[]{:S(2)}, u32[]{:S(2)}) async-start(f32[16,128,128]{2,1,0:T(8,128)} %pick_early.1), calls=%async_computation.1 | async-start | bytes 2097152 | tf_op jit(solution)/shard_map/all_to_all | solution.py:564
  49.7 141.3 %all-gather.4.cloned.1.call-start = ((), (), s32[]{:S(2)}) async-start(), calls=%async_computation.5 | async-start | bytes 8912896 | tf_op jit(solution)/shard_map/all_gather | solution.py:570
  52.5 32.5 %collective-permute-start.7 = (f32[128,1024]{1,0:T(8,128)}, f32[128,1024]{1,0:T(8,128)S(1)}, u32[]{:S(2)}, u32[]{:S(2)}) collective-permute-start(f32[128,1024]{1,0:T(8,128)} %add_add_fusion), channel_id=1, source_target_pairs={{0,0},{1,8},{2,16},{3,24},{4,32},{5,40},{6,48},{7,56},{8,64},{9,72... | collective-permute-start | bytes 1572872 | tf_op jit(solution)/shard_map/ppermute | solution.py:559
  85.0 0.8 copy-start.10
  85.8 1.0 copy-start.2
  96.0 6.7 %copy-start = (f32[128,1024]{1,0:T(8,128)S(1)}, f32[128,1024]{1,0:T(8,128)}, u32[]{:S(2)}) copy-start(f32[128,1024]{1,0:T(8,128)} %assemble_strip.1.refs_2_.refs_1_) | copy-start | bytes 1572868
  96.0 95.0 %all-to-all-start.2 = ((f32[8,1280,128]{2,1,0:T(8,128)}), f32[8,1280,128]{2,1,0:T(8,128)}, u32[]{:S(2)}, u32[]{:S(2)}) async-start(f32[8,1280,128]{2,1,0:T(8,128)} %pack_first.1), calls=%async_computation.2 | async-start | bytes 10485760 | tf_op jit(solution)/shard_map/all_to_all | solution.py:568
  102.7 155.6 %all-gather.6.cloned.1.call-start = ((), (), s32[]{:S(2)}) async-start(), calls=%async_computation.6 | async-start | bytes 4456448 | tf_op jit(solution)/shard_map/all_gather | solution.py:587
  102.8 1.4 collective-permute-start.10
  103.4 0.7 collective-permute-start.9
  104.2 3.4 collective-permute-start.17
  104.9 3.4 collective-permute-start.16
  105.6 4.1 collective-permute-start.15
  106.2 16.6 %collective-permute-start.14 = (f32[64,1024]{1,0:T(8,128)S(1)}, f32[64,1024]{1,0:T(8,128)S(1)}, u32[]{:S(2)}, u32[]{:S(2)}) collective-permute-start(f32[64,1024]{1,0:T(8,128)S(1)} %add.273), channel_id=1, source_target_pairs={{0,4},{8,12},{16,20},{24,28},{32,36},{40,44},{48,52},{56,60},{64,6... | collective-permute-start | bytes 786440 | tf_op jit(solution)/shard_map/ppermute | solution.py:584
  106.9 15.9 %collective-permute-start.13 = (f32[64,1024]{1,0:T(8,128)S(1)}, f32[64,1024]{1,0:T(8,128)S(1)}, u32[]{:S(2)}, u32[]{:S(2)}) collective-permute-start(f32[64,1024]{1,0:T(8,128)S(1)} %add.273), channel_id=1, source_target_pairs={{0,3},{8,11},{16,19},{24,27},{32,35},{40,43},{48,51},{56,59},{64,6... | collective-permute-start | bytes 786440 | tf_op jit(solution)/shard_map/ppermute | solution.py:584
  107.6 15.2 %collective-permute-start.12 = (f32[64,1024]{1,0:T(8,128)S(1)}, f32[64,1024]{1,0:T(8,128)S(1)}, u32[]{:S(2)}, u32[]{:S(2)}) collective-permute-start(f32[64,1024]{1,0:T(8,128)S(1)} %add.273), channel_id=1, source_target_pairs={{0,2},{8,10},{16,18},{24,26},{32,34},{40,42},{48,50},{56,58},{64,6... | collective-permute-start | bytes 786440 | tf_op jit(solution)/shard_map/ppermute | solution.py:584
  108.3 59.6 %collective-permute-start.11 = (f32[64,1024]{1,0:T(8,128)S(1)}, f32[64,1024]{1,0:T(8,128)S(1)}, u32[]{:S(2)}, u32[]{:S(2)}) collective-permute-start(f32[64,1024]{1,0:T(8,128)S(1)} %add.273), channel_id=1, source_target_pairs={{0,1},{8,9},{16,17},{24,25},{32,33},{40,41},{48,49},{56,57},{64,65... | collective-permute-start | bytes 786440 | tf_op jit(solution)/shard_map/ppermute | solution.py:584
  109.6 81.4 %collective-permute-start.8 = (f32[128,1024]{1,0:T(8,128)S(1)}, f32[128,1024]{1,0:T(8,128)S(1)}, u32[]{:S(2)}, u32[]{:S(2)}) collective-permute-start(f32[128,1024]{1,0:T(8,128)S(1)} %copy-done), channel_id=1, source_target_pairs={{0,0},{8,1},{16,2},{24,3},{32,4},{40,5},{48,6},{56,7},{64,8},{72,9... | collective-permute-start | bytes 1572872 | tf_op jit(solution)/shard_map/ppermute | solution.py:572
  191.0 0.8 copy-start.3
  263.4 95.4 %all-to-all-start.3 = ((f32[16,5,128,128]{3,2,1,0:T(8,128)}), f32[16,5,128,128]{3,2,1,0:T(8,128)}, u32[]{:S(2)}, u32[]{:S(2)}) async-start(f32[16,5,128,128]{3,2,1,0:T(8,128)} %pack_rows.2.refs_0_.refs_1_.refs_2_), calls=%async_computation.3 | async-start | bytes 10485760 | tf_op jit(solution)/shard_map/all_to_all | solution.py:593
  270.1 136.4 %all-gather.8.cloned.1.call-start = ((), (), s32[]{:S(2)}) async-start(), calls=%async_computation.7 | async-start | bytes 4718592 | tf_op jit(solution)/shard_map/all_gather | solution.py:606
  279.5 30.8 %collective-permute-start.18 = (f32[1280,128]{1,0:T(8,128)}, f32[1280,128]{1,0:T(8,128)S(1)}, u32[]{:S(2)}, u32[]{:S(2)}) collective-permute-start(f32[1280,128]{1,0:T(8,128)} %get-tuple-element.32), channel_id=1, source_target_pairs={{0,1},{1,2},{2,3},{3,4},{4,5},{5,6},{6,7},{7,0},{8,9},{9,10},{10,1... | collective-permute-start | bytes 1966088 | tf_op jit(solution)/shard_map/ppermute | solution.py:597
  281.9 45.2 %collective-permute-start.19 = (f32[1280,128]{1,0:T(8,128)}, f32[1280,128]{1,0:T(8,128)S(1)}, u32[]{:S(2)}, u32[]{:S(2)}) collective-permute-start(f32[1280,128]{1,0:T(8,128)} %get-tuple-element.33), channel_id=1, source_target_pairs={{0,2},{1,3},{2,4},{3,5},{4,6},{5,7},{6,0},{7,1},{8,10},{9,11},{10,... | collective-permute-start | bytes 1966088 | tf_op jit(solution)/shard_map/ppermute | solution.py:597
  283.2 64.9 %collective-permute-start.20 = (f32[1280,128]{1,0:T(8,128)}, f32[1280,128]{1,0:T(8,128)S(1)}, u32[]{:S(2)}, u32[]{:S(2)}) collective-permute-start(f32[1280,128]{1,0:T(8,128)} %get-tuple-element.34), channel_id=1, source_target_pairs={{0,3},{1,4},{2,5},{3,6},{4,7},{5,0},{6,1},{7,2},{8,11},{9,12},{10,... | collective-permute-start | bytes 1966088 | tf_op jit(solution)/shard_map/ppermute | solution.py:597
  284.8 73.3 %collective-permute-start.21 = (f32[1280,128]{1,0:T(8,128)}, f32[1280,128]{1,0:T(8,128)S(1)}, u32[]{:S(2)}, u32[]{:S(2)}) collective-permute-start(f32[1280,128]{1,0:T(8,128)} %get-tuple-element.35), channel_id=1, source_target_pairs={{0,4},{1,5},{2,6},{3,7},{4,0},{5,1},{6,2},{7,3},{8,12},{9,13},{10,... | collective-permute-start | bytes 1966088 | tf_op jit(solution)/shard_map/ppermute | solution.py:597
  285.2 25.1 %copy-start.15 = (f32[1280,128]{1,0:T(8,128)S(1)}, f32[1280,128]{1,0:T(8,128)}, u32[]{:S(2)}) copy-start(f32[1280,128]{1,0:T(8,128)} %get-tuple-element.37) | copy-start | bytes 1966084
  285.2 41.8 %copy-start.14 = (f32[1280,128]{1,0:T(8,128)S(1)}, f32[1280,128]{1,0:T(8,128)}, u32[]{:S(2)}) copy-start(f32[1280,128]{1,0:T(8,128)} %get-tuple-element.38) | copy-start | bytes 1966084
  285.2 73.5 %collective-permute-start.22 = (f32[1280,128]{1,0:T(8,128)}, f32[1280,128]{1,0:T(8,128)S(1)}, u32[]{:S(2)}, u32[]{:S(2)}) collective-permute-start(f32[1280,128]{1,0:T(8,128)} %get-tuple-element.36), channel_id=1, source_target_pairs={{0,5},{1,6},{2,7},{3,0},{4,1},{5,2},{6,3},{7,4},{8,13},{9,14},{10,... | collective-permute-start | bytes 1966088 | tf_op jit(solution)/shard_map/ppermute | solution.py:597
  310.3 37.8 %copy-start.4 = (f32[1280,128]{1,0:T(8,128)}, f32[1280,128]{1,0:T(8,128)S(1)}, u32[]{:S(2)}) copy-start(f32[1280,128]{1,0:T(8,128)S(1)} %collective-permute-done.18) | copy-start | bytes 1966084
  310.3 48.5 %collective-permute-start.23 = (f32[1280,128]{1,0:T(8,128)S(1)}, f32[1280,128]{1,0:T(8,128)}, u32[]{:S(2)}, u32[]{:S(2)}) collective-permute-start(f32[1280,128]{1,0:T(8,128)S(1)} %copy-done.15), channel_id=1, source_target_pairs={{0,6},{1,7},{2,0},{3,1},{4,2},{5,3},{6,4},{7,5},{8,14},{9,15},{10,... | collective-permute-start | bytes 1966088 | tf_op jit(solution)/shard_map/ppermute | solution.py:597
  327.1 21.0 %copy-start.5 = (f32[1280,128]{1,0:T(8,128)}, f32[1280,128]{1,0:T(8,128)S(1)}, u32[]{:S(2)}) copy-start(f32[1280,128]{1,0:T(8,128)S(1)} %collective-permute-done.19) | copy-start | bytes 1966084
  327.1 31.8 %collective-permute-start.24 = (f32[1280,128]{1,0:T(8,128)S(1)}, f32[1280,128]{1,0:T(8,128)}, u32[]{:S(2)}, u32[]{:S(2)}) collective-permute-start(f32[1280,128]{1,0:T(8,128)S(1)} %copy-done.14), channel_id=1, source_target_pairs={{0,7},{1,0},{2,1},{3,2},{4,3},{5,4},{6,5},{7,6},{8,15},{9,8},{10,9... | collective-permute-start | bytes 1966088 | tf_op jit(solution)/shard_map/ppermute | solution.py:597
  348.1 10.7 %copy-start.6 = (f32[1280,128]{1,0:T(8,128)}, f32[1280,128]{1,0:T(8,128)S(1)}, u32[]{:S(2)}) copy-start(f32[1280,128]{1,0:T(8,128)S(1)} %collective-permute-done.20) | copy-start | bytes 1966084
  358.2 0.9 copy-start.7
  358.8 0.8 copy-start.8
  365.0 90.7 %all-to-all-start.4 = ((f32[16,5,128,128]{3,2,1,0:T(8,128)}), f32[16,5,128,128]{3,2,1,0:T(8,128)}, u32[]{:S(2)}, u32[]{:S(2)}) async-start(f32[16,5,128,128]{3,2,1,0:T(8,128)} %pack_rows.3.refs_1_), calls=%async_computation.4 | async-start | bytes 10485760 | tf_op jit(solution)/shard_map/all_to_all | solution.py:602
Sparse Core Ops, SparseCore 0:
  90.0 83.3 all-gather.3
  193.6 64.6 all-gather.5
  274.1 88.0 all-gather.7

commit v8 on v6

--- a/solution.py
+++ b/solution.py
@@ -567,6 +567,8 @@
     first = pack_first(send_cols[0::2], children, [])
     first = lax.all_to_all(first, "col", split_axis=0, concat_axis=0, tiled=True)
 
+    row_raw = lax.ppermute(strip, axes, pairs)
+
     half = BLOCK // 2
     piece = total([
         lax.ppermute(
@@ -576,6 +578,7 @@
         )
         for part in range(2)
     ])
+    piece = hand_on(piece, [row_raw])
     piece = total([piece] + [
         lax.ppermute(piece, axes, [(number(r, 0), number(r, d)) for r in range(ROWS)])
         for d in range(1, COLS)
@@ -584,11 +587,9 @@
 
     col_strip = lax.all_gather(strip, "row", axis=0, tiled=True)
 
-    row_raw = lax.ppermute(strip, axes, pairs)
-
     sends = sends.astype(jnp.int32)
     work = factor_part(0, lead, strip)
-    near_out = pack_rows(send_rows, sends, pick_cols[:HALF], first, [], [row_raw])
+    near_out = pack_rows(send_rows, sends, pick_cols[:HALF], first, [], [])
     near = lax.all_to_all(near_out, "row", split_axis=0, concat_axis=0, tiled=True)
     shifts = (col_index + jnp.arange(COLS, dtype=jnp.int32)) % COLS
     parts = pack_second(jnp.take(send_cols, shifts * 2 + 1), children, [near_out])
@@ -596,9 +597,9 @@
         lax.ppermute(parts[d], "col", [(c, (c + d) % COLS) for c in range(COLS)])
         for d in range(1, COLS)
     ]
+    work = factor_part(1, work, near_out)
     far_out = pack_rows(send_rows, sends, pick_cols[HALF:], first, second, [near, work])
     far = lax.all_to_all(far_out, "row", split_axis=0, concat_axis=0, tiled=True)
-    work = factor_part(1, work, far_out)
     work = factor_part(2, work, far_out)
     inv_hi, inv_lo = factor_part(3, work, col_strip)
     row_piece = hand_on(row_raw, [near_out])

time: 455 us -> 437 us (0.960)
  waiting for transfers between devices: 171 us -> 146 us
    all_to_all x1, waiting for transfers between devices: 25.4 us -> 9.02 us  [body(): lax.all_to_all(near_out, 'row', split_axis=0, concat_axis=0, tiled=True)]
    ppermute x7, waiting for transfers between devices: 12.5 us -> 1.54 us  [body(): lax.ppermute(piece, axes, [(number(r, 0), number(r, d)) for r in range(RO...]
    ppermute x1, waiting for transfers between devices: 13.2 us -> 20.5 us  [body(): row_raw = lax.ppermute(strip, axes, pairs)]
    all_to_all x1, starting transfers between devices: 7.5 us -> 14.6 us  [body(): lax.all_to_all(near_out, 'row', split_axis=0, concat_axis=0, tiled=True)]
    ppermute x1, starting transfers between devices: 9.03 us -> 1.91 us  [body(): row_raw = lax.ppermute(strip, axes, pairs)]
  transfers between devices with their start and end apart: 33 -> 33, of which waited for: 12 -> 7; matrix products, arithmetic and copies ran while one was open for 3% -> 3% of each run, Pallas kernels for 32% -> 33%
where the time goes in v8:
time: 437 us; the launch traced here: 432 us
  Pallas kernels  163 us (37%)
  waiting for transfers between devices  146 us (33%)
  starting transfers between devices  88.6 us (20%)
  between operations  13.7 us (3%)
  other arithmetic  11.1 us (3%)
  local copies, waits for them, and re-layouts  8.46 us (2%)
    pallas_call x4, Pallas kernels, factor_part(): pl.pallas_call(functools.partial(factor_kernel, part * count, count, last...  79 us
    all_to_all x1, waiting for transfers between devices, body(): lax.all_to_all(first, 'col', split_axis=0, concat_axis=0, tiled=True)  56.4 us
    pallas_call x1, Pallas kernels, update_front(): pl.pallas_call(update_kernel, grid_spec=pltpu.PrefetchScalarGridSpec(num_...  33.4 us
    pallas_call x7, Pallas kernels, gather_call(): pl.pallas_call(run, in_specs=[pl.BlockSpec(memory_space=pltpu.SMEM)] * le...  32.1 us
    ppermute x7, waiting for transfers between devices, body(): lax.ppermute(parts[d], 'col', [(c, (c + d) % COLS) for c in range(COLS)])  27.5 us
    ppermute x1, waiting for transfers between devices, body(): strip_parent = lax.ppermute(own, axes, [(b, a) for a, b in pairs])  22.7 us
    ppermute x1, waiting for transfers between devices, body(): row_raw = lax.ppermute(strip, axes, pairs)  20.5 us
    all_to_all x1, starting transfers between devices, body(): lax.all_to_all(first, 'col', split_axis=0, concat_axis=0, tiled=True)  19.2 us
  transfers between devices with their start and end apart: 33, of which 7 were waited for; matrix products, arithmetic and copies ran while one was open for 3% of the time, Pallas kernels for 33%

profile of v8, /device:TPU:21, one launch (start us, length us, event | category | flops | bytes accessed | tf_op | source)
XLA Modules:
  0.0 431.7 jit_solution(16253017084909395109)
XLA Ops:
  6.5 3.6 cut_strip.1
  10.1 1.4 collective-permute-start
  11.6 0.7 collective-permute-start.1
  13.6 3.3 pack_early.1
  16.9 6.7 %all-to-all-start = ((f32[16,128,128]{2,1,0:T(8,128)}), f32[16,128,128]{2,1,0:T(8,128)S(1)}, u32[]{:S(2)}, u32[]{:S(2)}) async-start(f32[16,128,128]{2,1,0:T(8,128)} %pack_early.1), calls=%async_computation | async-start | bytes 2097152 | tf_op jit(solution)/shard_map/all_to_all | solution.py:562
  23.6 0.7 collective-permute-start.2
  24.3 1.5 collective-permute-start.3
  25.8 1.5 collective-permute-start.4
  27.3 1.5 collective-permute-start.5
  28.8 1.5 collective-permute-start.6
  31.1 7.7 %all-to-all-done.refs_1_ = f32[16,128,128]{2,1,0:T(8,128)S(1)} async-done(((f32[16,128,128]{2,1,0:T(8,128)}), f32[16,128,128]{2,1,0:T(8,128)S(1)}, u32[]{:S(2)}, u32[]{:S(2)}) %all-to-all-start) | async-done | bytes 1048608 | tf_op jit(solution)/shard_map/all_to_all | solution.py:562
  38.8 1.0 copy-done
  39.7 3.1 pick_early.1
  42.9 6.7 %all-to-all-start.1 = ((f32[16,128,128]{2,1,0:T(8,128)}), f32[16,128,128]{2,1,0:T(8,128)S(1)}, u32[]{:S(2)}, u32[]{:S(2)}) async-start(f32[16,128,128]{2,1,0:T(8,128)} %pick_early.1), calls=%async_computation.1 | async-start | bytes 2097152 | tf_op jit(solution)/shard_map/all_to_all | solution.py:564
  49.7 2.7 add_add_fusion
  52.4 8.3 %collective-permute-start.7 = (f32[128,1024]{1,0:T(8,128)}, f32[128,1024]{1,0:T(8,128)S(1)}, u32[]{:S(2)}, u32[]{:S(2)}) collective-permute-start(f32[128,1024]{1,0:T(8,128)} %add_add_fusion), channel_id=1, source_target_pairs={{0,0},{1,8},{2,16},{3,24},{4,32},{5,40},{6,48},{7,56},{8,64},{9,72... | collective-permute-start | bytes 1572872 | tf_op jit(solution)/shard_map/ppermute | solution.py:559
  61.5 0.7 select_n.247.place
  62.2 22.7 %collective-permute-done.7.parent = f32[128,1024]{1,0:T(8,128)S(1)} collective-permute-done((f32[128,1024]{1,0:T(8,128)}, f32[128,1024]{1,0:T(8,128)S(1)}, u32[]{:S(2)}, u32[]{:S(2)}) %collective-permute-start.7) | collective-permute-done | bytes 524320 | tf_op jit(solution)/shard_map/ppermute | solution.py:559
  84.9 0.8 copy-done.9
  85.7 1.0 copy-done.1
  86.7 3.0 assemble_strip.1.refs_1_
  89.7 1.9 collective-permute-start.8
  91.6 1.1 fusion.31
  92.7 0.7 collective-permute-start.10
  93.4 0.7 collective-permute-start.9
  94.1 0.7 add.273.given
  94.8 20.5 %collective-permute-done.8.given.refs_0_ = f32[128,1024]{1,0:T(8,128)S(1)} collective-permute-done((f32[128,1024]{1,0:T(8,128)}, f32[128,1024]{1,0:T(8,128)S(1)}, u32[]{:S(2)}, u32[]{:S(2)}) %collective-permute-start.8) | collective-permute-done | bytes 524320 | tf_op jit(solution)/shard_map/ppermute | solution.py:570
  115.3 0.8 copy-done.2
  116.1 1.7 hand_on.3
  117.8 1.3 collective-permute-start.11
  119.0 0.7 collective-permute-start.12
  119.7 0.7 collective-permute-start.13
  120.4 0.7 collective-permute-start.14
  121.1 0.7 collective-permute-start.15
  121.8 1.5 collective-permute-done.11
  123.3 0.7 collective-permute-start.16
  124.0 0.7 collective-permute-start.17
  124.7 1.8 add_add_fusion.1
  126.6 0.7 all-gather.6.cloned.1.call-update
  127.3 0.7 slice.20.refs_0_
  128.0 5.6 %pack_first.1 = f32[8,1280,128]{2,1,0:T(8,128)} custom-call(s32[8]{0:T(128)} %slice.20.refs_0_, f32[1280,1280]{1,0:T(8,128)} %refs_1_.5), custom_call_target="tpu_custom_call" | custom-call | bytes 10485760 | tf_op jit(solution)/shard_map/pack_first/pallas_call | solution.py:36
  133.6 19.2 %all-to-all-start.2 = ((f32[8,1280,128]{2,1,0:T(8,128)}), f32[8,1280,128]{2,1,0:T(8,128)}, u32[]{:S(2)}, u32[]{:S(2)}) async-start(f32[8,1280,128]{2,1,0:T(8,128)} %pack_first.1), calls=%async_computation.2 | async-start | bytes 10485760 | tf_op jit(solution)/shard_map/all_to_all | solution.py:568
  154.4 0.7 select_reduce_fusion.rank
  156.5 56.4 %all-to-all-done.2 = f32[8,1280,128]{2,1,0:T(8,128)} async-done(((f32[8,1280,128]{2,1,0:T(8,128)}), f32[8,1280,128]{2,1,0:T(8,128)}, u32[]{:S(2)}, u32[]{:S(2)}) %all-to-all-start.2) | async-done | bytes 5242912 | tf_op jit(solution)/shard_map/all_to_all | solution.py:568
  212.9 5.5 %pack_rows.2.refs_0_.refs_1_.refs_2_ = f32[16,5,128,128]{3,2,1,0:T(8,128)} custom-call(s32[16]{0:T(128)} %copy-done.12, s32[16]{0:T(128)} %convert_element_type.32.refs_1_, s32[5]{0:T(128)} %get-tuple-element.56.refs_2_, f32[8,10,128,128]{3,2,1,0:T(8,128)} %bitcast.8.refs_3_), custom_call_target="tpu_custom_call" | custom-call | bytes 10485760 | tf_op jit(solution)/shard_map/pack_rows/pallas_call | solution.py:36
  218.4 14.6 %all-to-all-start.3 = ((f32[16,5,128,128]{3,2,1,0:T(8,128)}), f32[16,5,128,128]{3,2,1,0:T(8,128)}, u32[]{:S(2)}, u32[]{:S(2)}) async-start(f32[16,5,128,128]{3,2,1,0:T(8,128)} %pack_rows.2.refs_0_.refs_1_.refs_2_), calls=%async_computation.3 | async-start | bytes 10485760 | tf_op jit(solution)/shard_map/all_to_all | solution.py:593
  233.1 0.7 pad_add_fusion.flags
  233.7 0.7 reshape.288.keep
  235.1 5.6 %pack_second.1 = (f32[1280,128]{1,0:T(8,128)}, f32[1280,128]{1,0:T(8,128)}, f32[1280,128]{1,0:T(8,128)}, f32[1280,128]{1,0:T(8,128)}, f32[1280,128]{1,0:T(8,128)...) custom-call(s32[8]{0:T(128)} %and_select_fusion.1.refs_0_, f32[1280,1280]{1,0:T(8,128)} %refs_1_.5, ...), custom_call_target="tpu_custom_call" | custom-call | bytes 10485760 | tf_op jit(solution)/shard_map/pack_second/pallas_call | solution.py:36
  240.7 1.8 collective-permute-start.18
  242.5 2.0 collective-permute-start.20
  244.5 1.7 collective-permute-start.21
  246.2 2.6 collective-permute-start.22
  248.9 1.9 hand_on.2
  250.8 23.3 %factor_lead.4.refs_0_ = f32[1024,1024]{1,0:T(8,128)} custom-call(f32[1024,1024]{1,0:T(8,128)} %all-gather.8.cloned.1.call-done.refs_0_, f32[128,1024]{1,0:T(8,128)} %assemble_strip.1.refs_1_), custom_call_target="tpu_custom_call" | custom-call | flops 24999999488 | bytes 8388608 | tf_op jit(solution)/shard_map/factor_lead/pallas_call | solution.py:347
  274.3 27.4 %collective-permute-done.19 = f32[1280,128]{1,0:T(8,128)S(1)} collective-permute-done((f32[1280,128]{1,0:T(8,128)}, f32[1280,128]{1,0:T(8,128)S(1)}, u32[]{:S(2)}, u32[]{:S(2)}) %collective-permute-start.19) | collective-permute-done | bytes 655392 | tf_op jit(solution)/shard_map/ppermute | solution.py:597
  301.8 21.0 %factor_lead.5.refs_13_.refs_0_ = f32[1024,1024]{1,0:T(8,128)} custom-call(f32[1024,1024]{1,0:T(8,128)} %factor_lead.4.refs_0_, f32[16,5,128,128]{3,2,1,0:T(8,128)} %pack_rows.2.refs_0_.refs_1_.refs_2_), custom_call_target="tpu_custom_call" | custom-call | flops 24999999488 | bytes 8388608 | tf_op jit(solution)/shard_map/factor_lead/pallas_call | solution.py:347
  322.8 9.0 %all-to-all-done.3.refs_12_.refs_0_.refs_2_ = f32[16,5,128,128]{3,2,1,0:T(8,128)} async-done(((f32[16,5,128,128]{3,2,1,0:T(8,128)}), f32[16,5,128,128]{3,2,1,0:T(8,128)}, u32[]{:S(2)}, u32[]{:S(2)}) %all-to-all-start.3) | async-done | bytes 5242912 | tf_op jit(solution)/shard_map/all_to_all | solution.py:593
  331.9 5.4 %pack_rows.3.refs_1_ = f32[16,5,128,128]{3,2,1,0:T(8,128)} custom-call(s32[16]{0:T(128)} %copy-done.12, s32[16]{0:T(128)} %convert_element_type.32.refs_1_, s32[5]{0:T(128)} %get-tuple-element.55.refs_2_, f32[8,10,128,128]{3,2,1,0:T(8,128)} %bitcast.8.refs_3_, f32[10,128,128]{2,1,0:T(8,128)} %bitcast.41, f32[10,128,128]{2,1,0:T(8,128)} %bitcast.42, ...), custom_call_target="tpu_custom_call" | custom-call | bytes 10485760 | tf_op jit(solution)/shard_map/pack_rows/pallas_call | solution.py:36
  337.3 7.3 %all-to-all-start.4 = ((f32[16,5,128,128]{3,2,1,0:T(8,128)}), f32[16,5,128,128]{3,2,1,0:T(8,128)}, u32[]{:S(2)}, u32[]{:S(2)}) async-start(f32[16,5,128,128]{3,2,1,0:T(8,128)} %pack_rows.3.refs_1_), calls=%async_computation.4 | async-start | bytes 10485760 | tf_op jit(solution)/shard_map/all_to_all | solution.py:602
  344.6 18.2 %factor_lead.6.refs_0_ = f32[1024,1024]{1,0:T(8,128)} custom-call(f32[1024,1024]{1,0:T(8,128)} %factor_lead.5.refs_13_.refs_0_, f32[16,5,128,128]{3,2,1,0:T(8,128)} %pack_rows.3.refs_1_), custom_call_target="tpu_custom_call" | custom-call | flops 24999999488 | bytes 8388608 | tf_op jit(solution)/shard_map/factor_lead/pallas_call | solution.py:347
  362.8 16.6 %factor_lead.7 = (bf16[1024,1024]{1,0:T(8,128)(2,1)}, bf16[1024,1024]{1,0:T(8,128)(2,1)}) custom-call(f32[1024,1024]{1,0:T(8,128)} %factor_lead.6.refs_0_, f32[2048,1024]{1,0:T(8,128)} %all-gather.6.cloned.1.call-done.refs_1_.col_strip), custom_call_target="tpu_custom_call" | custom-call | flops 24999999488 | bytes 8388608 | tf_op jit(solution)/shard_map/factor_lead/pallas_call | solution.py:347
  379.4 33.4 %update_front.1.front = f32[1024,2048]{1,0:T(8,128)} custom-call(s32[2]{0:T(128)} %pad_add_fusion.flags, f32[1024,1024]{1,0:T(8,128)} %all-gather.4.cloned.1.call-done.row_strip, f32[2048,1024]{1,0:T(8,128)} %all-gather.6.cloned.1.call-done.refs_1_.col_strip, bf16[1024,1024]{1,0:T(8,128)(2,1)} %get-tuple-element.39.inv_hi, ...), custom_call_target="tpu_custom_call" | custom-call | flops 40000000000 | bytes 33554432 | tf_op jit(solution)/shard_map/update_front/pallas_call | solution.py:417
  412.8 12.4 %place_children.1 = f32[1024,2048]{1,0:T(8,128)} custom-call(s32[2,8]{1,0:T(2,128)} %fusion.18.source, s32[2,16]{1,0:T(2,128)} %select_reduce_fusion.rank, s32[2,128]{1,0:T(2,128)} %reshape.288.keep, f32[1024,2048]{1,0:T(8,128)} %update_front.1.front, f32[16,5,128,128]{3,2,1,0:T(8,128)} %all-to-all-done.3.refs_12_.refs_0_.refs_2_, ...), custom_call_target="tpu_custom_call", output_to_operand_aliasing={{}: (3, {})} | custom-call | bytes 25165824 | tf_op jit(solution)/shard_map/place_children/pallas_call | solution.py:465
  (94 shorter events, 7.2 us)
Async XLA Ops:
  6.5 5.8 %copy-start.11 = (s32[2,80]{1,0:T(2,128)S(1)}, s32[2,80]{1,0:T(2,128)}, u32[]{:S(2)}) copy-start(s32[2,80]{1,0:T(2,128)} %param.6) | copy-start | bytes 1924
  10.1 20.7 %copy-start.10 = (s32[2,80,80]{2,1,0:T(8,128)S(1)}, s32[2,80,80]{2,1,0:T(8,128)}, u32[]{:S(2)}) copy-start(s32[2,80,80]{2,1,0:T(8,128)} %param.7) | copy-start | bytes 153604
  10.1 17.2 %collective-permute-start = (f32[128,1024]{1,0:T(8,128)}, f32[128,1024]{1,0:T(8,128)S(1)}, u32[]{:S(2)}, u32[]{:S(2)}) collective-permute-start(f32[128,1024]{1,0:T(8,128)} %get-tuple-element.24), channel_id=1, source_target_pairs={{0,1},{8,9},{16,17},{24,25},{32,33},{40,41},{48,49},{56,57},{64,65... | collective-permute-start | bytes 1572872 | tf_op jit(solution)/shard_map/ppermute | solution.py:555
  11.6 17.2 %collective-permute-start.1 = (f32[128,1024]{1,0:T(8,128)}, f32[128,1024]{1,0:T(8,128)S(1)}, u32[]{:S(2)}, u32[]{:S(2)}) collective-permute-start(f32[128,1024]{1,0:T(8,128)} %get-tuple-element.25), channel_id=1, source_target_pairs={{0,2},{8,10},{16,18},{24,26},{32,34},{40,42},{48,50},{56,58},{64,6... | collective-permute-start | bytes 1572872 | tf_op jit(solution)/shard_map/ppermute | solution.py:555
  13.0 29.9 %copy-start.12 = (s32[16]{0:T(128)}, s32[16]{0:T(128)S(1)}, u32[]{:S(2)}) copy-start(s32[16]{0:T(128)S(1)} %get-tuple-element.42.refs_0_) | copy-start | bytes 196
  13.6 36.0 %copy-start.8 = (f32[128,1024]{1,0:T(8,128)S(1)}, f32[128,1024]{1,0:T(8,128)}, u32[]{:S(2)}) copy-start(f32[128,1024]{1,0:T(8,128)} %get-tuple-element.23) | copy-start | bytes 1572868
  16.9 21.8 %all-to-all-start = ((f32[16,128,128]{2,1,0:T(8,128)}), f32[16,128,128]{2,1,0:T(8,128)S(1)}, u32[]{:S(2)}, u32[]{:S(2)}) async-start(f32[16,128,128]{2,1,0:T(8,128)} %pack_early.1), calls=%async_computation | async-start | bytes 2097152 | tf_op jit(solution)/shard_map/all_to_all | solution.py:562
  23.6 26.0 %collective-permute-start.2 = (f32[128,1024]{1,0:T(8,128)}, f32[128,1024]{1,0:T(8,128)S(1)}, u32[]{:S(2)}, u32[]{:S(2)}) collective-permute-start(f32[128,1024]{1,0:T(8,128)} %get-tuple-element.26), channel_id=1, source_target_pairs={{0,3},{8,11},{16,19},{24,27},{32,35},{40,43},{48,51},{56,59},{64,6... | collective-permute-start | bytes 1572872 | tf_op jit(solution)/shard_map/ppermute | solution.py:555
  24.3 25.3 %collective-permute-start.3 = (f32[128,1024]{1,0:T(8,128)}, f32[128,1024]{1,0:T(8,128)}, u32[]{:S(2)}, u32[]{:S(2)}) collective-permute-start(f32[128,1024]{1,0:T(8,128)} %get-tuple-element.27), channel_id=1, source_target_pairs={{0,4},{8,12},{16,20},{24,28},{32,36},{40,44},{48,52},{56,60},{64,6... | collective-permute-start | bytes 1572872 | tf_op jit(solution)/shard_map/ppermute | solution.py:555
  25.8 23.8 %collective-permute-start.4 = (f32[128,1024]{1,0:T(8,128)}, f32[128,1024]{1,0:T(8,128)}, u32[]{:S(2)}, u32[]{:S(2)}) collective-permute-start(f32[128,1024]{1,0:T(8,128)} %get-tuple-element.28), channel_id=1, source_target_pairs={{0,5},{8,13},{16,21},{24,29},{32,37},{40,45},{48,53},{56,61},{64,6... | collective-permute-start | bytes 1572872 | tf_op jit(solution)/shard_map/ppermute | solution.py:555
  27.3 22.3 %collective-permute-start.5 = (f32[128,1024]{1,0:T(8,128)}, f32[128,1024]{1,0:T(8,128)}, u32[]{:S(2)}, u32[]{:S(2)}) collective-permute-start(f32[128,1024]{1,0:T(8,128)} %get-tuple-element.29), channel_id=1, source_target_pairs={{0,6},{8,14},{16,22},{24,30},{32,38},{40,46},{48,54},{56,62},{64,7... | collective-permute-start | bytes 1572872 | tf_op jit(solution)/shard_map/ppermute | solution.py:555
  28.8 20.9 %collective-permute-start.6 = (f32[128,1024]{1,0:T(8,128)}, f32[128,1024]{1,0:T(8,128)}, u32[]{:S(2)}, u32[]{:S(2)}) collective-permute-start(f32[128,1024]{1,0:T(8,128)} %get-tuple-element.30), channel_id=1, source_target_pairs={{0,7},{8,15},{16,23},{24,31},{32,39},{40,47},{48,55},{56,63},{64,7... | collective-permute-start | bytes 1572872 | tf_op jit(solution)/shard_map/ppermute | solution.py:555
  38.8 1.0 copy-start
  42.9 42.0 %all-to-all-start.1 = ((f32[16,128,128]{2,1,0:T(8,128)}), f32[16,128,128]{2,1,0:T(8,128)S(1)}, u32[]{:S(2)}, u32[]{:S(2)}) async-start(f32[16,128,128]{2,1,0:T(8,128)} %pick_early.1), calls=%async_computation.1 | async-start | bytes 2097152 | tf_op jit(solution)/shard_map/all_to_all | solution.py:564
  49.6 201.2 %all-gather.8.cloned.1.call-start = ((), (), s32[]{:S(2)}) async-start(), calls=%async_computation.7 | async-start | bytes 4456448 | tf_op jit(solution)/shard_map/all_gather | solution.py:586
  52.4 32.5 %collective-permute-start.7 = (f32[128,1024]{1,0:T(8,128)}, f32[128,1024]{1,0:T(8,128)S(1)}, u32[]{:S(2)}, u32[]{:S(2)}) collective-permute-start(f32[128,1024]{1,0:T(8,128)} %add_add_fusion), channel_id=1, source_target_pairs={{0,0},{1,8},{2,16},{3,24},{4,32},{5,40},{6,48},{7,56},{8,64},{9,72... | collective-permute-start | bytes 1572872 | tf_op jit(solution)/shard_map/ppermute | solution.py:559
  84.9 0.8 copy-start.9
  85.7 1.0 copy-start.1
  89.7 25.6 %collective-permute-start.8 = (f32[128,1024]{1,0:T(8,128)}, f32[128,1024]{1,0:T(8,128)S(1)}, u32[]{:S(2)}, u32[]{:S(2)}) collective-permute-start(f32[128,1024]{1,0:T(8,128)} %assemble_strip.1.refs_1_), channel_id=1, source_target_pairs={{0,0},{8,1},{16,2},{24,3},{32,4},{40,5},{48,6},{56,7},{64,8},{72,9... | collective-permute-start | bytes 1572872 | tf_op jit(solution)/shard_map/ppermute | solution.py:570
  92.7 1.4 collective-permute-start.10
  93.4 0.7 collective-permute-start.9
  115.3 0.8 copy-start.2
  117.8 5.6 %collective-permute-start.11 = (f32[64,1024]{1,0:T(8,128)}, f32[64,1024]{1,0:T(8,128)S(1)}, u32[]{:S(2)}, u32[]{:S(2)}) collective-permute-start(f32[64,1024]{1,0:T(8,128)} %hand_on.3), channel_id=1, source_target_pairs={{0,1},{8,9},{16,17},{24,25},{32,33},{40,41},{48,49},{56,57},{64,65... | collective-permute-start | bytes 786440 | tf_op jit(solution)/shard_map/ppermute | solution.py:583
  119.0 4.9 %collective-permute-start.12 = (f32[64,1024]{1,0:T(8,128)}, f32[64,1024]{1,0:T(8,128)S(1)}, u32[]{:S(2)}, u32[]{:S(2)}) collective-permute-start(f32[64,1024]{1,0:T(8,128)} %hand_on.3), channel_id=1, source_target_pairs={{0,2},{8,10},{16,18},{24,26},{32,34},{40,42},{48,50},{56,58},{64,6... | collective-permute-start | bytes 786440 | tf_op jit(solution)/shard_map/ppermute | solution.py:583
  119.7 5.0 %collective-permute-start.13 = (f32[64,1024]{1,0:T(8,128)}, f32[64,1024]{1,0:T(8,128)S(1)}, u32[]{:S(2)}, u32[]{:S(2)}) collective-permute-start(f32[64,1024]{1,0:T(8,128)} %hand_on.3), channel_id=1, source_target_pairs={{0,3},{8,11},{16,19},{24,27},{32,35},{40,43},{48,51},{56,59},{64,6... | collective-permute-start | bytes 786440 | tf_op jit(solution)/shard_map/ppermute | solution.py:583
  120.4 4.3 collective-permute-start.14
  121.1 3.6 collective-permute-start.15
  123.3 1.4 collective-permute-start.16
  124.0 0.7 collective-permute-start.17
  126.6 236.2 %all-gather.6.cloned.1.call-start = ((), (), s32[]{:S(2)}) async-start(), calls=%async_computation.6 | async-start | bytes 8912896 | tf_op jit(solution)/shard_map/all_gather | solution.py:588
  133.6 79.3 %all-to-all-start.2 = ((f32[8,1280,128]{2,1,0:T(8,128)}), f32[8,1280,128]{2,1,0:T(8,128)}, u32[]{:S(2)}, u32[]{:S(2)}) async-start(f32[8,1280,128]{2,1,0:T(8,128)} %pack_first.1), calls=%async_computation.2 | async-start | bytes 10485760 | tf_op jit(solution)/shard_map/all_to_all | solution.py:568
  218.4 113.5 %all-to-all-start.3 = ((f32[16,5,128,128]{3,2,1,0:T(8,128)}), f32[16,5,128,128]{3,2,1,0:T(8,128)}, u32[]{:S(2)}, u32[]{:S(2)}) async-start(f32[16,5,128,128]{3,2,1,0:T(8,128)} %pack_rows.2.refs_0_.refs_1_.refs_2_), calls=%async_computation.3 | async-start | bytes 10485760 | tf_op jit(solution)/shard_map/all_to_all | solution.py:593
  233.0 146.3 %all-gather.4.cloned.1.call-start = ((), (), s32[]{:S(2)}) async-start(), calls=%async_computation.5 | async-start | bytes 4718592 | tf_op jit(solution)/shard_map/all_gather | solution.py:606
  240.7 33.4 %collective-permute-start.18 = (f32[1280,128]{1,0:T(8,128)}, f32[1280,128]{1,0:T(8,128)S(1)}, u32[]{:S(2)}, u32[]{:S(2)}) collective-permute-start(f32[1280,128]{1,0:T(8,128)} %get-tuple-element.32), channel_id=1, source_target_pairs={{0,1},{1,2},{2,3},{3,4},{4,5},{5,6},{6,7},{7,0},{8,9},{9,10},{10,1... | collective-permute-start | bytes 1966088 | tf_op jit(solution)/shard_map/ppermute | solution.py:597
  242.5 59.3 %collective-permute-start.19 = (f32[1280,128]{1,0:T(8,128)}, f32[1280,128]{1,0:T(8,128)S(1)}, u32[]{:S(2)}, u32[]{:S(2)}) collective-permute-start(f32[1280,128]{1,0:T(8,128)} %get-tuple-element.33), channel_id=1, source_target_pairs={{0,2},{1,3},{2,4},{3,5},{4,6},{5,7},{6,0},{7,1},{8,10},{9,11},{10,... | collective-permute-start | bytes 1966088 | tf_op jit(solution)/shard_map/ppermute | solution.py:597
  242.5 80.3 %collective-permute-start.20 = (f32[1280,128]{1,0:T(8,128)}, f32[1280,128]{1,0:T(8,128)S(1)}, u32[]{:S(2)}, u32[]{:S(2)}) collective-permute-start(f32[1280,128]{1,0:T(8,128)} %get-tuple-element.34), channel_id=1, source_target_pairs={{0,3},{1,4},{2,5},{3,6},{4,7},{5,0},{6,1},{7,2},{8,11},{9,12},{10,... | collective-permute-start | bytes 1966088 | tf_op jit(solution)/shard_map/ppermute | solution.py:597
  244.5 78.3 %collective-permute-start.21 = (f32[1280,128]{1,0:T(8,128)}, f32[1280,128]{1,0:T(8,128)S(1)}, u32[]{:S(2)}, u32[]{:S(2)}) collective-permute-start(f32[1280,128]{1,0:T(8,128)} %get-tuple-element.35), channel_id=1, source_target_pairs={{0,4},{1,5},{2,6},{3,7},{4,0},{5,1},{6,2},{7,3},{8,12},{9,13},{10,... | collective-permute-start | bytes 1966088 | tf_op jit(solution)/shard_map/ppermute | solution.py:597
  246.2 76.6 %collective-permute-start.22 = (f32[1280,128]{1,0:T(8,128)}, f32[1280,128]{1,0:T(8,128)S(1)}, u32[]{:S(2)}, u32[]{:S(2)}) collective-permute-start(f32[1280,128]{1,0:T(8,128)} %get-tuple-element.36), channel_id=1, source_target_pairs={{0,5},{1,6},{2,7},{3,0},{4,1},{5,2},{6,3},{7,4},{8,13},{9,14},{10,... | collective-permute-start | bytes 1966088 | tf_op jit(solution)/shard_map/ppermute | solution.py:597
  250.8 23.3 %copy-start.14 = (f32[1280,128]{1,0:T(8,128)S(1)}, f32[1280,128]{1,0:T(8,128)}, u32[]{:S(2)}) copy-start(f32[1280,128]{1,0:T(8,128)} %get-tuple-element.37) | copy-start | bytes 1966084
  250.8 51.0 %copy-start.13 = (f32[1280,128]{1,0:T(8,128)S(1)}, f32[1280,128]{1,0:T(8,128)}, u32[]{:S(2)}) copy-start(f32[1280,128]{1,0:T(8,128)} %get-tuple-element.38) | copy-start | bytes 1966084
  274.1 48.7 %copy-start.3 = (f32[1280,128]{1,0:T(8,128)}, f32[1280,128]{1,0:T(8,128)S(1)}, u32[]{:S(2)}) copy-start(f32[1280,128]{1,0:T(8,128)S(1)} %collective-permute-done.18) | copy-start | bytes 1966084
  274.1 48.7 %collective-permute-start.23 = (f32[1280,128]{1,0:T(8,128)S(1)}, f32[1280,128]{1,0:T(8,128)}, u32[]{:S(2)}, u32[]{:S(2)}) collective-permute-start(f32[1280,128]{1,0:T(8,128)S(1)} %copy-done.14), channel_id=1, source_target_pairs={{0,6},{1,7},{2,0},{3,1},{4,2},{5,3},{6,4},{7,5},{8,14},{9,15},{10,... | collective-permute-start | bytes 1966088 | tf_op jit(solution)/shard_map/ppermute | solution.py:597
  301.8 21.0 %copy-start.4 = (f32[1280,128]{1,0:T(8,128)}, f32[1280,128]{1,0:T(8,128)S(1)}, u32[]{:S(2)}) copy-start(f32[1280,128]{1,0:T(8,128)S(1)} %collective-permute-done.19) | copy-start | bytes 1966084
  301.8 21.0 %collective-permute-start.24 = (f32[1280,128]{1,0:T(8,128)S(1)}, f32[1280,128]{1,0:T(8,128)}, u32[]{:S(2)}, u32[]{:S(2)}) collective-permute-start(f32[1280,128]{1,0:T(8,128)S(1)} %copy-done.13), channel_id=1, source_target_pairs={{0,7},{1,0},{2,1},{3,2},{4,3},{5,4},{6,5},{7,6},{8,15},{9,8},{10,9... | collective-permute-start | bytes 1966088 | tf_op jit(solution)/shard_map/ppermute | solution.py:597
  322.8 9.1 %copy-start.5 = (f32[1280,128]{1,0:T(8,128)}, f32[1280,128]{1,0:T(8,128)S(1)}, u32[]{:S(2)}) copy-start(f32[1280,128]{1,0:T(8,128)S(1)} %collective-permute-done.20) | copy-start | bytes 1966084
  322.8 9.1 %copy-start.6 = (f32[1280,128]{1,0:T(8,128)}, f32[1280,128]{1,0:T(8,128)S(1)}, u32[]{:S(2)}) copy-start(f32[1280,128]{1,0:T(8,128)S(1)} %collective-permute-done.21) | copy-start | bytes 1966084
  322.8 9.1 %copy-start.7 = (f32[1280,128]{1,0:T(8,128)}, f32[1280,128]{1,0:T(8,128)S(1)}, u32[]{:S(2)}) copy-start(f32[1280,128]{1,0:T(8,128)S(1)} %collective-permute-done.22) | copy-start | bytes 1966084
  337.3 75.5 %all-to-all-start.4 = ((f32[16,5,128,128]{3,2,1,0:T(8,128)}), f32[16,5,128,128]{3,2,1,0:T(8,128)}, u32[]{:S(2)}, u32[]{:S(2)}) async-start(f32[16,5,128,128]{3,2,1,0:T(8,128)} %pack_rows.3.refs_1_), calls=%async_computation.4 | async-start | bytes 10485760 | tf_op jit(solution)/shard_map/all_to_all | solution.py:602
Sparse Core Ops, SparseCore 0:
  126.7 73.4 all-gather.7
  202.4 122.8 all-gather.5
  327.0 38.8 all-gather.3

commit v9 on v7

--- a/solution.py
+++ b/solution.py
@@ -564,9 +564,6 @@
     early = lax.all_to_all(early, "row", split_axis=0, concat_axis=0, tiled=True)
     strip = assemble_strip(strip_place, strip_keep, strip_parent, early, [])
 
-    first = pack_first(send_cols[0::2], children, [strip])
-    first = lax.all_to_all(first, "col", split_axis=0, concat_axis=0, tiled=True)
-
     col_strip = lax.all_gather(strip, "row", axis=0, tiled=True)
 
     row_raw = lax.ppermute(strip, axes, pairs)
@@ -580,16 +577,19 @@
         )
         for part in range(2)
     ])
+    piece = hand_on(piece, [row_raw])
     piece = total([piece] + [
         lax.ppermute(piece, axes, [(number(r, 0), number(r, d)) for r in range(ROWS)])
         for d in range(1, COLS)
     ])
-    lead = lax.all_gather(hand_on(piece, [first, row_raw, col_strip]), "row", axis=0, tiled=True)
+    lead = lax.all_gather(piece, "row", axis=0, tiled=True)
+
+    first = pack_first(send_cols[0::2], children, [piece])
+    first = lax.all_to_all(first, "col", split_axis=0, concat_axis=0, tiled=True)
 
 
     sends = sends.astype(jnp.int32)
-    work = factor_part(0, lead, strip)
-    near_out = pack_rows(send_rows, sends, pick_cols[:HALF], first, [], [lead])
+    near_out = pack_rows(send_rows, sends, pick_cols[:HALF], first, [], [col_strip])
     near = lax.all_to_all(near_out, "row", split_axis=0, concat_axis=0, tiled=True)
     shifts = (col_index + jnp.arange(COLS, dtype=jnp.int32)) % COLS
     parts = pack_second(jnp.take(send_cols, shifts * 2 + 1), children, [near_out])
@@ -597,6 +597,7 @@
         lax.ppermute(parts[d], "col", [(c, (c + d) % COLS) for c in range(COLS)])
         for d in range(1, COLS)
     ]
+    work = factor_part(0, lead, second[1])
     work = factor_part(1, work, near_out)
     far_out = pack_rows(send_rows, sends, pick_cols[HALF:], first, second, [near, work])
     far = lax.all_to_all(far_out, "row", split_axis=0, concat_axis=0, tiled=True)

time: 476 us -> 450 us (0.945); the launches traced: 475 us -> 441 us
  waiting for transfers between devices: 201 us -> 172 us
  starting transfers between devices: 79.5 us -> 70.5 us
    all_gather x1, waiting for transfers between devices: 61 us -> 0.01 us  [body(): lead = lax.all_gather(piece, 'row', axis=0, tiled=True)]
    all_to_all x1, waiting for transfers between devices: 0.01 us -> 56.6 us  [body(): lax.all_to_all(first, 'col', split_axis=0, concat_axis=0, tiled=True)]
    ppermute x7, waiting for transfers between devices: 45 us -> 29.6 us  [body(): lax.ppermute(piece, axes, [(number(r, 0), number(r, d)) for r in range(RO...]
    ppermute x1, starting transfers between devices: 13.2 us -> 6.56 us  [body(): row_raw = lax.ppermute(strip, axes, pairs)]
    ppermute x1, starting transfers between devices: 8.19 us -> 1.91 us  [body(): strip_parent = lax.ppermute(own, axes, [(b, a) for a, b in pairs])]
  transfers between devices with their start and end apart: 33 -> 33, of which waited for: 10 -> 11; matrix products, arithmetic and copies ran while one was open for 3% -> 3% of each run, Pallas kernels for 29% -> 33%
where the time goes in v9:
time: 450 us; the launch traced here: 441 us
  waiting for transfers between devices  172 us (38%)
  Pallas kernels  162 us (36%)
  starting transfers between devices  70.5 us (16%)
  between operations  13.6 us (3%)
  other arithmetic  13 us (3%)
  local copies, waits for them, and re-layouts  9.8 us (2%)
    pallas_call x4, Pallas kernels, factor_part(): pl.pallas_call(functools.partial(factor_kernel, part * count, count, last...  79.1 us
    all_to_all x1, waiting for transfers between devices, body(): lax.all_to_all(first, 'col', split_axis=0, concat_axis=0, tiled=True)  56.6 us
    pallas_call x1, Pallas kernels, update_front(): pl.pallas_call(update_kernel, grid_spec=pltpu.PrefetchScalarGridSpec(num_...  33.4 us
    pallas_call x7, Pallas kernels, gather_call(): pl.pallas_call(run, in_specs=[pl.BlockSpec(memory_space=pltpu.SMEM)] * le...  31.6 us
    ppermute x7, waiting for transfers between devices, body(): lax.ppermute(piece, axes, [(number(r, 0), number(r, d)) for r in range(RO...  29.6 us
    ppermute x7, waiting for transfers between devices, body(): lax.ppermute(parts[d], 'col', [(c, (c + d) % COLS) for c in range(COLS)])  25.1 us
    ppermute x1, waiting for transfers between devices, body(): strip_parent = lax.ppermute(own, axes, [(b, a) for a, b in pairs])  24 us
    ppermute x1, waiting for transfers between devices, body(): row_raw = lax.ppermute(strip, axes, pairs)  19.4 us
  transfers between devices with their start and end apart: 33, of which 11 were waited for; matrix products, arithmetic and copies ran while one was open for 3% of the time, Pallas kernels for 33%

profile of v9, /device:TPU:21, one launch (start us, length us, event | category | flops | bytes accessed | tf_op | source)
XLA Modules:
  0.0 441.3 jit_solution(14051209753069933181)
XLA Ops:
  6.6 0.7 compare_select_fusion.13
  7.3 0.7 compare_select_fusion.14
  8.4 0.7 bitcast_select_fusion
  9.3 0.7 pad_add_fusion.1.refs_0_
  9.9 2.9 pack_early.1
  12.9 6.0 %all-to-all-start = ((f32[16,128,128]{2,1,0:T(8,128)}), f32[16,128,128]{2,1,0:T(8,128)S(1)}, u32[]{:S(2)}, u32[]{:S(2)}) async-start(f32[16,128,128]{2,1,0:T(8,128)} %pack_early.1), calls=%async_computation | async-start | bytes 2097152 | tf_op jit(solution)/shard_map/all_to_all | solution.py:562
  18.9 3.6 cut_strip.1
  22.5 0.8 collective-permute-start.6
  23.3 0.7 collective-permute-start.5
  24.0 0.7 collective-permute-start.4
  24.7 0.7 collective-permute-start.3
  25.4 1.5 collective-permute-start.2
  26.9 1.5 collective-permute-start.1
  28.4 1.3 collective-permute-start
  29.8 0.7 select_reduce_fusion.4.refs_0_
  30.6 3.3 all-to-all-done.refs_1_
  34.0 1.0 copy-done
  34.9 3.1 pick_early.1
  38.1 6.7 %all-to-all-start.1 = ((f32[16,128,128]{2,1,0:T(8,128)}), f32[16,128,128]{2,1,0:T(8,128)S(1)}, u32[]{:S(2)}, u32[]{:S(2)}) async-start(f32[16,128,128]{2,1,0:T(8,128)} %pick_early.1), calls=%async_computation.1 | async-start | bytes 2097152 | tf_op jit(solution)/shard_map/all_to_all | solution.py:564
  45.5 1.0 collective-permute-done
  46.5 2.6 add_add_fusion
  49.2 1.9 collective-permute-start.7
  51.9 24.0 %collective-permute-done.7.parent = f32[128,1024]{1,0:T(8,128)S(1)} collective-permute-done((f32[128,1024]{1,0:T(8,128)}, f32[128,1024]{1,0:T(8,128)S(1)}, u32[]{:S(2)}, u32[]{:S(2)}) %collective-permute-start.7) | collective-permute-done | bytes 524320 | tf_op jit(solution)/shard_map/ppermute | solution.py:559
  75.9 0.8 copy-done.9
  76.7 1.0 copy-done.1
  77.7 2.3 assemble_strip.1
  80.1 6.6 %collective-permute-start.8 = (f32[128,1024]{1,0:T(8,128)}, f32[128,1024]{1,0:T(8,128)S(1)}, u32[]{:S(2)}, u32[]{:S(2)}) collective-permute-start(f32[128,1024]{1,0:T(8,128)} %assemble_strip.1), channel_id=1, source_target_pairs={{0,0},{8,1},{16,2},{24,3},{32,4},{40,5},{48,6},{56,7},{64,8},{72,9... | collective-permute-start | bytes 1572872 | tf_op jit(solution)/shard_map/ppermute | solution.py:569
  86.7 1.1 fusion.31
  87.8 0.7 collective-permute-start.9
  88.5 0.7 collective-permute-start.10
  89.2 0.7 add.273.given
  89.9 19.4 %collective-permute-done.8.refs_0_.given = f32[128,1024]{1,0:T(8,128)S(1)} collective-permute-done((f32[128,1024]{1,0:T(8,128)}, f32[128,1024]{1,0:T(8,128)S(1)}, u32[]{:S(2)}, u32[]{:S(2)}) %collective-permute-start.8) | collective-permute-done | bytes 524320 | tf_op jit(solution)/shard_map/ppermute | solution.py:569
  109.3 0.8 copy-done.2
  110.1 1.7 hand_on.2
  112.5 0.7 collective-permute-start.16
  113.2 0.7 collective-permute-start.15
  114.5 0.7 collective-permute-start.13
  115.9 1.3 collective-permute-start.11
  117.3 29.6 %collective-permute-done.11 = f32[64,1024]{1,0:T(8,128)S(1)} collective-permute-done((f32[64,1024]{1,0:T(8,128)}, f32[64,1024]{1,0:T(8,128)S(1)}, u32[]{:S(2)}, u32[]{:S(2)}) %collective-permute-start.11) | collective-permute-done | bytes 262176 | tf_op jit(solution)/shard_map/ppermute | solution.py:582
  146.9 1.8 add_add_fusion.1.refs_2_
  149.3 5.6 %pack_first.1 = f32[8,1280,128]{2,1,0:T(8,128)} custom-call(s32[8]{0:T(128)} %slice.20.refs_0_, f32[1280,1280]{1,0:T(8,128)} %refs_1_.5, f32[64,1024]{1,0:T(8,128)} %add_add_fusion.1.refs_2_), custom_call_target="tpu_custom_call" | custom-call | bytes 10485760 | tf_op jit(solution)/shard_map/pack_first/pallas_call | solution.py:36
  154.9 10.8 %all-to-all-start.2 = ((f32[8,1280,128]{2,1,0:T(8,128)}), f32[8,1280,128]{2,1,0:T(8,128)}, u32[]{:S(2)}, u32[]{:S(2)}) async-start(f32[8,1280,128]{2,1,0:T(8,128)} %pack_first.1), calls=%async_computation.2 | async-start | bytes 10485760 | tf_op jit(solution)/shard_map/all_to_all | solution.py:588
  169.2 56.6 %all-to-all-done.2 = f32[8,1280,128]{2,1,0:T(8,128)} async-done(((f32[8,1280,128]{2,1,0:T(8,128)}), f32[8,1280,128]{2,1,0:T(8,128)}, u32[]{:S(2)}, u32[]{:S(2)}) %all-to-all-start.2) | async-done | bytes 5242912 | tf_op jit(solution)/shard_map/all_to_all | solution.py:588
  225.9 5.2 %pack_rows.2.refs_0_.refs_2_.refs_1_ = f32[16,5,128,128]{3,2,1,0:T(8,128)} custom-call(s32[16]{0:T(128)} %copy-done.12, s32[16]{0:T(128)} %convert_element_type.32.refs_1_, s32[5]{0:T(128)} %get-tuple-element.56.refs_2_, f32[8,10,128,128]{3,2,1,0:T(8,128)} %bitcast.8.refs_3_, f32[2048,1024]{1,0:T(8,128)} %all-gather.4.cloned.1.call-done.refs_4_.col_strip), custom_call_target="tpu_custom_call" | custom-call | bytes 10485760 | tf_op jit(solution)/shard_map/pack_rows/pallas_call | solution.py:36
  231.1 5.7 %pack_second.1 = (f32[1280,128]{1,0:T(8,128)}, f32[1280,128]{1,0:T(8,128)}, f32[1280,128]{1,0:T(8,128)}, f32[1280,128]{1,0:T(8,128)}, f32[1280,128]{1,0:T(8,128)...) custom-call(s32[8]{0:T(128)} %and_select_fusion.1.refs_0_, f32[1280,1280]{1,0:T(8,128)} %refs_1_.5, ...), custom_call_target="tpu_custom_call" | custom-call | bytes 10485760 | tf_op jit(solution)/shard_map/pack_second/pallas_call | solution.py:36
  236.8 1.2 collective-permute-start.18
  238.2 10.2 %all-to-all-start.3 = ((f32[16,5,128,128]{3,2,1,0:T(8,128)}), f32[16,5,128,128]{3,2,1,0:T(8,128)}, u32[]{:S(2)}, u32[]{:S(2)}) async-start(f32[16,5,128,128]{3,2,1,0:T(8,128)} %pack_rows.2.refs_0_.refs_2_.refs_1_), calls=%async_computation.3 | async-start | bytes 10485760 | tf_op jit(solution)/shard_map/all_to_all | solution.py:593
  250.3 2.7 collective-permute-start.20
  253.0 1.2 collective-permute-start.21
  254.1 2.3 collective-permute-start.22
  256.4 1.9 hand_on.3
  259.2 23.3 %factor_lead.4.refs_0_ = f32[1024,1024]{1,0:T(8,128)} custom-call(f32[1024,1024]{1,0:T(8,128)} %all-gather.8.cloned.1.call-done.refs_0_, f32[1280,128]{1,0:T(8,128)} %copy-done.3), custom_call_target="tpu_custom_call" | custom-call | flops 24999999488 | bytes 8388608 | tf_op jit(solution)/shard_map/factor_lead/pallas_call | solution.py:347
  282.7 20.9 %factor_lead.5.refs_13_.refs_0_ = f32[1024,1024]{1,0:T(8,128)} custom-call(f32[1024,1024]{1,0:T(8,128)} %factor_lead.4.refs_0_, f32[16,5,128,128]{3,2,1,0:T(8,128)} %pack_rows.2.refs_0_.refs_2_.refs_1_), custom_call_target="tpu_custom_call" | custom-call | flops 24999999488 | bytes 8388608 | tf_op jit(solution)/shard_map/factor_lead/pallas_call | solution.py:347
  303.6 10.5 %collective-permute-done.21 = f32[1280,128]{1,0:T(8,128)S(1)} collective-permute-done((f32[1280,128]{1,0:T(8,128)}, f32[1280,128]{1,0:T(8,128)S(1)}, u32[]{:S(2)}, u32[]{:S(2)}) %collective-permute-start.21) | collective-permute-done | bytes 655392 | tf_op jit(solution)/shard_map/ppermute | solution.py:597
  314.1 6.4 %collective-permute-done.22 = f32[1280,128]{1,0:T(8,128)S(1)} collective-permute-done((f32[1280,128]{1,0:T(8,128)}, f32[1280,128]{1,0:T(8,128)S(1)}, u32[]{:S(2)}, u32[]{:S(2)}) %collective-permute-start.22) | collective-permute-done | bytes 655392 | tf_op jit(solution)/shard_map/ppermute | solution.py:597
  320.5 7.7 %collective-permute-done.23 = f32[1280,128]{1,0:T(8,128)} collective-permute-done((f32[1280,128]{1,0:T(8,128)}, f32[1280,128]{1,0:T(8,128)}, u32[]{:S(2)}, u32[]{:S(2)}) %collective-permute-start.23) | collective-permute-done | bytes 655392 | tf_op jit(solution)/shard_map/ppermute | solution.py:597
  328.7 0.8 copy-done.8
  329.6 5.5 %pack_rows.3.refs_1_ = f32[16,5,128,128]{3,2,1,0:T(8,128)} custom-call(s32[16]{0:T(128)} %copy-done.12, s32[16]{0:T(128)} %convert_element_type.32.refs_1_, s32[5]{0:T(128)} %get-tuple-element.55.refs_2_, f32[8,10,128,128]{3,2,1,0:T(8,128)} %bitcast.8.refs_3_, f32[10,128,128]{2,1,0:T(8,128)} %bitcast.41, f32[10,128,128]{2,1,0:T(8,128)} %bitcast.42, ...), custom_call_target="tpu_custom_call" | custom-call | bytes 10485760 | tf_op jit(solution)/shard_map/pack_rows/pallas_call | solution.py:36
  335.1 6.7 %all-to-all-start.4 = ((f32[16,5,128,128]{3,2,1,0:T(8,128)}), f32[16,5,128,128]{3,2,1,0:T(8,128)}, u32[]{:S(2)}, u32[]{:S(2)}) async-start(f32[16,5,128,128]{3,2,1,0:T(8,128)} %pack_rows.3.refs_1_), calls=%async_computation.4 | async-start | bytes 10485760 | tf_op jit(solution)/shard_map/all_to_all | solution.py:603
  341.7 18.2 %factor_lead.6.refs_0_ = f32[1024,1024]{1,0:T(8,128)} custom-call(f32[1024,1024]{1,0:T(8,128)} %factor_lead.5.refs_13_.refs_0_, f32[16,5,128,128]{3,2,1,0:T(8,128)} %pack_rows.3.refs_1_), custom_call_target="tpu_custom_call" | custom-call | flops 24999999488 | bytes 8388608 | tf_op jit(solution)/shard_map/factor_lead/pallas_call | solution.py:347
  359.9 16.6 %factor_lead.7 = (bf16[1024,1024]{1,0:T(8,128)(2,1)}, bf16[1024,1024]{1,0:T(8,128)(2,1)}) custom-call(f32[1024,1024]{1,0:T(8,128)} %factor_lead.6.refs_0_, f32[16,5,128,128]{3,2,1,0:T(8,128)} %pack_rows.3.refs_1_), custom_call_target="tpu_custom_call" | custom-call | flops 24999999488 | bytes 8388608 | tf_op jit(solution)/shard_map/factor_lead/pallas_call | solution.py:347
  376.6 33.4 %update_front.1.front = f32[1024,2048]{1,0:T(8,128)} custom-call(s32[2]{0:T(128)} %pad_add_fusion.flags, f32[1024,1024]{1,0:T(8,128)} %all-gather.6.cloned.1.call-done.row_strip, f32[2048,1024]{1,0:T(8,128)} %all-gather.4.cloned.1.call-done.refs_4_.col_strip, bf16[1024,1024]{1,0:T(8,128)(2,1)} %get-tuple-element.39.inv_hi, ...), custom_call_target="tpu_custom_call" | custom-call | flops 40000000000 | bytes 33554432 | tf_op jit(solution)/shard_map/update_front/pallas_call | solution.py:417
  410.0 12.4 %all-to-all-done.4.refs_1_.refs_3_ = f32[16,5,128,128]{3,2,1,0:T(8,128)} async-done(((f32[16,5,128,128]{3,2,1,0:T(8,128)}), f32[16,5,128,128]{3,2,1,0:T(8,128)}, u32[]{:S(2)}, u32[]{:S(2)}) %all-to-all-start.4) | async-done | bytes 5242912 | tf_op jit(solution)/shard_map/all_to_all | solution.py:603
  422.4 12.4 %place_children.1 = f32[1024,2048]{1,0:T(8,128)} custom-call(s32[2,8]{1,0:T(2,128)} %fusion.18.source, s32[2,16]{1,0:T(2,128)} %select_reduce_fusion.rank, s32[2,128]{1,0:T(2,128)} %reshape.288.keep, f32[1024,2048]{1,0:T(8,128)} %update_front.1.front, f32[16,5,128,128]{3,2,1,0:T(8,128)} %all-to-all-done.3.refs_12_.refs_0_.refs_2_, ...), custom_call_target="tpu_custom_call", output_to_operand_aliasing={{}: (3, {})} | custom-call | bytes 25165824 | tf_op jit(solution)/shard_map/place_children/pallas_call | solution.py:465
  (92 shorter events, 12.4 us)
Async XLA Ops:
  9.3 13.2 %copy-start.12 = (s32[16]{0:T(128)}, s32[16]{0:T(128)S(1)}, u32[]{:S(2)}) copy-start(s32[16]{0:T(128)S(1)} %get-tuple-element.42.refs_0_) | copy-start | bytes 196
  12.9 17.6 %copy-start.11 = (s32[2,80]{1,0:T(2,128)S(1)}, s32[2,80]{1,0:T(2,128)}, u32[]{:S(2)}) copy-start(s32[2,80]{1,0:T(2,128)} %param.6) | copy-start | bytes 1924
  12.9 21.1 %all-to-all-start = ((f32[16,128,128]{2,1,0:T(8,128)}), f32[16,128,128]{2,1,0:T(8,128)S(1)}, u32[]{:S(2)}, u32[]{:S(2)}) async-start(f32[16,128,128]{2,1,0:T(8,128)} %pack_early.1), calls=%async_computation | async-start | bytes 2097152 | tf_op jit(solution)/shard_map/all_to_all | solution.py:562
  22.5 28.6 %copy-start.10 = (s32[2,80,80]{2,1,0:T(8,128)S(1)}, s32[2,80,80]{2,1,0:T(8,128)}, u32[]{:S(2)}) copy-start(s32[2,80,80]{2,1,0:T(8,128)} %param.7) | copy-start | bytes 153604
  22.5 4.4 collective-permute-start.6
  23.3 5.1 %collective-permute-start.5 = (f32[128,1024]{1,0:T(8,128)}, f32[128,1024]{1,0:T(8,128)S(1)}, u32[]{:S(2)}, u32[]{:S(2)}) collective-permute-start(f32[128,1024]{1,0:T(8,128)} %get-tuple-element.29), channel_id=1, source_target_pairs={{0,6},{8,14},{16,22},{24,30},{32,38},{40,46},{48,54},{56,62},{64,7... | collective-permute-start | bytes 1572872 | tf_op jit(solution)/shard_map/ppermute | solution.py:555
  24.0 21.5 %collective-permute-start.4 = (f32[128,1024]{1,0:T(8,128)}, f32[128,1024]{1,0:T(8,128)S(1)}, u32[]{:S(2)}, u32[]{:S(2)}) collective-permute-start(f32[128,1024]{1,0:T(8,128)} %get-tuple-element.28), channel_id=1, source_target_pairs={{0,5},{8,13},{16,21},{24,29},{32,37},{40,45},{48,53},{56,61},{64,6... | collective-permute-start | bytes 1572872 | tf_op jit(solution)/shard_map/ppermute | solution.py:555
  24.7 20.8 %collective-permute-start.3 = (f32[128,1024]{1,0:T(8,128)}, f32[128,1024]{1,0:T(8,128)S(1)}, u32[]{:S(2)}, u32[]{:S(2)}) collective-permute-start(f32[128,1024]{1,0:T(8,128)} %get-tuple-element.27), channel_id=1, source_target_pairs={{0,4},{8,12},{16,20},{24,28},{32,36},{40,44},{48,52},{56,60},{64,6... | collective-permute-start | bytes 1572872 | tf_op jit(solution)/shard_map/ppermute | solution.py:555
  25.4 20.1 %collective-permute-start.2 = (f32[128,1024]{1,0:T(8,128)}, f32[128,1024]{1,0:T(8,128)}, u32[]{:S(2)}, u32[]{:S(2)}) collective-permute-start(f32[128,1024]{1,0:T(8,128)} %get-tuple-element.26), channel_id=1, source_target_pairs={{0,3},{8,11},{16,19},{24,27},{32,35},{40,43},{48,51},{56,59},{64,6... | collective-permute-start | bytes 1572872 | tf_op jit(solution)/shard_map/ppermute | solution.py:555
  26.9 18.6 %collective-permute-start.1 = (f32[128,1024]{1,0:T(8,128)}, f32[128,1024]{1,0:T(8,128)}, u32[]{:S(2)}, u32[]{:S(2)}) collective-permute-start(f32[128,1024]{1,0:T(8,128)} %get-tuple-element.25), channel_id=1, source_target_pairs={{0,2},{8,10},{16,18},{24,26},{32,34},{40,42},{48,50},{56,58},{64,6... | collective-permute-start | bytes 1572872 | tf_op jit(solution)/shard_map/ppermute | solution.py:555
  28.4 18.2 %collective-permute-start = (f32[128,1024]{1,0:T(8,128)}, f32[128,1024]{1,0:T(8,128)}, u32[]{:S(2)}, u32[]{:S(2)}) collective-permute-start(f32[128,1024]{1,0:T(8,128)} %get-tuple-element.24), channel_id=1, source_target_pairs={{0,1},{8,9},{16,17},{24,25},{32,33},{40,41},{48,49},{56,57},{64,65... | collective-permute-start | bytes 1572872 | tf_op jit(solution)/shard_map/ppermute | solution.py:555
  34.0 1.0 copy-start
  38.1 37.9 %all-to-all-start.1 = ((f32[16,128,128]{2,1,0:T(8,128)}), f32[16,128,128]{2,1,0:T(8,128)S(1)}, u32[]{:S(2)}, u32[]{:S(2)}) async-start(f32[16,128,128]{2,1,0:T(8,128)} %pick_early.1), calls=%async_computation.1 | async-start | bytes 2097152 | tf_op jit(solution)/shard_map/all_to_all | solution.py:564
  44.8 181.1 %all-gather.4.cloned.1.call-start = ((), (), s32[]{:S(2)}) async-start(), calls=%async_computation.5 | async-start | bytes 8912896 | tf_op jit(solution)/shard_map/all_gather | solution.py:567
  49.2 26.8 %collective-permute-start.7 = (f32[128,1024]{1,0:T(8,128)}, f32[128,1024]{1,0:T(8,128)S(1)}, u32[]{:S(2)}, u32[]{:S(2)}) collective-permute-start(f32[128,1024]{1,0:T(8,128)} %add_add_fusion), channel_id=1, source_target_pairs={{0,0},{1,8},{2,16},{3,24},{4,32},{5,40},{6,48},{7,56},{8,64},{9,72... | collective-permute-start | bytes 1572872 | tf_op jit(solution)/shard_map/ppermute | solution.py:559
  75.9 0.8 copy-start.9
  76.7 1.0 copy-start.1
  80.1 178.6 %all-gather.8.cloned.1.call-start = ((), (), s32[]{:S(2)}) async-start(), calls=%async_computation.7 | async-start | bytes 4456448 | tf_op jit(solution)/shard_map/all_gather | solution.py:585
  80.1 29.2 %collective-permute-start.8 = (f32[128,1024]{1,0:T(8,128)}, f32[128,1024]{1,0:T(8,128)S(1)}, u32[]{:S(2)}, u32[]{:S(2)}) collective-permute-start(f32[128,1024]{1,0:T(8,128)} %assemble_strip.1), channel_id=1, source_target_pairs={{0,0},{8,1},{16,2},{24,3},{32,4},{40,5},{48,6},{56,7},{64,8},{72,9... | collective-permute-start | bytes 1572872 | tf_op jit(solution)/shard_map/ppermute | solution.py:569
  87.8 1.4 collective-permute-start.9
  88.5 0.7 collective-permute-start.10
  109.3 0.8 copy-start.2
  111.8 3.4 collective-permute-start.17
  112.5 3.4 collective-permute-start.16
  113.2 4.1 collective-permute-start.15
  113.9 3.4 collective-permute-start.14
  114.5 2.7 collective-permute-start.13
  115.2 2.0 collective-permute-start.12
  115.9 30.9 %collective-permute-start.11 = (f32[64,1024]{1,0:T(8,128)}, f32[64,1024]{1,0:T(8,128)S(1)}, u32[]{:S(2)}, u32[]{:S(2)}) collective-permute-start(f32[64,1024]{1,0:T(8,128)} %hand_on.2), channel_id=1, source_target_pairs={{0,1},{8,9},{16,17},{24,25},{32,33},{40,41},{48,49},{56,57},{64,65... | collective-permute-start | bytes 786440 | tf_op jit(solution)/shard_map/ppermute | solution.py:582
  154.9 71.0 %all-to-all-start.2 = ((f32[8,1280,128]{2,1,0:T(8,128)}), f32[8,1280,128]{2,1,0:T(8,128)}, u32[]{:S(2)}, u32[]{:S(2)}) async-start(f32[8,1280,128]{2,1,0:T(8,128)} %pack_first.1), calls=%async_computation.2 | async-start | bytes 10485760 | tf_op jit(solution)/shard_map/all_to_all | solution.py:588
  236.8 21.6 %collective-permute-start.18 = (f32[1280,128]{1,0:T(8,128)}, f32[1280,128]{1,0:T(8,128)S(1)}, u32[]{:S(2)}, u32[]{:S(2)}) collective-permute-start(f32[1280,128]{1,0:T(8,128)} %get-tuple-element.31), channel_id=1, source_target_pairs={{0,1},{1,2},{2,3},{3,4},{4,5},{5,6},{6,7},{7,0},{8,9},{9,10},{10,1... | collective-permute-start | bytes 1966088 | tf_op jit(solution)/shard_map/ppermute | solution.py:597
  238.2 90.5 %all-to-all-start.3 = ((f32[16,5,128,128]{3,2,1,0:T(8,128)}), f32[16,5,128,128]{3,2,1,0:T(8,128)}, u32[]{:S(2)}, u32[]{:S(2)}) async-start(f32[16,5,128,128]{3,2,1,0:T(8,128)} %pack_rows.2.refs_0_.refs_2_.refs_1_), calls=%async_computation.3 | async-start | bytes 10485760 | tf_op jit(solution)/shard_map/all_to_all | solution.py:593
  248.3 128.2 %all-gather.6.cloned.1.call-start = ((), (), s32[]{:S(2)}) async-start(), calls=%async_computation.6 | async-start | bytes 4718592 | tf_op jit(solution)/shard_map/all_gather | solution.py:607
  250.3 32.3 %collective-permute-start.19 = (f32[1280,128]{1,0:T(8,128)}, f32[1280,128]{1,0:T(8,128)S(1)}, u32[]{:S(2)}, u32[]{:S(2)}) collective-permute-start(f32[1280,128]{1,0:T(8,128)} %get-tuple-element.33), channel_id=1, source_target_pairs={{0,2},{1,3},{2,4},{3,5},{4,6},{5,7},{6,0},{7,1},{8,10},{9,11},{10,... | collective-permute-start | bytes 1966088 | tf_op jit(solution)/shard_map/ppermute | solution.py:597
  250.3 53.3 %collective-permute-start.20 = (f32[1280,128]{1,0:T(8,128)}, f32[1280,128]{1,0:T(8,128)S(1)}, u32[]{:S(2)}, u32[]{:S(2)}) collective-permute-start(f32[1280,128]{1,0:T(8,128)} %get-tuple-element.34), channel_id=1, source_target_pairs={{0,3},{1,4},{2,5},{3,6},{4,7},{5,0},{6,1},{7,2},{8,11},{9,12},{10,... | collective-permute-start | bytes 1966088 | tf_op jit(solution)/shard_map/ppermute | solution.py:597
  253.0 61.2 %collective-permute-start.21 = (f32[1280,128]{1,0:T(8,128)}, f32[1280,128]{1,0:T(8,128)S(1)}, u32[]{:S(2)}, u32[]{:S(2)}) collective-permute-start(f32[1280,128]{1,0:T(8,128)} %get-tuple-element.35), channel_id=1, source_target_pairs={{0,4},{1,5},{2,6},{3,7},{4,0},{5,1},{6,2},{7,3},{8,12},{9,13},{10,... | collective-permute-start | bytes 1966088 | tf_op jit(solution)/shard_map/ppermute | solution.py:597
  254.1 66.4 %collective-permute-start.22 = (f32[1280,128]{1,0:T(8,128)}, f32[1280,128]{1,0:T(8,128)S(1)}, u32[]{:S(2)}, u32[]{:S(2)}) collective-permute-start(f32[1280,128]{1,0:T(8,128)} %get-tuple-element.36), channel_id=1, source_target_pairs={{0,5},{1,6},{2,7},{3,0},{4,1},{5,2},{6,3},{7,4},{8,13},{9,14},{10,... | collective-permute-start | bytes 1966088 | tf_op jit(solution)/shard_map/ppermute | solution.py:597
  258.4 0.9 copy-start.3
  258.4 69.8 %collective-permute-start.23 = (f32[1280,128]{1,0:T(8,128)}, f32[1280,128]{1,0:T(8,128)}, u32[]{:S(2)}, u32[]{:S(2)}) collective-permute-start(f32[1280,128]{1,0:T(8,128)} %get-tuple-element.37), channel_id=1, source_target_pairs={{0,6},{1,7},{2,0},{3,1},{4,2},{5,3},{6,4},{7,5},{8,14},{9,15},{10,... | collective-permute-start | bytes 1966088 | tf_op jit(solution)/shard_map/ppermute | solution.py:597
  259.2 23.4 %copy-start.13 = (f32[1280,128]{1,0:T(8,128)S(1)}, f32[1280,128]{1,0:T(8,128)}, u32[]{:S(2)}) copy-start(f32[1280,128]{1,0:T(8,128)} %get-tuple-element.38) | copy-start | bytes 1966084
  282.6 21.0 %copy-start.4 = (f32[1280,128]{1,0:T(8,128)}, f32[1280,128]{1,0:T(8,128)S(1)}, u32[]{:S(2)}) copy-start(f32[1280,128]{1,0:T(8,128)S(1)} %collective-permute-done.19) | copy-start | bytes 1966084
  282.6 46.1 %collective-permute-start.24 = (f32[1280,128]{1,0:T(8,128)S(1)}, f32[1280,128]{1,0:T(8,128)S(1)}, u32[]{:S(2)}, u32[]{:S(2)}) collective-permute-start(f32[1280,128]{1,0:T(8,128)S(1)} %copy-done.13), channel_id=1, source_target_pairs={{0,7},{1,0},{2,1},{3,2},{4,3},{5,4},{6,5},{7,6},{8,15},{9,8},{10,9... | collective-permute-start | bytes 1966088 | tf_op jit(solution)/shard_map/ppermute | solution.py:597
  303.6 25.1 %copy-start.5 = (f32[1280,128]{1,0:T(8,128)}, f32[1280,128]{1,0:T(8,128)S(1)}, u32[]{:S(2)}) copy-start(f32[1280,128]{1,0:T(8,128)S(1)} %collective-permute-done.20) | copy-start | bytes 1966084
  314.1 14.6 %copy-start.6 = (f32[1280,128]{1,0:T(8,128)}, f32[1280,128]{1,0:T(8,128)S(1)}, u32[]{:S(2)}) copy-start(f32[1280,128]{1,0:T(8,128)S(1)} %collective-permute-done.21) | copy-start | bytes 1966084
  320.5 8.2 %copy-start.7 = (f32[1280,128]{1,0:T(8,128)}, f32[1280,128]{1,0:T(8,128)S(1)}, u32[]{:S(2)}) copy-start(f32[1280,128]{1,0:T(8,128)S(1)} %collective-permute-done.22) | copy-start | bytes 1966084
  328.7 0.9 copy-start.8
  335.1 87.3 %all-to-all-start.4 = ((f32[16,5,128,128]{3,2,1,0:T(8,128)}), f32[16,5,128,128]{3,2,1,0:T(8,128)}, u32[]{:S(2)}, u32[]{:S(2)}) async-start(f32[16,5,128,128]{3,2,1,0:T(8,128)} %pack_rows.3.refs_1_), calls=%async_computation.4 | async-start | bytes 10485760 | tf_op jit(solution)/shard_map/all_to_all | solution.py:603
Sparse Core Ops, SparseCore 0:
  80.2 103.7 all-gather.3
  186.1 51.0 all-gather.7
  258.5 66.3 all-gather.5

commit v10 on v8

--- a/solution.py
+++ b/solution.py
@@ -239,6 +239,19 @@
         compiler_params=params(),
         cost_estimate=cost(0, 1 << 20),
         name="hand_on",
+    )(given, *after)
+
+
+def pass_on(given, after):
+    place = pl.BlockSpec(memory_space=pl.ANY)
+    return pl.pallas_call(
+        lambda *refs: None,
+        in_specs=[place] * (1 + len(after)),
+        out_specs=place,
+        out_shape=jax.ShapeDtypeStruct(given.shape, F32),
+        input_output_aliases={0: 0},
+        compiler_params=params(),
+        name="pass_on",
     )(given, *after)
 
 
@@ -351,7 +364,7 @@
         out_shape=(half, half) if last else full,
         scratch_shapes=[pltpu.VMEM((LEAD, LEAD), F32)] if last else [],
         compiler_params=params(),
-        cost_estimate=cost(25 * 10**9, 8 << 20),
+        cost_estimate=cost(0, 0),
         name="factor_lead",
     )(given, after)
 
@@ -598,9 +611,10 @@
         for d in range(1, COLS)
     ]
     work = factor_part(1, work, near_out)
-    far_out = pack_rows(send_rows, sends, pick_cols[HALF:], first, second, [near, work])
+    far_out = pack_rows(send_rows, sends, pick_cols[HALF:], first, second, [work])
+    far_out = pass_on(far_out, [near])
+    work = factor_part(2, work, far_out)
     far = lax.all_to_all(far_out, "row", split_axis=0, concat_axis=0, tiled=True)
-    work = factor_part(2, work, far_out)
     inv_hi, inv_lo = factor_part(3, work, col_strip)
     row_piece = hand_on(row_raw, [near_out])
     row_strip = lax.all_gather(row_piece, "col", axis=0, tiled=True)

time: 437 us -> 450 us (1.030)
  starting transfers between devices: 88.6 us -> 104 us
    all_to_all x1, starting transfers between devices: 7.27 us -> 23.8 us  [body(): lax.all_to_all(far_out, 'row', split_axis=0, concat_axis=0, tiled=True)]
  transfers between devices with their start and end apart: 33 -> 33, of which waited for: 7 -> 8; matrix products, arithmetic and copies ran while one was open for 3% -> 3% of each run, Pallas kernels for 33% -> 32%
where the time goes in v10:
time: 450 us; the launch traced here: 447 us
  Pallas kernels  164 us (36%)
  waiting for transfers between devices  145 us (32%)
  starting transfers between devices  104 us (23%)
  between operations  13.6 us (3%)
  other arithmetic  10.9 us (2%)
  local copies, waits for them, and re-layouts  9.61 us (2%)
    pallas_call x4, Pallas kernels, factor_part(): pl.pallas_call(functools.partial(factor_kernel, part * count, count, last...  79 us
    all_to_all x1, waiting for transfers between devices, body(): lax.all_to_all(first, 'col', split_axis=0, concat_axis=0, tiled=True)  58.8 us
    pallas_call x1, Pallas kernels, update_front(): pl.pallas_call(update_kernel, grid_spec=pltpu.PrefetchScalarGridSpec(num_...  33.4 us
    pallas_call x7, Pallas kernels, gather_call(): pl.pallas_call(run, in_specs=[pl.BlockSpec(memory_space=pltpu.SMEM)] * le...  31.8 us
    ppermute x7, waiting for transfers between devices, body(): lax.ppermute(parts[d], 'col', [(c, (c + d) % COLS) for c in range(COLS)])  23.8 us
    all_to_all x1, starting transfers between devices, body(): lax.all_to_all(far_out, 'row', split_axis=0, concat_axis=0, tiled=True)  23.8 us
    ppermute x1, waiting for transfers between devices, body(): strip_parent = lax.ppermute(own, axes, [(b, a) for a, b in pairs])  22.5 us
    ppermute x1, waiting for transfers between devices, body(): row_raw = lax.ppermute(strip, axes, pairs)  21.5 us
  transfers between devices with their start and end apart: 33, of which 8 were waited for; matrix products, arithmetic and copies ran while one was open for 3% of the time, Pallas kernels for 32%

profile of v10, /device:TPU:21, one launch (start us, length us, event | category | flops | bytes accessed | tf_op | source)
XLA Modules:
  0.0 447.3 jit_solution(10037477635795960267)
XLA Ops:
  6.5 3.6 cut_strip.1
  10.1 1.4 collective-permute-start
  11.6 0.7 collective-permute-start.1
  13.6 3.0 pack_early.1
  16.6 6.7 %all-to-all-start = ((f32[16,128,128]{2,1,0:T(8,128)}), f32[16,128,128]{2,1,0:T(8,128)S(1)}, u32[]{:S(2)}, u32[]{:S(2)}) async-start(f32[16,128,128]{2,1,0:T(8,128)} %pack_early.1), calls=%async_computation | async-start | bytes 2097152 | tf_op jit(solution)/shard_map/all_to_all | solution.py:575
  23.4 0.7 collective-permute-start.2
  24.0 1.5 collective-permute-start.3
  25.5 1.5 collective-permute-start.4
  27.0 1.5 collective-permute-start.5
  28.5 1.5 collective-permute-start.6
  29.9 0.7 select_reduce_fusion.4.refs_0_
  30.9 7.6 %all-to-all-done.refs_1_ = f32[16,128,128]{2,1,0:T(8,128)S(1)} async-done(((f32[16,128,128]{2,1,0:T(8,128)}), f32[16,128,128]{2,1,0:T(8,128)S(1)}, u32[]{:S(2)}, u32[]{:S(2)}) %all-to-all-start) | async-done | bytes 1048608 | tf_op jit(solution)/shard_map/all_to_all | solution.py:575
  38.5 1.0 copy-done
  39.4 3.1 pick_early.1
  42.6 6.7 %all-to-all-start.1 = ((f32[16,128,128]{2,1,0:T(8,128)}), f32[16,128,128]{2,1,0:T(8,128)S(1)}, u32[]{:S(2)}, u32[]{:S(2)}) async-start(f32[16,128,128]{2,1,0:T(8,128)} %pick_early.1), calls=%async_computation.1 | async-start | bytes 2097152 | tf_op jit(solution)/shard_map/all_to_all | solution.py:577
  49.4 2.8 add_add_fusion
  52.2 8.4 %collective-permute-start.7 = (f32[128,1024]{1,0:T(8,128)}, f32[128,1024]{1,0:T(8,128)S(1)}, u32[]{:S(2)}, u32[]{:S(2)}) collective-permute-start(f32[128,1024]{1,0:T(8,128)} %add_add_fusion), channel_id=1, source_target_pairs={{0,0},{1,8},{2,16},{3,24},{4,32},{5,40},{6,48},{7,56},{8,64},{9,72... | collective-permute-start | bytes 1572872 | tf_op jit(solution)/shard_map/ppermute | solution.py:572
  62.2 22.5 %collective-permute-done.7.parent = f32[128,1024]{1,0:T(8,128)S(1)} collective-permute-done((f32[128,1024]{1,0:T(8,128)}, f32[128,1024]{1,0:T(8,128)S(1)}, u32[]{:S(2)}, u32[]{:S(2)}) %collective-permute-start.7) | collective-permute-done | bytes 524320 | tf_op jit(solution)/shard_map/ppermute | solution.py:572
  84.7 0.8 copy-done.9
  85.5 1.0 copy-done.1
  86.5 3.5 assemble_strip.1.refs_1_
  89.9 1.9 collective-permute-start.8
  91.9 1.1 fusion.31
  92.9 0.7 collective-permute-start.10
  93.6 0.7 collective-permute-start.9
  94.3 0.7 add.273.given
  95.1 21.5 %collective-permute-done.8.given.refs_0_ = f32[128,1024]{1,0:T(8,128)S(1)} collective-permute-done((f32[128,1024]{1,0:T(8,128)}, f32[128,1024]{1,0:T(8,128)S(1)}, u32[]{:S(2)}, u32[]{:S(2)}) %collective-permute-start.8) | collective-permute-done | bytes 524320 | tf_op jit(solution)/shard_map/ppermute | solution.py:583
  116.6 0.9 copy-done.2
  117.5 1.7 hand_on.3
  119.1 1.3 collective-permute-start.11
  120.4 0.7 collective-permute-start.12
  121.1 0.7 collective-permute-start.13
  121.8 0.7 collective-permute-start.14
  122.5 0.7 collective-permute-start.15
  123.1 1.5 collective-permute-done.11
  124.7 0.7 collective-permute-start.16
  125.4 0.7 collective-permute-start.17
  126.1 1.8 add_add_fusion.1
  128.0 0.7 all-gather.6.cloned.1.call-update
  129.3 5.6 %pack_first.1 = f32[8,1280,128]{2,1,0:T(8,128)} custom-call(s32[8]{0:T(128)} %slice.20.refs_0_, f32[1280,1280]{1,0:T(8,128)} %refs_1_.5), custom_call_target="tpu_custom_call" | custom-call | bytes 10485760 | tf_op jit(solution)/shard_map/pack_first/pallas_call | solution.py:36
  134.9 18.1 %all-to-all-start.2 = ((f32[8,1280,128]{2,1,0:T(8,128)}), f32[8,1280,128]{2,1,0:T(8,128)}, u32[]{:S(2)}, u32[]{:S(2)}) async-start(f32[8,1280,128]{2,1,0:T(8,128)} %pack_first.1), calls=%async_computation.2 | async-start | bytes 10485760 | tf_op jit(solution)/shard_map/all_to_all | solution.py:581
  154.3 58.8 %all-to-all-done.2 = f32[8,1280,128]{2,1,0:T(8,128)} async-done(((f32[8,1280,128]{2,1,0:T(8,128)}), f32[8,1280,128]{2,1,0:T(8,128)}, u32[]{:S(2)}, u32[]{:S(2)}) %all-to-all-start.2) | async-done | bytes 5242912 | tf_op jit(solution)/shard_map/all_to_all | solution.py:581
  213.2 5.1 %pack_rows.2.refs_0_.refs_1_.refs_2_ = f32[16,5,128,128]{3,2,1,0:T(8,128)} custom-call(s32[16]{0:T(128)} %copy-done.12, s32[16]{0:T(128)} %convert_element_type.32.refs_1_, s32[5]{0:T(128)} %get-tuple-element.56.refs_2_, f32[8,10,128,128]{3,2,1,0:T(8,128)} %bitcast.8.refs_3_), custom_call_target="tpu_custom_call" | custom-call | bytes 10485760 | tf_op jit(solution)/shard_map/pack_rows/pallas_call | solution.py:36
  218.3 1.9 hand_on.2
  220.2 13.3 %all-to-all-start.3 = ((f32[16,5,128,128]{3,2,1,0:T(8,128)}), f32[16,5,128,128]{3,2,1,0:T(8,128)}, u32[]{:S(2)}, u32[]{:S(2)}) async-start(f32[16,5,128,128]{3,2,1,0:T(8,128)} %pack_rows.2.refs_0_.refs_1_.refs_2_), calls=%async_computation.3 | async-start | bytes 10485760 | tf_op jit(solution)/shard_map/all_to_all | solution.py:606
  234.8 6.0 %pack_second.1 = (f32[1280,128]{1,0:T(8,128)}, f32[1280,128]{1,0:T(8,128)}, f32[1280,128]{1,0:T(8,128)}, f32[1280,128]{1,0:T(8,128)}, f32[1280,128]{1,0:T(8,128)...) custom-call(s32[8]{0:T(128)} %and_select_fusion.1.refs_0_, f32[1280,1280]{1,0:T(8,128)} %refs_1_.5, ...), custom_call_target="tpu_custom_call" | custom-call | bytes 10485760 | tf_op jit(solution)/shard_map/pack_second/pallas_call | solution.py:36
  240.8 1.6 collective-permute-start.18
  242.4 1.8 collective-permute-start.20
  244.2 1.5 collective-permute-start.21
  245.7 2.5 collective-permute-start.22
  248.2 8.5 %collective-permute-done.18 = f32[1280,128]{1,0:T(8,128)S(1)} collective-permute-done((f32[1280,128]{1,0:T(8,128)}, f32[1280,128]{1,0:T(8,128)S(1)}, u32[]{:S(2)}, u32[]{:S(2)}) %collective-permute-start.18) | collective-permute-done | bytes 655392 | tf_op jit(solution)/shard_map/ppermute | solution.py:610
  256.7 2.0 collective-permute-start.23
  258.7 15.3 %collective-permute-done.19 = f32[1280,128]{1,0:T(8,128)S(1)} collective-permute-done((f32[1280,128]{1,0:T(8,128)}, f32[1280,128]{1,0:T(8,128)S(1)}, u32[]{:S(2)}, u32[]{:S(2)}) %collective-permute-start.19) | collective-permute-done | bytes 655392 | tf_op jit(solution)/shard_map/ppermute | solution.py:610
  274.0 23.5 %factor_lead.4.refs_0_ = f32[1024,1024]{1,0:T(8,128)} custom-call(f32[1024,1024]{1,0:T(8,128)} %all-gather.8.cloned.1.call-done.refs_0_, f32[128,1024]{1,0:T(8,128)} %assemble_strip.1.refs_1_), custom_call_target="tpu_custom_call" | custom-call | tf_op jit(solution)/shard_map/factor_lead/pallas_call | solution.py:360
  297.5 20.7 %factor_lead.5.refs_12_.refs_0_ = f32[1024,1024]{1,0:T(8,128)} custom-call(f32[1024,1024]{1,0:T(8,128)} %factor_lead.4.refs_0_, f32[16,5,128,128]{3,2,1,0:T(8,128)} %pack_rows.2.refs_0_.refs_1_.refs_2_), custom_call_target="tpu_custom_call" | custom-call | tf_op jit(solution)/shard_map/factor_lead/pallas_call | solution.py:360
  318.3 0.8 copy-done.5
  319.5 5.4 %pack_rows.3.refs_0_ = f32[16,5,128,128]{3,2,1,0:T(8,128)} custom-call(s32[16]{0:T(128)} %copy-done.12, s32[16]{0:T(128)} %convert_element_type.32.refs_1_, s32[5]{0:T(128)} %get-tuple-element.55.refs_2_, f32[8,10,128,128]{3,2,1,0:T(8,128)} %bitcast.8.refs_3_, f32[10,128,128]{2,1,0:T(8,128)} %bitcast.41, f32[10,128,128]{2,1,0:T(8,128)} %bitcast.42, ...), custom_call_target="tpu_custom_call" | custom-call | bytes 10485760 | tf_op jit(solution)/shard_map/pack_rows/pallas_call | solution.py:36
  324.9 8.3 %all-to-all-done.3.refs_1_.refs_0_.refs_2_ = f32[16,5,128,128]{3,2,1,0:T(8,128)} async-done(((f32[16,5,128,128]{3,2,1,0:T(8,128)}), f32[16,5,128,128]{3,2,1,0:T(8,128)}, u32[]{:S(2)}, u32[]{:S(2)}) %all-to-all-start.3) | async-done | bytes 5242912 | tf_op jit(solution)/shard_map/all_to_all | solution.py:606
  333.2 23.8 %all-to-all-start.4 = ((f32[16,5,128,128]{3,2,1,0:T(8,128)}), f32[16,5,128,128]{3,2,1,0:T(8,128)}, u32[]{:S(2)}, u32[]{:S(2)}) async-start(f32[16,5,128,128]{3,2,1,0:T(8,128)} %pass_on.1.refs_1_), calls=%async_computation.4 | async-start | bytes 10485760 | tf_op jit(solution)/shard_map/all_to_all | solution.py:617
  358.6 0.7 select_reduce_fusion.rank
  359.8 18.3 %factor_lead.6.refs_0_ = f32[1024,1024]{1,0:T(8,128)} custom-call(f32[1024,1024]{1,0:T(8,128)} %factor_lead.5.refs_12_.refs_0_, f32[16,5,128,128]{3,2,1,0:T(8,128)} %pass_on.1.refs_1_), custom_call_target="tpu_custom_call" | custom-call | tf_op jit(solution)/shard_map/factor_lead/pallas_call | solution.py:360
  378.1 16.6 %factor_lead.7 = (bf16[1024,1024]{1,0:T(8,128)(2,1)}, bf16[1024,1024]{1,0:T(8,128)(2,1)}) custom-call(f32[1024,1024]{1,0:T(8,128)} %factor_lead.6.refs_0_, f32[2048,1024]{1,0:T(8,128)} %all-gather.6.cloned.1.call-done.refs_1_.col_strip), custom_call_target="tpu_custom_call" | custom-call | tf_op jit(solution)/shard_map/factor_lead/pallas_call | solution.py:360
  394.6 33.4 %update_front.1.front = f32[1024,2048]{1,0:T(8,128)} custom-call(s32[2]{0:T(128)} %pad_add_fusion.flags, f32[1024,1024]{1,0:T(8,128)} %all-gather.4.cloned.1.call-done.row_strip, f32[2048,1024]{1,0:T(8,128)} %all-gather.6.cloned.1.call-done.refs_1_.col_strip, bf16[1024,1024]{1,0:T(8,128)(2,1)} %get-tuple-element.39.inv_hi, ...), custom_call_target="tpu_custom_call" | custom-call | flops 40000000000 | bytes 33554432 | tf_op jit(solution)/shard_map/update_front/pallas_call | solution.py:430
  428.1 12.7 %place_children.1 = f32[1024,2048]{1,0:T(8,128)} custom-call(s32[2,8]{1,0:T(2,128)} %fusion.18.source, s32[2,16]{1,0:T(2,128)} %select_reduce_fusion.rank, s32[2,128]{1,0:T(2,128)} %reshape.288.keep, f32[1024,2048]{1,0:T(8,128)} %update_front.1.front, f32[16,5,128,128]{3,2,1,0:T(8,128)} %all-to-all-done.3.refs_1_.refs_0_.refs_2_, ...), custom_call_target="tpu_custom_call", output_to_operand_aliasing={{}: (3, {})} | custom-call | bytes 25165824 | tf_op jit(solution)/shard_map/place_children/pallas_call | solution.py:478
  (91 shorter events, 9.0 us)
Async XLA Ops:
  6.5 5.8 %copy-start.11 = (s32[2,80]{1,0:T(2,128)S(1)}, s32[2,80]{1,0:T(2,128)}, u32[]{:S(2)}) copy-start(s32[2,80]{1,0:T(2,128)} %param.6) | copy-start | bytes 1924
  10.1 20.5 %copy-start.10 = (s32[2,80,80]{2,1,0:T(8,128)S(1)}, s32[2,80,80]{2,1,0:T(8,128)}, u32[]{:S(2)}) copy-start(s32[2,80,80]{2,1,0:T(8,128)} %param.7) | copy-start | bytes 153604
  10.1 16.9 %collective-permute-start = (f32[128,1024]{1,0:T(8,128)}, f32[128,1024]{1,0:T(8,128)S(1)}, u32[]{:S(2)}, u32[]{:S(2)}) collective-permute-start(f32[128,1024]{1,0:T(8,128)} %get-tuple-element.24), channel_id=1, source_target_pairs={{0,1},{8,9},{16,17},{24,25},{32,33},{40,41},{48,49},{56,57},{64,65... | collective-permute-start | bytes 1572872 | tf_op jit(solution)/shard_map/ppermute | solution.py:568
  11.6 16.9 %collective-permute-start.1 = (f32[128,1024]{1,0:T(8,128)}, f32[128,1024]{1,0:T(8,128)S(1)}, u32[]{:S(2)}, u32[]{:S(2)}) collective-permute-start(f32[128,1024]{1,0:T(8,128)} %get-tuple-element.25), channel_id=1, source_target_pairs={{0,2},{8,10},{16,18},{24,26},{32,34},{40,42},{48,50},{56,58},{64,6... | collective-permute-start | bytes 1572872 | tf_op jit(solution)/shard_map/ppermute | solution.py:568
  13.0 29.6 %copy-start.12 = (s32[16]{0:T(128)}, s32[16]{0:T(128)S(1)}, u32[]{:S(2)}) copy-start(s32[16]{0:T(128)S(1)} %get-tuple-element.42.refs_0_) | copy-start | bytes 196
  13.6 35.8 %copy-start.8 = (f32[128,1024]{1,0:T(8,128)S(1)}, f32[128,1024]{1,0:T(8,128)}, u32[]{:S(2)}) copy-start(f32[128,1024]{1,0:T(8,128)} %get-tuple-element.23) | copy-start | bytes 1572868
  16.6 21.8 %all-to-all-start = ((f32[16,128,128]{2,1,0:T(8,128)}), f32[16,128,128]{2,1,0:T(8,128)S(1)}, u32[]{:S(2)}, u32[]{:S(2)}) async-start(f32[16,128,128]{2,1,0:T(8,128)} %pack_early.1), calls=%async_computation | async-start | bytes 2097152 | tf_op jit(solution)/shard_map/all_to_all | solution.py:575
  23.4 26.0 %collective-permute-start.2 = (f32[128,1024]{1,0:T(8,128)}, f32[128,1024]{1,0:T(8,128)S(1)}, u32[]{:S(2)}, u32[]{:S(2)}) collective-permute-start(f32[128,1024]{1,0:T(8,128)} %get-tuple-element.26), channel_id=1, source_target_pairs={{0,3},{8,11},{16,19},{24,27},{32,35},{40,43},{48,51},{56,59},{64,6... | collective-permute-start | bytes 1572872 | tf_op jit(solution)/shard_map/ppermute | solution.py:568
  24.0 25.3 %collective-permute-start.3 = (f32[128,1024]{1,0:T(8,128)}, f32[128,1024]{1,0:T(8,128)}, u32[]{:S(2)}, u32[]{:S(2)}) collective-permute-start(f32[128,1024]{1,0:T(8,128)} %get-tuple-element.27), channel_id=1, source_target_pairs={{0,4},{8,12},{16,20},{24,28},{32,36},{40,44},{48,52},{56,60},{64,6... | collective-permute-start | bytes 1572872 | tf_op jit(solution)/shard_map/ppermute | solution.py:568
  25.5 23.8 %collective-permute-start.4 = (f32[128,1024]{1,0:T(8,128)}, f32[128,1024]{1,0:T(8,128)}, u32[]{:S(2)}, u32[]{:S(2)}) collective-permute-start(f32[128,1024]{1,0:T(8,128)} %get-tuple-element.28), channel_id=1, source_target_pairs={{0,5},{8,13},{16,21},{24,29},{32,37},{40,45},{48,53},{56,61},{64,6... | collective-permute-start | bytes 1572872 | tf_op jit(solution)/shard_map/ppermute | solution.py:568
  27.0 22.4 %collective-permute-start.5 = (f32[128,1024]{1,0:T(8,128)}, f32[128,1024]{1,0:T(8,128)}, u32[]{:S(2)}, u32[]{:S(2)}) collective-permute-start(f32[128,1024]{1,0:T(8,128)} %get-tuple-element.29), channel_id=1, source_target_pairs={{0,6},{8,14},{16,22},{24,30},{32,38},{40,46},{48,54},{56,62},{64,7... | collective-permute-start | bytes 1572872 | tf_op jit(solution)/shard_map/ppermute | solution.py:568
  28.5 20.9 %collective-permute-start.6 = (f32[128,1024]{1,0:T(8,128)}, f32[128,1024]{1,0:T(8,128)}, u32[]{:S(2)}, u32[]{:S(2)}) collective-permute-start(f32[128,1024]{1,0:T(8,128)} %get-tuple-element.30), channel_id=1, source_target_pairs={{0,7},{8,15},{16,23},{24,31},{32,39},{40,47},{48,55},{56,63},{64,7... | collective-permute-start | bytes 1572872 | tf_op jit(solution)/shard_map/ppermute | solution.py:568
  38.5 1.0 copy-start
  42.6 42.1 %all-to-all-start.1 = ((f32[16,128,128]{2,1,0:T(8,128)}), f32[16,128,128]{2,1,0:T(8,128)S(1)}, u32[]{:S(2)}, u32[]{:S(2)}) async-start(f32[16,128,128]{2,1,0:T(8,128)} %pick_early.1), calls=%async_computation.1 | async-start | bytes 2097152 | tf_op jit(solution)/shard_map/all_to_all | solution.py:577
  49.3 224.7 %all-gather.8.cloned.1.call-start = ((), (), s32[]{:S(2)}) async-start(), calls=%async_computation.7 | async-start | bytes 4456448 | tf_op jit(solution)/shard_map/all_gather | solution.py:599
  52.2 32.5 %collective-permute-start.7 = (f32[128,1024]{1,0:T(8,128)}, f32[128,1024]{1,0:T(8,128)S(1)}, u32[]{:S(2)}, u32[]{:S(2)}) collective-permute-start(f32[128,1024]{1,0:T(8,128)} %add_add_fusion), channel_id=1, source_target_pairs={{0,0},{1,8},{2,16},{3,24},{4,32},{5,40},{6,48},{7,56},{8,64},{9,72... | collective-permute-start | bytes 1572872 | tf_op jit(solution)/shard_map/ppermute | solution.py:572
  84.7 0.8 copy-start.9
  85.5 1.0 copy-start.1
  89.9 26.6 %collective-permute-start.8 = (f32[128,1024]{1,0:T(8,128)}, f32[128,1024]{1,0:T(8,128)S(1)}, u32[]{:S(2)}, u32[]{:S(2)}) collective-permute-start(f32[128,1024]{1,0:T(8,128)} %assemble_strip.1.refs_1_), channel_id=1, source_target_pairs={{0,0},{8,1},{16,2},{24,3},{32,4},{40,5},{48,6},{56,7},{64,8},{72,9... | collective-permute-start | bytes 1572872 | tf_op jit(solution)/shard_map/ppermute | solution.py:583
  92.9 1.4 collective-permute-start.10
  93.6 0.7 collective-permute-start.9
  116.6 0.9 copy-start.2
  119.1 5.6 %collective-permute-start.11 = (f32[64,1024]{1,0:T(8,128)}, f32[64,1024]{1,0:T(8,128)S(1)}, u32[]{:S(2)}, u32[]{:S(2)}) collective-permute-start(f32[64,1024]{1,0:T(8,128)} %hand_on.3), channel_id=1, source_target_pairs={{0,1},{8,9},{16,17},{24,25},{32,33},{40,41},{48,49},{56,57},{64,65... | collective-permute-start | bytes 786440 | tf_op jit(solution)/shard_map/ppermute | solution.py:596
  120.4 5.0 %collective-permute-start.12 = (f32[64,1024]{1,0:T(8,128)}, f32[64,1024]{1,0:T(8,128)S(1)}, u32[]{:S(2)}, u32[]{:S(2)}) collective-permute-start(f32[64,1024]{1,0:T(8,128)} %hand_on.3), channel_id=1, source_target_pairs={{0,2},{8,10},{16,18},{24,26},{32,34},{40,42},{48,50},{56,58},{64,6... | collective-permute-start | bytes 786440 | tf_op jit(solution)/shard_map/ppermute | solution.py:596
  121.1 5.0 %collective-permute-start.13 = (f32[64,1024]{1,0:T(8,128)}, f32[64,1024]{1,0:T(8,128)S(1)}, u32[]{:S(2)}, u32[]{:S(2)}) collective-permute-start(f32[64,1024]{1,0:T(8,128)} %hand_on.3), channel_id=1, source_target_pairs={{0,3},{8,11},{16,19},{24,27},{32,35},{40,43},{48,51},{56,59},{64,6... | collective-permute-start | bytes 786440 | tf_op jit(solution)/shard_map/ppermute | solution.py:596
  121.8 4.3 collective-permute-start.14
  122.5 3.6 collective-permute-start.15
  124.7 1.4 collective-permute-start.16
  125.4 0.7 collective-permute-start.17
  127.9 250.1 %all-gather.6.cloned.1.call-start = ((), (), s32[]{:S(2)}) async-start(), calls=%async_computation.6 | async-start | bytes 8912896 | tf_op jit(solution)/shard_map/all_gather | solution.py:601
  134.9 78.3 %all-to-all-start.2 = ((f32[8,1280,128]{2,1,0:T(8,128)}), f32[8,1280,128]{2,1,0:T(8,128)}, u32[]{:S(2)}, u32[]{:S(2)}) async-start(f32[8,1280,128]{2,1,0:T(8,128)} %pack_first.1), calls=%async_computation.2 | async-start | bytes 10485760 | tf_op jit(solution)/shard_map/all_to_all | solution.py:581
  153.0 241.6 %all-gather.4.cloned.1.call-start = ((), (), s32[]{:S(2)}) async-start(), calls=%async_computation.5 | async-start | bytes 4718592 | tf_op jit(solution)/shard_map/all_gather | solution.py:620
  220.2 113.0 %all-to-all-start.3 = ((f32[16,5,128,128]{3,2,1,0:T(8,128)}), f32[16,5,128,128]{3,2,1,0:T(8,128)}, u32[]{:S(2)}, u32[]{:S(2)}) async-start(f32[16,5,128,128]{3,2,1,0:T(8,128)} %pack_rows.2.refs_0_.refs_1_.refs_2_), calls=%async_computation.3 | async-start | bytes 10485760 | tf_op jit(solution)/shard_map/all_to_all | solution.py:606
  240.8 15.9 %collective-permute-start.18 = (f32[1280,128]{1,0:T(8,128)}, f32[1280,128]{1,0:T(8,128)S(1)}, u32[]{:S(2)}, u32[]{:S(2)}) collective-permute-start(f32[1280,128]{1,0:T(8,128)} %get-tuple-element.32), channel_id=1, source_target_pairs={{0,1},{1,2},{2,3},{3,4},{4,5},{5,6},{6,7},{7,0},{8,9},{9,10},{10,1... | collective-permute-start | bytes 1966088 | tf_op jit(solution)/shard_map/ppermute | solution.py:610
  242.4 31.6 %collective-permute-start.19 = (f32[1280,128]{1,0:T(8,128)}, f32[1280,128]{1,0:T(8,128)S(1)}, u32[]{:S(2)}, u32[]{:S(2)}) collective-permute-start(f32[1280,128]{1,0:T(8,128)} %get-tuple-element.33), channel_id=1, source_target_pairs={{0,2},{1,3},{2,4},{3,5},{4,6},{5,7},{6,0},{7,1},{8,10},{9,11},{10,... | collective-permute-start | bytes 1966088 | tf_op jit(solution)/shard_map/ppermute | solution.py:610
  242.4 75.8 %collective-permute-start.20 = (f32[1280,128]{1,0:T(8,128)}, f32[1280,128]{1,0:T(8,128)S(1)}, u32[]{:S(2)}, u32[]{:S(2)}) collective-permute-start(f32[1280,128]{1,0:T(8,128)} %get-tuple-element.34), channel_id=1, source_target_pairs={{0,3},{1,4},{2,5},{3,6},{4,7},{5,0},{6,1},{7,2},{8,11},{9,12},{10,... | collective-permute-start | bytes 1966088 | tf_op jit(solution)/shard_map/ppermute | solution.py:610
  244.2 74.0 %collective-permute-start.21 = (f32[1280,128]{1,0:T(8,128)}, f32[1280,128]{1,0:T(8,128)S(1)}, u32[]{:S(2)}, u32[]{:S(2)}) collective-permute-start(f32[1280,128]{1,0:T(8,128)} %get-tuple-element.35), channel_id=1, source_target_pairs={{0,4},{1,5},{2,6},{3,7},{4,0},{5,1},{6,2},{7,3},{8,12},{9,13},{10,... | collective-permute-start | bytes 1966088 | tf_op jit(solution)/shard_map/ppermute | solution.py:610
  245.7 72.5 %collective-permute-start.22 = (f32[1280,128]{1,0:T(8,128)}, f32[1280,128]{1,0:T(8,128)S(1)}, u32[]{:S(2)}, u32[]{:S(2)}) collective-permute-start(f32[1280,128]{1,0:T(8,128)} %get-tuple-element.36), channel_id=1, source_target_pairs={{0,5},{1,6},{2,7},{3,0},{4,1},{5,2},{6,3},{7,4},{8,13},{9,14},{10,... | collective-permute-start | bytes 1966088 | tf_op jit(solution)/shard_map/ppermute | solution.py:610
  256.7 61.5 %copy-start.3 = (f32[1280,128]{1,0:T(8,128)}, f32[1280,128]{1,0:T(8,128)S(1)}, u32[]{:S(2)}) copy-start(f32[1280,128]{1,0:T(8,128)S(1)} %collective-permute-done.18) | copy-start | bytes 1966084
  256.7 61.6 %collective-permute-start.23 = (f32[1280,128]{1,0:T(8,128)}, f32[1280,128]{1,0:T(8,128)}, u32[]{:S(2)}, u32[]{:S(2)}) collective-permute-start(f32[1280,128]{1,0:T(8,128)} %get-tuple-element.37), channel_id=1, source_target_pairs={{0,6},{1,7},{2,0},{3,1},{4,2},{5,3},{6,4},{7,5},{8,14},{9,15},{10,... | collective-permute-start | bytes 1966088 | tf_op jit(solution)/shard_map/ppermute | solution.py:610
  274.0 44.2 %copy-start.4 = (f32[1280,128]{1,0:T(8,128)}, f32[1280,128]{1,0:T(8,128)S(1)}, u32[]{:S(2)}) copy-start(f32[1280,128]{1,0:T(8,128)S(1)} %collective-permute-done.19) | copy-start | bytes 1966084
  274.0 44.3 %collective-permute-start.24 = (f32[1280,128]{1,0:T(8,128)}, f32[1280,128]{1,0:T(8,128)}, u32[]{:S(2)}, u32[]{:S(2)}) collective-permute-start(f32[1280,128]{1,0:T(8,128)} %get-tuple-element.38), channel_id=1, source_target_pairs={{0,7},{1,0},{2,1},{3,2},{4,3},{5,4},{6,5},{7,6},{8,15},{9,8},{10,9... | collective-permute-start | bytes 1966088 | tf_op jit(solution)/shard_map/ppermute | solution.py:610
  318.2 0.8 copy-start.5
  318.2 1.1 copy-start.6
  318.2 1.2 copy-start.7
  333.2 94.9 %all-to-all-start.4 = ((f32[16,5,128,128]{3,2,1,0:T(8,128)}), f32[16,5,128,128]{3,2,1,0:T(8,128)}, u32[]{:S(2)}, u32[]{:S(2)}) async-start(f32[16,5,128,128]{3,2,1,0:T(8,128)} %pass_on.1.refs_1_), calls=%async_computation.4 | async-start | bytes 10485760 | tf_op jit(solution)/shard_map/all_to_all | solution.py:617
Sparse Core Ops, SparseCore 0:
  128.1 70.7 all-gather.7
  201.0 125.3 all-gather.5
  328.1 38.1 all-gather.3
